TPU v7x, 32 devices: a whole 2x2x4 slice. The times are simulated.
32 devices in a mesh: row: 4 (over z), head: 8 (over y, x, core).
Axes of the slice: x: 2, y: 2, z: 4, core: 2. Of those that a mesh axis runs over, the one named last changes fastest.
Arguments:
- layer_in: bfloat16 [8192, 2048], P(('row', 'head')), may hold values from -6 to 6
- cotangent: bfloat16 [8192, 2048], P(('row', 'head')), may hold values from -6 to 6
- mix_gain: bfloat16 [2048], P(('row', 'head')), may hold values from 0.5 to 1.5
- ffn_gain: bfloat16 [2048], P(('row', 'head')), may hold values from 0.5 to 1.5
- x_weight: bfloat16 [2048, 2736], P('row', 'head'), may hold values from -0.125 to 0.125
- y_weight: bfloat16 [2048, 2736], P('row', 'head'), may hold values from -0.125 to 0.125
- out_weight: bfloat16 [2048, 2736], P('row', 'head'), may hold values from -0.4375 to 0.4375
- conv_weight: float32 [4, 2736], P(None, 'head'), may hold values from -3 to 3
- conv_bias: float32 [2736], P('head'), may hold values from -3 to 3
- rate_weight: bfloat16 [16, 171, 171], P('head'), may hold values from -0.4375 to 0.4375
- rate_bias: float32 [2736], P('head'), may hold values from -3 to 3
- entry_weight: bfloat16 [16, 171, 171], P('head'), may hold values from -0.4375 to 0.4375
- entry_bias: float32 [2736], P('head'), may hold values from -3 to 3
- decay_param: float32 [2736], P('head'), may hold values from 2 to 6
- gate_weight: bfloat16 [2048, 6144], P('row', 'head'), may hold values from -0.125 to 0.125
- up_weight: bfloat16 [2048, 6144], P('row', 'head'), may hold values from -0.125 to 0.125
- down_weight: bfloat16 [2048, 6144], P('row', 'head'), may hold values from -0.109375 to 0.109375
- resets: int32 [4, 2048], P('row'), may hold values 0 or 1
Outputs:
- layer_out: bfloat16 [8192, 2048], P(('row', 'head'))
- layer_in_grad: bfloat16 [8192, 2048], P(('row', 'head'))
- mix_gain_grad: float32 [2048], P(('row', 'head'))
- ffn_gain_grad: float32 [2048], P(('row', 'head'))
- x_weight_grad: float32 [2048, 2736], P('row', 'head')
- y_weight_grad: float32 [2048, 2736], P('row', 'head')
- out_weight_grad: float32 [2048, 2736], P('row', 'head')
- conv_weight_grad: float32 [4, 2736], P(None, 'head')
- conv_bias_grad: float32 [2736], P('head')
- rate_weight_grad: float32 [16, 171, 171], P('head')
- rate_bias_grad: float32 [2736], P('head')
- entry_weight_grad: float32 [16, 171, 171], P('head')
- entry_bias_grad: float32 [2736], P('head')
- decay_param_grad: float32 [2736], P('head')
- gate_weight_grad: float32 [2048, 6144], P('row', 'head')
- up_weight_grad: float32 [2048, 6144], P('row', 'head')
- down_weight_grad: float32 [2048, 6144], P('row', 'head')
Inputs may be any that keep to these rules, and one draw needn't show every extreme that they name: resets[s, t] = 1 marks a document that starts at position t of sequence s; position 0 starts a document whatever resets holds there.
All inputs are finite; a program needn't handle non-finite values. No bound on the sum of `resets` on one device may be relied on, other than what follows from the above.
Results may differ from a plain program's by a relative error of at most 0.015.
Values may be sent and summed in bfloat16 or wider, within the bound.
A program may use at most 576 MiB of HBM per device.

v0:
```python
import jax
import jax.numpy as jnp
from jax import lax
from jax.sharding import PartitionSpec as P

EPSILON = 1e-06


def norm_apply(rows, gain):
    return rows * lax.rsqrt(jnp.mean(rows * rows, axis=-1, keepdims=True) + EPSILON) * gain


def combine(earlier, later):
    return (earlier[0] * later[0], later[0] * earlier[1] + later[1])


def run_mixer(
    flat_values,
    conv_weight,
    conv_bias,
    rate_weight,
    rate_bias,
    entry_weight,
    entry_bias,
    decay_param,
    resets,
):
    seqs_here, length = resets.shape
    channels = conv_bias.shape[0]
    heads_here = rate_weight.shape[0]
    values = flat_values.reshape(seqs_here, length, channels)
    position = lax.broadcasted_iota(jnp.int32, (seqs_here, length), 1)
    starts = jnp.maximum(resets, (position == 0).astype(jnp.int32)).astype(jnp.float32)
    carried = 1.0 - starts

    def conv_part(inputs, conv_taps, conv_shift):
        convolved = conv_taps[0] * inputs + conv_shift
        within = jnp.ones_like(carried)
        for offset in range(1, conv_taps.shape[0]):
            within = within * jnp.pad(carried, ((0, 0), (offset - 1, 0)))[:, :length]
            shifted = jnp.pad(inputs, ((0, 0), (offset, 0), (0, 0)))[:, :length]
            convolved = convolved + conv_taps[offset] * within[:, :, None] * shifted
        return convolved

    convolved, conv_back = jax.vjp(conv_part, values, conv_weight, conv_bias)
    conv_low = convolved.astype(jnp.bfloat16).reshape(seqs_here, length, heads_here, -1)
    raw_rate = jnp.einsum(
        "slhi,hij->slhj", conv_low, rate_weight, preferred_element_type=jnp.float32
    ).reshape(seqs_here, length, channels)
    raw_entry = jnp.einsum(
        "slhi,hij->slhj", conv_low, entry_weight, preferred_element_type=jnp.float32
    ).reshape(seqs_here, length, channels)

    def gate_part(rate_in, entry_in, conv_in, rate_shift, entry_shift, decay_values):
        pre_rate = rate_in + rate_shift
        pre_entry = entry_in + entry_shift
        log_decay = -8.0 * jax.nn.sigmoid(pre_rate) * jax.nn.softplus(-decay_values)
        decays = jnp.exp(log_decay) * carried[:, :, None]
        scaling = starts[:, :, None] + carried[:, :, None] * jnp.sqrt(-jnp.expm1(2.0 * log_decay))
        driven = scaling * jax.nn.sigmoid(pre_entry) * conv_in
        unused, states = lax.associative_scan(combine, (decays, driven), axis=1)
        return states

    states, gate_back = jax.vjp(
        gate_part, raw_rate, raw_entry, convolved, rate_bias, entry_bias, decay_param
    )

    def backward(d_states):
        grads = gate_back(d_states.reshape(seqs_here, length, channels))
        g_rate = grads[0].astype(jnp.bfloat16).reshape(seqs_here, length, heads_here, -1)
        g_entry = grads[1].astype(jnp.bfloat16).reshape(seqs_here, length, heads_here, -1)
        rate_grad = jnp.einsum(
            "slhi,slhj->hij", conv_low, g_rate, preferred_element_type=jnp.float32
        )
        entry_grad = jnp.einsum(
            "slhi,slhj->hij", conv_low, g_entry, preferred_element_type=jnp.float32
        )
        through = jnp.einsum(
            "slhj,hij->slhi", g_rate, rate_weight, preferred_element_type=jnp.float32
        ) + jnp.einsum("slhj,hij->slhi", g_entry, entry_weight, preferred_element_type=jnp.float32)
        d_conv = grads[2] + through.reshape(seqs_here, length, channels)
        d_values, d_taps, d_shift = conv_back(d_conv)
        return (
            d_values.reshape(seqs_here * length, channels),
            d_taps,
            d_shift,
            rate_grad,
            grads[3],
            entry_grad,
            grads[4],
            grads[5],
        )

    return (states.reshape(seqs_here * length, channels), backward)


def contract_last(left, right):
    return lax.dot_general(
        left, right, (((1,), (1,)), ((), ())), preferred_element_type=jnp.float32
    )


def contract_first(left, right):
    return lax.dot_general(
        left, right, (((0,), (0,)), ((), ())), preferred_element_type=jnp.float32
    )


def shards(
    layer_in,
    cotangent,
    mix_gain,
    ffn_gain,
    x_weight,
    y_weight,
    out_weight,
    conv_weight,
    conv_bias,
    rate_weight,
    rate_bias,
    entry_weight,
    entry_bias,
    decay_param,
    gate_weight,
    up_weight,
    down_weight,
    resets,
):
    mix_full, ffn_full = (
        lax.all_gather(mix_gain, ("row", "head"), axis=0, tiled=True),
        lax.all_gather(ffn_gain, ("row", "head"), axis=0, tiled=True),
    )
    x_rows, y_rows, out_rows, gate_rows, up_rows, down_rows = (
        lax.all_gather(x_weight, "row", axis=0, tiled=True),
        lax.all_gather(y_weight, "row", axis=0, tiled=True),
        lax.all_gather(out_weight, "row", axis=0, tiled=True),
        lax.all_gather(gate_weight, "row", axis=0, tiled=True),
        lax.all_gather(up_weight, "row", axis=0, tiled=True),
        lax.all_gather(down_weight, "row", axis=0, tiled=True),
    )
    inputs = layer_in.astype(jnp.float32)
    normed_f, norm_back_one = jax.vjp(norm_apply, inputs, mix_full.astype(jnp.float32))
    normed = normed_f.astype(jnp.bfloat16)
    normed_group = lax.all_gather(normed, "head", axis=0, tiled=True)
    branch_x = jnp.dot(normed_group, x_rows, preferred_element_type=jnp.float32).astype(
        jnp.bfloat16
    )
    branch_y = jnp.dot(normed_group, y_rows, preferred_element_type=jnp.float32)
    states, mixer_back = run_mixer(
        branch_x.astype(jnp.float32),
        conv_weight,
        conv_bias,
        rate_weight,
        rate_bias,
        entry_weight,
        entry_bias,
        decay_param,
        resets,
    )
    gelu_y, gelu_back = jax.vjp(jax.nn.gelu, branch_y)
    states_f = states.astype(jnp.bfloat16).astype(jnp.float32)
    mixed = (states_f * gelu_y).astype(jnp.bfloat16)
    residual = inputs + lax.psum_scatter(
        contract_last(mixed, out_rows), "head", scatter_dimension=0, tiled=True
    )
    normed_two_f, norm_back_two = jax.vjp(norm_apply, residual, ffn_full.astype(jnp.float32))
    normed_two = normed_two_f.astype(jnp.bfloat16)
    gate_full, up_full, down_full = (
        lax.all_gather(gate_rows, "head", axis=1, tiled=True),
        lax.all_gather(up_rows, "head", axis=1, tiled=True),
        lax.all_gather(down_rows, "head", axis=1, tiled=True),
    )
    gates = jnp.dot(normed_two, gate_full, preferred_element_type=jnp.float32)
    up_proj = jnp.dot(normed_two, up_full, preferred_element_type=jnp.float32)
    activated, gelu_back_two = jax.vjp(jax.nn.gelu, gates)
    hidden = (activated * up_proj).astype(jnp.bfloat16)
    ffn_result = contract_last(hidden, down_full)
    layer_out = (residual + ffn_result).astype(jnp.bfloat16)
    d_hidden = jnp.dot(cotangent, down_full, preferred_element_type=jnp.float32)
    d_gates = gelu_back_two(d_hidden * up_proj)[0].astype(jnp.bfloat16)
    d_ups = (d_hidden * activated).astype(jnp.bfloat16)
    d_normed_two = contract_last(d_gates, gate_full) + contract_last(d_ups, up_full)
    gate_grad = contract_first(normed_two, d_gates)
    up_grad = contract_first(normed_two, d_ups)
    down_grad = contract_first(cotangent, hidden)
    gate_grad, up_grad, down_grad = (
        lax.psum_scatter(
            gate_grad.astype(jnp.bfloat16), "head", scatter_dimension=1, tiled=True
        ).astype(jnp.float32),
        lax.psum_scatter(
            up_grad.astype(jnp.bfloat16), "head", scatter_dimension=1, tiled=True
        ).astype(jnp.float32),
        lax.psum_scatter(
            down_grad.astype(jnp.bfloat16), "head", scatter_dimension=1, tiled=True
        ).astype(jnp.float32),
    )
    d_resid_norm, d_ffn_gain = norm_back_two(d_normed_two)
    d_residual = cotangent.astype(jnp.float32) + d_resid_norm
    d_res_low = d_residual.astype(jnp.bfloat16)
    d_res_group = lax.all_gather(d_res_low, "head", axis=0, tiled=True)
    d_mixed = jnp.dot(d_res_group, out_rows, preferred_element_type=jnp.float32)
    out_grad = contract_first(d_res_group, mixed)
    d_states = (d_mixed * gelu_y).astype(jnp.bfloat16)
    d_branch_y = gelu_back(d_mixed * states_f)[0].astype(jnp.bfloat16)
    mixer_grads = mixer_back(d_states.astype(jnp.float32))
    d_branch_x = mixer_grads[0].astype(jnp.bfloat16)
    d_normed = lax.psum_scatter(
        (contract_last(d_branch_x, x_rows) + contract_last(d_branch_y, y_rows)).astype(
            jnp.bfloat16
        ),
        "head",
        scatter_dimension=0,
        tiled=True,
    ).astype(jnp.float32)
    x_grad = contract_first(normed_group, d_branch_x)
    y_grad = contract_first(normed_group, d_branch_y)
    head_parts = (
        lax.psum(mixer_grads[1].astype(jnp.bfloat16), "row").astype(jnp.float32),
        lax.psum(mixer_grads[2].astype(jnp.bfloat16), "row").astype(jnp.float32),
        lax.psum(mixer_grads[3].astype(jnp.bfloat16), "row").astype(jnp.float32),
        lax.psum(mixer_grads[4].astype(jnp.bfloat16), "row").astype(jnp.float32),
        lax.psum(mixer_grads[5].astype(jnp.bfloat16), "row").astype(jnp.float32),
        lax.psum(mixer_grads[6].astype(jnp.bfloat16), "row").astype(jnp.float32),
        lax.psum(mixer_grads[7].astype(jnp.bfloat16), "row").astype(jnp.float32),
    )
    d_inputs, d_mix_gain = norm_back_one(d_normed)
    layer_in_grad = (d_inputs + d_residual).astype(jnp.bfloat16)
    x_part, y_part, out_part, gate_part, up_part, down_part = (
        lax.psum_scatter(
            x_grad.astype(jnp.bfloat16), "row", scatter_dimension=0, tiled=True
        ).astype(jnp.float32),
        lax.psum_scatter(
            y_grad.astype(jnp.bfloat16), "row", scatter_dimension=0, tiled=True
        ).astype(jnp.float32),
        lax.psum_scatter(
            out_grad.astype(jnp.bfloat16), "row", scatter_dimension=0, tiled=True
        ).astype(jnp.float32),
        lax.psum_scatter(
            gate_grad.astype(jnp.bfloat16), "row", scatter_dimension=0, tiled=True
        ).astype(jnp.float32),
        lax.psum_scatter(
            up_grad.astype(jnp.bfloat16), "row", scatter_dimension=0, tiled=True
        ).astype(jnp.float32),
        lax.psum_scatter(
            down_grad.astype(jnp.bfloat16), "row", scatter_dimension=0, tiled=True
        ).astype(jnp.float32),
    )
    mix_part, ffn_part = (
        lax.psum_scatter(d_mix_gain, ("row", "head"), scatter_dimension=0, tiled=True),
        lax.psum_scatter(d_ffn_gain, ("row", "head"), scatter_dimension=0, tiled=True),
    )
    return (
        layer_out,
        layer_in_grad,
        mix_part,
        ffn_part,
        x_part,
        y_part,
        out_part,
        head_parts[0],
        head_parts[1],
        head_parts[2],
        head_parts[3],
        head_parts[4],
        head_parts[5],
        head_parts[6],
        gate_part,
        up_part,
        down_part,
    )


def solution(mesh):
    return jax.shard_map(
        shards,
        mesh=mesh,
        in_specs=(
            P(("row", "head"), None),
            P(("row", "head"), None),
            P(("row", "head")),
            P(("row", "head")),
            P("row", "head"),
            P("row", "head"),
            P("row", "head"),
            P(None, "head"),
            P("head"),
            P("head", None, None),
            P("head"),
            P("head", None, None),
            P("head"),
            P("head"),
            P("row", "head"),
            P("row", "head"),
            P("row", "head"),
            P("row", None),
        ),
        out_specs=(
            P(("row", "head"), None),
            P(("row", "head"), None),
            P(("row", "head")),
            P(("row", "head")),
            P("row", "head"),
            P("row", "head"),
            P("row", "head"),
            P(None, "head"),
            P("head"),
            P("head", None, None),
            P("head"),
            P("head", None, None),
            P("head"),
            P("head"),
            P("row", "head"),
            P("row", "head"),
            P("row", "head"),
        ),
        check_vma=False,
    )
```

profile of v0, /device:TPU:0, one launch (start us, length us, event | category | flops | bytes accessed | tf_op | source)
XLA Modules:
  0.0 3137.5 jit_solution(354809961635998092)
XLA Ops:
  63.1 50.0 %all-gather.12.cloned.1.call-done = bf16[2048,2048]{1,0:T(8,128)(2,1)} async-done(((bf16[256,2048]{1,0:T(8,128)(2,1)}), bf16[2048,2048]{1,0:T(8,128)(2,1)}) %all-gather.12.cloned.1.call-update) | async-done | bytes 8388624 | tf_op jit(solution)/shard_map/all_gather | solution.py:144
  146.5 49.7 %slice.380 = f32[1,1024,342]{1,2,0:T(8,128)} slice(f32[1,2048,342]{1,2,0:T(8,128)} %get-tuple-element.153), slice={[0:1:1], [0:2047:2], [0:342:1]} | slice | bytes 2801664 | tf_op jit(solution)/shard_map/jvp()/slice | solution.py:61
  196.3 49.3 %slice.381 = f32[1,1024,342]{1,2,0:T(8,128)} slice(f32[1,2048,342]{1,2,0:T(8,128)S(1)} %copy-done.18), slice={[0:1:1], [1:2048:2], [0:342:1]} | slice | bytes 2801664 | tf_op jit(solution)/shard_map/jvp()/slice | solution.py:61
  245.5 49.2 %slice.379 = f32[1,1024,342]{1,2,0:T(8,128)S(1)} slice(f32[1,2048,342]{1,2,0:T(8,128)} %get-tuple-element.152), slice={[0:1:1], [1:2048:2], [0:342:1]} | slice | bytes 2801664 | tf_op jit(solution)/shard_map/jvp()/slice | solution.py:61
  294.7 49.8 %slice.383 = f32[1,1024,342]{1,2,0:T(8,128)} slice(f32[1,2048,342]{1,2,0:T(8,128)} %get-tuple-element.152), slice={[0:1:1], [0:2047:2], [0:342:1]} | slice | bytes 2801664 | tf_op jit(solution)/shard_map/jvp()/slice | solution.py:61
  739.3 49.5 %slice.378 = f32[1,1023,342]{1,2,0:T(8,128)} slice(f32[1,2048,342]{1,2,0:T(8,128)} %get-tuple-element.152), slice={[0:1:1], [2:2048:2], [0:342:1]} | slice | bytes 2798928 | tf_op jit(solution)/shard_map/jvp()/slice | solution.py:61
  788.8 49.2 %slice.459 = f32[1,1023,342]{1,2,0:T(8,128)} slice(f32[1,2048,342]{1,2,0:T(8,128)S(1)} %copy-done.19), slice={[0:1:1], [2:2048:2], [0:342:1]} | slice | bytes 2798928 | tf_op jit(solution)/shard_map/jvp()/slice | solution.py:61
  948.3 55.9 %pad.490 = f32[1,2048,342]{1,2,0:T(8,128)} pad(f32[1,1024,342]{1,2,0:T(8,128)} %add.652, f32[]{:T(128)} %constant.17.clone.1), padding=0_0_0x1_0_1x0_0_0 | pad | bytes 4202500 | tf_op jit(solution)/shard_map/jvp()/pad | solution.py:61
  1008.2 56.0 %pad.489 = f32[1,2048,342]{1,2,0:T(8,128)} pad(f32[1,1024,342]{1,2,0:T(8,128)} %pad_maximum_fusion, f32[]{:T(128)} %constant.17.clone.1), padding=0_0_0x0_1_1x0_0_0 | pad | bytes 4202500 | tf_op jit(solution)/shard_map/jvp()/pad | solution.py:61
  1091.6 114.0 %reduce-scatter.12.cloned.1.call-done = f32[256,2048]{1,0:T(8,128)} async-done(((f32[2048,2048]{1,0:T(8,128)}), f32[256,2048]{1,0:T(8,128)}) %reduce-scatter.12.cloned.1.call-update) | async-done | bytes 2097168 | tf_op jit(solution)/shard_map/reduce_scatter | solution.py:163
  1207.8 124.5 %all-gather.22.cloned.1.call-done = bf16[2048,6144]{1,0:T(8,128)(2,1)} async-done(((bf16[2048,768]{1,0:T(8,128)(2,1)}), bf16[2048,6144]{1,0:T(8,128)(2,1)}) %all-gather.22.cloned.1.call-update) | async-done | bytes 25165840 | tf_op jit(solution)/shard_map/all_gather | solution.py:169
  1347.4 111.5 %all-gather.26.cloned.1.call-done = bf16[2048,6144]{1,0:T(8,128)(2,1)} async-done(((bf16[2048,768]{1,0:T(8,128)(2,1)}), bf16[2048,6144]{1,0:T(8,128)(2,1)}) %all-gather.26.cloned.1.call-update) | async-done | bytes 25165840 | tf_op jit(solution)/shard_map/all_gather | solution.py:170
  1473.8 111.8 %all-gather.30.cloned.1.call-done = bf16[2048,6144]{1,0:T(8,128)(2,1)} async-done(((bf16[2048,768]{1,0:T(8,128)(2,1)}), bf16[2048,6144]{1,0:T(8,128)(2,1)}) %all-gather.30.cloned.1.call-update) | async-done | bytes 25165840 | tf_op jit(solution)/shard_map/all_gather | solution.py:171
  1708.4 50.1 %slice.460 = f32[1,1024,342]{1,2,0:T(8,128)} slice(f32[1,2047,342]{1,2,0:T(8,128)} %get-tuple-element.157), slice={[0:1:1], [0:2047:2], [0:342:1]} | slice | bytes 2801664 | tf_op jit(solution)/shard_map/transpose(jvp())/slice | solution.py:61
  1758.5 49.6 %slice.461 = f32[1,1024,342]{1,2,0:T(8,128)} slice(f32[1,2047,342]{1,2,0:T(8,128)} %get-tuple-element.158), slice={[0:1:1], [0:2047:2], [0:342:1]} | slice | bytes 2801664 | tf_op jit(solution)/shard_map/transpose(jvp())/slice | solution.py:61
  2111.7 52.0 %pad.563 = f32[1,2048,342]{1,2,0:T(8,128)} pad(f32[1,1024,342]{1,2,0:T(8,128)S(1)} %get-tuple-element.120, f32[]{:T(128)} %constant.17.clone.1), padding=0_0_0x1_0_1x0_0_0 | pad | bytes 4202500 | tf_op jit(solution)/shard_map/transpose(jvp())/pad | solution.py:61
  2163.7 55.9 %pad.564 = f32[1,2048,342]{1,2,0:T(8,128)} pad(f32[1,1024,342]{1,2,0:T(8,128)} %get-tuple-element.119, f32[]{:T(128)} %constant.17.clone.1), padding=0_0_0x0_1_1x0_0_0 | pad | bytes 4202500 | tf_op jit(solution)/shard_map/transpose(jvp())/pad | solution.py:61
  2219.7 55.7 %pad.493 = f32[1,2048,342]{1,2,0:T(8,128)} pad(f32[1,1023,342]{1,2,0:T(8,128)} %get-tuple-element.161, f32[]{:T(128)} %constant.17.clone.1), padding=0_0_0x2_1_1x0_0_0 | pad | bytes 4201132 | tf_op jit(solution)/shard_map/transpose(jvp())/pad | solution.py:61
  2510.2 55.7 %pad.594 = f32[1,2048,342]{1,2,0:T(8,128)} pad(f32[1,1024,342]{1,2,0:T(8,128)} %get-tuple-element.150, f32[]{:T(128)} %constant.17.clone.1), padding=0_0_0x1_0_1x0_0_0 | pad | bytes 4202500 | tf_op jit(solution)/shard_map/transpose(jvp())/pad | solution.py:61
  2566.0 52.0 %pad.595 = f32[1,2048,342]{1,2,0:T(8,128)} pad(f32[1,1024,342]{1,2,0:T(8,128)S(1)} %copy-done.46, f32[]{:T(128)} %constant.17.clone.1), padding=0_0_0x0_1_1x0_0_0 | pad | bytes 4202500 | tf_op jit(solution)/shard_map/transpose(jvp())/pad | solution.py:61
  2618.0 56.1 %pad.565 = f32[1,2048,342]{1,2,0:T(8,128)} pad(f32[1,1023,342]{1,2,0:T(8,128)} %get-tuple-element.163, f32[]{:T(128)} %constant.17.clone.1), padding=0_0_0x2_1_1x0_0_0 | pad | bytes 4201132 | tf_op jit(solution)/shard_map/transpose(jvp())/pad | solution.py:61
  2867.5 71.6 %reduce-scatter.14.cloned.1.call-done = bf16[256,2048]{1,0:T(8,128)(2,1)} async-done(((bf16[2048,2048]{1,0:T(8,128)(2,1)}), bf16[256,2048]{1,0:T(8,128)(2,1)}) %reduce-scatter.14.cloned.1.call-update) | async-done | bytes 1048592 | tf_op jit(solution)/shard_map/reduce_scatter | solution.py:207
  3005.1 60.3 %reduce-scatter.28.cloned.1.call-done = bf16[512,768]{1,0:T(8,128)(2,1)} async-done(((bf16[2048,768]{1,0:T(8,128)(2,1)}), bf16[512,768]{1,0:T(8,128)(2,1)}) %reduce-scatter.28.cloned.1.call-update) | async-done | bytes 786448 | tf_op jit(solution)/shard_map/reduce_scatter | solution.py:241
  3067.8 60.3 %reduce-scatter.32.cloned.1.call-done = bf16[512,768]{0,1:T(8,128)(2,1)} async-done(((bf16[2048,768]{0,1:T(8,128)(2,1)}), bf16[512,768]{0,1:T(8,128)(2,1)}) %reduce-scatter.32.cloned.1.call-update) | async-done | bytes 786448 | tf_op jit(solution)/shard_map/reduce_scatter | solution.py:244
  (809 shorter events, 1580.4 us)
Async XLA Ops:
  7.2 55.9 %all-gather.14.cloned.1.call-start = ((), (), s32[]{:S(2)}) async-start(), calls=%async_computation.12 | async-start | bytes 1761280 | tf_op jit(solution)/shard_map/all_gather | solution.py:134
  7.9 105.2 %all-gather.12.cloned.1.call-start = ((), (), s32[]{:S(2)}) async-start(), calls=%async_computation.11 | async-start | bytes 9437184 | tf_op jit(solution)/shard_map/all_gather | solution.py:144
  59.0 1008.7 %all-gather.16.cloned.1.call-start = ((), (), s32[]{:S(2)}) async-start(), calls=%async_computation.13 | async-start | bytes 1761280 | tf_op jit(solution)/shard_map/all_gather | solution.py:135
  59.7 1016.6 %all-gather.18.cloned.1.call-start = ((), (), s32[]{:S(2)}) async-start(), calls=%async_computation.14 | async-start | bytes 1761280 | tf_op jit(solution)/shard_map/all_gather | solution.py:136
  60.3 1029.2 %all-gather.20.cloned.1.call-start = ((), (), s32[]{:S(2)}) async-start(), calls=%async_computation.16 | async-start | bytes 3932160 | tf_op jit(solution)/shard_map/all_gather | solution.py:137
  60.9 1029.4 %all-gather.24.cloned.1.call-start = ((), (), s32[]{:S(2)}) async-start(), calls=%async_computation.18 | async-start | bytes 3932160 | tf_op jit(solution)/shard_map/all_gather | solution.py:138
  61.4 1029.4 %all-gather.28.cloned.1.call-start = ((), (), s32[]{:S(2)}) async-start(), calls=%async_computation.20 | async-start | bytes 3932160 | tf_op jit(solution)/shard_map/all_gather | solution.py:139
  62.2 1143.4 %reduce-scatter.12.cloned.1.call-start = ((), (), s32[]{:S(2)}) async-start(), calls=%async_computation.15 | async-start | bytes 18874368 | tf_op jit(solution)/shard_map/reduce_scatter | solution.py:163
  1089.5 242.8 %all-gather.22.cloned.1.call-start = ((), (), s32[]{:S(2)}) async-start(), calls=%async_computation.17 | async-start | bytes 28311552 | tf_op jit(solution)/shard_map/all_gather | solution.py:169
  1090.2 368.6 %all-gather.26.cloned.1.call-start = ((), (), s32[]{:S(2)}) async-start(), calls=%async_computation.19 | async-start | bytes 28311552 | tf_op jit(solution)/shard_map/all_gather | solution.py:170
  1090.8 494.8 %all-gather.30.cloned.1.call-start = ((), (), s32[]{:S(2)}) async-start(), calls=%async_computation.21 | async-start | bytes 28311552 | tf_op jit(solution)/shard_map/all_gather | solution.py:171
  1091.5 602.1 %all-gather.32.cloned.1.call-start = ((), (), s32[]{:S(2)}) async-start(), calls=%async_computation.22 | async-start | bytes 9437184 | tf_op jit(solution)/shard_map/all_gather | solution.py:200
  1091.6 543.3 %copy-start.171 = (f32[2048]{0:T(1024)}, f32[2048]{0:T(1024)S(1)}, u32[]{:S(2)}) copy-start(f32[2048]{0:T(1024)S(1)} %convert_element_type.209) | copy-start | bytes 24580
  1639.1 1138.5 %reduce-scatter.22.cloned.1.call-start = ((), (), s32[]{:S(2)}) async-start(), calls=%async_computation.27 | async-start | bytes 28311552 | tf_op jit(solution)/shard_map/reduce_scatter | solution.py:187
  1653.6 1124.7 %reduce-scatter.26.cloned.1.call-start = ((), (), s32[]{:S(2)}) async-start(), calls=%async_computation.29 | async-start | bytes 28311552 | tf_op jit(solution)/shard_map/reduce_scatter | solution.py:190
  1668.6 1110.5 %reduce-scatter.30.cloned.1.call-start = ((), (), s32[]{:S(2)}) async-start(), calls=%async_computation.31 | async-start | bytes 28311552 | tf_op jit(solution)/shard_map/reduce_scatter | solution.py:193
  1683.9 1124.6 %all-reduce.127.cloned.1.call-start = ((), (), s32[]{:S(2)}) async-start(), calls=%async_computation.33 | async-start | bytes 720896 | tf_op jit(solution)/shard_map/psum | solution.py:220
  2725.1 87.0 %reduce-scatter.16.cloned.1.call-start = ((), (), s32[]{:S(2)}) async-start(), calls=%async_computation.24 | async-start | bytes 1761280 | tf_op jit(solution)/shard_map/reduce_scatter | solution.py:229
  2740.2 90.8 %reduce-scatter.20.cloned.1.call-start = ((), (), s32[]{:S(2)}) async-start(), calls=%async_computation.26 | async-start | bytes 1761280 | tf_op jit(solution)/shard_map/reduce_scatter | solution.py:235
  2749.1 116.5 %reduce-scatter.18.cloned.1.call-start = ((), (), s32[]{:S(2)}) async-start(), calls=%async_computation.25 | async-start | bytes 1761280 | tf_op jit(solution)/shard_map/reduce_scatter | solution.py:232
  2757.0 182.1 %reduce-scatter.14.cloned.1.call-start = ((), (), s32[]{:S(2)}) async-start(), calls=%async_computation.23 | async-start | bytes 9437184 | tf_op jit(solution)/shard_map/reduce_scatter | solution.py:207
  2777.5 225.3 %reduce-scatter.24.cloned.1.call-start = ((), (), s32[]{:S(2)}) async-start(), calls=%async_computation.28 | async-start | bytes 3932160 | tf_op jit(solution)/shard_map/reduce_scatter | solution.py:238
  2778.2 287.2 %reduce-scatter.28.cloned.1.call-start = ((), (), s32[]{:S(2)}) async-start(), calls=%async_computation.30 | async-start | bytes 3932160 | tf_op jit(solution)/shard_map/reduce_scatter | solution.py:241
  2779.0 349.2 %reduce-scatter.32.cloned.1.call-start = ((), (), s32[]{:S(2)}) async-start(), calls=%async_computation.32 | async-start | bytes 3932160 | tf_op jit(solution)/shard_map/reduce_scatter | solution.py:244
  (204 other events, 6322.4 us)
Sparse Core Ops, SparseCore 0:
  9.6 38.1 all-gather.13
  59.1 54.0 all-gather.11
  114.7 34.3 all-gather.15
  150.6 33.2 all-gather.17
  185.3 62.4 all-gather.19
  249.2 62.1 all-gather.23
  312.9 62.1 all-gather.27
  1089.6 115.9 reduce-scatter.11
  1207.5 124.7 all-gather.21
  1334.0 124.7 all-gather.25
  1460.8 124.7 all-gather.29
  1639.2 54.3 all-gather.31
  1697.2 156.8 reduce-scatter.21
  1857.6 156.8 reduce-scatter.25
  2018.0 156.8 reduce-scatter.29
  2725.2 36.9 all-reduce.126
  2765.0 32.2 reduce-scatter.15
  2799.4 31.5 reduce-scatter.19
  2833.9 31.5 reduce-scatter.17
  2868.9 70.1 reduce-scatter.13
  2941.5 61.2 reduce-scatter.23
  3005.2 60.2 reduce-scatter.27
  3067.9 60.2 reduce-scatter.31
where the time goes:
time: 3150 us; the launch traced here: 3140 us
  local copies, waits for them, and re-layouts  1840 us (58%)
  waiting for transfers between devices  783 us (25%)
  matrix products  235 us (7%)
  other arithmetic  161 us (5%)
  blocking collectives  99.9 us (3%)
    pad x88, local copies, waits for them, and re-layouts, gate_part(): unused, states = lax.associative_scan(combine, (decays, driven), axis=1)  911 us
    slice x82, local copies, waits for them, and re-layouts, gate_part(): unused, states = lax.associative_scan(combine, (decays, driven), axis=1)  891 us
    all_gather x1, waiting for transfers between devices, shards(): lax.all_gather(gate_rows, 'head', axis=1, tiled=True)  124 us
    reduce_scatter x1, waiting for transfers between devices, shards(): lax.psum_scatter(contract_last(mixed, out_rows), 'head', scatter_dimensio...  114 us
    all_gather x1, waiting for transfers between devices, shards(): lax.all_gather(down_rows, 'head', axis=1, tiled=True)  112 us
    all_gather x1, waiting for transfers between devices, shards(): lax.all_gather(up_rows, 'head', axis=1, tiled=True)  111 us
    unnamed x2, blocking collectives  87.8 us
    dot_general x6, matrix products, contract_last(): lax.dot_general(left, right, (((1,), (1,)), ((), ())), preferred_element_...  75.4 us
  transfers between devices with their start and end apart: 23, of which 12 were waited for; matrix products, arithmetic and copies ran while one was open for 69% of the time, Pallas kernels for 0%

commit v1 on v0

v1 whole, which is shorter than its diff:
```python
import jax
import jax.numpy as jnp
from jax import lax
from jax.experimental import pallas as pl
from jax.experimental.pallas import tpu as pltpu
from jax.sharding import PartitionSpec as P

EPSILON = 1e-06
ROWS = 256
GELU_A = 0.7978845608028654
GELU_B = 0.044715
CHUNK = 16


def gelu_only(x):
    return 0.5 * x * (1.0 + jnp.tanh(GELU_A * (x + GELU_B * x * x * x)))


def gelu_both(x):
    square = x * x
    bent = jnp.tanh(GELU_A * x * (1.0 + GELU_B * square))
    half = 0.5 * (1.0 + bent)
    slope = half + 0.5 * x * (1.0 - bent * bent) * (GELU_A * (1.0 + 3.0 * GELU_B * square))
    return x * half, slope


def one_minus_exp(x, exp_x):
    series = 1.0 + x * (1.0 / 7.0)
    for order in (6.0, 5.0, 4.0, 3.0, 2.0):
        series = 1.0 + x * (1.0 / order) * series
    return jnp.where(x > -0.25, -x * series, 1.0 - exp_x)


def dot_plain(left, right):
    return jnp.dot(left, right, preferred_element_type=jnp.float32)


def contract_last(left, right):
    return lax.dot_general(
        left, right, (((1,), (1,)), ((), ())), preferred_element_type=jnp.float32
    )


def contract_first(left, right):
    return lax.dot_general(
        left, right, (((0,), (0,)), ((), ())), preferred_element_type=jnp.float32
    )


def conv_rows(window, keep, taps, shift):
    rows = window.shape[0] - 8
    total = taps[0:1] * window[8:] + shift
    for offset in range(1, 4):
        total = total + taps[offset : offset + 1] * (
            keep[:, offset : offset + 1] * window[8 - offset : 8 - offset + rows]
        )
    return total


def scan_down(decays, driven, carry):
    rows = decays.shape[0]
    place = lax.broadcasted_iota(jnp.int32, decays.shape, 0)
    step = 1
    while step < rows:
        inside = place >= step
        driven = jnp.where(inside, decays * pltpu.roll(driven, step, 0) + driven, driven)
        decays = jnp.where(inside, decays * pltpu.roll(decays, step, 0), decays)
        step *= 2
    return decays * carry + driven


def scan_up(decays, driven, carry):
    rows = decays.shape[0]
    place = lax.broadcasted_iota(jnp.int32, decays.shape, 0)
    step = 1
    while step < rows:
        inside = place < rows - step
        driven = jnp.where(inside, decays * pltpu.roll(driven, rows - step, 0) + driven, driven)
        decays = jnp.where(inside, decays * pltpu.roll(decays, rows - step, 0), decays)
        step *= 2
    return decays * carry + driven


def forward_body(
    normed_ref, xw_ref, yw_ref, ow_ref, taps_ref, vec_ref, wr_ref, we_ref, keep_ref,
    u_ref, by_ref, before_ref, states_ref, mixed_ref, part_ref,
    window, conv, conv_low, rate, entry, carry,
):
    rows = normed_ref.shape[0]

    @pl.when(pl.program_id(0) == 0)
    def _():
        window[0:8, :] = jnp.zeros_like(window[0:8, :])
        carry[...] = jnp.zeros_like(carry)

    branch_x = dot_plain(normed_ref[...], xw_ref[...]).astype(jnp.bfloat16)
    u_ref[...] = branch_x
    window[pl.ds(8, rows), :] = branch_x.astype(jnp.float32)
    by_ref[...] = dot_plain(normed_ref[...], yw_ref[...])

    def conv_step(j, unused):
        at = pl.multiple_of(j * CHUNK, CHUNK)
        made = conv_rows(
            window[pl.ds(at, CHUNK + 8), :], keep_ref[pl.ds(at, CHUNK), :],
            taps_ref[...], vec_ref[0:1, :],
        )
        conv[pl.ds(at, CHUNK), :] = made
        conv_low[pl.ds(at, CHUNK), :] = made.astype(jnp.bfloat16)
        return unused

    lax.fori_loop(0, rows // CHUNK, conv_step, 0)
    window[0:8, :] = window[pl.ds(rows, 8), :]
    rate[...] = dot_plain(conv_low[...], wr_ref[...]) + vec_ref[1:2, :]
    entry[...] = dot_plain(conv_low[...], we_ref[...]) + vec_ref[2:3, :]

    def scan_step(j, before):
        at = pl.multiple_of(j * CHUNK, CHUNK)
        here = pl.ds(at, CHUNK)
        carried = keep_ref[here, 0:1]
        log_decay = jax.nn.sigmoid(rate[here, :]) * vec_ref[3:4, :]
        exp_decay = jnp.exp(log_decay)
        drop = jnp.sqrt(one_minus_exp(2.0 * log_decay, exp_decay * exp_decay))
        scaling = (1.0 - carried) + carried * drop
        driven = scaling * jax.nn.sigmoid(entry[here, :]) * conv[here, :]
        states = scan_down(exp_decay * carried, driven, before)
        first = lax.broadcasted_iota(jnp.int32, states.shape, 0) == 0
        before_ref[here, :] = jnp.where(first, before, pltpu.roll(states, 1, 0))
        states_low = states.astype(jnp.bfloat16)
        states_ref[here, :] = states_low
        mixed_ref[here, :] = (
            states_low.astype(jnp.float32) * gelu_only(by_ref[here, :])
        ).astype(jnp.bfloat16)
        return states[CHUNK - 1 : CHUNK, :]

    carry[0:1, :] = lax.fori_loop(0, rows // CHUNK, scan_step, carry[0:1, :])
    part_ref[...] = contract_last(mixed_ref[...], ow_ref[...]).astype(jnp.bfloat16)


def backward_body(
    d_res_ref, xw_ref, yw_ref, ow_ref, taps_ref, vec_ref, wr_ref, we_ref, keep_ref,
    u_ref, u_prev_ref, by_ref, before_ref, states_ref,
    d_bx_ref, d_by_ref, part_ref, taps_out, vec_out, wr_out, we_out,
    window, conv, conv_low, rate, entry, d_mixed, d_conv, g_rate, g_entry, carry, sums,
):
    rows = d_res_ref.shape[0]
    step_id = pl.program_id(0)

    @pl.when(step_id == 0)
    def _():
        d_conv[pl.ds(rows, 8), :] = jnp.zeros_like(d_conv[pl.ds(rows, 8), :])
        carry[...] = jnp.zeros_like(carry)
        sums[...] = jnp.zeros_like(sums)
        wr_out[...] = jnp.zeros_like(wr_out)
        we_out[...] = jnp.zeros_like(we_out)

    @pl.when(step_id > 0)
    def _():
        d_conv[pl.ds(rows, 8), :] = d_conv[0:8, :]

    d_mixed[...] = dot_plain(d_res_ref[...], ow_ref[...])
    window[0:8, :] = u_prev_ref[8:16, :].astype(jnp.float32)
    window[pl.ds(8, rows), :] = u_ref[...].astype(jnp.float32)

    def conv_step(j, unused):
        at = pl.multiple_of(j * CHUNK, CHUNK)
        made = conv_rows(
            window[pl.ds(at, CHUNK + 8), :], keep_ref[pl.ds(at, CHUNK), :],
            taps_ref[...], vec_ref[0:1, :],
        )
        conv[pl.ds(at, CHUNK), :] = made
        conv_low[pl.ds(at, CHUNK), :] = made.astype(jnp.bfloat16)
        return unused

    lax.fori_loop(0, rows // CHUNK, conv_step, 0)
    rate[...] = dot_plain(conv_low[...], wr_ref[...]) + vec_ref[1:2, :]
    entry[...] = dot_plain(conv_low[...], we_ref[...]) + vec_ref[2:3, :]

    def fold(value):
        return value[0:8, :] + value[8:16, :]

    def scan_step(j, after):
        at = pl.multiple_of(rows - CHUNK - j * CHUNK, CHUNK)
        here = pl.ds(at, CHUNK)
        carried = keep_ref[here, 0:1]
        rate_gate = jax.nn.sigmoid(rate[here, :])
        entry_gate = jax.nn.sigmoid(entry[here, :])
        log_decay = rate_gate * vec_ref[3:4, :]
        exp_decay = jnp.exp(log_decay)
        exp_twice = exp_decay * exp_decay
        drop = jnp.sqrt(one_minus_exp(2.0 * log_decay, exp_twice))
        scaling = (1.0 - carried) + carried * drop
        decays = exp_decay * carried
        gelu_y, slope_y = gelu_both(by_ref[here, :])
        through = d_mixed[here, :]
        d_states = (through * gelu_y).astype(jnp.bfloat16).astype(jnp.float32)
        d_by_ref[here, :] = (
            through * states_ref[here, :].astype(jnp.float32) * slope_y
        ).astype(jnp.bfloat16)
        passed = scan_up(decays, decays * d_states, after)
        last = lax.broadcasted_iota(jnp.int32, passed.shape, 0) == CHUNK - 1
        adjoint = d_states + jnp.where(last, after, pltpu.roll(passed, CHUNK - 1, 0))
        convolved = conv[here, :]
        gated = adjoint * entry_gate
        g_log = adjoint * before_ref[here, :] * decays - gated * convolved * (
            carried * (exp_twice / drop)
        )
        g_pre_rate = g_log * vec_ref[3:4, :] * (rate_gate * (1.0 - rate_gate))
        direct = gated * scaling
        g_pre_entry = direct * convolved * (1.0 - entry_gate)
        d_conv[here, :] = direct
        g_rate[here, :] = g_pre_rate.astype(jnp.bfloat16)
        g_entry[here, :] = g_pre_entry.astype(jnp.bfloat16)
        sums[8:16, :] += fold(g_pre_rate)
        sums[16:24, :] += fold(g_pre_entry)
        sums[24:32, :] += fold(g_log * rate_gate)
        return passed[0:1, :]

    carry[0:1, :] = lax.fori_loop(0, rows // CHUNK, scan_step, carry[0:1, :])
    wr_out[...] += contract_first(conv_low[...], g_rate[...])
    we_out[...] += contract_first(conv_low[...], g_entry[...])
    d_conv[0:rows, :] += contract_last(g_rate[...], wr_ref[...]) + contract_last(
        g_entry[...], we_ref[...]
    )

    def back_step(j, unused):
        at = pl.multiple_of(j * CHUNK, CHUNK)
        here = pl.ds(at, CHUNK)
        keep = keep_ref[here, :]
        ahead = d_conv[pl.ds(at, CHUNK + 8), :]
        behind = window[pl.ds(at, CHUNK + 8), :]
        now = ahead[0:CHUNK]
        total = taps_ref[0:1, :] * now
        sums[0:8, :] += fold(now)
        sums[32:40, :] += fold(now * behind[8:])
        for offset in range(1, 4):
            total = total + taps_ref[offset : offset + 1, :] * (
                keep[:, 3 + offset : 4 + offset] * ahead[offset : offset + CHUNK]
            )
            base = 32 + 8 * offset
            sums[base : base + 8, :] += fold(
                now * (keep[:, offset : offset + 1] * behind[8 - offset : 8 - offset + CHUNK])
            )
        d_bx_ref[here, :] = total.astype(jnp.bfloat16)
        return unused

    lax.fori_loop(0, rows // CHUNK, back_step, 0)
    part_ref[...] = (
        contract_last(d_bx_ref[...], xw_ref[...]) + contract_last(d_by_ref[...], yw_ref[...])
    ).astype(jnp.bfloat16)

    @pl.when(step_id == pl.num_programs(0) - 1)
    def _():
        vec_out[...] = jnp.zeros_like(vec_out)
        for place in range(4):
            vec_out[place : place + 1, :] = jnp.sum(
                sums[8 * place : 8 * place + 8, :], axis=0, keepdims=True
            )
            taps_out[place : place + 1, :] = jnp.sum(
                sums[32 + 8 * place : 40 + 8 * place, :], axis=0, keepdims=True
            )


def whole(shape):
    return pl.BlockSpec(shape, lambda i: (0,) * len(shape))


def mixer_forward(normed, xw, yw, ow, taps, vec, wr, we, keep, rows):
    length, width = normed.shape
    chans = xw.shape[1]
    tile = lambda columns: pl.BlockSpec((rows, columns), lambda i: (i, 0))
    return pl.pallas_call(
        forward_body,
        grid=(length // rows,),
        in_specs=[
            tile(width), whole(xw.shape), whole(yw.shape), whole(ow.shape), whole(taps.shape),
            whole(vec.shape), whole(wr.shape), whole(we.shape), tile(keep.shape[1]),
        ],
        out_specs=[tile(chans)] * 5 + [tile(width)],
        out_shape=[
            jax.ShapeDtypeStruct((length, chans), jnp.bfloat16),
            jax.ShapeDtypeStruct((length, chans), jnp.float32),
            jax.ShapeDtypeStruct((length, chans), jnp.float32),
            jax.ShapeDtypeStruct((length, chans), jnp.bfloat16),
            jax.ShapeDtypeStruct((length, chans), jnp.bfloat16),
            jax.ShapeDtypeStruct((length, width), jnp.bfloat16),
        ],
        scratch_shapes=[
            pltpu.VMEM((rows + 8, chans), jnp.float32),
            pltpu.VMEM((rows, chans), jnp.float32),
            pltpu.VMEM((rows, chans), jnp.bfloat16),
            pltpu.VMEM((rows, chans), jnp.float32),
            pltpu.VMEM((rows, chans), jnp.float32),
            pltpu.VMEM((8, chans), jnp.float32),
        ],
        compiler_params=pltpu.CompilerParams(vmem_limit_bytes=48 * 2**20),
        cost_estimate=pl.CostEstimate(
            flops=6 * length * width * chans,
            bytes_accessed=4 * length * width + 30 * length * chans,
            transcendentals=6 * length * chans,
        ),
        name="mixer_forward",
    )(normed, xw, yw, ow, taps, vec, wr, we, keep)


def mixer_backward(d_res, xw, yw, ow, taps, vec, wr, we, keep, u, by, before, states, rows):
    length, width = d_res.shape
    chans = xw.shape[1]
    blocks = length // rows
    tile = lambda columns: pl.BlockSpec((rows, columns), lambda i: (blocks - 1 - i, 0))
    ahead = pl.BlockSpec(
        (16, chans), lambda i: (jnp.maximum((blocks - 1 - i) * (rows // 16) - 1, 0), 0)
    )
    return pl.pallas_call(
        backward_body,
        grid=(blocks,),
        in_specs=[
            tile(width), whole(xw.shape), whole(yw.shape), whole(ow.shape), whole(taps.shape),
            whole(vec.shape), whole(wr.shape), whole(we.shape), tile(keep.shape[1]),
            tile(chans), ahead, tile(chans), tile(chans), tile(chans),
        ],
        out_specs=[
            tile(chans), tile(chans), tile(width), whole(taps.shape), whole(vec.shape),
            whole(wr.shape), whole(we.shape),
        ],
        out_shape=[
            jax.ShapeDtypeStruct((length, chans), jnp.bfloat16),
            jax.ShapeDtypeStruct((length, chans), jnp.bfloat16),
            jax.ShapeDtypeStruct((length, width), jnp.bfloat16),
            jax.ShapeDtypeStruct(taps.shape, jnp.float32),
            jax.ShapeDtypeStruct(vec.shape, jnp.float32),
            jax.ShapeDtypeStruct(wr.shape, jnp.float32),
            jax.ShapeDtypeStruct(we.shape, jnp.float32),
        ],
        scratch_shapes=[
            pltpu.VMEM((rows + 8, chans), jnp.float32),
            pltpu.VMEM((rows, chans), jnp.float32),
            pltpu.VMEM((rows, chans), jnp.bfloat16),
            pltpu.VMEM((rows, chans), jnp.float32),
            pltpu.VMEM((rows, chans), jnp.float32),
            pltpu.VMEM((rows, chans), jnp.float32),
            pltpu.VMEM((rows + 8, chans), jnp.float32),
            pltpu.VMEM((rows, chans), jnp.bfloat16),
            pltpu.VMEM((rows, chans), jnp.bfloat16),
            pltpu.VMEM((8, chans), jnp.float32),
            pltpu.VMEM((64, chans), jnp.float32),
        ],
        compiler_params=pltpu.CompilerParams(vmem_limit_bytes=48 * 2**20),
        cost_estimate=pl.CostEstimate(
            flops=6 * length * width * chans,
            bytes_accessed=4 * length * width + 30 * length * chans,
            transcendentals=6 * length * chans,
        ),
        name="mixer_backward",
    )(d_res, xw, yw, ow, taps, vec, wr, we, keep, u, u, by, before, states)


def keep_columns(resets):
    length = resets.shape[1]
    position = lax.broadcasted_iota(jnp.int32, resets.shape, 1)
    starts = jnp.maximum(resets, (position == 0).astype(jnp.int32)).astype(jnp.float32)
    carried = (1.0 - starts).reshape(-1)
    seqs = resets.shape[0]

    def back(values, by):
        values = values.reshape(seqs, length)
        return jnp.pad(values, ((0, 0), (by, 0)))[:, :length].reshape(-1)

    def ahead(values, by):
        values = values.reshape(seqs, length)
        return jnp.pad(values, ((0, 0), (0, by)))[:, by:].reshape(-1)

    one = carried
    two = one * back(carried, 1)
    three = two * back(carried, 2)
    return jnp.stack(
        [carried, one, two, three, ahead(one, 1), ahead(two, 2), ahead(three, 3), carried], axis=1
    )


def block_diagonal(blocks, chans):
    heads, width, unused = blocks.shape
    rows = [
        jnp.pad(blocks[h], ((0, 0), (h * width, chans - (h + 1) * width))) for h in range(heads)
    ]
    full = jnp.concatenate(rows, axis=0)
    return jnp.pad(full, ((0, chans - heads * width), (0, 0)))


def diagonal_blocks(full, heads, width):
    return jnp.stack(
        [full[h * width : (h + 1) * width, h * width : (h + 1) * width] for h in range(heads)]
    )


def norm_apply(rows, gain):
    return rows * lax.rsqrt(jnp.mean(rows * rows, axis=-1, keepdims=True) + EPSILON) * gain


def gather(values, axis_name, axis):
    return lax.all_gather(values, axis_name, axis=axis, tiled=True)


def scatter(values, axis_name, axis):
    return lax.psum_scatter(values, axis_name, scatter_dimension=axis, tiled=True)


def shards(
    layer_in,
    cotangent,
    mix_gain,
    ffn_gain,
    x_weight,
    y_weight,
    out_weight,
    conv_weight,
    conv_bias,
    rate_weight,
    rate_bias,
    entry_weight,
    entry_bias,
    decay_param,
    gate_weight,
    up_weight,
    down_weight,
    resets,
):
    heads, head_width = rate_weight.shape[:2]
    used = conv_bias.shape[0]
    chans = -(-used // 128) * 128
    widen = lambda values: jnp.pad(values, ((0, 0), (0, chans - used)))
    mix_full = gather(mix_gain, ("row", "head"), 0)
    ffn_full = gather(ffn_gain, ("row", "head"), 0)
    x_rows = gather(widen(x_weight), "row", 0)
    y_rows = gather(widen(y_weight), "row", 0)
    out_rows = gather(widen(out_weight), "row", 0)
    gate_rows = gather(gate_weight, "row", 0)
    up_rows = gather(up_weight, "row", 0)
    down_rows = gather(down_weight, "row", 0)

    spare = (0, chans - used)
    decay_wide = jnp.pad(decay_param, spare, constant_values=2.0)
    blank = jnp.zeros((chans,), jnp.float32)
    vec = jnp.stack(
        [
            jnp.pad(conv_bias, spare),
            jnp.pad(rate_bias, spare),
            jnp.pad(entry_bias, spare),
            -8.0 * jax.nn.softplus(-decay_wide),
            blank,
            blank,
            blank,
            blank,
        ]
    )
    taps = widen(conv_weight)
    wr = block_diagonal(rate_weight, chans)
    we = block_diagonal(entry_weight, chans)
    keep = keep_columns(resets)

    inputs = layer_in.astype(jnp.float32)
    normed_f, norm_back_one = jax.vjp(norm_apply, inputs, mix_full.astype(jnp.float32))
    normed_group = gather(normed_f.astype(jnp.bfloat16), "head", 0)
    u, by, before, states, mixed, part = mixer_forward(
        normed_group, x_rows, y_rows, out_rows, taps, vec, wr, we, keep, ROWS
    )
    residual = inputs + scatter(part, "head", 0).astype(jnp.float32)
    normed_two_f, norm_back_two = jax.vjp(norm_apply, residual, ffn_full.astype(jnp.float32))
    cot_group = gather(cotangent, "head", 0)
    two_group = gather(normed_two_f.astype(jnp.bfloat16), "head", 0)
    gates = dot_plain(two_group, gate_rows)
    ups = dot_plain(two_group, up_rows)
    activated, slope = gelu_both(gates)
    hidden = (activated * ups).astype(jnp.bfloat16)
    ffn_part = contract_last(hidden, down_rows).astype(jnp.bfloat16)
    d_hidden = dot_plain(cot_group, down_rows)
    d_gates = (d_hidden * ups * slope).astype(jnp.bfloat16)
    d_ups = (d_hidden * activated).astype(jnp.bfloat16)
    d_two_part = (contract_last(d_gates, gate_rows) + contract_last(d_ups, up_rows)).astype(
        jnp.bfloat16
    )
    gate_grad = scatter(contract_first(two_group, d_gates).astype(jnp.bfloat16), "row", 0)
    up_grad = scatter(contract_first(two_group, d_ups).astype(jnp.bfloat16), "row", 0)
    down_grad = scatter(contract_first(cot_group, hidden).astype(jnp.bfloat16), "row", 0)
    layer_out = (residual + scatter(ffn_part, "head", 0).astype(jnp.float32)).astype(jnp.bfloat16)
    d_two = scatter(d_two_part, "head", 0).astype(jnp.float32)
    d_resid_norm, d_ffn_gain = norm_back_two(d_two)
    d_residual = cotangent.astype(jnp.float32) + d_resid_norm
    d_res_group = gather(d_residual.astype(jnp.bfloat16), "head", 0)
    d_bx, d_by, d_part, d_taps, d_vec, d_wr, d_we = mixer_backward(
        d_res_group, x_rows, y_rows, out_rows, taps, vec, wr, we, keep, u, by, before, states, ROWS
    )
    out_grad = scatter(contract_first(d_res_group, mixed).astype(jnp.bfloat16), "row", 0)
    x_grad = scatter(contract_first(normed_group, d_bx).astype(jnp.bfloat16), "row", 0)
    y_grad = scatter(contract_first(normed_group, d_by).astype(jnp.bfloat16), "row", 0)
    d_normed = scatter(d_part, "head", 0).astype(jnp.float32)
    d_inputs, d_mix_gain = norm_back_one(d_normed)
    layer_in_grad = (d_inputs + d_residual).astype(jnp.bfloat16)

    small = [
        d_taps[:, :used],
        d_vec[0, :used],
        diagonal_blocks(d_wr, heads, head_width),
        d_vec[1, :used],
        diagonal_blocks(d_we, heads, head_width),
        d_vec[2, :used],
        d_vec[3, :used] * (8.0 * jax.nn.sigmoid(-decay_param)),
    ]
    small = [lax.psum(item.astype(jnp.bfloat16), "row").astype(jnp.float32) for item in small]
    mix_part = scatter(d_mix_gain, ("row", "head"), 0)
    ffn_part_grad = scatter(d_ffn_gain, ("row", "head"), 0)
    wide = lambda values: values[:, :used].astype(jnp.float32)
    return (
        layer_out,
        layer_in_grad,
        mix_part,
        ffn_part_grad,
        wide(x_grad),
        wide(y_grad),
        wide(out_grad),
        *small,
        gate_grad.astype(jnp.float32),
        up_grad.astype(jnp.float32),
        down_grad.astype(jnp.float32),
    )


def solution(mesh):
    return jax.shard_map(
        shards,
        mesh=mesh,
        in_specs=(
            P(("row", "head"), None),
            P(("row", "head"), None),
            P(("row", "head")),
            P(("row", "head")),
            P("row", "head"),
            P("row", "head"),
            P("row", "head"),
            P(None, "head"),
            P("head"),
            P("head", None, None),
            P("head"),
            P("head", None, None),
            P("head"),
            P("head"),
            P("row", "head"),
            P("row", "head"),
            P("row", "head"),
            P("row", None),
        ),
        out_specs=(
            P(("row", "head"), None),
            P(("row", "head"), None),
            P(("row", "head")),
            P(("row", "head")),
            P("row", "head"),
            P("row", "head"),
            P("row", "head"),
            P(None, "head"),
            P("head"),
            P("head", None, None),
            P("head"),
            P("head", None, None),
            P("head"),
            P("head"),
            P("row", "head"),
            P("row", "head"),
            P("row", "head"),
        ),
        check_vma=False,
    )
```

time: 3150 us -> 1280 us (0.41)
  local copies, waits for them, and re-layouts: 1840 us -> 23.6 us
  other arithmetic: 161 us -> 32.2 us
  Pallas kernels: 0 us -> 113 us
  matrix products: 235 us -> 138 us
  waiting for transfers between devices: 783 us -> 859 us
    pad x88 -> x9, local copies, waits for them, and re-layouts: 911 us -> 2.46 us  [the longest x4 2.38 us: shards(): widen = lambda values: jnp.pad(values, ((0, 0), (0, chans - used)))]
    slice x83 -> x5, local copies, waits for them, and re-layouts: 891 us -> 0.55 us  [the longest x2 0.49 us: block_diagonal(): blocks[h]]
    pallas_call x0 -> x2, Pallas kernels: none -> 113 us  [the longest x1 66.4 us: mixer_backward(): pl.pallas_call(backward_body, grid=(blocks,), in_specs=[tile(width), whol...]
    dot_general x12 -> x3, matrix products: 92 us -> 40.8 us  [dot_plain(): return jnp.dot(left, right, preferred_element_type=jnp.float32)]
    reduce_scatter x11 -> x10, waiting for transfers between devices: 368 us -> 416 us  [scatter(): lax.psum_scatter(values, axis_name, scatter_dimension=axis, tiled=True)]
    dot_general x6 -> x3, matrix products: 75.4 us -> 33.7 us  [contract_last(): lax.dot_general(left, right, (((1,), (1,)), ((), ())), preferred_element_...]
    all_gather x11 -> x10, waiting for transfers between devices: 407 us -> 416 us  [gather(): return lax.all_gather(values, axis_name, axis=axis, tiled=True)]
  transfers between devices with their start and end apart: 23 -> 21, of which waited for: 12 -> 19; matrix products, arithmetic and copies ran while one was open for 69% -> 11% of each run, Pallas kernels for 0% -> 5%
where the time goes in v1:
time: 1280 us
  waiting for transfers between devices  859 us (67%)
  matrix products  138 us (11%)
  Pallas kernels  113 us (9%)
  blocking collectives  94.6 us (7%)
  other arithmetic  32.2 us (3%)
  local copies, waits for them, and re-layouts  23.6 us (2%)
  between operations  15.4 us (1%)
    reduce_scatter x10, waiting for transfers between devices, scatter(): lax.psum_scatter(values, axis_name, scatter_dimension=axis, tiled=True)  416 us
    all_gather x10, waiting for transfers between devices, gather(): return lax.all_gather(values, axis_name, axis=axis, tiled=True)  416 us
    unnamed x2, blocking collectives  84 us
    pallas_call x1, Pallas kernels, mixer_backward(): pl.pallas_call(backward_body, grid=(blocks,), in_specs=[tile(width), whol...  66.4 us
    dot_general x6, matrix products, contract_first(): lax.dot_general(left, right, (((0,), (0,)), ((), ())), preferred_element_...  63.4 us
    pallas_call x1, Pallas kernels, mixer_forward(): pl.pallas_call(forward_body, grid=(length // rows,), in_specs=[tile(width...  46.8 us
    dot_general x3, matrix products, dot_plain(): return jnp.dot(left, right, preferred_element_type=jnp.float32)  40.8 us
    dot_general x3, matrix products, contract_last(): lax.dot_general(left, right, (((1,), (1,)), ((), ())), preferred_element_...  33.7 us
  transfers between devices with their start and end apart: 21, of which 19 were waited for; matrix products, arithmetic and copies ran while one was open for 11% of the time, Pallas kernels for 5%

profile of v1, /device:TPU:0, one launch (start us, length us, event | category | flops | bytes accessed | tf_op | source)
XLA Modules:
  0.0 1277.7 jit_solution(2672944789376567503)
XLA Ops:
  13.2 44.3 %all-reduce.24 = (bf16[2048]{0:T(1024)(128)(2,1)S(1)}, bf16[2048]{0:T(1024)(128)(2,1)S(1)}) all-reduce(bf16[2048]{0:T(1024)(128)(2,1)S(1)} %dynamic-update-slice, bf16[2048]{0:T(1024)(128)(2,1)S(1)} %dynamic-update-slice.1), channel_id=1, replica_groups=mesh['row'=4,'head'=8] {'row','head'}, use_global_device_ids=true, to_apply=%add.19 | all-reduce | flops 4096 | bytes 16384
  61.1 28.1 %all-gather.15.cloned.1.call-done.yw_ref = bf16[2048,384]{1,0:T(8,128)(2,1)} async-done(((bf16[512,384]{1,0:T(8,128)(2,1)}), bf16[2048,384]{1,0:T(8,128)(2,1)}) %all-gather.15.cloned.1.call-update) | async-done | bytes 1572880 | tf_op jit(solution)/shard_map/all_gather | solution.py:400
  89.2 38.1 %all-gather.17.cloned.1.call-done.ow_ref = bf16[2048,384]{1,0:T(8,128)(2,1)} async-done(((bf16[512,384]{1,0:T(8,128)(2,1)}), bf16[2048,384]{1,0:T(8,128)(2,1)}) %all-gather.17.cloned.1.call-update) | async-done | bytes 1572880 | tf_op jit(solution)/shard_map/all_gather | solution.py:400
  127.4 55.6 %all-gather.11.cloned.1.call-done.normed_ref = bf16[2048,2048]{1,0:T(8,128)(2,1)} async-done(((bf16[256,2048]{1,0:T(8,128)(2,1)}), bf16[2048,2048]{1,0:T(8,128)(2,1)}) %all-gather.11.cloned.1.call-update) | async-done | bytes 8388624 | tf_op jit(solution)/shard_map/all_gather | solution.py:400
  183.0 46.8 %mixer_forward.1 = (bf16[2048,384]{1,0:T(8,128)(2,1)S(1)}, f32[2048,384]{1,0:T(8,128)}, f32[2048,384]{1,0:T(8,128)}, bf16[2048,384]{1,0:T(8,128)(2,1)S(1)}, bf16...) custom-call(bf16[2048,2048]{1,0:T(8,128)(2,1)} %all-gather.11.cloned.1.call-done.normed_ref, ...), custom_call_target="tpu_custom_call" | custom-call | flops 9663676416 | bytes 40370176 | tf_op jit(solution)/shard_map/mixer_forward/pallas_call | solution.py:271
  232.7 70.8 %reduce-scatter.11.cloned.1.call-done = bf16[256,2048]{1,0:T(8,128)(2,1)} async-done(((bf16[2048,2048]{1,0:T(8,128)(2,1)}), bf16[256,2048]{1,0:T(8,128)(2,1)}) %reduce-scatter.11.cloned.1.call-update) | async-done | bytes 1048592 | tf_op jit(solution)/shard_map/reduce_scatter | solution.py:404
  310.1 58.4 %all-gather.23.cloned.1.call-done = bf16[2048,768]{1,0:T(8,128)(2,1)} async-done(((bf16[512,768]{1,0:T(8,128)(2,1)}), bf16[2048,768]{1,0:T(8,128)(2,1)}) %all-gather.23.cloned.1.call-update) | async-done | bytes 3145744 | tf_op jit(solution)/shard_map/all_gather | solution.py:400
  368.5 55.7 %all-gather.19.cloned.1.call-done = bf16[2048,2048]{1,0:T(8,128)(2,1)} async-done(((bf16[256,2048]{1,0:T(8,128)(2,1)}), bf16[2048,2048]{1,0:T(8,128)(2,1)}) %all-gather.19.cloned.1.call-update) | async-done | bytes 8388624 | tf_op jit(solution)/shard_map/all_gather | solution.py:400
  435.9 53.5 %all-gather.21.cloned.1.call-done = bf16[2048,768]{1,0:T(8,128)(2,1)} async-done(((bf16[512,768]{1,0:T(8,128)(2,1)}), bf16[2048,768]{1,0:T(8,128)(2,1)}) %all-gather.21.cloned.1.call-update) | async-done | bytes 3145744 | tf_op jit(solution)/shard_map/all_gather | solution.py:400
  501.1 52.1 %all-gather.25.cloned.1.call-done = bf16[2048,768]{1,0:T(8,128)(2,1)} async-done(((bf16[512,768]{1,0:T(8,128)(2,1)}), bf16[2048,768]{1,0:T(8,128)(2,1)}) %all-gather.25.cloned.1.call-update) | async-done | bytes 3145744 | tf_op jit(solution)/shard_map/all_gather | solution.py:400
  553.2 55.0 %all-gather.27.cloned.1.call-done = bf16[2048,2048]{1,0:T(8,128)(2,1)} async-done(((bf16[256,2048]{1,0:T(8,128)(2,1)}), bf16[2048,2048]{1,0:T(8,128)(2,1)}) %all-gather.27.cloned.1.call-update) | async-done | bytes 8388624 | tf_op jit(solution)/shard_map/all_gather | solution.py:400
  608.2 17.4 %multiply_convert_fusion = (bf16[2048,768]{1,0:T(8,128)(2,1)S(1)}, bf16[2048,768]{1,0:T(8,128)(2,1)S(1)}, bf16[2048,768]{1,0:T(8,128)(2,1)}) fusion(f32[2048,768]{1,0:T(8,128)} %fusion.36, f32[2048,768]{1,0:T(8,128)} %fusion.37, bf16[2048,2048]{1,0:T(8,128)(2,1)} %all-gather.27.cloned.1.call-done, bf16[2048,768]{1,0:T(8,128)(2,1)} %all-gather.25.cloned.1.call-done), kind=kOutput, calls=%fused_computation.2 | convolution fusion | flops 6480199680 | bytes 33554432 | tf_op jit(solution)/shard_map/dot_general | solution.py:35
  635.2 12.8 %add_convert_fusion = bf16[2048,2048]{1,0:T(8,128)(2,1)} fusion(f32[2048,2048]{1,0:T(8,128)} %fusion.38, bf16[2048,768]{1,0:T(8,128)(2,1)S(1)} %get-tuple-element.116, bf16[2048,768]{1,0:T(8,128)(2,1)S(1)} %copy-done.27), kind=kOutput, calls=%fused_computation | convolution fusion | flops 6450839552 | bytes 31457280 | tf_op jit(solution)/shard_map/dot_general | solution.py:39
  648.1 71.4 %reduce-scatter.15.cloned.1.call-done = bf16[256,2048]{1,0:T(8,128)(2,1)} async-done(((bf16[2048,2048]{1,0:T(8,128)(2,1)}), bf16[256,2048]{1,0:T(8,128)(2,1)}) %reduce-scatter.15.cloned.1.call-update) | async-done | bytes 1048592 | tf_op jit(solution)/shard_map/reduce_scatter | solution.py:404
  759.5 19.3 %all-gather.29.cloned.1.call-done.d_res_ref = bf16[2048,2048]{1,0:T(8,128)(2,1)} async-done(((bf16[256,2048]{1,0:T(8,128)(2,1)}), bf16[2048,2048]{1,0:T(8,128)(2,1)}) %all-gather.29.cloned.1.call-update) | async-done | bytes 8388624 | tf_op jit(solution)/shard_map/all_gather | solution.py:400
  778.7 66.4 %mixer_backward.1 = (bf16[2048,384]{1,0:T(8,128)(2,1)S(1)}, bf16[2048,384]{1,0:T(8,128)(2,1)S(1)}, bf16[2048,2048]{1,0:T(8,128)(2,1)}, f32[4,384]{1,0:T(4,128)S(...) custom-call(bf16[2048,2048]{1,0:T(8,128)(2,1)} %all-gather.29.cloned.1.call-done.d_res_ref, ...), custom_call_target="tpu_custom_call" | custom-call | flops 9663676416 | bytes 40370176 | tf_op jit(solution)/shard_map/mixer_backward/pallas_call | solution.py:313
  906.2 60.1 %reduce-scatter.25.cloned.1.call-done = bf16[512,768]{1,0:T(8,128)(2,1)} async-done(((bf16[2048,768]{1,0:T(8,128)(2,1)}), bf16[512,768]{1,0:T(8,128)(2,1)}) %reduce-scatter.25.cloned.1.call-update) | async-done | bytes 786448 | tf_op jit(solution)/shard_map/reduce_scatter | solution.py:404
  982.3 23.8 %all-reduce.29.cloned.1.call-done = (bf16[2,171,171]{2,1,0:T(8,128)(2,1)}, bf16[2,171,171]{2,1,0:T(8,128)(2,1)}) async-done(((bf16[2,171,171]{2,1,0:T(8,128)(2,1)}, bf16[2,171,171]{2,1,0:T(8,128)(2,1)}), (bf16[2,171,171]{2,1,0:T(8,128)(2,1)}, bf16[2,171,171]{2,1,0:T(8,128)(2,1)})) %all-reduce.29.cloned.1.call-update) | async-done | bytes 233944 | tf_op jit(solution)/shard_map/psum | solution.py:508
  1009.7 33.4 %reduce-scatter.23.cloned.1.call-done = bf16[512,384]{1,0:T(8,128)(2,1)} async-done(((bf16[2048,384]{1,0:T(8,128)(2,1)}), bf16[512,384]{1,0:T(8,128)(2,1)}) %reduce-scatter.23.cloned.1.call-update) | async-done | bytes 393232 | tf_op jit(solution)/shard_map/reduce_scatter | solution.py:404
  1045.3 34.2 %reduce-scatter.19.cloned.1.call-done = bf16[512,384]{1,0:T(8,128)(2,1)} async-done(((bf16[2048,384]{1,0:T(8,128)(2,1)}), bf16[512,384]{1,0:T(8,128)(2,1)}) %reduce-scatter.19.cloned.1.call-update) | async-done | bytes 393232 | tf_op jit(solution)/shard_map/reduce_scatter | solution.py:404
  1083.9 32.3 %reduce-scatter.21.cloned.1.call-done = bf16[512,384]{1,0:T(8,128)(2,1)} async-done(((bf16[2048,384]{1,0:T(8,128)(2,1)}), bf16[512,384]{1,0:T(8,128)(2,1)}) %reduce-scatter.21.cloned.1.call-update) | async-done | bytes 393232 | tf_op jit(solution)/shard_map/reduce_scatter | solution.py:404
  1120.3 69.4 %reduce-scatter.17.cloned.1.call-done = bf16[256,2048]{1,0:T(8,128)(2,1)} async-done(((bf16[2048,2048]{1,0:T(8,128)(2,1)}), bf16[256,2048]{1,0:T(8,128)(2,1)}) %reduce-scatter.17.cloned.1.call-update) | async-done | bytes 1048592 | tf_op jit(solution)/shard_map/reduce_scatter | solution.py:404
  1192.0 39.8 %all-reduce.23 = (f32[2048]{0:T(1024)S(1)}, f32[2048]{0:T(1024)S(1)}) all-reduce(f32[2048]{0:T(1024)S(1)} %get-tuple-element.96, f32[2048]{0:T(1024)S(1)} %get-tuple-element.94), channel_id=6, replica_groups=mesh['row'=4,'head'=8] {'row','head'}, use_global_device_ids=true, to_apply=%region_9.10.clone | all-reduce | flops 4096 | bytes 32768
  1233.0 32.5 %reduce-scatter.13.cloned.1.call-done = bf16[256,2048]{1,0:T(8,128)(2,1)} async-done(((bf16[2048,2048]{1,0:T(8,128)(2,1)}), bf16[256,2048]{1,0:T(8,128)(2,1)}) %reduce-scatter.13.cloned.1.call-update) | async-done | bytes 1048592 | tf_op jit(solution)/shard_map/reduce_scatter | solution.py:404
  (201 shorter events, 191.1 us)
Async XLA Ops:
  7.2 53.9 %all-gather.13.cloned.1.call-start = ((), (), s32[]{:S(2)}) async-start(), calls=%async_computation.11 | async-start | bytes 1966080 | tf_op jit(solution)/shard_map/all_gather | solution.py:400
  9.4 79.8 %all-gather.15.cloned.1.call-start = ((), (), s32[]{:S(2)}) async-start(), calls=%async_computation.12 | async-start | bytes 1966080 | tf_op jit(solution)/shard_map/all_gather | solution.py:400
  11.5 115.8 %all-gather.17.cloned.1.call-start = ((), (), s32[]{:S(2)}) async-start(), calls=%async_computation.13 | async-start | bytes 1966080 | tf_op jit(solution)/shard_map/all_gather | solution.py:400
  12.6 170.3 %all-gather.11.cloned.1.call-start = ((), (), s32[]{:S(2)}) async-start(), calls=%async_computation.10 | async-start | bytes 9437184 | tf_op jit(solution)/shard_map/all_gather | solution.py:400
  59.1 244.4 %reduce-scatter.11.cloned.1.call-start = ((), (), s32[]{:S(2)}) async-start(), calls=%async_computation.14 | async-start | bytes 9437184 | tf_op jit(solution)/shard_map/reduce_scatter | solution.py:404
  232.1 136.5 %all-gather.23.cloned.1.call-start = ((), (), s32[]{:S(2)}) async-start(), calls=%async_computation.17 | async-start | bytes 3932160 | tf_op jit(solution)/shard_map/all_gather | solution.py:400
  232.6 191.6 %all-gather.19.cloned.1.call-start = ((), (), s32[]{:S(2)}) async-start(), calls=%async_computation.15 | async-start | bytes 9437184 | tf_op jit(solution)/shard_map/all_gather | solution.py:400
  307.8 181.6 %all-gather.21.cloned.1.call-start = ((), (), s32[]{:S(2)}) async-start(), calls=%async_computation.16 | async-start | bytes 3932160 | tf_op jit(solution)/shard_map/all_gather | solution.py:400
  308.5 244.7 %all-gather.25.cloned.1.call-start = ((), (), s32[]{:S(2)}) async-start(), calls=%async_computation.18 | async-start | bytes 3932160 | tf_op jit(solution)/shard_map/all_gather | solution.py:400
  309.2 298.9 %all-gather.27.cloned.1.call-start = ((), (), s32[]{:S(2)}) async-start(), calls=%async_computation.20 | async-start | bytes 9437184 | tf_op jit(solution)/shard_map/all_gather | solution.py:400
  309.8 409.6 %reduce-scatter.15.cloned.1.call-start = ((), (), s32[]{:S(2)}) async-start(), calls=%async_computation.21 | async-start | bytes 9437184 | tf_op jit(solution)/shard_map/reduce_scatter | solution.py:404
  648.0 130.7 %all-gather.29.cloned.1.call-start = ((), (), s32[]{:S(2)}) async-start(), calls=%async_computation.22 | async-start | bytes 9437184 | tf_op jit(solution)/shard_map/all_gather | solution.py:400
  724.2 164.9 %reduce-scatter.29.cloned.1.call-start = ((), (), s32[]{:S(2)}) async-start(), calls=%async_computation.29 | async-start | bytes 3932160 | tf_op jit(solution)/shard_map/reduce_scatter | solution.py:404
  736.3 167.6 %reduce-scatter.27.cloned.1.call-start = ((), (), s32[]{:S(2)}) async-start(), calls=%async_computation.28 | async-start | bytes 3932160 | tf_op jit(solution)/shard_map/reduce_scatter | solution.py:404
  747.7 218.6 %reduce-scatter.25.cloned.1.call-start = ((), (), s32[]{:S(2)}) async-start(), calls=%async_computation.27 | async-start | bytes 3932160 | tf_op jit(solution)/shard_map/reduce_scatter | solution.py:404
  759.4 246.7 %all-reduce.29.cloned.1.call-start = ((), (), s32[]{:S(2)}) async-start(), calls=%async_computation.30 | async-start | bytes 720896 | tf_op jit(solution)/shard_map/psum | solution.py:508
  847.9 195.2 %reduce-scatter.23.cloned.1.call-start = ((), (), s32[]{:S(2)}) async-start(), calls=%async_computation.26 | async-start | bytes 1966080 | tf_op jit(solution)/shard_map/reduce_scatter | solution.py:404
  858.2 221.4 %reduce-scatter.19.cloned.1.call-start = ((), (), s32[]{:S(2)}) async-start(), calls=%async_computation.24 | async-start | bytes 1966080 | tf_op jit(solution)/shard_map/reduce_scatter | solution.py:404
  867.6 248.5 %reduce-scatter.21.cloned.1.call-start = ((), (), s32[]{:S(2)}) async-start(), calls=%async_computation.25 | async-start | bytes 1966080 | tf_op jit(solution)/shard_map/reduce_scatter | solution.py:404
  876.8 312.9 %reduce-scatter.17.cloned.1.call-start = ((), (), s32[]{:S(2)}) async-start(), calls=%async_computation.23 | async-start | bytes 9437184 | tf_op jit(solution)/shard_map/reduce_scatter | solution.py:404
  877.4 388.1 %reduce-scatter.13.cloned.1.call-start = ((), (), s32[]{:S(2)}) async-start(), calls=%async_computation.19 | async-start | bytes 9437184 | tf_op jit(solution)/shard_map/reduce_scatter | solution.py:404
  1081.5 151.4 %copy-start.20 = (f32[256]{0:T(256)S(1)}, f32[256]{0:T(256)}, u32[]{:S(2)}) copy-start(f32[256]{0:T(256)} %copy-done.19) | copy-start | bytes 3076
  1081.5 184.0 %copy-start.7 = (bf16[256,2048]{1,0:T(8,128)(2,1)S(1)}, bf16[256,2048]{1,0:T(8,128)(2,1)}, u32[]{:S(2)}) copy-start(bf16[256,2048]{1,0:T(8,128)(2,1)} %reduce-scatter.11.cloned.1.call-done) | copy-start | bytes 3145732
  1081.5 184.0 %copy-start.9 = (bf16[256,2048]{1,0:T(8,128)(2,1)S(1)}, bf16[256,2048]{1,0:T(8,128)(2,1)}, u32[]{:S(2)}) copy-start(bf16[256,2048]{1,0:T(8,128)(2,1)} %param.19) | copy-start | bytes 3145732
  (30 other events, 992.6 us)
Sparse Core Ops, SparseCore 0:
  10.2 40.8 all-gather.12
  53.2 35.9 all-gather.14
  91.4 35.9 all-gather.16
  129.7 53.2 all-gather.10
  232.2 71.2 reduce-scatter.10
  305.0 63.4 all-gather.22
  371.1 53.0 all-gather.18
  425.8 63.4 all-gather.20
  491.0 62.1 all-gather.24
  555.1 53.0 all-gather.26
  648.2 71.2 reduce-scatter.14
  724.3 54.3 all-gather.28
  781.0 60.2 reduce-scatter.28
  843.5 60.3 reduce-scatter.26
  906.0 60.2 reduce-scatter.24
  969.1 36.9 all-reduce.28
  1008.3 34.7 reduce-scatter.22
  1045.3 34.2 reduce-scatter.18
  1081.9 34.2 reduce-scatter.20
  1119.5 70.2 reduce-scatter.16
  1193.6 71.8 reduce-scatter.12

commit v2 on v1

--- a/solution.py
+++ b/solution.py
@@ -81,9 +81,9 @@
     return decays * carry + driven
 
 
-def forward_body(
+def forward_step(
     normed_ref, xw_ref, yw_ref, ow_ref, taps_ref, vec_ref, wr_ref, we_ref, keep_ref,
-    u_ref, by_ref, before_ref, states_ref, mixed_ref, part_ref,
+    u_ref, by_ref, before_ref, states_ref, mixed_ref,
     window, conv, conv_low, rate, entry, carry,
 ):
     rows = normed_ref.shape[0]
@@ -133,7 +133,17 @@
         return states[CHUNK - 1 : CHUNK, :]
 
     carry[0:1, :] = lax.fori_loop(0, rows // CHUNK, scan_step, carry[0:1, :])
-    part_ref[...] = contract_last(mixed_ref[...], ow_ref[...]).astype(jnp.bfloat16)
+    return contract_last(mixed_ref[...], ow_ref[...]).astype(jnp.bfloat16)
+
+
+def forward_body(
+    normed_ref, xw_ref, yw_ref, ow_ref, taps_ref, vec_ref, wr_ref, we_ref, keep_ref,
+    u_ref, by_ref, before_ref, states_ref, mixed_ref, part_ref, *scratch,
+):
+    part_ref[...] = forward_step(
+        normed_ref, xw_ref, yw_ref, ow_ref, taps_ref, vec_ref, wr_ref, we_ref, keep_ref,
+        u_ref, by_ref, before_ref, states_ref, mixed_ref, *scratch,
+    )
 
 
 def backward_body(
@@ -392,6 +402,414 @@
     )
 
 
+MESH = pl.DeviceIdType.MESH
+ANYWHERE = pl.BlockSpec(memory_space=pl.ANY)
+IN_VMEM = pl.BlockSpec(memory_space=pltpu.VMEM)
+LINE = 4
+PLANE = 8
+PIECES = 4
+
+
+def send_to(src, dst, sent, arrived, axis, target):
+    return pltpu.make_async_remote_copy(
+        src_ref=src,
+        dst_ref=dst,
+        send_sem=sent,
+        recv_sem=arrived,
+        device_id={axis: target},
+        device_id_type=MESH,
+    )
+
+
+def sibling_of(h):
+    return h + 1 - 2 * lax.rem(h, 2)
+
+
+def across_of(h):
+    return h + 2 - 4 * lax.rem(lax.div(h, 2), 2)
+
+
+def along_of(h):
+    return lax.rem(h + 4, PLANE)
+
+
+def meet(row_line, plane):
+    r, h = lax.axis_index("row"), lax.axis_index("head")
+    barrier = pltpu.get_barrier_semaphore()
+    count = 0
+    if row_line:
+        for step in range(1, LINE):
+            pl.semaphore_signal(
+                barrier, inc=1, device_id={"row": lax.rem(r + step, LINE)}, device_id_type=MESH
+            )
+        count += LINE - 1
+    if plane == "all":
+        for step in range(1, PLANE):
+            pl.semaphore_signal(
+                barrier, inc=1, device_id={"head": lax.rem(h + step, PLANE)}, device_id_type=MESH
+            )
+        count += PLANE - 1
+    if plane == "near":
+        for target in (sibling_of(h), across_of(h), along_of(h), across_of(along_of(h))):
+            pl.semaphore_signal(barrier, inc=1, device_id={"head": target}, device_id_type=MESH)
+        count += 4
+    pl.semaphore_wait(barrier, count)
+
+
+class LineGather:
+    semaphores = (
+        pltpu.SemaphoreType.DMA((LINE,)),
+        pltpu.SemaphoreType.DMA((LINE,)),
+        pltpu.SemaphoreType.DMA((2,)),
+    )
+
+    def __init__(self, shard, full, sent, arrived, other):
+        self.r = lax.axis_index("row")
+        self.shard, self.full, self.sent, self.arrived, self.other = (
+            shard, full, sent, arrived, other,
+        )
+
+    def near(self, t):
+        gap = self.r - t
+        return (gap != 0) & (gap < 3) & (gap > -3)
+
+    def own(self, t):
+        return send_to(
+            self.shard, self.full.at[self.r], self.sent.at[t], self.arrived.at[self.r], "row", t
+        )
+
+    def handed(self, origin, target):
+        return send_to(
+            self.full.at[origin], self.full.at[origin], self.other.at[0], self.arrived.at[origin],
+            "row", target,
+        )
+
+    def local(self):
+        return pltpu.make_async_copy(self.shard, self.full.at[self.r], self.other.at[1])
+
+    def start(self):
+        for t in range(LINE):
+
+            @pl.when(self.near(t))
+            def _(t=t):
+                self.own(t).start()
+
+        self.local().start()
+
+    def forward(self):
+        for me, origin, target in ((2, 0, 3), (1, 3, 0)):
+
+            @pl.when(self.r == me)
+            def _(origin=origin, target=target):
+                copy = self.handed(origin, target)
+                copy.wait_recv()
+                copy.start()
+
+    def finish(self):
+        r = self.r
+        for t in range(LINE):
+            known = (r == t) | ((r == 2) & (t == 0)) | ((r == 1) & (t == 3))
+
+            @pl.when(jnp.logical_not(known))
+            def _(t=t):
+                self.handed(t, t).wait_recv()
+
+            @pl.when(self.near(t))
+            def _(t=t):
+                self.own(t).wait_send()
+
+        for me, origin, target in ((2, 0, 3), (1, 3, 0)):
+
+            @pl.when(r == me)
+            def _(origin=origin, target=target):
+                self.handed(origin, target).wait_send()
+
+        self.local().wait()
+
+
+class LineReduce:
+    semaphores = (
+        pltpu.SemaphoreType.DMA((LINE,)),
+        pltpu.SemaphoreType.DMA((LINE,)),
+        pltpu.SemaphoreType.DMA((2,)),
+    )
+
+    def __init__(self, parts, landed, passed, sent, arrived, other):
+        self.r = lax.axis_index("row")
+        self.parts, self.landed, self.passed = parts, landed, passed
+        self.sent, self.arrived, self.other = sent, arrived, other
+
+    def to_pass(self, me, origin, via):
+        return send_to(
+            self.parts.at[origin], self.passed, self.sent.at[origin], self.other.at[0], "row", via
+        )
+
+    def direct(self, t):
+        return send_to(
+            self.parts.at[t], self.landed.at[self.r], self.sent.at[t], self.arrived.at[self.r],
+            "row", t,
+        )
+
+    def plain(self, t):
+        r = self.r
+        ends = ((r == 0) & (t == 3)) | ((r == 3) & (t == 0))
+        added = ((r == 1) & (t == 3)) | ((r == 2) & (t == 0))
+        return jnp.logical_not(ends | added | (r == t))
+
+    def start(self):
+        for me, end, via in ((0, 3, 1), (3, 0, 2)):
+
+            @pl.when(self.r == me)
+            def _(me=me, end=end, via=via):
+                self.to_pass(me, end, via).start()
+
+        for t in range(LINE):
+
+            @pl.when(self.plain(t))
+            def _(t=t):
+                self.direct(t).start()
+
+    def forward(self):
+        for me, end in ((1, 3), (2, 0)):
+
+            @pl.when(self.r == me)
+            def _(me=me, end=end):
+                self.to_pass(me, end, end).wait_recv()
+                rows = self.passed.shape[0]
+                step = 64
+
+                def add(i, unused):
+                    at = pl.ds(pl.multiple_of(i * step, step), step)
+                    self.parts[end, at, :] = (
+                        self.parts[end, at, :].astype(jnp.float32)
+                        + self.passed[at, :].astype(jnp.float32)
+                    ).astype(jnp.bfloat16)
+                    return unused
+
+                lax.fori_loop(0, rows // step, add, 0)
+                self.direct(end).start()
+
+    def finish(self, write):
+        r = self.r
+        for t in range(LINE):
+
+            @pl.when(jnp.logical_not(unsent_to(r, t)))
+            def _(t=t):
+                send_to(
+                    self.parts.at[t], self.landed.at[t], self.sent.at[t], self.arrived.at[t],
+                    "row", t,
+                ).wait_recv()
+
+        rows = self.passed.shape[0]
+        step = 64
+
+        def add(i, unused):
+            at = pl.ds(pl.multiple_of(i * step, step), step)
+            total = self.parts[r, at, :].astype(jnp.float32)
+            for t in range(LINE):
+                total = total + jnp.where(
+                    unsent_to(r, t), 0.0, self.landed[t, at, :].astype(jnp.float32)
+                )
+            write(at, total)
+            return unused
+
+        lax.fori_loop(0, rows // step, add, 0)
+        for me, end, via in ((0, 3, 1), (3, 0, 2)):
+
+            @pl.when(r == me)
+            def _(me=me, end=end, via=via):
+                self.to_pass(me, end, via).wait_send()
+
+        for t in range(LINE):
+
+            @pl.when(jnp.logical_not(unsent_to(r, t)))
+            def _(t=t):
+                self.direct(t).wait_send()
+
+
+def unsent_to(r, t):
+    return ((r == 0) & (t == 3)) | ((r == 3) & (t == 0)) | (r == t)
+
+
+class PlaneGather:
+    semaphores = (
+        pltpu.SemaphoreType.DMA((PIECES, 7)),
+        pltpu.SemaphoreType.DMA((PIECES, 7)),
+        pltpu.SemaphoreType.DMA((1,)),
+    )
+    first = tuple(range(PIECES // 2))
+    second = tuple(range(PIECES // 2, PIECES))
+
+    def __init__(self, block, full, sent, arrived, other):
+        h = lax.axis_index("head")
+        self.h, self.side, self.x, self.y = h, sibling_of(h), across_of(h), along_of(h)
+        self.far = across_of(self.y)
+        self.block, self.full = block, full
+        self.sent, self.arrived, self.other = sent, arrived, other
+        self.rows = block.shape[0] // PIECES
+
+    def piece(self, owner, c):
+        return self.full.at[owner, pl.ds(c * self.rows, self.rows)]
+
+    def own(self, c, lane, target):
+        return send_to(
+            self.block.at[pl.ds(c * self.rows, self.rows)], self.piece(self.h, c),
+            self.sent.at[c, lane], self.arrived.at[c, lane], "head", target,
+        )
+
+    def hand(self, owner, c, lane, target):
+        return send_to(
+            self.piece(owner, c), self.piece(owner, c), self.sent.at[c, lane],
+            self.arrived.at[c, lane], "head", target,
+        )
+
+    def local(self):
+        return pltpu.make_async_copy(self.block, self.full.at[self.h], self.other.at[0])
+
+    def start(self):
+        for a, b in zip(self.first, self.second):
+            self.own(a, 1, self.x).start()
+            self.own(b, 2, self.y).start()
+        for a, b in zip(self.first, self.second):
+            self.own(b, 1, self.x).start()
+            self.own(a, 2, self.y).start()
+        for c in range(PIECES):
+            self.own(c, 0, self.side).start()
+        self.local().start()
+
+    def relay(self, place):
+        a, b = self.first[place], self.second[place]
+        self.hand(self.x, a, 1, self.x).wait_recv()
+        self.hand(self.x, a, 3, self.y).start()
+        self.hand(self.x, a, 4, self.side).start()
+        self.hand(self.y, b, 2, self.y).wait_recv()
+        self.hand(self.y, b, 3, self.x).start()
+        self.hand(self.y, b, 5, self.side).start()
+
+    def rest(self):
+        for a, b in zip(self.first, self.second):
+            self.hand(self.x, b, 1, self.x).wait_recv()
+            self.hand(self.x, b, 4, self.side).start()
+            self.hand(self.y, a, 2, self.y).wait_recv()
+            self.hand(self.y, a, 5, self.side).start()
+
+    def end(self):
+        for pair in zip(self.first, self.second):
+            for c in pair:
+                self.hand(self.far, c, 3, self.side).wait_recv()
+                self.hand(self.far, c, 6, self.side).start()
+        side = self.side
+        for c in range(PIECES):
+            for owner, lane in (
+                (side, 0), (across_of(side), 4), (along_of(side), 5),
+                (across_of(along_of(side)), 6),
+            ):
+                self.hand(owner, c, lane, side).wait_recv()
+        for c in range(PIECES):
+            for lane in range(7):
+                self.own(c, lane, side).wait_send()
+        self.local().wait()
+
+
+class PlaneReduce:
+    semaphores = (
+        pltpu.SemaphoreType.DMA((4,)),
+        pltpu.SemaphoreType.DMA((4,)),
+        pltpu.SemaphoreType.DMA((4,)),
+        pltpu.SemaphoreType.DMA((3,)),
+    )
+
+    @staticmethod
+    def buffers(rows, width):
+        return [
+            pltpu.VMEM((4, rows, width), jnp.bfloat16),
+            pltpu.VMEM((4, rows, width), jnp.bfloat16),
+            pltpu.VMEM((4, rows, width), jnp.bfloat16),
+            pltpu.VMEM((3, rows, width), jnp.bfloat16),
+        ]
+
+    def __init__(self, staged, beside, mine, landed, side_sent, side_arrived, sent, arrived):
+        h = lax.axis_index("head")
+        self.h, self.core, self.chip = h, lax.rem(h, 2), lax.div(h, 2)
+        self.staged, self.beside, self.mine, self.landed = staged, beside, mine, landed
+        self.side_sent, self.side_arrived = side_sent, side_arrived
+        self.sent, self.arrived = sent, arrived
+
+    def aside(self, chip):
+        return send_to(
+            self.staged.at[chip], self.beside.at[chip], self.side_sent.at[chip],
+            self.side_arrived.at[chip], "head", sibling_of(self.h),
+        )
+
+    def place(self, chip):
+        flip_x = lax.rem(chip + self.chip, 2)
+        flip_y = lax.rem(lax.div(chip, 2) + lax.div(self.chip, 2), 2)
+        return flip_x + 2 * flip_y - 1
+
+    def across(self, chip):
+        at = self.place(chip)
+        return send_to(
+            self.mine.at[chip], self.landed.at[at], self.sent.at[chip], self.arrived.at[at],
+            "head", 2 * chip + self.core,
+        )
+
+    def put(self, block, value):
+        chip, core = lax.div(block, 2), lax.rem(block, 2)
+
+        @pl.when(core == self.core)
+        def _():
+            self.mine[chip] = value
+
+        @pl.when(core != self.core)
+        def _():
+            self.staged[chip] = value
+            self.aside(chip).start()
+
+    def pass_on(self, block):
+        chip, core = lax.div(block, 2), lax.rem(block, 2)
+
+        @pl.when(core == self.core)
+        def _():
+            self.aside(chip).wait_recv()
+            rows = self.mine.shape[1]
+            step = 32
+
+            def add(i, unused):
+                at = pl.ds(pl.multiple_of(i * step, step), step)
+                self.mine[chip, at, :] = (
+                    self.mine[chip, at, :].astype(jnp.float32)
+                    + self.beside[chip, at, :].astype(jnp.float32)
+                ).astype(jnp.bfloat16)
+                return unused
+
+            lax.fori_loop(0, rows // step, add, 0)
+
+            @pl.when(chip != self.chip)
+            def _():
+                self.across(chip).start()
+
+    def arrive(self):
+        for at in range(3):
+            send_to(
+                self.landed.at[at], self.landed.at[at], self.sent.at[0], self.arrived.at[at],
+                "head", self.h,
+            ).wait_recv()
+
+    def total(self, at):
+        value = self.mine[self.chip, at, :].astype(jnp.float32)
+        for place in range(3):
+            value = value + self.landed[place, at, :].astype(jnp.float32)
+        return value
+
+    def finish(self):
+        for chip in range(4):
+            self.aside(chip).wait_send()
+
+            @pl.when(chip != self.chip)
+            def _(chip=chip):
+                self.across(chip).wait_send()
+
+
 def norm_apply(rows, gain):
     return rows * lax.rsqrt(jnp.mean(rows * rows, axis=-1, keepdims=True) + EPSILON) * gain
 
@@ -402,6 +820,320 @@
 
 def scatter(values, axis_name, axis):
     return lax.psum_scatter(values, axis_name, scatter_dimension=axis, tiled=True)
+
+def norm_rows(rows, gain):
+    return rows * lax.rsqrt(jnp.mean(rows * rows, axis=-1, keepdims=True) + EPSILON) * gain
+
+
+def open_body(
+    x_ref, tile_ref, xs, ys, zs, full, xf, yf, zf, gains_ref,
+    normed, column, spread, gain_sent, gain_arrived, wide_sent, wide_arrived, *semaphores,
+):
+    r, h = lax.axis_index("row"), lax.axis_index("head")
+    lines = [
+        LineGather(src, dst, *semaphores[3 * k : 3 * k + 3])
+        for k, (src, dst) in enumerate(((xs, xf), (ys, yf), (zs, zf)))
+    ]
+    plane = PlaneGather(normed, full, *semaphores[9:12])
+    meet(True, "all")
+
+    def up_line(t):
+        return send_to(
+            column.at[r], column.at[r], gain_sent.at[t], gain_arrived.at[r], "row", t
+        )
+
+    def from_line(t):
+        return send_to(
+            column.at[t], column.at[t], gain_sent.at[t], gain_arrived.at[t], "row", t
+        )
+
+    def over_plane(step, owner):
+        return send_to(
+            column, spread.at[owner], wide_sent.at[step], wide_arrived.at[owner], "head",
+            lax.rem(h + step, PLANE),
+        )
+
+    column[r] = tile_ref[...]
+    for step in range(1, LINE):
+        up_line(lax.rem(r + step, LINE)).start()
+    for line in lines:
+        line.start()
+    for step in range(1, LINE):
+        from_line(lax.rem(r + step, LINE)).wait_recv()
+    for step in range(1, PLANE):
+        over_plane(step, h).start()
+    spread[h] = column[...]
+    for step in range(1, PLANE):
+        over_plane(step, lax.rem(h + step, PLANE)).wait_recv()
+
+    share = tile_ref.shape[1] // 2
+    low = lax.broadcasted_iota(jnp.int32, (1, 2 * share), 1) < share
+    for line_place in range(LINE):
+        for pair in range(PLANE // 2):
+            even = spread[2 * pair, line_place][0:1, :]
+            odd = spread[2 * pair + 1, line_place][0:1, :]
+            at = (line_place * (PLANE // 2) + pair) * 2 * share
+            gains_ref[0:1, at : at + 2 * share] = jnp.where(low, even, pltpu.roll(odd, share, 1))
+            gains_ref[1:2, at : at + 2 * share] = jnp.where(low, pltpu.roll(even, share, 1), odd)
+
+    def make(i, unused):
+        at = pl.ds(pl.multiple_of(i * CHUNK, CHUNK), CHUNK)
+        normed[at, :] = norm_rows(x_ref[at, :].astype(jnp.float32), gains_ref[0:1, :]).astype(
+            jnp.bfloat16
+        )
+        return unused
+
+    lax.fori_loop(0, x_ref.shape[0] // CHUNK, make, 0)
+    plane.start()
+    plane.relay(0)
+    lines[0].forward()
+    plane.relay(1)
+    plane.rest()
+    plane.end()
+    for line in lines[1:]:
+        line.forward()
+    for line in lines:
+        line.finish()
+    for step in range(1, LINE):
+        up_line(lax.rem(r + step, LINE)).wait_send()
+    for step in range(1, PLANE):
+        over_plane(step, h).wait_send()
+
+
+def open_block(layer_in, tile, weights):
+    rows, width = layer_in.shape
+    return pl.pallas_call(
+        open_body,
+        in_specs=[IN_VMEM, IN_VMEM] + [ANYWHERE] * 3,
+        out_specs=[ANYWHERE] * 4 + [IN_VMEM],
+        out_shape=[jax.ShapeDtypeStruct((PLANE, rows, width), jnp.bfloat16)]
+        + [jax.ShapeDtypeStruct((LINE,) + item.shape, item.dtype) for item in weights]
+        + [jax.ShapeDtypeStruct((2, width), jnp.float32)],
+        scratch_shapes=[
+            pltpu.VMEM((rows, width), jnp.bfloat16),
+            pltpu.VMEM((LINE,) + tile.shape, jnp.float32),
+            pltpu.VMEM((PLANE, LINE) + tile.shape, jnp.float32),
+            pltpu.SemaphoreType.DMA((LINE,)),
+            pltpu.SemaphoreType.DMA((LINE,)),
+            pltpu.SemaphoreType.DMA((PLANE,)),
+            pltpu.SemaphoreType.DMA((PLANE,)),
+            *(LineGather.semaphores * 3),
+            *PlaneGather.semaphores,
+        ],
+        compiler_params=pltpu.CompilerParams(
+            collective_id=0, has_side_effects=True, vmem_limit_bytes=24 * 2**20
+        ),
+        name="open_block",
+    )(layer_in, tile, *weights)
+
+
+def forward_linked_body(
+    normed_ref, xw_ref, yw_ref, ow_ref, taps_ref, vec_ref, wr_ref, we_ref, keep_ref,
+    x_ref, gain_ref, shard,
+    u_ref, by_ref, before_ref, states_ref, mixed_ref, residual_ref, two_ref, gathered,
+    window, conv, conv_low, rate, entry, carry, *links,
+):
+    step = pl.program_id(0)
+    plane = PlaneReduce(*links[:8])
+    line = LineGather(shard, gathered, *links[8:11])
+
+    @pl.when(step == 0)
+    def _():
+        meet(True, "near")
+        line.start()
+
+    @pl.when(step > 0)
+    def _():
+        plane.pass_on(step - 1)
+
+    value = forward_step(
+        normed_ref, xw_ref, yw_ref, ow_ref, taps_ref, vec_ref, wr_ref, we_ref, keep_ref,
+        u_ref, by_ref, before_ref, states_ref, mixed_ref,
+        window, conv, conv_low, rate, entry, carry,
+    )
+    plane.put(step, value)
+
+    @pl.when(step == 6)
+    def _():
+        line.forward()
+
+    @pl.when(step == PLANE - 1)
+    def _():
+        plane.pass_on(step)
+        plane.arrive()
+
+        def make(i, unused):
+            at = pl.ds(pl.multiple_of(i * CHUNK, CHUNK), CHUNK)
+            residual = x_ref[at, :].astype(jnp.float32) + plane.total(at)
+            residual_ref[at, :] = residual
+            two_ref[at, :] = norm_rows(residual, gain_ref[...]).astype(jnp.bfloat16)
+            return unused
+
+        lax.fori_loop(0, x_ref.shape[0] // CHUNK, make, 0)
+        plane.finish()
+        line.finish()
+
+
+def forward_linked(normed, xw, yw, ow, taps, vec, wr, we, keep, layer_in, gain, shard):
+    length, width = normed.shape
+    chans = xw.shape[1]
+    rows = length // PLANE
+    tile = lambda columns: pl.BlockSpec((rows, columns), lambda i: (i, 0))
+    return pl.pallas_call(
+        forward_linked_body,
+        grid=(PLANE,),
+        in_specs=[
+            tile(width), whole(xw.shape), whole(yw.shape), whole(ow.shape), whole(taps.shape),
+            whole(vec.shape), whole(wr.shape), whole(we.shape), tile(keep.shape[1]),
+            whole(layer_in.shape), whole(gain.shape), ANYWHERE,
+        ],
+        out_specs=[tile(chans)] * 5 + [whole((rows, width))] * 2 + [ANYWHERE],
+        out_shape=[
+            jax.ShapeDtypeStruct((length, chans), jnp.bfloat16),
+            jax.ShapeDtypeStruct((length, chans), jnp.float32),
+            jax.ShapeDtypeStruct((length, chans), jnp.float32),
+            jax.ShapeDtypeStruct((length, chans), jnp.bfloat16),
+            jax.ShapeDtypeStruct((length, chans), jnp.bfloat16),
+            jax.ShapeDtypeStruct((rows, width), jnp.float32),
+            jax.ShapeDtypeStruct((rows, width), jnp.bfloat16),
+            jax.ShapeDtypeStruct((LINE,) + shard.shape, shard.dtype),
+        ],
+        scratch_shapes=[
+            pltpu.VMEM((rows + 8, chans), jnp.float32),
+            pltpu.VMEM((rows, chans), jnp.float32),
+            pltpu.VMEM((rows, chans), jnp.bfloat16),
+            pltpu.VMEM((rows, chans), jnp.float32),
+            pltpu.VMEM((rows, chans), jnp.float32),
+            pltpu.VMEM((8, chans), jnp.float32),
+            *PlaneReduce.buffers(rows, width),
+            *PlaneReduce.semaphores,
+            *LineGather.semaphores,
+        ],
+        compiler_params=pltpu.CompilerParams(
+            collective_id=1, has_side_effects=True, vmem_limit_bytes=56 * 2**20
+        ),
+        name="mixer_forward_linked",
+    )(normed, xw, yw, ow, taps, vec, wr, we, keep, layer_in, gain, shard)
+
+
+def spread_body(block, shard, full, gathered, *semaphores):
+    plane = PlaneGather(block, full, *semaphores[:3])
+    line = LineGather(shard, gathered, *semaphores[3:6])
+    meet(True, "near")
+    line.start()
+    plane.start()
+    plane.relay(0)
+    plane.relay(1)
+    plane.rest()
+    line.forward()
+    plane.end()
+    line.finish()
+
+
+def spread(block, shard, place):
+    return pl.pallas_call(
+        spread_body,
+        in_specs=[ANYWHERE] * 2,
+        out_specs=[ANYWHERE] * 2,
+        out_shape=[
+            jax.ShapeDtypeStruct((PLANE,) + block.shape, block.dtype),
+            jax.ShapeDtypeStruct((LINE,) + shard.shape, shard.dtype),
+        ],
+        scratch_shapes=[*PlaneGather.semaphores, *LineGather.semaphores],
+        compiler_params=pltpu.CompilerParams(collective_id=place, has_side_effects=True),
+        name="spread",
+    )(block, shard)
+
+
+def ffn_up_body(
+    two_ref, gate_ref, up_ref, cot, shard,
+    gates_ref, ups_ref, hidden_ref, full, gathered, *semaphores,
+):
+    step = pl.program_id(0)
+    plane = PlaneGather(cot, full, *semaphores[:3])
+    line = LineGather(shard, gathered, *semaphores[3:6])
+
+    @pl.when(step == 0)
+    def _():
+        meet(True, "near")
+        line.start()
+        plane.start()
+
+    @pl.when(step == 3)
+    def _():
+        plane.relay(0)
+
+    @pl.when(step == 5)
+    def _():
+        plane.relay(1)
+
+    gates = dot_plain(two_ref[...], gate_ref[...])
+    ups = dot_plain(two_ref[...], up_ref[...])
+    gates_ref[...] = gates
+    ups_ref[...] = ups
+    rows = gates_ref.shape[0]
+
+    def make(i, unused):
+        at = pl.ds(pl.multiple_of(i * CHUNK, CHUNK), CHUNK)
+        hidden_ref[at, :] = (gelu_only(gates_ref[at, :]) * ups_ref[at, :]).astype(jnp.bfloat16)
+        return unused
+
+    lax.fori_loop(0, rows // CHUNK, make, 0)
+
+    @pl.when(step == PLANE - 1)
+    def _():
+        plane.rest()
+        line.forward()
+        plane.end()
+        line.finish()
+
+
+def ffn_up(two, gate, up, cot, shard):
+    length, width = two.shape
+    units = gate.shape[1]
+    rows = length // PLANE
+    tile = lambda columns: pl.BlockSpec((rows, columns), lambda i: (i, 0))
+    return pl.pallas_call(
+        ffn_up_body,
+        grid=(PLANE,),
+        in_specs=[tile(width), whole(gate.shape), whole(up.shape), ANYWHERE, ANYWHERE],
+        out_specs=[tile(units)] * 3 + [ANYWHERE] * 2,
+        out_shape=[
+            jax.ShapeDtypeStruct((length, units), jnp.float32),
+            jax.ShapeDtypeStruct((length, units), jnp.float32),
+            jax.ShapeDtypeStruct((length, units), jnp.bfloat16),
+            jax.ShapeDtypeStruct((PLANE,) + cot.shape, cot.dtype),
+            jax.ShapeDtypeStruct((LINE,) + shard.shape, shard.dtype),
+        ],
+        scratch_shapes=[*PlaneGather.semaphores, *LineGather.semaphores],
+        compiler_params=pltpu.CompilerParams(
+            collective_id=3, has_side_effects=True, vmem_limit_bytes=40 * 2**20
+        ),
+        name="ffn_up",
+    )(two, gate, up, cot, shard)
+
+
+def mixer_params(
+    conv_weight, conv_bias, rate_weight, rate_bias, entry_weight, entry_bias, decay_param, chans
+):
+    used = conv_bias.shape[0]
+    spare = (0, chans - used)
+    decay_wide = jnp.pad(decay_param, spare, constant_values=2.0)
+    blank = jnp.zeros((chans,), jnp.float32)
+    vec = jnp.stack(
+        [
+            jnp.pad(conv_bias, spare),
+            jnp.pad(rate_bias, spare),
+            jnp.pad(entry_bias, spare),
+            -8.0 * jax.nn.softplus(-decay_wide),
+            blank,
+            blank,
+            blank,
+            blank,
+        ]
+    )
+    taps = jnp.pad(conv_weight, ((0, 0), spare))
+    return taps, vec, block_diagonal(rate_weight, chans), block_diagonal(entry_weight, chans)
 
 
 def shards(
@@ -437,24 +1169,9 @@
     up_rows = gather(up_weight, "row", 0)
     down_rows = gather(down_weight, "row", 0)
 
-    spare = (0, chans - used)
-    decay_wide = jnp.pad(decay_param, spare, constant_values=2.0)
-    blank = jnp.zeros((chans,), jnp.float32)
-    vec = jnp.stack(
-        [
-            jnp.pad(conv_bias, spare),
-            jnp.pad(rate_bias, spare),
-            jnp.pad(entry_bias, spare),
-            -8.0 * jax.nn.softplus(-decay_wide),
-            blank,
-            blank,
-            blank,
-            blank,
-        ]
-    )
-    taps = widen(conv_weight)
-    wr = block_diagonal(rate_weight, chans)
-    we = block_diagonal(entry_weight, chans)
+    taps, vec, wr, we = mixer_params(
+        conv_weight, conv_bias, rate_weight, rate_bias, entry_weight, entry_bias, decay_param, chans
+    )
     keep = keep_columns(resets)
 
     inputs = layer_in.astype(jnp.float32)
@@ -523,10 +1240,114 @@
         down_grad.astype(jnp.float32),
     )
 
+def shards_linked(
+    layer_in,
+    cotangent,
+    mix_gain,
+    ffn_gain,
+    x_weight,
+    y_weight,
+    out_weight,
+    conv_weight,
+    conv_bias,
+    rate_weight,
+    rate_bias,
+    entry_weight,
+    entry_bias,
+    decay_param,
+    gate_weight,
+    up_weight,
+    down_weight,
+    resets,
+):
+    heads, head_width = rate_weight.shape[:2]
+    used = conv_bias.shape[0]
+    chans = -(-used // 128) * 128
+    widen = lambda values: jnp.pad(values, ((0, 0), (0, chans - used)))
+    flat = lambda values: values.reshape((-1, values.shape[-1]))
+    taps, vec, wr, we = mixer_params(
+        conv_weight, conv_bias, rate_weight, rate_bias, entry_weight, entry_bias, decay_param, chans
+    )
+    keep = keep_columns(resets)
+    own_gains = jnp.concatenate([mix_gain, ffn_gain]).astype(jnp.float32)
+    tile = jnp.broadcast_to(own_gains, (8, own_gains.shape[0]))
+
+    normed_group, x_rows, y_rows, out_rows, gains = open_block(
+        layer_in, tile, (widen(x_weight), widen(y_weight), widen(out_weight))
+    )
+    normed_group, x_rows, y_rows, out_rows = map(flat, (normed_group, x_rows, y_rows, out_rows))
+    u, by, before, states, mixed, residual, normed_two, gate_rows = forward_linked(
+        normed_group, x_rows, y_rows, out_rows, taps, vec, wr, we, keep, layer_in, gains[1:2],
+        gate_weight,
+    )
+    two_group, up_rows = spread(normed_two, up_weight, 2)
+    gate_rows, two_group, up_rows = map(flat, (gate_rows, two_group, up_rows))
+    gates, ups, hidden, cot_group, down_rows = ffn_up(
+        two_group, gate_rows, up_rows, cotangent, down_weight
+    )
+    cot_group, down_rows = map(flat, (cot_group, down_rows))
+
+    inputs = layer_in.astype(jnp.float32)
+    normed_f, norm_back_one = jax.vjp(norm_apply, inputs, gains[0])
+    normed_two_f, norm_back_two = jax.vjp(norm_apply, residual, gains[1])
+    activated, slope = gelu_both(gates)
+    ffn_part = contract_last(hidden, down_rows).astype(jnp.bfloat16)
+    d_hidden = dot_plain(cot_group, down_rows)
+    d_gates = (d_hidden * ups * slope).astype(jnp.bfloat16)
+    d_ups = (d_hidden * activated).astype(jnp.bfloat16)
+    d_two_part = (contract_last(d_gates, gate_rows) + contract_last(d_ups, up_rows)).astype(
+        jnp.bfloat16
+    )
+    gate_grad = scatter(contract_first(two_group, d_gates).astype(jnp.bfloat16), "row", 0)
+    up_grad = scatter(contract_first(two_group, d_ups).astype(jnp.bfloat16), "row", 0)
+    down_grad = scatter(contract_first(cot_group, hidden).astype(jnp.bfloat16), "row", 0)
+    layer_out = (residual + scatter(ffn_part, "head", 0).astype(jnp.float32)).astype(jnp.bfloat16)
+    d_two = scatter(d_two_part, "head", 0).astype(jnp.float32)
+    d_resid_norm, d_ffn_gain = norm_back_two(d_two)
+    d_residual = cotangent.astype(jnp.float32) + d_resid_norm
+    d_res_group = gather(d_residual.astype(jnp.bfloat16), "head", 0)
+    d_bx, d_by, d_part, d_taps, d_vec, d_wr, d_we = mixer_backward(
+        d_res_group, x_rows, y_rows, out_rows, taps, vec, wr, we, keep, u, by, before, states, ROWS
+    )
+    out_grad = scatter(contract_first(d_res_group, mixed).astype(jnp.bfloat16), "row", 0)
+    x_grad = scatter(contract_first(normed_group, d_bx).astype(jnp.bfloat16), "row", 0)
+    y_grad = scatter(contract_first(normed_group, d_by).astype(jnp.bfloat16), "row", 0)
+    d_normed = scatter(d_part, "head", 0).astype(jnp.float32)
+    d_inputs, d_mix_gain = norm_back_one(d_normed)
+    layer_in_grad = (d_inputs + d_residual).astype(jnp.bfloat16)
+
+    small = [
+        d_taps[:, :used],
+        d_vec[0, :used],
+        diagonal_blocks(d_wr, heads, head_width),
+        d_vec[1, :used],
+        diagonal_blocks(d_we, heads, head_width),
+        d_vec[2, :used],
+        d_vec[3, :used] * (8.0 * jax.nn.sigmoid(-decay_param)),
+    ]
+    small = [lax.psum(item.astype(jnp.bfloat16), "row").astype(jnp.float32) for item in small]
+    mix_part = scatter(d_mix_gain, ("row", "head"), 0)
+    ffn_part_grad = scatter(d_ffn_gain, ("row", "head"), 0)
+    wide = lambda values: values[:, :used].astype(jnp.float32)
+    return (
+        layer_out,
+        layer_in_grad,
+        mix_part,
+        ffn_part_grad,
+        wide(x_grad),
+        wide(y_grad),
+        wide(out_grad),
+        *small,
+        gate_grad.astype(jnp.float32),
+        up_grad.astype(jnp.float32),
+        down_grad.astype(jnp.float32),
+    )
+
 
 def solution(mesh):
+    linked = mesh.shape["row"] == LINE and mesh.shape["head"] == PLANE
     return jax.shard_map(
-        shards,
+        shards_linked if linked else shards,
         mesh=mesh,
         in_specs=(
             P(("row", "head"), None),

time: 1280 us -> 1010 us (0.79)
  waiting for transfers between devices: 859 us -> 357 us
  Pallas kernels: 113 us -> 395 us
  blocking collectives: 94.6 us -> 50.3 us
  matrix products: 138 us -> 114 us
  local copies, waits for them, and re-layouts: 23.6 us -> 37.2 us
    all_gather x10 -> x1, waiting for transfers between devices: 416 us -> 19.8 us  [gather(): return lax.all_gather(values, axis_name, axis=axis, tiled=True)]
    pallas_call x1 -> x4, Pallas kernels: 46.8 us -> 329 us  [the longest x1 94.9 us: forward_linked(): pl.pallas_call(forward_linked_body, grid=(PLANE,), in_specs=[tile(width),...]
    reduce_scatter x10 -> x9, waiting for transfers between devices: 416 us -> 313 us  [scatter(): lax.psum_scatter(values, axis_name, scatter_dimension=axis, tiled=True)]
    unnamed x2 -> x1, blocking collectives: 84 us -> 39.8 us
    dot_general x3 -> x1, matrix products: 40.8 us -> 17.8 us  [dot_plain(): return jnp.dot(left, right, preferred_element_type=jnp.float32)]
    unnamed x81 -> x82, local copies, waits for them, and re-layouts: 19.7 us -> 26.5 us
  transfers between devices with their start and end apart: 21 -> 11, of which waited for: 19 -> 9; matrix products, arithmetic and copies ran while one was open for 11% -> 10% of each run, Pallas kernels for 5% -> 7%
where the time goes in v2:
time: 1010 us; the launch traced here: 1000 us
  Pallas kernels  395 us (39%)
  waiting for transfers between devices  357 us (35%)
  matrix products  114 us (11%)
  blocking collectives  50.3 us (5%)
  local copies, waits for them, and re-layouts  37.2 us (4%)
  other arithmetic  30.5 us (3%)
  between operations  16.5 us (2%)
    reduce_scatter x9, waiting for transfers between devices, scatter(): lax.psum_scatter(values, axis_name, scatter_dimension=axis, tiled=True)  313 us
    pallas_call x1, Pallas kernels, forward_linked(): pl.pallas_call(forward_linked_body, grid=(PLANE,), in_specs=[tile(width),...  94.9 us
    pallas_call x1, Pallas kernels, open_block(): pl.pallas_call(open_body, in_specs=[IN_VMEM, IN_VMEM] + [ANYWHERE] * 3, o...  86.5 us
    pallas_call x1, Pallas kernels, spread(): pl.pallas_call(spread_body, in_specs=[ANYWHERE] * 2, out_specs=[ANYWHERE]...  77.1 us
    pallas_call x1, Pallas kernels, ffn_up(): pl.pallas_call(ffn_up_body, grid=(PLANE,), in_specs=[tile(width), whole(g...  70.3 us
    pallas_call x1, Pallas kernels, mixer_backward(): pl.pallas_call(backward_body, grid=(blocks,), in_specs=[tile(width), whol...  66.4 us
    dot_general x6, matrix products, contract_first(): lax.dot_general(left, right, (((0,), (0,)), ((), ())), preferred_element_...  62.4 us
    unnamed x1, blocking collectives  39.8 us
  transfers between devices with their start and end apart: 11, of which 9 were waited for; matrix products, arithmetic and copies ran while one was open for 10% of the time, Pallas kernels for 7%

profile of v2, /device:TPU:0, one launch (start us, length us, event | category | flops | bytes accessed | tf_op | source)
XLA Modules:
  0.0 1002.2 jit_solution(1028636419993629805)
XLA Ops:
  20.8 86.5 %open_block.1 = (bf16[8,256,2048]{2,1,0:T(8,128)(2,1)S(1)}, bf16[4,512,384]{2,1,0:T(8,128)(2,1)S(1)}, bf16[4,512,384]{2,1,0:T(8,128)(2,1)S(1)}, bf16[4,512,384]{2,1,0:T(8,128)(2,1)S(1)}, f32[2,2048]{1,0:T(2,128)S(1)}) custom-call(bf16[256,2048]{1,0:T(8,128)(2,1)S(1)} %copy-done, f32[8,128]{1,0:T(8,128)S(1)} %broadcast_in_dim.11.tile_ref, ...), custom_call_target="tpu_custom_call" | custom-call | tf_op jit(solution)/shard_map/open_block/pallas_call | solution.py:905
  115.3 94.9 %mixer_forward_linked.1 = (bf16[2048,384]{1,0:T(8,128)(2,1)}, f32[2048,384]{1,0:T(8,128)}, f32[2048,384]{1,0:T(8,128)}, bf16[2048,384]{1,0:T(8,128)(2,1)}, bf16[...) custom-call(bf16[2048,2048]{1,0:T(8,128)(2,1)} %bitcast.62, ...), custom_call_target="tpu_custom_call" | custom-call | tf_op jit(solution)/shard_map/mixer_forward_linked/pallas_call | solution.py:982
  210.2 77.1 %spread.1 = (bf16[8,256,2048]{2,1,0:T(8,128)(2,1)}, bf16[4,512,768]{2,1,0:T(8,128)(2,1)}) custom-call(bf16[256,2048]{1,0:T(8,128)(2,1)} %get-tuple-element.50.block, bf16[512,768]{1,0:T(8,128)(2,1)} %shard.4), custom_call_target="tpu_custom_call" | custom-call | tf_op jit(solution)/shard_map/spread/pallas_call | solution.py:1034
  291.2 70.3 %ffn_up.1 = (f32[2048,768]{1,0:T(8,128)}, f32[2048,768]{1,0:T(8,128)}, bf16[2048,768]{1,0:T(8,128)(2,1)S(1)}, bf16[8,256,2048]{2,1,0:T(8,128)(2,1)}, bf16[4,512,768]{2,1,0:T(8,128)(2,1)S(1)}) custom-call(bf16[2048,2048]{1,0:T(8,128)(2,1)} %bitcast.77, bf16[2048,768]{1,0:T(8,128)(2,1)S(1)} %bitcast.65, bf16[2048,768]{1,0:T(8,128)(2,1)S(1)} %bitcast.67, ...), custom_call_target="tpu_custom_call" | custom-call | tf_op jit(solution)/shard_map/ffn_up/pallas_call | solution.py:1096
  361.5 17.8 %multiply_convert_fusion = (bf16[2048,768]{1,0:T(8,128)(2,1)S(1)}, bf16[2048,768]{1,0:T(8,128)(2,1)S(1)}) fusion(f32[2048,768]{1,0:T(8,128)} %get-tuple-element.58, f32[2048,768]{1,0:T(8,128)} %get-tuple-element.57, bf16[2048,2048]{1,0:T(8,128)(2,1)} %bitcast.85, bf16[2048,768]{1,0:T(8,128)(2,1)S(1)} %bitcast.75), kind=kOutput, calls=%fused_computation.2 | convolution fusion | flops 6477053952 | bytes 30408704 | tf_op jit(solution)/shard_map/dot_general | solution.py:35
  379.5 9.6 fusion.33
  389.1 12.9 %add_convert_fusion = bf16[2048,2048]{1,0:T(8,128)(2,1)} fusion(f32[2048,2048]{1,0:T(8,128)} %fusion.33, bf16[2048,768]{1,0:T(8,128)(2,1)S(1)} %get-tuple-element.142, bf16[2048,768]{1,0:T(8,128)(2,1)S(1)} %bitcast.68), kind=kOutput, calls=%fused_computation | convolution fusion | flops 6450839552 | bytes 31457280 | tf_op jit(solution)/shard_map/dot_general | solution.py:39
  403.8 86.3 %reduce-scatter.12.cloned.1.call-done = bf16[256,2048]{1,0:T(8,128)(2,1)} async-done(((bf16[2048,2048]{1,0:T(8,128)(2,1)}), bf16[256,2048]{1,0:T(8,128)(2,1)}) %reduce-scatter.12.cloned.1.call-update) | async-done | bytes 1048592 | tf_op jit(solution)/shard_map/reduce_scatter | solution.py:822
  493.9 11.4 %convolution_convert_fusion.1 = bf16[2048,768]{1,0:T(8,128)(2,1)} fusion(bf16[2048,2048]{1,0:T(8,128)(2,1)} %bitcast.86, bf16[2048,768]{1,0:T(8,128)(2,1)} %copy-done.17), kind=kOutput, calls=%fused_computation.10 | convolution fusion | flops 6444023808 | bytes 14680064 | tf_op jit(solution)/shard_map/dot_general | solution.py:45
  505.3 11.4 %convolution_convert_fusion.2 = bf16[2048,768]{1,0:T(8,128)(2,1)} fusion(bf16[2048,2048]{1,0:T(8,128)(2,1)} %bitcast.78, bf16[2048,768]{1,0:T(8,128)(2,1)} %copy-done.35), kind=kOutput, calls=%fused_computation.11 | convolution fusion | flops 6444023808 | bytes 14680064 | tf_op jit(solution)/shard_map/dot_general | solution.py:45
  516.8 11.7 %convolution_convert_fusion.3 = bf16[2048,768]{1,0:T(8,128)(2,1)} fusion(bf16[2048,2048]{1,0:T(8,128)(2,1)} %bitcast.79, bf16[2048,768]{1,0:T(8,128)(2,1)} %copy-done.34), kind=kOutput, calls=%fused_computation.12 | convolution fusion | flops 6444023808 | bytes 14680064 | tf_op jit(solution)/shard_map/dot_general | solution.py:45
  528.6 19.8 %all-gather.2.cloned.1.call-done.d_res_ref = bf16[2048,2048]{1,0:T(8,128)(2,1)} async-done(((bf16[256,2048]{1,0:T(8,128)(2,1)}), bf16[2048,2048]{1,0:T(8,128)(2,1)}) %all-gather.2.cloned.1.call-update) | async-done | bytes 8388624 | tf_op jit(solution)/shard_map/all_gather | solution.py:818
  548.4 66.4 %mixer_backward.1 = (bf16[2048,384]{1,0:T(8,128)(2,1)S(1)}, bf16[2048,384]{1,0:T(8,128)(2,1)S(1)}, bf16[2048,2048]{1,0:T(8,128)(2,1)}, f32[4,384]{1,0:T(4,128)S(...) custom-call(bf16[2048,2048]{1,0:T(8,128)(2,1)} %all-gather.2.cloned.1.call-done.d_res_ref, ...), custom_call_target="tpu_custom_call" | custom-call | flops 9663676416 | bytes 40370176 | tf_op jit(solution)/shard_map/mixer_backward/pallas_call | solution.py:323
  628.5 9.7 convolution_convert_fusion.6
  648.2 11.3 %convolution_convert_fusion = bf16[2048,2048]{1,0:T(8,128)(2,1)} fusion(bf16[2048,768]{1,0:T(8,128)(2,1)} %copy-done.17, bf16[2048,768]{1,0:T(8,128)(2,1)} %bitcast.76), kind=kOutput, calls=%fused_computation.1 | convolution fusion | flops 6446645248 | bytes 14680064 | tf_op jit(solution)/shard_map/dot_general | solution.py:39
  665.9 24.6 %reduce-scatter.22.cloned.1.call-done = bf16[512,768]{1,0:T(8,128)(2,1)} async-done(((bf16[2048,768]{1,0:T(8,128)(2,1)}), bf16[512,768]{1,0:T(8,128)(2,1)}) %reduce-scatter.22.cloned.1.call-update) | async-done | bytes 786448 | tf_op jit(solution)/shard_map/reduce_scatter | solution.py:822
  692.9 10.5 %all-reduce.22 = (bf16[4,342]{1,0:T(4,128)(2,1)S(1)}, bf16[342]{0:T(512)(128)(2,1)S(1)}, bf16[342]{0:T(512)(128)(2,1)S(1)}, bf16[342]{0:T(512)(128)(2,1)S(1)}, bf16[342]{0:T(512)(128)(2,1)S(1)}) all-reduce(bf16[4,342]{1,0:T(4,128)(2,1)S(1)} %slice.143, ...), channel_id=1, replica_groups=mesh['row'=4,'head'=8] {'row'}, use_global_device_ids=true, to_apply=%region_14.15 | all-reduce | flops 2736 | bytes 10944 | tf_op jit(solution)/shard_map/psum | solution.py:1328
  706.4 23.8 %all-reduce.26.cloned.1.call-done = (bf16[2,171,171]{2,1,0:T(8,128)(2,1)}, bf16[2,171,171]{2,1,0:T(8,128)(2,1)}) async-done(((bf16[2,171,171]{2,1,0:T(8,128)(2,1)}, bf16[2,171,171]{2,1,0:T(8,128)(2,1)}), (bf16[2,171,171]{2,1,0:T(8,128)(2,1)}, bf16[2,171,171]{2,1,0:T(8,128)(2,1)})) %all-reduce.26.cloned.1.call-update) | async-done | bytes 233944 | tf_op jit(solution)/shard_map/psum | solution.py:1328
  733.8 33.9 %reduce-scatter.20.cloned.1.call-done = bf16[512,384]{1,0:T(8,128)(2,1)} async-done(((bf16[2048,384]{1,0:T(8,128)(2,1)}), bf16[512,384]{1,0:T(8,128)(2,1)}) %reduce-scatter.20.cloned.1.call-update) | async-done | bytes 393232 | tf_op jit(solution)/shard_map/reduce_scatter | solution.py:822
  769.8 34.5 %reduce-scatter.16.cloned.1.call-done = bf16[512,384]{1,0:T(8,128)(2,1)} async-done(((bf16[2048,384]{1,0:T(8,128)(2,1)}), bf16[512,384]{1,0:T(8,128)(2,1)}) %reduce-scatter.16.cloned.1.call-update) | async-done | bytes 393232 | tf_op jit(solution)/shard_map/reduce_scatter | solution.py:822
  808.5 32.2 %reduce-scatter.18.cloned.1.call-done = bf16[512,384]{1,0:T(8,128)(2,1)} async-done(((bf16[2048,384]{1,0:T(8,128)(2,1)}), bf16[512,384]{1,0:T(8,128)(2,1)}) %reduce-scatter.18.cloned.1.call-update) | async-done | bytes 393232 | tf_op jit(solution)/shard_map/reduce_scatter | solution.py:822
  844.9 69.6 %reduce-scatter.14.cloned.1.call-done = bf16[256,2048]{1,0:T(8,128)(2,1)} async-done(((bf16[2048,2048]{1,0:T(8,128)(2,1)}), bf16[256,2048]{1,0:T(8,128)(2,1)}) %reduce-scatter.14.cloned.1.call-update) | async-done | bytes 1048592 | tf_op jit(solution)/shard_map/reduce_scatter | solution.py:822
  916.8 39.8 %all-reduce.21 = (f32[2048]{0:T(1024)S(1)}, f32[2048]{0:T(1024)S(1)}) all-reduce(f32[2048]{0:T(1024)S(1)} %get-tuple-element.124, f32[2048]{0:T(1024)S(1)} %get-tuple-element.122), channel_id=5, replica_groups=mesh['row'=4,'head'=8] {'row','head'}, use_global_device_ids=true, to_apply=%region_8.9.clone | all-reduce | flops 4096 | bytes 32768
  957.7 31.9 %reduce-scatter.10.cloned.1.call-done = bf16[256,2048]{1,0:T(8,128)(2,1)} async-done(((bf16[2048,2048]{1,0:T(8,128)(2,1)}), bf16[256,2048]{1,0:T(8,128)(2,1)}) %reduce-scatter.10.cloned.1.call-update) | async-done | bytes 1048592 | tf_op jit(solution)/shard_map/reduce_scatter | solution.py:822
  (172 shorter events, 87.8 us)
Async XLA Ops:
  8.0 482.0 %reduce-scatter.12.cloned.1.call-start = ((), (), s32[]{:S(2)}) async-start(), calls=%async_computation.10 | async-start | bytes 9437184 | tf_op jit(solution)/shard_map/reduce_scatter | solution.py:822
  115.2 172.1 %copy-start.2 = (bf16[256,2048]{1,0:T(8,128)(2,1)S(1)}, bf16[256,2048]{1,0:T(8,128)(2,1)}, u32[]{:S(2)}) copy-start(bf16[256,2048]{1,0:T(8,128)(2,1)} %cot.1) | copy-start | bytes 3145732
  115.3 172.1 %copy-start.14 = (bf16[512,768]{1,0:T(8,128)(2,1)S(1)}, bf16[512,768]{1,0:T(8,128)(2,1)}, u32[]{:S(2)}) copy-start(bf16[512,768]{1,0:T(8,128)(2,1)} %shard.5) | copy-start | bytes 2359300
  361.5 17.9 %copy-start.17 = (bf16[2048,768]{1,0:T(8,128)(2,1)}, bf16[2048,768]{1,0:T(8,128)(2,1)S(1)}, u32[]{:S(2)}) copy-start(bf16[2048,768]{1,0:T(8,128)(2,1)S(1)} %get-tuple-element.54) | copy-start | bytes 9437188
  361.5 17.9 %copy-start.6 = (bf16[4,512,768]{2,1,0:T(8,128)(2,1)S(1)}, bf16[4,512,768]{2,1,0:T(8,128)(2,1)}, u32[]{:S(2)}) copy-start(bf16[4,512,768]{2,1,0:T(8,128)(2,1)} %get-tuple-element.52) | copy-start | bytes 9437188
  402.0 88.1 %copy-start.28 = (f32[1,2048]{1,0:T(1,128)S(1)}, f32[1,2048]{1,0:T(1,128)}, u32[]{:S(2)}) copy-start(f32[1,2048]{1,0:T(1,128)} %get-tuple-element.155.gain_ref) | copy-start | bytes 24580
  402.0 146.4 %all-gather.2.cloned.1.call-start = ((), (), s32[]{:S(2)}) async-start(), calls=%async_computation.11 | async-start | bytes 9437184 | tf_op jit(solution)/shard_map/all_gather | solution.py:818
  493.8 167.2 %reduce-scatter.26.cloned.1.call-start = ((), (), s32[]{:S(2)}) async-start(), calls=%async_computation.18 | async-start | bytes 3932160 | tf_op jit(solution)/shard_map/reduce_scatter | solution.py:822
  505.3 158.2 %reduce-scatter.24.cloned.1.call-start = ((), (), s32[]{:S(2)}) async-start(), calls=%async_computation.17 | async-start | bytes 3932160 | tf_op jit(solution)/shard_map/reduce_scatter | solution.py:822
  516.7 173.7 %reduce-scatter.22.cloned.1.call-start = ((), (), s32[]{:S(2)}) async-start(), calls=%async_computation.16 | async-start | bytes 3932160 | tf_op jit(solution)/shard_map/reduce_scatter | solution.py:822
  528.5 19.9 %copy-start.4 = (f32[2048,8]{1,0:T(8,128)S(1)}, f32[2048,8]{1,0:T(8,128)}, u32[]{:S(2)}) copy-start(f32[2048,8]{1,0:T(8,128)} %copy.75.keep_ref) | copy-start | bytes 196612
  528.5 19.9 %copy-start.12 = (bf16[384,384]{1,0:T(8,128)(2,1)S(1)}, bf16[384,384]{1,0:T(8,128)(2,1)}, u32[]{:S(2)}) copy-start(bf16[384,384]{1,0:T(8,128)(2,1)} %pad.79.wr_ref) | copy-start | bytes 884740
  528.5 19.9 %copy-start.13 = (bf16[384,384]{1,0:T(8,128)(2,1)S(1)}, bf16[384,384]{1,0:T(8,128)(2,1)}, u32[]{:S(2)}) copy-start(bf16[384,384]{1,0:T(8,128)(2,1)} %pad.82.we_ref) | copy-start | bytes 884740
  528.5 19.9 %copy-start.15 = (f32[8,384]{1,0:T(8,128)S(1)}, f32[8,384]{1,0:T(8,128)}, u32[]{:S(2)}) copy-start(f32[8,384]{1,0:T(8,128)} %stack.52.vec_ref) | copy-start | bytes 36868
  528.5 19.9 %copy-start.16 = (f32[4,384]{1,0:T(4,128)S(1)}, f32[4,384]{1,0:T(4,128)}, u32[]{:S(2)}) copy-start(f32[4,384]{1,0:T(4,128)} %pad.72.taps_ref) | copy-start | bytes 18436
  528.5 201.7 %all-reduce.26.cloned.1.call-start = ((), (), s32[]{:S(2)}) async-start(), calls=%async_computation.19 | async-start | bytes 720896 | tf_op jit(solution)/shard_map/psum | solution.py:1328
  618.7 148.9 %reduce-scatter.20.cloned.1.call-start = ((), (), s32[]{:S(2)}) async-start(), calls=%async_computation.15 | async-start | bytes 1966080 | tf_op jit(solution)/shard_map/reduce_scatter | solution.py:822
  628.0 176.2 %reduce-scatter.16.cloned.1.call-start = ((), (), s32[]{:S(2)}) async-start(), calls=%async_computation.13 | async-start | bytes 1966080 | tf_op jit(solution)/shard_map/reduce_scatter | solution.py:822
  638.2 202.6 %reduce-scatter.18.cloned.1.call-start = ((), (), s32[]{:S(2)}) async-start(), calls=%async_computation.14 | async-start | bytes 1966080 | tf_op jit(solution)/shard_map/reduce_scatter | solution.py:822
  647.4 267.1 %reduce-scatter.14.cloned.1.call-start = ((), (), s32[]{:S(2)}) async-start(), calls=%async_computation.12 | async-start | bytes 9437184 | tf_op jit(solution)/shard_map/reduce_scatter | solution.py:822
  647.9 341.7 %reduce-scatter.10.cloned.1.call-start = ((), (), s32[]{:S(2)}) async-start(), calls=%async_computation.9 | async-start | bytes 9437184 | tf_op jit(solution)/shard_map/reduce_scatter | solution.py:822
  661.0 31.9 %copy-start.30 = (f32[342]{0:T(512)S(1)}, f32[342]{0:T(512)}, u32[]{:S(2)}) copy-start(f32[342]{0:T(512)} %param.31) | copy-start | bytes 4108
  768.7 145.8 %copy-start.29 = (f32[1,2048]{1,0:T(1,128)S(1)}, f32[1,2048]{1,0:T(1,128)}, u32[]{:S(2)}) copy-start(f32[1,2048]{1,0:T(1,128)} %get-tuple-element.154) | copy-start | bytes 24580
  806.2 183.4 %copy-start.24 = (bf16[256,2048]{1,0:T(8,128)(2,1)S(1)}, bf16[256,2048]{1,0:T(8,128)(2,1)}, u32[]{:S(2)}) copy-start(bf16[256,2048]{1,0:T(8,128)(2,1)} %reduce-scatter.12.cloned.1.call-done) | copy-start | bytes 3145732
  (23 other events, 109.7 us)
Sparse Core Ops, SparseCore 0:
  402.1 87.9 reduce-scatter.11
  494.0 54.3 all-gather.1
Sparse Core Ops, SparseCore 1:
  505.4 60.2 reduce-scatter.25
  567.8 60.2 reduce-scatter.23
  630.3 60.1 reduce-scatter.21
  693.6 36.5 all-reduce.25
  732.6 35.0 reduce-scatter.19
  770.1 34.1 reduce-scatter.15
  806.5 34.1 reduce-scatter.17
  844.5 70.0 reduce-scatter.13
  917.8 71.7 reduce-scatter.9

commit v3 on v2

--- a/solution.py
+++ b/solution.py
@@ -146,10 +146,10 @@
     )
 
 
-def backward_body(
+def backward_step(
     d_res_ref, xw_ref, yw_ref, ow_ref, taps_ref, vec_ref, wr_ref, we_ref, keep_ref,
     u_ref, u_prev_ref, by_ref, before_ref, states_ref,
-    d_bx_ref, d_by_ref, part_ref, taps_out, vec_out, wr_out, we_out,
+    d_bx_ref, d_by_ref, taps_out, vec_out, wr_out, we_out,
     window, conv, conv_low, rate, entry, d_mixed, d_conv, g_rate, g_entry, carry, sums,
 ):
     rows = d_res_ref.shape[0]
@@ -254,9 +254,6 @@
         return unused
 
     lax.fori_loop(0, rows // CHUNK, back_step, 0)
-    part_ref[...] = (
-        contract_last(d_bx_ref[...], xw_ref[...]) + contract_last(d_by_ref[...], yw_ref[...])
-    ).astype(jnp.bfloat16)
 
     @pl.when(step_id == pl.num_programs(0) - 1)
     def _():
@@ -268,6 +265,21 @@
             taps_out[place : place + 1, :] = jnp.sum(
                 sums[32 + 8 * place : 40 + 8 * place, :], axis=0, keepdims=True
             )
+
+    return (
+        contract_last(d_bx_ref[...], xw_ref[...]) + contract_last(d_by_ref[...], yw_ref[...])
+    ).astype(jnp.bfloat16)
+
+
+def backward_body(
+    d_res_ref, xw_ref, yw_ref, ow_ref, taps_ref, vec_ref, wr_ref, we_ref, keep_ref,
+    u_ref, u_prev_ref, by_ref, before_ref, states_ref,
+    d_bx_ref, d_by_ref, part_ref, *rest,
+):
+    part_ref[...] = backward_step(
+        d_res_ref, xw_ref, yw_ref, ow_ref, taps_ref, vec_ref, wr_ref, we_ref, keep_ref,
+        u_ref, u_prev_ref, by_ref, before_ref, states_ref, d_bx_ref, d_by_ref, *rest,
+    )
 
 
 def whole(shape):
@@ -534,6 +546,13 @@
         pltpu.SemaphoreType.DMA((2,)),
     )
 
+    @staticmethod
+    def buffers(rows, width):
+        return [
+            pltpu.VMEM((LINE, rows, width), jnp.bfloat16),
+            pltpu.VMEM((rows, width), jnp.bfloat16),
+        ]
+
     def __init__(self, parts, landed, passed, sent, arrived, other):
         self.r = lax.axis_index("row")
         self.parts, self.landed, self.passed = parts, landed, passed
@@ -548,6 +567,11 @@
         return send_to(
             self.parts.at[t], self.landed.at[self.r], self.sent.at[t], self.arrived.at[self.r],
             "row", t,
+        )
+
+    def added(self, t):
+        return send_to(
+            self.passed, self.landed.at[self.r], self.sent.at[t], self.arrived.at[self.r], "row", t
         )
 
     def plain(self, t):
@@ -580,14 +604,14 @@
 
                 def add(i, unused):
                     at = pl.ds(pl.multiple_of(i * step, step), step)
-                    self.parts[end, at, :] = (
+                    self.passed[at, :] = (
                         self.parts[end, at, :].astype(jnp.float32)
                         + self.passed[at, :].astype(jnp.float32)
                     ).astype(jnp.bfloat16)
                     return unused
 
                 lax.fori_loop(0, rows // step, add, 0)
-                self.direct(end).start()
+                self.added(end).start()
 
     def finish(self, write):
         r = self.r
@@ -600,20 +624,29 @@
                     "row", t,
                 ).wait_recv()
 
-        rows = self.passed.shape[0]
-        step = 64
-
-        def add(i, unused):
-            at = pl.ds(pl.multiple_of(i * step, step), step)
-            total = self.parts[r, at, :].astype(jnp.float32)
-            for t in range(LINE):
-                total = total + jnp.where(
-                    unsent_to(r, t), 0.0, self.landed[t, at, :].astype(jnp.float32)
-                )
-            write(at, total)
-            return unused
-
-        lax.fori_loop(0, rows // step, add, 0)
+        def total_of(sources):
+            step = 32
+
+            def add(i, unused):
+                at = pl.ds(pl.multiple_of(i * step, step), step)
+                total = self.parts[r, at, :].astype(jnp.float32)
+                for t in sources:
+                    total = total + self.landed[t, at, :].astype(jnp.float32)
+                write(at, total)
+                return unused
+
+            lax.fori_loop(0, self.passed.shape[0] // step, add, 0)
+
+        at_end = (r == 0) | (r == 3)
+
+        @pl.when(at_end)
+        def _():
+            total_of((1, 2))
+
+        @pl.when(jnp.logical_not(at_end))
+        def _():
+            total_of((0, 3, 3 - r))
+
         for me, end, via in ((0, 3, 1), (3, 0, 2)):
 
             @pl.when(r == me)
@@ -1111,6 +1144,497 @@
         ),
         name="ffn_up",
     )(two, gate, up, cot, shard)
+def once(shape):
+    return pl.BlockSpec(
+        shape, lambda i: (0,) * len(shape), pipeline_mode=pl.Buffered(buffer_count=1)
+    )
+
+
+def norm_back(rows, gain, incoming):
+    scale = lax.rsqrt(jnp.mean(rows * rows, axis=-1, keepdims=True) + EPSILON)
+    scaled = incoming * gain
+    inner = jnp.mean(scaled * rows, axis=-1, keepdims=True)
+    return scale * scaled - rows * (scale * scale * scale * inner), incoming * rows * scale
+
+
+def to_parts(total, parts):
+    rows = parts.shape[1]
+    step = 64
+
+    def move(i, unused):
+        at = pl.ds(pl.multiple_of(i * step, step), step)
+        for t in range(LINE):
+            here = pl.ds(pl.multiple_of(t * rows + i * step, step), step)
+            parts[t, at, :] = total[here, :].astype(jnp.bfloat16)
+        return unused
+
+    lax.fori_loop(0, rows // step, move, 0)
+
+
+def sum_eight(value):
+    total = value[0:8, :]
+    for k in range(1, value.shape[0] // 8):
+        total = total + value[8 * k : 8 * k + 8, :]
+    return total
+
+
+def ffn_back_body(
+    cot_ref, hidden_ref, two_ref, gates_ref, ups_ref, gate_ref, up_ref, down_ref,
+    residual_ref, own_cot_ref, gain_ref,
+    d_gates_ref, d_ups_ref, gate_parts, down_out, d_res_ref, d_low_ref, gain_out,
+    total, parts, eight, *links,
+):
+    step = pl.program_id(0)
+    line = LineReduce(parts, *links[:5])
+    plane = PlaneReduce(*links[5:])
+
+    @pl.when(step == 0)
+    def _():
+        total[...] = jnp.zeros_like(total)
+        meet(True, "near")
+
+    @pl.when(step < PLANE)
+    def _():
+        total[...] += contract_first(cot_ref[...], hidden_ref[...])
+
+    @pl.when(step == PLANE - 1)
+    def _():
+        to_parts(total, parts)
+        line.start()
+        total[...] = jnp.zeros_like(total)
+
+    @pl.when(step > PLANE)
+    def _():
+        plane.pass_on(step - PLANE - 1)
+
+    @pl.when(step >= PLANE)
+    def _():
+        d_hidden = dot_plain(cot_ref[...], down_ref[...])
+        gelu_gate, slope = gelu_both(gates_ref[...])
+        d_gates_ref[...] = (d_hidden * ups_ref[...] * slope).astype(jnp.bfloat16)
+        d_ups_ref[...] = (d_hidden * gelu_gate).astype(jnp.bfloat16)
+        value = contract_last(d_gates_ref[...], gate_ref[...]) + contract_last(
+            d_ups_ref[...], up_ref[...]
+        )
+        plane.put(step - PLANE, value.astype(jnp.bfloat16))
+        total[...] += contract_first(two_ref[...], d_gates_ref[...])
+
+    @pl.when(step == PLANE + 4)
+    def _():
+        line.forward()
+
+    @pl.when(step == 2 * PLANE - 1)
+    def _():
+        plane.pass_on(step - PLANE)
+        to_parts(total, gate_parts)
+        plane.arrive()
+        eight[...] = jnp.zeros_like(eight)
+
+        def back(i, unused):
+            at = pl.ds(pl.multiple_of(i * CHUNK, CHUNK), CHUNK)
+            d_rows, d_gain = norm_back(residual_ref[at, :], gain_ref[...], plane.total(at))
+            d_residual = own_cot_ref[at, :].astype(jnp.float32) + d_rows
+            d_res_ref[at, :] = d_residual
+            d_low_ref[at, :] = d_residual.astype(jnp.bfloat16)
+            eight[...] += sum_eight(d_gain)
+            return unused
+
+        lax.fori_loop(0, residual_ref.shape[0] // CHUNK, back, 0)
+        gain_out[...] = jnp.sum(eight[...], axis=0, keepdims=True)
+
+        def write(at, value):
+            down_out[at, :] = value
+
+        line.finish(write)
+        plane.finish()
+
+
+def ffn_back(
+    cot_group, hidden, two_group, gates, ups, gate, up, down, residual, own_cot, gain
+):
+    length, width = cot_group.shape
+    units = gate.shape[1]
+    rows, share = length // PLANE, width // LINE
+    early = lambda columns: pl.BlockSpec((rows, columns), lambda i: (jnp.minimum(i, PLANE - 1), 0))
+    late = lambda columns: pl.BlockSpec(
+        (rows, columns), lambda i: (jnp.maximum(i - PLANE, 0), 0)
+    )
+    both = pl.BlockSpec((rows, width), lambda i: (lax.rem(i, PLANE), 0))
+    return pl.pallas_call(
+        ffn_back_body,
+        grid=(2 * PLANE,),
+        in_specs=[
+            both, early(units), late(width), late(units), late(units), once(gate.shape),
+            once(up.shape), once(down.shape), once(residual.shape), once(own_cot.shape),
+            once(gain.shape),
+        ],
+        out_specs=[
+            late(units), late(units), once((LINE, share, units)), once((share, units)),
+            once((rows, width)), once((rows, width)), once((1, width)),
+        ],
+        out_shape=[
+            jax.ShapeDtypeStruct((length, units), jnp.bfloat16),
+            jax.ShapeDtypeStruct((length, units), jnp.bfloat16),
+            jax.ShapeDtypeStruct((LINE, share, units), jnp.bfloat16),
+            jax.ShapeDtypeStruct((share, units), jnp.float32),
+            jax.ShapeDtypeStruct((rows, width), jnp.float32),
+            jax.ShapeDtypeStruct((rows, width), jnp.bfloat16),
+            jax.ShapeDtypeStruct((1, width), jnp.float32),
+        ],
+        scratch_shapes=[
+            pltpu.VMEM((width, units), jnp.float32),
+            pltpu.VMEM((LINE, share, units), jnp.bfloat16),
+            pltpu.VMEM((8, width), jnp.float32),
+            *LineReduce.buffers(share, units),
+            *LineReduce.semaphores,
+            *PlaneReduce.buffers(rows, width),
+            *PlaneReduce.semaphores,
+        ],
+        compiler_params=pltpu.CompilerParams(
+            collective_id=4, has_side_effects=True, vmem_limit_bytes=62 * 2**20
+        ),
+        name="ffn_back",
+    )(cot_group, hidden, two_group, gates, ups, gate, up, down, residual, own_cot, gain)
+
+
+def turn_body(
+    two_ref, d_ups_ref, gate_parts, block, up_parts, gate_out, full, total, *links
+):
+    step = pl.program_id(0)
+    line = LineReduce(gate_parts, *links[:5])
+    plane = PlaneGather(block, full, *links[5:])
+
+    @pl.when(step == 0)
+    def _():
+        meet(True, "near")
+        line.start()
+        plane.start()
+        total[...] = jnp.zeros_like(total)
+
+    total[...] += contract_first(two_ref[...], d_ups_ref[...])
+
+    @pl.when(step == PLANE - 2)
+    def _():
+        plane.relay(0)
+
+    @pl.when(step == PLANE - 1)
+    def _():
+        plane.relay(1)
+        to_parts(total, up_parts)
+        line.forward()
+        plane.rest()
+        plane.end()
+
+        def write(at, value):
+            gate_out[at, :] = value
+
+        line.finish(write)
+
+
+def turn(two_group, d_ups, gate_parts, block):
+    length, width = two_group.shape
+    units = d_ups.shape[1]
+    rows, share = length // PLANE, width // LINE
+    tile = lambda columns: pl.BlockSpec((rows, columns), lambda i: (i, 0))
+    return pl.pallas_call(
+        turn_body,
+        grid=(PLANE,),
+        in_specs=[tile(width), tile(units), once(gate_parts.shape), ANYWHERE],
+        out_specs=[once(gate_parts.shape), once((share, units)), ANYWHERE],
+        out_shape=[
+            jax.ShapeDtypeStruct(gate_parts.shape, jnp.bfloat16),
+            jax.ShapeDtypeStruct((share, units), jnp.float32),
+            jax.ShapeDtypeStruct((PLANE, rows, width), jnp.bfloat16),
+        ],
+        scratch_shapes=[
+            pltpu.VMEM((width, units), jnp.float32),
+            *LineReduce.buffers(share, units),
+            *LineReduce.semaphores,
+            *PlaneGather.semaphores,
+        ],
+        compiler_params=pltpu.CompilerParams(
+            collective_id=5, has_side_effects=True, vmem_limit_bytes=48 * 2**20
+        ),
+        name="turn",
+    )(two_group, d_ups, gate_parts, block)
+
+
+def backward_linked_body(
+    d_res_ref, xw_ref, yw_ref, ow_ref, taps_ref, vec_ref, wr_ref, we_ref, keep_ref,
+    u_ref, u_prev_ref, by_ref, before_ref, states_ref, normed_ref, mixed_ref, up_parts,
+    x_ref, gain_ref, d_residual_ref,
+    x_parts, y_parts, out_parts, up_out, in_grad, gain_out, taps_out, vec_out, wr_out, we_out,
+    d_bx, d_by, x_total, y_total, out_total, eight, *rest,
+):
+    scratch, links = rest[:11], rest[11:]
+    step = pl.program_id(0)
+    block = PLANE - 1 - step
+    line = LineReduce(up_parts, *links[:5])
+    plane = PlaneReduce(*links[5:])
+
+    @pl.when(step == 0)
+    def _():
+        meet(True, "near")
+        line.start()
+        x_total[...] = jnp.zeros_like(x_total)
+        y_total[...] = jnp.zeros_like(y_total)
+        out_total[...] = jnp.zeros_like(out_total)
+
+    @pl.when(step > 0)
+    def _():
+        plane.pass_on(block + 1)
+
+    value = backward_step(
+        d_res_ref, xw_ref, yw_ref, ow_ref, taps_ref, vec_ref, wr_ref, we_ref, keep_ref,
+        u_ref, u_prev_ref, by_ref, before_ref, states_ref, d_bx, d_by,
+        taps_out, vec_out, wr_out, we_out, *scratch,
+    )
+    plane.put(block, value)
+    x_total[...] += contract_first(normed_ref[...], d_bx[...])
+    y_total[...] += contract_first(normed_ref[...], d_by[...])
+    out_total[...] += contract_first(d_res_ref[...], mixed_ref[...])
+
+    @pl.when(step == 4)
+    def _():
+        line.forward()
+
+    @pl.when(step == PLANE - 1)
+    def _():
+        plane.pass_on(block)
+        to_parts(x_total, x_parts)
+        to_parts(y_total, y_parts)
+        to_parts(out_total, out_parts)
+        plane.arrive()
+        eight[...] = jnp.zeros_like(eight)
+
+        def back(i, unused):
+            at = pl.ds(pl.multiple_of(i * CHUNK, CHUNK), CHUNK)
+            d_rows, d_gain = norm_back(
+                x_ref[at, :].astype(jnp.float32), gain_ref[...], plane.total(at)
+            )
+            in_grad[at, :] = (d_residual_ref[at, :] + d_rows).astype(jnp.bfloat16)
+            eight[...] += sum_eight(d_gain)
+            return unused
+
+        lax.fori_loop(0, x_ref.shape[0] // CHUNK, back, 0)
+        gain_out[...] = jnp.sum(eight[...], axis=0, keepdims=True)
+
+        def write(at, value):
+            up_out[at, :] = value
+
+        line.finish(write)
+        plane.finish()
+
+
+def backward_linked(
+    d_res, xw, yw, ow, taps, vec, wr, we, keep, u, by, before, states, normed, mixed, up_parts,
+    layer_in, gain, d_residual,
+):
+    length, width = d_res.shape
+    chans, units = xw.shape[1], up_parts.shape[2]
+    rows, share = length // PLANE, width // LINE
+    tile = lambda columns: pl.BlockSpec((rows, columns), lambda i: (PLANE - 1 - i, 0))
+    ahead = pl.BlockSpec(
+        (16, chans), lambda i: (jnp.maximum((PLANE - 1 - i) * (rows // 16) - 1, 0), 0)
+    )
+    weights = (LINE, share, chans)
+    return pl.pallas_call(
+        backward_linked_body,
+        grid=(PLANE,),
+        in_specs=[
+            tile(width), once(xw.shape), once(yw.shape), once(ow.shape), once(taps.shape),
+            once(vec.shape), once(wr.shape), once(we.shape), tile(keep.shape[1]),
+            tile(chans), ahead, tile(chans), tile(chans), tile(chans), tile(width), tile(chans),
+            once(up_parts.shape), once(layer_in.shape), once(gain.shape), once(d_residual.shape),
+        ],
+        out_specs=[
+            once(weights), once(weights), once(weights), once((share, units)),
+            once((rows, width)), once((1, width)), once(taps.shape), once(vec.shape),
+            once(wr.shape), once(we.shape),
+        ],
+        out_shape=[
+            jax.ShapeDtypeStruct(weights, jnp.bfloat16),
+            jax.ShapeDtypeStruct(weights, jnp.bfloat16),
+            jax.ShapeDtypeStruct(weights, jnp.bfloat16),
+            jax.ShapeDtypeStruct((share, units), jnp.float32),
+            jax.ShapeDtypeStruct((rows, width), jnp.bfloat16),
+            jax.ShapeDtypeStruct((1, width), jnp.float32),
+            jax.ShapeDtypeStruct(taps.shape, jnp.float32),
+            jax.ShapeDtypeStruct(vec.shape, jnp.float32),
+            jax.ShapeDtypeStruct(wr.shape, jnp.float32),
+            jax.ShapeDtypeStruct(we.shape, jnp.float32),
+        ],
+        scratch_shapes=[
+            pltpu.VMEM((rows, chans), jnp.bfloat16),
+            pltpu.VMEM((rows, chans), jnp.bfloat16),
+            pltpu.VMEM((width, chans), jnp.float32),
+            pltpu.VMEM((width, chans), jnp.float32),
+            pltpu.VMEM((width, chans), jnp.float32),
+            pltpu.VMEM((8, width), jnp.float32),
+            pltpu.VMEM((rows + 8, chans), jnp.float32),
+            pltpu.VMEM((rows, chans), jnp.float32),
+            pltpu.VMEM((rows, chans), jnp.bfloat16),
+            pltpu.VMEM((rows, chans), jnp.float32),
+            pltpu.VMEM((rows, chans), jnp.float32),
+            pltpu.VMEM((rows, chans), jnp.float32),
+            pltpu.VMEM((rows + 8, chans), jnp.float32),
+            pltpu.VMEM((rows, chans), jnp.bfloat16),
+            pltpu.VMEM((rows, chans), jnp.bfloat16),
+            pltpu.VMEM((8, chans), jnp.float32),
+            pltpu.VMEM((64, chans), jnp.float32),
+            *LineReduce.buffers(share, units),
+            *LineReduce.semaphores,
+            *PlaneReduce.buffers(rows, width),
+            *PlaneReduce.semaphores,
+        ],
+        compiler_params=pltpu.CompilerParams(
+            collective_id=6, has_side_effects=True, vmem_limit_bytes=62 * 2**20
+        ),
+        name="mixer_backward_linked",
+    )(
+        d_res, xw, yw, ow, taps, vec, wr, we, keep, u, u, by, before, states, normed, mixed,
+        up_parts, layer_in, gain, d_residual,
+    )
+
+
+def close_body(
+    hidden_ref, down_ref, x_parts, y_parts, out_parts, residual_ref, gains_ref, small,
+    layer_out, x_out, y_out, out_out, gains_out, small_out,
+    gathered, line_gains, both_gains, plane_gains,
+    gain_sent, gain_arrived, wide_sent, wide_arrived, *links,
+):
+    r, h = lax.axis_index("row"), lax.axis_index("head")
+    step = pl.program_id(0)
+    reduces = [
+        LineReduce(parts, *links[5 * k : 5 * k + 5])
+        for k, parts in enumerate((out_parts, x_parts, y_parts))
+    ]
+    outs = (out_out, x_out, y_out)
+    line = LineGather(small, gathered, *links[15:18])
+    plane = PlaneReduce(*links[18:26])
+
+    def to_row(t, owner):
+        return send_to(
+            gains_ref.at[t], line_gains.at[owner], gain_sent.at[t], gain_arrived.at[owner],
+            "row", t,
+        )
+
+    def over_plane(place, owner):
+        return send_to(
+            both_gains, plane_gains.at[owner], wide_sent.at[place], wide_arrived.at[owner],
+            "head", lax.rem(h + place, PLANE),
+        )
+
+    @pl.when(step == 0)
+    def _():
+        meet(True, "all")
+        for place in range(1, LINE):
+            to_row(lax.rem(r + place, LINE), r).start()
+        line.start()
+        for item in reduces:
+            item.start()
+
+    @pl.when(step > 0)
+    def _():
+        plane.pass_on(step - 1)
+
+    plane.put(step, contract_last(hidden_ref[...], down_ref[...]).astype(jnp.bfloat16))
+
+    @pl.when(step == 2)
+    def _():
+        total = gains_ref[r]
+        for place in range(1, LINE):
+            t = lax.rem(r + place, LINE)
+            to_row(t, t).wait_recv()
+            total = total + line_gains[t]
+        both_gains[...] = total
+        for place in range(1, PLANE):
+            over_plane(place, h).start()
+
+    @pl.when(step == PLANE - 1)
+    def _():
+        plane.pass_on(step)
+        reduces[0].forward()
+        line.forward()
+        total = both_gains[...]
+        for place in range(1, PLANE):
+            owner = lax.rem(h + place, PLANE)
+            over_plane(place, owner).wait_recv()
+            total = total + plane_gains[owner]
+        mine = lax.broadcasted_iota(jnp.int32, total.shape, 0) == h
+        gains_out[...] = jnp.sum(jnp.where(mine, total, 0.0), axis=0, keepdims=True)
+        reduces[1].forward()
+        plane.arrive()
+
+        def make(i, unused):
+            at = pl.ds(pl.multiple_of(i * CHUNK, CHUNK), CHUNK)
+            layer_out[at, :] = (residual_ref[at, :] + plane.total(at)).astype(jnp.bfloat16)
+            return unused
+
+        lax.fori_loop(0, residual_ref.shape[0] // CHUNK, make, 0)
+        reduces[2].forward()
+        line.finish()
+        total = gathered[0].astype(jnp.float32)
+        for t in range(1, LINE):
+            total = total + gathered[t].astype(jnp.float32)
+        small_out[...] = total
+        for item, out in zip(reduces, outs):
+
+            def write(at, value, out=out):
+                out[at, :] = value
+
+            item.finish(write)
+        plane.finish()
+        for place in range(1, LINE):
+            to_row(lax.rem(r + place, LINE), r).wait_send()
+        for place in range(1, PLANE):
+            over_plane(place, h).wait_send()
+
+
+def close_block(hidden, down, x_parts, y_parts, out_parts, residual, gains, small):
+    length, units = hidden.shape
+    rows, width = residual.shape
+    share, chans = x_parts.shape[1:]
+    return pl.pallas_call(
+        close_body,
+        grid=(PLANE,),
+        in_specs=[
+            pl.BlockSpec((rows, units), lambda i: (i, 0)), once(down.shape),
+            once(x_parts.shape), once(y_parts.shape), once(out_parts.shape),
+            once(residual.shape), once(gains.shape), once(small.shape),
+        ],
+        out_specs=[
+            once((rows, width)), once((share, chans)), once((share, chans)),
+            once((share, chans)), once((1, gains.shape[2])), once(small.shape),
+        ],
+        out_shape=[
+            jax.ShapeDtypeStruct((rows, width), jnp.bfloat16),
+            jax.ShapeDtypeStruct((share, chans), jnp.float32),
+            jax.ShapeDtypeStruct((share, chans), jnp.float32),
+            jax.ShapeDtypeStruct((share, chans), jnp.float32),
+            jax.ShapeDtypeStruct((1, gains.shape[2]), jnp.float32),
+            jax.ShapeDtypeStruct(small.shape, jnp.float32),
+        ],
+        scratch_shapes=[
+            pltpu.VMEM((LINE,) + small.shape, jnp.bfloat16),
+            pltpu.VMEM(gains.shape, jnp.float32),
+            pltpu.VMEM(gains.shape[1:], jnp.float32),
+            pltpu.VMEM((PLANE,) + gains.shape[1:], jnp.float32),
+            pltpu.SemaphoreType.DMA((LINE,)),
+            pltpu.SemaphoreType.DMA((LINE,)),
+            pltpu.SemaphoreType.DMA((PLANE,)),
+            pltpu.SemaphoreType.DMA((PLANE,)),
+            *LineReduce.buffers(share, chans), *LineReduce.semaphores,
+            *LineReduce.buffers(share, chans), *LineReduce.semaphores,
+            *LineReduce.buffers(share, chans), *LineReduce.semaphores,
+            *LineGather.semaphores,
+            *PlaneReduce.buffers(rows, width), *PlaneReduce.semaphores,
+        ],
+        compiler_params=pltpu.CompilerParams(
+            collective_id=7, has_side_effects=True, vmem_limit_bytes=56 * 2**20
+        ),
+        name="close_block",
+    )(hidden, down, x_parts, y_parts, out_parts, residual, gains, small)
 
 
 def mixer_params(
@@ -1287,60 +1811,55 @@
     )
     cot_group, down_rows = map(flat, (cot_group, down_rows))
 
-    inputs = layer_in.astype(jnp.float32)
-    normed_f, norm_back_one = jax.vjp(norm_apply, inputs, gains[0])
-    normed_two_f, norm_back_two = jax.vjp(norm_apply, residual, gains[1])
-    activated, slope = gelu_both(gates)
-    ffn_part = contract_last(hidden, down_rows).astype(jnp.bfloat16)
-    d_hidden = dot_plain(cot_group, down_rows)
-    d_gates = (d_hidden * ups * slope).astype(jnp.bfloat16)
-    d_ups = (d_hidden * activated).astype(jnp.bfloat16)
-    d_two_part = (contract_last(d_gates, gate_rows) + contract_last(d_ups, up_rows)).astype(
-        jnp.bfloat16
-    )
-    gate_grad = scatter(contract_first(two_group, d_gates).astype(jnp.bfloat16), "row", 0)
-    up_grad = scatter(contract_first(two_group, d_ups).astype(jnp.bfloat16), "row", 0)
-    down_grad = scatter(contract_first(cot_group, hidden).astype(jnp.bfloat16), "row", 0)
-    layer_out = (residual + scatter(ffn_part, "head", 0).astype(jnp.float32)).astype(jnp.bfloat16)
-    d_two = scatter(d_two_part, "head", 0).astype(jnp.float32)
-    d_resid_norm, d_ffn_gain = norm_back_two(d_two)
-    d_residual = cotangent.astype(jnp.float32) + d_resid_norm
-    d_res_group = gather(d_residual.astype(jnp.bfloat16), "head", 0)
-    d_bx, d_by, d_part, d_taps, d_vec, d_wr, d_we = mixer_backward(
-        d_res_group, x_rows, y_rows, out_rows, taps, vec, wr, we, keep, u, by, before, states, ROWS
-    )
-    out_grad = scatter(contract_first(d_res_group, mixed).astype(jnp.bfloat16), "row", 0)
-    x_grad = scatter(contract_first(normed_group, d_bx).astype(jnp.bfloat16), "row", 0)
-    y_grad = scatter(contract_first(normed_group, d_by).astype(jnp.bfloat16), "row", 0)
-    d_normed = scatter(d_part, "head", 0).astype(jnp.float32)
-    d_inputs, d_mix_gain = norm_back_one(d_normed)
-    layer_in_grad = (d_inputs + d_residual).astype(jnp.bfloat16)
-
-    small = [
-        d_taps[:, :used],
-        d_vec[0, :used],
-        diagonal_blocks(d_wr, heads, head_width),
-        d_vec[1, :used],
-        diagonal_blocks(d_we, heads, head_width),
-        d_vec[2, :used],
-        d_vec[3, :used] * (8.0 * jax.nn.sigmoid(-decay_param)),
-    ]
-    small = [lax.psum(item.astype(jnp.bfloat16), "row").astype(jnp.float32) for item in small]
-    mix_part = scatter(d_mix_gain, ("row", "head"), 0)
-    ffn_part_grad = scatter(d_ffn_gain, ("row", "head"), 0)
-    wide = lambda values: values[:, :used].astype(jnp.float32)
+    d_gates, d_ups, gate_parts, down_grad, d_residual, d_low, d_ffn_gain = ffn_back(
+        cot_group, hidden, two_group, gates, ups, gate_rows, up_rows, down_rows, residual,
+        cotangent, gains[1:2],
+    )
+    up_parts, gate_grad, d_res_group = turn(two_group, d_ups, gate_parts, d_low)
+    (
+        x_parts, y_parts, out_parts, up_grad, layer_in_grad, d_mix_gain, d_taps, d_vec, d_wr, d_we,
+    ) = backward_linked(
+        flat(d_res_group), x_rows, y_rows, out_rows, taps, vec, wr, we, keep, u, by, before,
+        states, normed_group, mixed, up_parts, layer_in, gains[0:1], d_residual,
+    )
+
+    share = mix_gain.shape[0]
+    split = lambda values: values.reshape(LINE, PLANE, share)
+    gain_terms = jnp.concatenate([split(d_mix_gain), split(d_ffn_gain)], axis=2)
+    blocks = [slice(h * head_width, (h + 1) * head_width) for h in range(heads)]
+    packed = jnp.concatenate(
+        [jnp.concatenate([d_wr[at, at], d_we[at, at]], axis=1) for at in blocks]
+        + [
+            d_taps[:, :used],
+            d_vec[0:3, :used],
+            d_vec[3:4, :used] * (8.0 * jax.nn.sigmoid(-decay_param)),
+        ],
+        axis=0,
+    ).astype(jnp.bfloat16)
+    packed = jnp.pad(packed, ((0, -packed.shape[0] % 16), (0, chans - used)))
+    layer_out, x_grad, y_grad, out_grad, gain_grads, sums = close_block(
+        hidden, down_rows, x_parts, y_parts, out_parts, residual, gain_terms, packed
+    )
+    gates_end = heads * head_width
+    wide = lambda values: values[:, :used]
     return (
         layer_out,
         layer_in_grad,
-        mix_part,
-        ffn_part_grad,
+        gain_grads[0, :share],
+        gain_grads[0, share:],
         wide(x_grad),
         wide(y_grad),
         wide(out_grad),
-        *small,
-        gate_grad.astype(jnp.float32),
-        up_grad.astype(jnp.float32),
-        down_grad.astype(jnp.float32),
+        sums[gates_end : gates_end + 4, :used],
+        sums[gates_end + 4, :used],
+        sums[:gates_end, :head_width].reshape(heads, head_width, head_width),
+        sums[gates_end + 5, :used],
+        sums[:gates_end, head_width : 2 * head_width].reshape(heads, head_width, head_width),
+        sums[gates_end + 6, :used],
+        sums[gates_end + 7, :used],
+        gate_grad,
+        up_grad,
+        down_grad,
     )
 
 

time: 1010 us -> 820 us (0.81)
  Pallas kernels: 395 us -> 761 us
  waiting for transfers between devices: 357 us -> 0 us
  matrix products: 114 us -> 0 us
  blocking collectives: 50.3 us -> 0 us
  other arithmetic: 30.5 us -> 7.14 us
  between operations: 16.5 us -> 1.2 us
  local copies, waits for them, and re-layouts: 37.2 us -> 49.5 us
    pallas_call x1 -> x4, Pallas kernels: 66.4 us -> 432 us  [the longest x1 137 us: backward_linked(): pl.pallas_call(backward_linked_body, grid=(PLANE,), in_specs=[tile(width)...]
    reduce_scatter x9 -> x0, waiting for transfers between devices: 313 us -> none  [scatter(): lax.psum_scatter(values, axis_name, scatter_dimension=axis, tiled=True)]
    dot_general x10 -> x0, matrix products: 114 us -> none  [the longest x6 62.4 us: contract_first(): lax.dot_general(left, right, (((0,), (0,)), ((), ())), preferred_element_...]
    unnamed x1 -> x0, blocking collectives: 39.8 us -> none
    psum x1 -> x0, waiting for transfers between devices: 23.8 us -> none  [shards_linked(): lax.psum(item.astype(jnp.bfloat16), 'row').astype(jnp.float32)]
    convert_element_type x14 -> x0, other arithmetic: 21.5 us -> none  [the longest x3 4.9 us: shards_linked(): wide = lambda values: values[:, :used].astype(jnp.float32)]
    all_gather x1 -> x0, waiting for transfers between devices: 19.8 us -> none  [gather(): return lax.all_gather(values, axis_name, axis=axis, tiled=True)]
    psum x1 -> x0, blocking collectives: 10.5 us -> none  [shards_linked(): lax.psum(item.astype(jnp.bfloat16), 'row').astype(jnp.float32)]
  transfers between devices with their start and end apart: 11 -> 0, of which waited for: 9 -> 0; matrix products, arithmetic and copies ran while one was open for 10% -> 0% of each run, Pallas kernels for 7% -> 0%
where the time goes in v3:
time: 820 us; the launch traced here: 819 us
  Pallas kernels  761 us (93%)
  local copies, waits for them, and re-layouts  49.5 us (6%)
    pallas_call x1, Pallas kernels, backward_linked(): pl.pallas_call(backward_linked_body, grid=(PLANE,), in_specs=[tile(width)...  137 us
    pallas_call x1, Pallas kernels, ffn_back(): pl.pallas_call(ffn_back_body, grid=(2 * PLANE,), in_specs=[both, early(un...  117 us
    pallas_call x1, Pallas kernels, close_block(): pl.pallas_call(close_body, grid=(PLANE,), in_specs=[pl.BlockSpec((rows, u...  104 us
    pallas_call x1, Pallas kernels, forward_linked(): pl.pallas_call(forward_linked_body, grid=(PLANE,), in_specs=[tile(width),...  94.9 us
    pallas_call x1, Pallas kernels, open_block(): pl.pallas_call(open_body, in_specs=[IN_VMEM, IN_VMEM] + [ANYWHERE] * 3, o...  86.5 us
    pallas_call x1, Pallas kernels, spread(): pl.pallas_call(spread_body, in_specs=[ANYWHERE] * 2, out_specs=[ANYWHERE]...  77.1 us
    pallas_call x1, Pallas kernels, turn(): pl.pallas_call(turn_body, grid=(PLANE,), in_specs=[tile(width), tile(unit...  74.5 us
    pallas_call x1, Pallas kernels, ffn_up(): pl.pallas_call(ffn_up_body, grid=(PLANE,), in_specs=[tile(width), whole(g...  70.3 us

profile of v3, /device:TPU:0, one launch (start us, length us, event | category | flops | bytes accessed | tf_op | source)
XLA Modules:
  0.0 818.7 jit_solution(9320215891092611907)
XLA Ops:
  2.6 1.3 copy.77.keep_ref
  3.9 1.4 fusion.20
  8.8 86.5 %open_block.1 = (bf16[8,256,2048]{2,1,0:T(8,128)(2,1)S(1)}, bf16[4,512,384]{2,1,0:T(8,128)(2,1)S(1)}, bf16[4,512,384]{2,1,0:T(8,128)(2,1)S(1)}, bf16[4,512,384]{2,1,0:T(8,128)(2,1)S(1)}, f32[2,2048]{1,0:T(2,128)S(1)}) custom-call(bf16[256,2048]{1,0:T(8,128)(2,1)S(1)} %copy-done.5, f32[8,128]{1,0:T(8,128)S(1)} %broadcast_in_dim.6.tile_ref, ...), custom_call_target="tpu_custom_call" | custom-call | tf_op jit(solution)/shard_map/open_block/pallas_call | solution.py:938
  95.3 3.3 copy-done
  104.0 94.9 %mixer_forward_linked.1 = (bf16[2048,384]{1,0:T(8,128)(2,1)}, f32[2048,384]{1,0:T(8,128)}, f32[2048,384]{1,0:T(8,128)}, bf16[2048,384]{1,0:T(8,128)(2,1)}, bf16[...) custom-call(bf16[2048,2048]{1,0:T(8,128)(2,1)} %bitcast.40, ...), custom_call_target="tpu_custom_call" | custom-call | tf_op jit(solution)/shard_map/mixer_forward_linked/pallas_call | solution.py:1015
  198.9 77.1 %spread.1 = (bf16[8,256,2048]{2,1,0:T(8,128)(2,1)}, bf16[4,512,768]{2,1,0:T(8,128)(2,1)}) custom-call(bf16[256,2048]{1,0:T(8,128)(2,1)} %get-tuple-element.67.block, bf16[512,768]{1,0:T(8,128)(2,1)} %shard.4), custom_call_target="tpu_custom_call" | custom-call | tf_op jit(solution)/shard_map/spread/pallas_call | solution.py:1067
  276.1 1.9 copy-done.3
  277.9 1.9 copy-done.4
  279.8 70.3 %ffn_up.1 = (f32[2048,768]{1,0:T(8,128)}, f32[2048,768]{1,0:T(8,128)}, bf16[2048,768]{1,0:T(8,128)(2,1)S(1)}, bf16[8,256,2048]{2,1,0:T(8,128)(2,1)}, bf16[4,512,768]{2,1,0:T(8,128)(2,1)S(1)}) custom-call(bf16[2048,2048]{1,0:T(8,128)(2,1)} %bitcast.54, bf16[2048,768]{1,0:T(8,128)(2,1)S(1)} %bitcast.45, bf16[2048,768]{1,0:T(8,128)(2,1)S(1)} %bitcast.47, ...), custom_call_target="tpu_custom_call" | custom-call | tf_op jit(solution)/shard_map/ffn_up/pallas_call | solution.py:1129
  350.2 1.6 copy-done.1
  351.8 1.7 copy-done.2
  353.4 116.7 %ffn_back.1 = (bf16[2048,768]{1,0:T(8,128)(2,1)}, bf16[2048,768]{1,0:T(8,128)(2,1)}, bf16[4,512,768]{2,1,0:T(8,128)(2,1)}, f32[512,768]{1,0:T(8,128)}, f32[256,2...) custom-call(bf16[2048,2048]{1,0:T(8,128)(2,1)} %bitcast.58, bf16[2048,768]{1,0:T(8,128)(2,1)} %copy-done.1, ...), custom_call_target="tpu_custom_call" | custom-call | tf_op jit(solution)/shard_map/ffn_back/pallas_call | solution.py:1263
  470.2 1.2 copy-done.11
  471.4 74.5 %turn.1 = (bf16[4,512,768]{2,1,0:T(8,128)(2,1)S(1)}, f32[512,768]{1,0:T(8,128)S(1)}, bf16[8,256,2048]{2,1,0:T(8,128)(2,1)}) custom-call(bf16[2048,2048]{1,0:T(8,128)(2,1)} %bitcast.56, bf16[2048,768]{1,0:T(8,128)(2,1)} %get-tuple-element.77.d_ups_ref, bf16[4,512,768]{2,1,0:T(8,128)(2,1)} %get-tuple-element.78.gate_parts, bf16[256,2048]{1,0:T(8,128)(2,1)S(1)} %copy-done.11), custom_call_target="tpu_custom_call" | custom-call | tf_op jit(solution)/shard_map/turn/pallas_call | solution.py:1339
  545.9 1.6 copy-done.10
  547.5 136.9 %mixer_backward_linked.1 = (bf16[4,512,384]{2,1,0:T(8,128)(2,1)}, bf16[4,512,384]{2,1,0:T(8,128)(2,1)}, bf16[4,512,384]{2,1,0:T(8,128)(2,1)}, f32[512,768]{1,0:T...) custom-call(bf16[2048,2048]{1,0:T(8,128)(2,1)} %bitcast.57, ...), custom_call_target="tpu_custom_call" | custom-call | tf_op jit(solution)/shard_map/mixer_backward_linked/pallas_call | solution.py:1441
  692.8 104.0 %close_block.1 = (bf16[256,2048]{1,0:T(8,128)(2,1)}, f32[512,384]{1,0:T(8,128)}, f32[512,384]{1,0:T(8,128)}, f32[512,384]{1,0:T(8,128)}, f32[1,128]{1,0:T(1,128)}, /*index=5*/f32[352,384]{1,0:T(8,128)}) custom-call(bf16[2048,768]{1,0:T(8,128)(2,1)} %copy-done.1, bf16[2048,768]{1,0:T(8,128)(2,1)} %bitcast.43, bf16[4,512,384]{2,1,0:T(8,128)(2,1)} %get-tuple-element.88.x_parts, ...), custom_call_target="tpu_custom_call" | custom-call | tf_op jit(solution)/shard_map/close_block/pallas_call | solution.py:1598
  796.8 1.2 fusion.16
  800.1 2.2 copy.81
  802.4 2.2 copy.82
  804.6 2.3 copy.83
  806.9 1.5 slice_reduce_fusion
  808.4 1.3 slice.120
  810.3 2.3 copy.103
  (115 shorter events, 27.6 us)
Async XLA Ops:
  0.7 5.5 copy-start.16
  3.9 3.4 copy-start.17
  5.4 2.2 copy-start.18
  6.4 1.5 copy-start.19
  7.9 94.7 %copy-start.24 = (f32[342]{0:T(512)S(1)}, f32[342]{0:T(512)}, u32[]{:S(2)}) copy-start(f32[342]{0:T(512)} %param.26) | copy-start | bytes 4108
  7.9 94.7 %copy-start.25 = (f32[342]{0:T(512)S(1)}, f32[342]{0:T(512)}, u32[]{:S(2)}) copy-start(f32[342]{0:T(512)} %param.28) | copy-start | bytes 4108
  7.9 94.8 %copy-start.26 = (f32[342]{0:T(512)S(1)}, f32[342]{0:T(512)}, u32[]{:S(2)}) copy-start(f32[342]{0:T(512)} %param.30) | copy-start | bytes 4108
  7.9 94.8 %copy-start.22 = (f32[342]{0:T(512)S(1)}, f32[342]{0:T(512)}, u32[]{:S(2)}) copy-start(f32[342]{0:T(512)} %param.31) | copy-start | bytes 4108
  7.9 95.4 %copy-start.23 = (f32[4,342]{1,0:T(4,128)S(1)}, f32[4,342]{1,0:T(4,128)}, u32[]{:S(2)}) copy-start(f32[4,342]{1,0:T(4,128)} %param.25) | copy-start | bytes 16420
  95.3 3.3 copy-start
  198.9 77.2 %copy-start.9 = (bf16[256,2048]{1,0:T(8,128)(2,1)S(1)}, bf16[256,2048]{1,0:T(8,128)(2,1)}, u32[]{:S(2)}) copy-start(bf16[256,2048]{1,0:T(8,128)(2,1)} %own_cot_ref.1) | copy-start | bytes 3145732
  198.9 77.2 %copy-start.12 = (bf16[512,768]{1,0:T(8,128)(2,1)S(1)}, bf16[512,768]{1,0:T(8,128)(2,1)}, u32[]{:S(2)}) copy-start(bf16[512,768]{1,0:T(8,128)(2,1)} %shard.5) | copy-start | bytes 2359300
  276.1 1.9 copy-start.3
  277.9 1.9 copy-start.4
  350.1 1.6 copy-start.1
  351.8 1.7 copy-start.2
  545.9 1.6 copy-start.10
  684.4 4.1 copy-start.28
  684.4 6.2 copy-start.21
  684.4 6.9 copy-start.20
  800.1 9.6 %copy-start.27 = (f32[1,128]{1,0:T(1,128)S(1)}, f32[1,128]{1,0:T(1,128)}, u32[]{:S(2)}) copy-start(f32[1,128]{1,0:T(1,128)} %get-tuple-element.99) | copy-start | bytes 1540
  804.6 8.0 copy-start.15
  813.6 2.0 copy-start.14
  815.6 2.0 copy-start.13
  (7 other events, 7.3 us)

commit v4 on v3

--- a/solution.py
+++ b/solution.py
@@ -10,6 +10,7 @@
 GELU_A = 0.7978845608028654
 GELU_B = 0.044715
 CHUNK = 16
+UNROLL = 4
 
 
 def gelu_only(x):
@@ -25,10 +26,7 @@
 
 
 def one_minus_exp(x, exp_x):
-    series = 1.0 + x * (1.0 / 7.0)
-    for order in (6.0, 5.0, 4.0, 3.0, 2.0):
-        series = 1.0 + x * (1.0 / order) * series
-    return jnp.where(x > -0.25, -x * series, 1.0 - exp_x)
+    return -jnp.tanh(0.5 * x) * (1.0 + exp_x)
 
 
 def dot_plain(left, right):
@@ -45,6 +43,13 @@
     return lax.dot_general(
         left, right, (((0,), (0,)), ((), ())), preferred_element_type=jnp.float32
     )
+
+
+def sum_eight(value):
+    total = value[0:8, :]
+    for k in range(1, value.shape[0] // 8):
+        total = total + value[8 * k : 8 * k + 8, :]
+    return total
 
 
 def conv_rows(window, keep, taps, shift):
@@ -82,7 +87,7 @@
 
 
 def forward_step(
-    normed_ref, xw_ref, yw_ref, ow_ref, taps_ref, vec_ref, wr_ref, we_ref, keep_ref,
+    normed_ref, xy_ref, ow_ref, taps_ref, vec_ref, wr_ref, we_ref, keep_ref,
     u_ref, by_ref, before_ref, states_ref, mixed_ref,
     window, conv, conv_low, rate, entry, carry,
 ):
@@ -93,10 +98,12 @@
         window[0:8, :] = jnp.zeros_like(window[0:8, :])
         carry[...] = jnp.zeros_like(carry)
 
-    branch_x = dot_plain(normed_ref[...], xw_ref[...]).astype(jnp.bfloat16)
+    chans = u_ref.shape[1]
+    branches = dot_plain(normed_ref[...], xy_ref[...])
+    branch_x = branches[:, :chans].astype(jnp.bfloat16)
     u_ref[...] = branch_x
     window[pl.ds(8, rows), :] = branch_x.astype(jnp.float32)
-    by_ref[...] = dot_plain(normed_ref[...], yw_ref[...])
+    by_ref[...] = branches[:, chans:]
 
     def conv_step(j, unused):
         at = pl.multiple_of(j * CHUNK, CHUNK)
@@ -108,7 +115,7 @@
         conv_low[pl.ds(at, CHUNK), :] = made.astype(jnp.bfloat16)
         return unused
 
-    lax.fori_loop(0, rows // CHUNK, conv_step, 0)
+    lax.fori_loop(0, rows // CHUNK, conv_step, 0, unroll=UNROLL)
     window[0:8, :] = window[pl.ds(rows, 8), :]
     rate[...] = dot_plain(conv_low[...], wr_ref[...]) + vec_ref[1:2, :]
     entry[...] = dot_plain(conv_low[...], we_ref[...]) + vec_ref[2:3, :]
@@ -119,7 +126,8 @@
         carried = keep_ref[here, 0:1]
         log_decay = jax.nn.sigmoid(rate[here, :]) * vec_ref[3:4, :]
         exp_decay = jnp.exp(log_decay)
-        drop = jnp.sqrt(one_minus_exp(2.0 * log_decay, exp_decay * exp_decay))
+        lost = one_minus_exp(2.0 * log_decay, exp_decay * exp_decay)
+        drop = lost * lax.rsqrt(jnp.maximum(lost, 1e-30))
         scaling = (1.0 - carried) + carried * drop
         driven = scaling * jax.nn.sigmoid(entry[here, :]) * conv[here, :]
         states = scan_down(exp_decay * carried, driven, before)
@@ -132,27 +140,27 @@
         ).astype(jnp.bfloat16)
         return states[CHUNK - 1 : CHUNK, :]
 
-    carry[0:1, :] = lax.fori_loop(0, rows // CHUNK, scan_step, carry[0:1, :])
+    carry[0:1, :] = lax.fori_loop(0, rows // CHUNK, scan_step, carry[0:1, :], unroll=UNROLL)
     return contract_last(mixed_ref[...], ow_ref[...]).astype(jnp.bfloat16)
 
 
 def forward_body(
-    normed_ref, xw_ref, yw_ref, ow_ref, taps_ref, vec_ref, wr_ref, we_ref, keep_ref,
+    normed_ref, xy_ref, ow_ref, taps_ref, vec_ref, wr_ref, we_ref, keep_ref,
     u_ref, by_ref, before_ref, states_ref, mixed_ref, part_ref, *scratch,
 ):
     part_ref[...] = forward_step(
-        normed_ref, xw_ref, yw_ref, ow_ref, taps_ref, vec_ref, wr_ref, we_ref, keep_ref,
+        normed_ref, xy_ref, ow_ref, taps_ref, vec_ref, wr_ref, we_ref, keep_ref,
         u_ref, by_ref, before_ref, states_ref, mixed_ref, *scratch,
     )
 
 
 def backward_step(
-    d_res_ref, xw_ref, yw_ref, ow_ref, taps_ref, vec_ref, wr_ref, we_ref, keep_ref,
+    d_res_ref, xy_ref, ow_ref, taps_ref, vec_ref, wr_ref, we_ref, keep_ref,
     u_ref, u_prev_ref, by_ref, before_ref, states_ref,
-    d_bx_ref, d_by_ref, taps_out, vec_out, wr_out, we_out,
+    d_xy_ref, taps_out, vec_out, wr_out, we_out,
     window, conv, conv_low, rate, entry, d_mixed, d_conv, g_rate, g_entry, carry, sums,
 ):
-    rows = d_res_ref.shape[0]
+    rows, chans = d_res_ref.shape[0], u_ref.shape[1]
     step_id = pl.program_id(0)
 
     @pl.when(step_id == 0)
@@ -181,12 +189,12 @@
         conv_low[pl.ds(at, CHUNK), :] = made.astype(jnp.bfloat16)
         return unused
 
-    lax.fori_loop(0, rows // CHUNK, conv_step, 0)
+    lax.fori_loop(0, rows // CHUNK, conv_step, 0, unroll=UNROLL)
     rate[...] = dot_plain(conv_low[...], wr_ref[...]) + vec_ref[1:2, :]
     entry[...] = dot_plain(conv_low[...], we_ref[...]) + vec_ref[2:3, :]
 
     def fold(value):
-        return value[0:8, :] + value[8:16, :]
+        return sum_eight(value)
 
     def scan_step(j, after):
         at = pl.multiple_of(rows - CHUNK - j * CHUNK, CHUNK)
@@ -197,13 +205,15 @@
         log_decay = rate_gate * vec_ref[3:4, :]
         exp_decay = jnp.exp(log_decay)
         exp_twice = exp_decay * exp_decay
-        drop = jnp.sqrt(one_minus_exp(2.0 * log_decay, exp_twice))
+        lost = one_minus_exp(2.0 * log_decay, exp_twice)
+        inverse = lax.rsqrt(jnp.maximum(lost, 1e-30))
+        drop = lost * inverse
         scaling = (1.0 - carried) + carried * drop
         decays = exp_decay * carried
         gelu_y, slope_y = gelu_both(by_ref[here, :])
         through = d_mixed[here, :]
         d_states = (through * gelu_y).astype(jnp.bfloat16).astype(jnp.float32)
-        d_by_ref[here, :] = (
+        d_xy_ref[here, chans:] = (
             through * states_ref[here, :].astype(jnp.float32) * slope_y
         ).astype(jnp.bfloat16)
         passed = scan_up(decays, decays * d_states, after)
@@ -212,7 +222,7 @@
         convolved = conv[here, :]
         gated = adjoint * entry_gate
         g_log = adjoint * before_ref[here, :] * decays - gated * convolved * (
-            carried * (exp_twice / drop)
+            carried * (exp_twice * inverse)
         )
         g_pre_rate = g_log * vec_ref[3:4, :] * (rate_gate * (1.0 - rate_gate))
         direct = gated * scaling
@@ -225,7 +235,7 @@
         sums[24:32, :] += fold(g_log * rate_gate)
         return passed[0:1, :]
 
-    carry[0:1, :] = lax.fori_loop(0, rows // CHUNK, scan_step, carry[0:1, :])
+    carry[0:1, :] = lax.fori_loop(0, rows // CHUNK, scan_step, carry[0:1, :], unroll=UNROLL)
     wr_out[...] += contract_first(conv_low[...], g_rate[...])
     we_out[...] += contract_first(conv_low[...], g_entry[...])
     d_conv[0:rows, :] += contract_last(g_rate[...], wr_ref[...]) + contract_last(
@@ -250,10 +260,10 @@
             sums[base : base + 8, :] += fold(
                 now * (keep[:, offset : offset + 1] * behind[8 - offset : 8 - offset + CHUNK])
             )
-        d_bx_ref[here, :] = total.astype(jnp.bfloat16)
+        d_xy_ref[here, :chans] = total.astype(jnp.bfloat16)
         return unused
 
-    lax.fori_loop(0, rows // CHUNK, back_step, 0)
+    lax.fori_loop(0, rows // CHUNK, back_step, 0, unroll=UNROLL)
 
     @pl.when(step_id == pl.num_programs(0) - 1)
     def _():
@@ -266,19 +276,17 @@
                 sums[32 + 8 * place : 40 + 8 * place, :], axis=0, keepdims=True
             )
 
-    return (
-        contract_last(d_bx_ref[...], xw_ref[...]) + contract_last(d_by_ref[...], yw_ref[...])
-    ).astype(jnp.bfloat16)
+    return contract_last(d_xy_ref[...], xy_ref[...]).astype(jnp.bfloat16)
 
 
 def backward_body(
-    d_res_ref, xw_ref, yw_ref, ow_ref, taps_ref, vec_ref, wr_ref, we_ref, keep_ref,
+    d_res_ref, xy_ref, ow_ref, taps_ref, vec_ref, wr_ref, we_ref, keep_ref,
     u_ref, u_prev_ref, by_ref, before_ref, states_ref,
-    d_bx_ref, d_by_ref, part_ref, *rest,
+    d_xy_ref, part_ref, *rest,
 ):
     part_ref[...] = backward_step(
-        d_res_ref, xw_ref, yw_ref, ow_ref, taps_ref, vec_ref, wr_ref, we_ref, keep_ref,
-        u_ref, u_prev_ref, by_ref, before_ref, states_ref, d_bx_ref, d_by_ref, *rest,
+        d_res_ref, xy_ref, ow_ref, taps_ref, vec_ref, wr_ref, we_ref, keep_ref,
+        u_ref, u_prev_ref, by_ref, before_ref, states_ref, d_xy_ref, *rest,
     )
 
 
@@ -286,15 +294,15 @@
     return pl.BlockSpec(shape, lambda i: (0,) * len(shape))
 
 
-def mixer_forward(normed, xw, yw, ow, taps, vec, wr, we, keep, rows):
+def mixer_forward(normed, xy, ow, taps, vec, wr, we, keep, rows):
     length, width = normed.shape
-    chans = xw.shape[1]
+    chans = ow.shape[1]
     tile = lambda columns: pl.BlockSpec((rows, columns), lambda i: (i, 0))
     return pl.pallas_call(
         forward_body,
         grid=(length // rows,),
         in_specs=[
-            tile(width), whole(xw.shape), whole(yw.shape), whole(ow.shape), whole(taps.shape),
+            tile(width), whole(xy.shape), whole(ow.shape), whole(taps.shape),
             whole(vec.shape), whole(wr.shape), whole(we.shape), tile(keep.shape[1]),
         ],
         out_specs=[tile(chans)] * 5 + [tile(width)],
@@ -321,12 +329,12 @@
             transcendentals=6 * length * chans,
         ),
         name="mixer_forward",
-    )(normed, xw, yw, ow, taps, vec, wr, we, keep)
-
-
-def mixer_backward(d_res, xw, yw, ow, taps, vec, wr, we, keep, u, by, before, states, rows):
+    )(normed, xy, ow, taps, vec, wr, we, keep)
+
+
+def mixer_backward(d_res, xy, ow, taps, vec, wr, we, keep, u, by, before, states, rows):
     length, width = d_res.shape
-    chans = xw.shape[1]
+    chans = ow.shape[1]
     blocks = length // rows
     tile = lambda columns: pl.BlockSpec((rows, columns), lambda i: (blocks - 1 - i, 0))
     ahead = pl.BlockSpec(
@@ -336,17 +344,16 @@
         backward_body,
         grid=(blocks,),
         in_specs=[
-            tile(width), whole(xw.shape), whole(yw.shape), whole(ow.shape), whole(taps.shape),
+            tile(width), whole(xy.shape), whole(ow.shape), whole(taps.shape),
             whole(vec.shape), whole(wr.shape), whole(we.shape), tile(keep.shape[1]),
             tile(chans), ahead, tile(chans), tile(chans), tile(chans),
         ],
         out_specs=[
-            tile(chans), tile(chans), tile(width), whole(taps.shape), whole(vec.shape),
+            tile(2 * chans), tile(width), whole(taps.shape), whole(vec.shape),
             whole(wr.shape), whole(we.shape),
         ],
         out_shape=[
-            jax.ShapeDtypeStruct((length, chans), jnp.bfloat16),
-            jax.ShapeDtypeStruct((length, chans), jnp.bfloat16),
+            jax.ShapeDtypeStruct((length, 2 * chans), jnp.bfloat16),
             jax.ShapeDtypeStruct((length, width), jnp.bfloat16),
             jax.ShapeDtypeStruct(taps.shape, jnp.float32),
             jax.ShapeDtypeStruct(vec.shape, jnp.float32),
@@ -373,7 +380,7 @@
             transcendentals=6 * length * chans,
         ),
         name="mixer_backward",
-    )(d_res, xw, yw, ow, taps, vec, wr, we, keep, u, u, by, before, states)
+    )(d_res, xy, ow, taps, vec, wr, we, keep, u, u, by, before, states)
 
 
 def keep_columns(resets):
@@ -462,9 +469,9 @@
             )
         count += PLANE - 1
     if plane == "near":
-        for target in (sibling_of(h), across_of(h), along_of(h), across_of(along_of(h))):
+        for target in (sibling_of(h), across_of(h), along_of(h)):
             pl.semaphore_signal(barrier, inc=1, device_id={"head": target}, device_id_type=MESH)
-        count += 4
+        count += 3
     pl.semaphore_wait(barrier, count)
 
 
@@ -748,8 +755,9 @@
     semaphores = (
         pltpu.SemaphoreType.DMA((4,)),
         pltpu.SemaphoreType.DMA((4,)),
-        pltpu.SemaphoreType.DMA((4,)),
-        pltpu.SemaphoreType.DMA((3,)),
+        pltpu.SemaphoreType.DMA((4, 2)),
+        pltpu.SemaphoreType.DMA((2, 2)),
+        pltpu.SemaphoreType.DMA((2,)),
     )
 
     @staticmethod
@@ -758,15 +766,21 @@
             pltpu.VMEM((4, rows, width), jnp.bfloat16),
             pltpu.VMEM((4, rows, width), jnp.bfloat16),
             pltpu.VMEM((4, rows, width), jnp.bfloat16),
-            pltpu.VMEM((3, rows, width), jnp.bfloat16),
+            pltpu.VMEM((2, rows // 2, width), jnp.bfloat16),
+            pltpu.VMEM((2, rows, width), jnp.bfloat16),
         ]
 
-    def __init__(self, staged, beside, mine, landed, side_sent, side_arrived, sent, arrived):
+    def __init__(
+        self, staged, beside, mine, relayed, landed,
+        side_sent, side_arrived, sent, arrived, relay_arrived,
+    ):
         h = lax.axis_index("head")
         self.h, self.core, self.chip = h, lax.rem(h, 2), lax.div(h, 2)
-        self.staged, self.beside, self.mine, self.landed = staged, beside, mine, landed
+        self.staged, self.beside, self.mine = staged, beside, mine
+        self.relayed, self.landed = relayed, landed
         self.side_sent, self.side_arrived = side_sent, side_arrived
-        self.sent, self.arrived = sent, arrived
+        self.sent, self.arrived, self.relay_arrived = sent, arrived, relay_arrived
+        self.half = mine.shape[1] // 2
 
     def aside(self, chip):
         return send_to(
@@ -774,16 +788,25 @@
             self.side_arrived.at[chip], "head", sibling_of(self.h),
         )
 
-    def place(self, chip):
+    def relation(self, chip):
         flip_x = lax.rem(chip + self.chip, 2)
         flip_y = lax.rem(lax.div(chip, 2) + lax.div(self.chip, 2), 2)
-        return flip_x + 2 * flip_y - 1
-
-    def across(self, chip):
-        at = self.place(chip)
+        return flip_x + 2 * flip_y
+
+    def part(self, half):
+        return pl.ds(half * self.half, self.half)
+
+    def home(self, chip, way, half):
         return send_to(
-            self.mine.at[chip], self.landed.at[at], self.sent.at[chip], self.arrived.at[at],
-            "head", 2 * chip + self.core,
+            self.mine.at[chip, self.part(half)], self.landed.at[way, self.part(half)],
+            self.sent.at[chip, half], self.arrived.at[way, half], "head",
+            (across_of, along_of)[way](self.h),
+        )
+
+    def opposite(self, chip, half):
+        return send_to(
+            self.mine.at[chip, self.part(half)], self.relayed.at[half], self.sent.at[chip, half],
+            self.relay_arrived.at[half], "head", (along_of, across_of)[half](self.h),
         )
 
     def put(self, block, value):
@@ -804,7 +827,6 @@
         @pl.when(core == self.core)
         def _():
             self.aside(chip).wait_recv()
-            rows = self.mine.shape[1]
             step = 32
 
             def add(i, unused):
@@ -815,24 +837,55 @@
                 ).astype(jnp.bfloat16)
                 return unused
 
-            lax.fori_loop(0, rows // step, add, 0)
-
-            @pl.when(chip != self.chip)
+            lax.fori_loop(0, 2 * self.half // step, add, 0)
+            relation = self.relation(chip)
+
+            @pl.when(relation == 1)
             def _():
-                self.across(chip).start()
+                self.home(chip, 0, 1).start()
+
+            @pl.when(relation == 2)
+            def _():
+                self.home(chip, 1, 0).start()
+
+            @pl.when(relation == 3)
+            def _():
+                self.opposite(chip, 0).start()
+                self.opposite(chip, 1).start()
+
+    def relay(self, block):
+        chip, core = lax.div(block, 2), lax.rem(block, 2)
+        for way in (0, 1):
+
+            @pl.when((core == self.core) & (self.relation(chip) == way + 1))
+            def _(way=way):
+                self.opposite(chip, way).wait_recv()
+                step = 32
+
+                def add(i, unused):
+                    at = pl.ds(pl.multiple_of(i * step, step), step)
+                    here = pl.ds(pl.multiple_of(way * self.half + i * step, step), step)
+                    self.mine[chip, here, :] = (
+                        self.mine[chip, here, :].astype(jnp.float32)
+                        + self.relayed[way, at, :].astype(jnp.float32)
+                    ).astype(jnp.bfloat16)
+                    return unused
+
+                lax.fori_loop(0, self.half // step, add, 0)
+                self.home(chip, way, way).start()
 
     def arrive(self):
-        for at in range(3):
-            send_to(
-                self.landed.at[at], self.landed.at[at], self.sent.at[0], self.arrived.at[at],
-                "head", self.h,
-            ).wait_recv()
+        for way in (0, 1):
+            for half in (0, 1):
+                self.home(self.chip, way, half).wait_recv()
 
     def total(self, at):
         value = self.mine[self.chip, at, :].astype(jnp.float32)
-        for place in range(3):
-            value = value + self.landed[place, at, :].astype(jnp.float32)
-        return value
+        return (
+            value
+            + self.landed[0, at, :].astype(jnp.float32)
+            + self.landed[1, at, :].astype(jnp.float32)
+        )
 
     def finish(self):
         for chip in range(4):
@@ -840,7 +893,8 @@
 
             @pl.when(chip != self.chip)
             def _(chip=chip):
-                self.across(chip).wait_send()
+                self.home(chip, 0, 0).wait_send()
+                self.home(chip, 0, 1).wait_send()
 
 
 def norm_apply(rows, gain):
@@ -859,15 +913,15 @@
 
 
 def open_body(
-    x_ref, tile_ref, xs, ys, zs, full, xf, yf, zf, gains_ref,
+    x_ref, tile_ref, xy_shard, out_shard, full, xy_full, out_full, gains_ref,
     normed, column, spread, gain_sent, gain_arrived, wide_sent, wide_arrived, *semaphores,
 ):
     r, h = lax.axis_index("row"), lax.axis_index("head")
     lines = [
         LineGather(src, dst, *semaphores[3 * k : 3 * k + 3])
-        for k, (src, dst) in enumerate(((xs, xf), (ys, yf), (zs, zf)))
+        for k, (src, dst) in enumerate(((xy_shard, xy_full), (out_shard, out_full)))
     ]
-    plane = PlaneGather(normed, full, *semaphores[9:12])
+    plane = PlaneGather(normed, full, *semaphores[6:9])
     meet(True, "all")
 
     def up_line(t):
@@ -937,8 +991,8 @@
     rows, width = layer_in.shape
     return pl.pallas_call(
         open_body,
-        in_specs=[IN_VMEM, IN_VMEM] + [ANYWHERE] * 3,
-        out_specs=[ANYWHERE] * 4 + [IN_VMEM],
+        in_specs=[IN_VMEM, IN_VMEM] + [ANYWHERE] * 2,
+        out_specs=[ANYWHERE] * 3 + [IN_VMEM],
         out_shape=[jax.ShapeDtypeStruct((PLANE, rows, width), jnp.bfloat16)]
         + [jax.ShapeDtypeStruct((LINE,) + item.shape, item.dtype) for item in weights]
         + [jax.ShapeDtypeStruct((2, width), jnp.float32)],
@@ -950,7 +1004,7 @@
             pltpu.SemaphoreType.DMA((LINE,)),
             pltpu.SemaphoreType.DMA((PLANE,)),
             pltpu.SemaphoreType.DMA((PLANE,)),
-            *(LineGather.semaphores * 3),
+            *(LineGather.semaphores * 2),
             *PlaneGather.semaphores,
         ],
         compiler_params=pltpu.CompilerParams(
@@ -961,14 +1015,14 @@
 
 
 def forward_linked_body(
-    normed_ref, xw_ref, yw_ref, ow_ref, taps_ref, vec_ref, wr_ref, we_ref, keep_ref,
+    normed_ref, xy_ref, ow_ref, taps_ref, vec_ref, wr_ref, we_ref, keep_ref,
     x_ref, gain_ref, shard,
     u_ref, by_ref, before_ref, states_ref, mixed_ref, residual_ref, two_ref, gathered,
     window, conv, conv_low, rate, entry, carry, *links,
 ):
     step = pl.program_id(0)
-    plane = PlaneReduce(*links[:8])
-    line = LineGather(shard, gathered, *links[8:11])
+    plane = PlaneReduce(*links[:10])
+    line = LineGather(shard, gathered, *links[10:13])
 
     @pl.when(step == 0)
     def _():
@@ -979,8 +1033,12 @@
     def _():
         plane.pass_on(step - 1)
 
+    @pl.when(step > 2)
+    def _():
+        plane.relay(step - 3)
+
     value = forward_step(
-        normed_ref, xw_ref, yw_ref, ow_ref, taps_ref, vec_ref, wr_ref, we_ref, keep_ref,
+        normed_ref, xy_ref, ow_ref, taps_ref, vec_ref, wr_ref, we_ref, keep_ref,
         u_ref, by_ref, before_ref, states_ref, mixed_ref,
         window, conv, conv_low, rate, entry, carry,
     )
@@ -992,7 +1050,10 @@
 
     @pl.when(step == PLANE - 1)
     def _():
+        plane.relay(step - 2)
         plane.pass_on(step)
+        plane.relay(step - 1)
+        plane.relay(step)
         plane.arrive()
 
         def make(i, unused):
@@ -1007,16 +1068,16 @@
         line.finish()
 
 
-def forward_linked(normed, xw, yw, ow, taps, vec, wr, we, keep, layer_in, gain, shard):
+def forward_linked(normed, xy, ow, taps, vec, wr, we, keep, layer_in, gain, shard):
     length, width = normed.shape
-    chans = xw.shape[1]
+    chans = ow.shape[1]
     rows = length // PLANE
     tile = lambda columns: pl.BlockSpec((rows, columns), lambda i: (i, 0))
     return pl.pallas_call(
         forward_linked_body,
         grid=(PLANE,),
         in_specs=[
-            tile(width), whole(xw.shape), whole(yw.shape), whole(ow.shape), whole(taps.shape),
+            tile(width), whole(xy.shape), whole(ow.shape), whole(taps.shape),
             whole(vec.shape), whole(wr.shape), whole(we.shape), tile(keep.shape[1]),
             whole(layer_in.shape), whole(gain.shape), ANYWHERE,
         ],
@@ -1046,104 +1107,133 @@
             collective_id=1, has_side_effects=True, vmem_limit_bytes=56 * 2**20
         ),
         name="mixer_forward_linked",
-    )(normed, xw, yw, ow, taps, vec, wr, we, keep, layer_in, gain, shard)
-
-
-def spread_body(block, shard, full, gathered, *semaphores):
-    plane = PlaneGather(block, full, *semaphores[:3])
-    line = LineGather(shard, gathered, *semaphores[3:6])
+    )(normed, xy, ow, taps, vec, wr, we, keep, layer_in, gain, shard)
+
+
+def ffn_up_body(
+    own_two, gate_ref, own_cot, up_shard, down_shard,
+    two_out, cot_out, up_out, down_out, gates_out, ups_out, hidden_out, down_parts,
+    two, cot, up, gates, ups, hidden, total, copied, *semaphores,
+):
+    h = lax.axis_index("head")
+    rows = own_two.shape[0]
+    units = gates.shape[1]
+    up_line = LineGather(up_shard, up, *semaphores[0:3])
+    down_line = LineGather(down_shard, down_out, *semaphores[3:6])
+    two_plane = PlaneGather(own_two, two, *semaphores[6:9])
+    cot_plane = PlaneGather(own_cot, cot, *semaphores[9:12])
+    outward = [
+        pltpu.make_async_copy(src, dst, copied.at[k])
+        for k, (src, dst) in enumerate(
+            (
+                (two, two_out), (cot, cot_out), (up, up_out), (gates, gates_out),
+                (ups, ups_out), (hidden, hidden_out),
+            )
+        )
+    ]
     meet(True, "near")
-    line.start()
-    plane.start()
-    plane.relay(0)
-    plane.relay(1)
-    plane.rest()
-    line.forward()
-    plane.end()
-    line.finish()
-
-
-def spread(block, shard, place):
-    return pl.pallas_call(
-        spread_body,
-        in_specs=[ANYWHERE] * 2,
-        out_specs=[ANYWHERE] * 2,
-        out_shape=[
-            jax.ShapeDtypeStruct((PLANE,) + block.shape, block.dtype),
-            jax.ShapeDtypeStruct((LINE,) + shard.shape, shard.dtype),
-        ],
-        scratch_shapes=[*PlaneGather.semaphores, *LineGather.semaphores],
-        compiler_params=pltpu.CompilerParams(collective_id=place, has_side_effects=True),
-        name="spread",
-    )(block, shard)
-
-
-def ffn_up_body(
-    two_ref, gate_ref, up_ref, cot, shard,
-    gates_ref, ups_ref, hidden_ref, full, gathered, *semaphores,
-):
-    step = pl.program_id(0)
-    plane = PlaneGather(cot, full, *semaphores[:3])
-    line = LineGather(shard, gathered, *semaphores[3:6])
-
-    @pl.when(step == 0)
-    def _():
-        meet(True, "near")
-        line.start()
-        plane.start()
-
-    @pl.when(step == 3)
-    def _():
-        plane.relay(0)
-
-    @pl.when(step == 5)
-    def _():
-        plane.relay(1)
-
-    gates = dot_plain(two_ref[...], gate_ref[...])
-    ups = dot_plain(two_ref[...], up_ref[...])
-    gates_ref[...] = gates
-    ups_ref[...] = ups
-    rows = gates_ref.shape[0]
-
-    def make(i, unused):
-        at = pl.ds(pl.multiple_of(i * CHUNK, CHUNK), CHUNK)
-        hidden_ref[at, :] = (gelu_only(gates_ref[at, :]) * ups_ref[at, :]).astype(jnp.bfloat16)
+    up_line.start()
+    down_line.start()
+    two_plane.start()
+
+    def at_block(block):
+        return pl.ds(pl.multiple_of(block * rows, rows), rows)
+
+    def make_gates(k, unused):
+        block = lax.rem(h + k, PLANE)
+        gates[at_block(block), :] = dot_plain(two[block], gate_ref[...])
         return unused
 
-    lax.fori_loop(0, rows // CHUNK, make, 0)
-
-    @pl.when(step == PLANE - 1)
-    def _():
-        plane.rest()
-        line.forward()
-        plane.end()
-        line.finish()
-
-
-def ffn_up(two, gate, up, cot, shard):
-    length, width = two.shape
-    units = gate.shape[1]
-    rows = length // PLANE
-    tile = lambda columns: pl.BlockSpec((rows, columns), lambda i: (i, 0))
+    gates[at_block(h), :] = dot_plain(own_two[...], gate_ref[...])
+    two_plane.relay(0)
+    two_plane.relay(1)
+    two_plane.rest()
+    cot_plane.start()
+    two_plane.end()
+    outward[0].start()
+    up_line.forward()
+    lax.fori_loop(1, 3, make_gates, 0)
+    cot_plane.relay(0)
+    lax.fori_loop(3, 6, make_gates, 0)
+    cot_plane.relay(1)
+    lax.fori_loop(6, PLANE, make_gates, 0)
+    outward[3].start()
+    cot_plane.rest()
+    up_line.finish()
+    outward[2].start()
+
+    def make_hidden(block, unused):
+        at = at_block(block)
+        value = jnp.zeros((rows, units), jnp.float32)
+        share = up.shape[1]
+        for t in range(LINE):
+            value = value + dot_plain(two[block, :, t * share : (t + 1) * share], up[t])
+        ups[at, :] = value
+
+        def make(i, unused):
+            here = pl.ds(pl.multiple_of(block * rows + i * CHUNK, CHUNK), CHUNK)
+            hidden[here, :] = (gelu_only(gates[here, :]) * ups[here, :]).astype(jnp.bfloat16)
+            return unused
+
+        lax.fori_loop(0, rows // CHUNK, make, 0, unroll=UNROLL)
+        return unused
+
+    lax.fori_loop(0, PLANE, make_hidden, 0)
+    outward[4].start()
+    outward[5].start()
+    cot_plane.end()
+    outward[1].start()
+    down_line.forward()
+    total[...] = contract_first(cot[0], hidden[0:rows, :])
+
+    def add_down(block, unused):
+        total[...] += contract_first(cot[block], hidden[at_block(block), :])
+        return unused
+
+    lax.fori_loop(1, PLANE, add_down, 0)
+    to_parts(total, down_parts)
+    down_line.finish()
+    for copy in outward:
+        copy.wait()
+
+
+def ffn_up(own_two, gate, own_cot, up_shard, down_shard):
+    rows, width = own_two.shape
+    share, units = up_shard.shape
+    length = rows * PLANE
+    group = jax.ShapeDtypeStruct((PLANE, rows, width), jnp.bfloat16)
+    weight = jax.ShapeDtypeStruct((LINE, share, units), jnp.bfloat16)
     return pl.pallas_call(
         ffn_up_body,
-        grid=(PLANE,),
-        in_specs=[tile(width), whole(gate.shape), whole(up.shape), ANYWHERE, ANYWHERE],
-        out_specs=[tile(units)] * 3 + [ANYWHERE] * 2,
+        in_specs=[IN_VMEM, IN_VMEM, ANYWHERE, ANYWHERE, ANYWHERE],
+        out_specs=[ANYWHERE] * 7 + [IN_VMEM],
         out_shape=[
+            group,
+            group,
+            weight,
+            weight,
             jax.ShapeDtypeStruct((length, units), jnp.float32),
             jax.ShapeDtypeStruct((length, units), jnp.float32),
             jax.ShapeDtypeStruct((length, units), jnp.bfloat16),
-            jax.ShapeDtypeStruct((PLANE,) + cot.shape, cot.dtype),
-            jax.ShapeDtypeStruct((LINE,) + shard.shape, shard.dtype),
-        ],
-        scratch_shapes=[*PlaneGather.semaphores, *LineGather.semaphores],
+            weight,
+        ],
+        scratch_shapes=[
+            pltpu.VMEM((PLANE, rows, width), jnp.bfloat16),
+            pltpu.VMEM((PLANE, rows, width), jnp.bfloat16),
+            pltpu.VMEM((LINE, share, units), jnp.bfloat16),
+            pltpu.VMEM((length, units), jnp.float32),
+            pltpu.VMEM((length, units), jnp.float32),
+            pltpu.VMEM((length, units), jnp.bfloat16),
+            pltpu.VMEM((width, units), jnp.float32),
+            pltpu.SemaphoreType.DMA((6,)),
+            *(LineGather.semaphores * 2),
+            *(PlaneGather.semaphores * 2),
+        ],
         compiler_params=pltpu.CompilerParams(
-            collective_id=3, has_side_effects=True, vmem_limit_bytes=40 * 2**20
+            collective_id=2, has_side_effects=True, vmem_limit_bytes=60 * 2**20
         ),
         name="ffn_up",
-    )(two, gate, up, cot, shard)
+    )(own_two, gate, own_cot, up_shard, down_shard)
 def once(shape):
     return pl.BlockSpec(
         shape, lambda i: (0,) * len(shape), pipeline_mode=pl.Buffered(buffer_count=1)
@@ -1171,62 +1261,57 @@
     lax.fori_loop(0, rows // step, move, 0)
 
 
-def sum_eight(value):
-    total = value[0:8, :]
-    for k in range(1, value.shape[0] // 8):
-        total = total + value[8 * k : 8 * k + 8, :]
-    return total
-
-
 def ffn_back_body(
-    cot_ref, hidden_ref, two_ref, gates_ref, ups_ref, gate_ref, up_ref, down_ref,
+    cot_ref, two_ref, gates_ref, ups_ref, gate_ref, up_ref, down_ref, parts,
     residual_ref, own_cot_ref, gain_ref,
-    d_gates_ref, d_ups_ref, gate_parts, down_out, d_res_ref, d_low_ref, gain_out,
-    total, parts, eight, *links,
+    d_ups_ref, gate_parts, down_out, d_res_ref, d_low_ref, gain_out,
+    total, d_gates, d_hidden, eight, *links,
 ):
     step = pl.program_id(0)
     line = LineReduce(parts, *links[:5])
     plane = PlaneReduce(*links[5:])
+    rows = cot_ref.shape[0]
 
     @pl.when(step == 0)
     def _():
-        total[...] = jnp.zeros_like(total)
         meet(True, "near")
-
-    @pl.when(step < PLANE)
-    def _():
-        total[...] += contract_first(cot_ref[...], hidden_ref[...])
-
-    @pl.when(step == PLANE - 1)
-    def _():
-        to_parts(total, parts)
         line.start()
         total[...] = jnp.zeros_like(total)
 
-    @pl.when(step > PLANE)
-    def _():
-        plane.pass_on(step - PLANE - 1)
-
-    @pl.when(step >= PLANE)
-    def _():
-        d_hidden = dot_plain(cot_ref[...], down_ref[...])
-        gelu_gate, slope = gelu_both(gates_ref[...])
-        d_gates_ref[...] = (d_hidden * ups_ref[...] * slope).astype(jnp.bfloat16)
-        d_ups_ref[...] = (d_hidden * gelu_gate).astype(jnp.bfloat16)
-        value = contract_last(d_gates_ref[...], gate_ref[...]) + contract_last(
-            d_ups_ref[...], up_ref[...]
-        )
-        plane.put(step - PLANE, value.astype(jnp.bfloat16))
-        total[...] += contract_first(two_ref[...], d_gates_ref[...])
-
-    @pl.when(step == PLANE + 4)
+    @pl.when(step > 0)
+    def _():
+        plane.pass_on(step - 1)
+
+    @pl.when(step > 2)
+    def _():
+        plane.relay(step - 3)
+
+    d_hidden[...] = dot_plain(cot_ref[...], down_ref[...])
+
+    def make(i, unused):
+        at = pl.ds(pl.multiple_of(i * CHUNK, CHUNK), CHUNK)
+        gelu_gate, slope = gelu_both(gates_ref[at, :])
+        through = d_hidden[at, :]
+        d_gates[at, :] = (through * ups_ref[at, :] * slope).astype(jnp.bfloat16)
+        d_ups_ref[at, :] = (through * gelu_gate).astype(jnp.bfloat16)
+        return unused
+
+    lax.fori_loop(0, rows // CHUNK, make, 0, unroll=UNROLL)
+    value = contract_last(d_gates[...], gate_ref[...]) + contract_last(d_ups_ref[...], up_ref[...])
+    plane.put(step, value.astype(jnp.bfloat16))
+    total[...] += contract_first(two_ref[...], d_gates[...])
+
+    @pl.when(step == 4)
     def _():
         line.forward()
 
-    @pl.when(step == 2 * PLANE - 1)
-    def _():
-        plane.pass_on(step - PLANE)
+    @pl.when(step == PLANE - 1)
+    def _():
+        plane.relay(step - 2)
+        plane.pass_on(step)
+        plane.relay(step - 1)
         to_parts(total, gate_parts)
+        plane.relay(step)
         plane.arrive()
         eight[...] = jnp.zeros_like(eight)
 
@@ -1239,7 +1324,7 @@
             eight[...] += sum_eight(d_gain)
             return unused
 
-        lax.fori_loop(0, residual_ref.shape[0] // CHUNK, back, 0)
+        lax.fori_loop(0, rows // CHUNK, back, 0)
         gain_out[...] = jnp.sum(eight[...], axis=0, keepdims=True)
 
         def write(at, value):
@@ -1250,30 +1335,25 @@
 
 
 def ffn_back(
-    cot_group, hidden, two_group, gates, ups, gate, up, down, residual, own_cot, gain
+    cot_group, two_group, gates, ups, gate, up, down, parts, residual, own_cot, gain
 ):
     length, width = cot_group.shape
     units = gate.shape[1]
     rows, share = length // PLANE, width // LINE
-    early = lambda columns: pl.BlockSpec((rows, columns), lambda i: (jnp.minimum(i, PLANE - 1), 0))
-    late = lambda columns: pl.BlockSpec(
-        (rows, columns), lambda i: (jnp.maximum(i - PLANE, 0), 0)
-    )
-    both = pl.BlockSpec((rows, width), lambda i: (lax.rem(i, PLANE), 0))
+    tile = lambda columns: pl.BlockSpec((rows, columns), lambda i: (i, 0))
     return pl.pallas_call(
         ffn_back_body,
-        grid=(2 * PLANE,),
+        grid=(PLANE,),
         in_specs=[
-            both, early(units), late(width), late(units), late(units), once(gate.shape),
-            once(up.shape), once(down.shape), once(residual.shape), once(own_cot.shape),
-            once(gain.shape),
+            tile(width), tile(width), tile(units), tile(units), once(gate.shape),
+            once(up.shape), once(down.shape), once(parts.shape), once(residual.shape),
+            once(own_cot.shape), once(gain.shape),
         ],
         out_specs=[
-            late(units), late(units), once((LINE, share, units)), once((share, units)),
+            tile(units), once((LINE, share, units)), once((share, units)),
             once((rows, width)), once((rows, width)), once((1, width)),
         ],
         out_shape=[
-            jax.ShapeDtypeStruct((length, units), jnp.bfloat16),
             jax.ShapeDtypeStruct((length, units), jnp.bfloat16),
             jax.ShapeDtypeStruct((LINE, share, units), jnp.bfloat16),
             jax.ShapeDtypeStruct((share, units), jnp.float32),
@@ -1283,7 +1363,8 @@
         ],
         scratch_shapes=[
             pltpu.VMEM((width, units), jnp.float32),
-            pltpu.VMEM((LINE, share, units), jnp.bfloat16),
+            pltpu.VMEM((rows, units), jnp.bfloat16),
+            pltpu.VMEM((rows, units), jnp.float32),
             pltpu.VMEM((8, width), jnp.float32),
             *LineReduce.buffers(share, units),
             *LineReduce.semaphores,
@@ -1291,18 +1372,22 @@
             *PlaneReduce.semaphores,
         ],
         compiler_params=pltpu.CompilerParams(
-            collective_id=4, has_side_effects=True, vmem_limit_bytes=62 * 2**20
+            collective_id=4, has_side_effects=True, vmem_limit_bytes=60 * 2**20
         ),
         name="ffn_back",
-    )(cot_group, hidden, two_group, gates, ups, gate, up, down, residual, own_cot, gain)
+    )(cot_group, two_group, gates, ups, gate, up, down, parts, residual, own_cot, gain)
 
 
 def turn_body(
-    two_ref, d_ups_ref, gate_parts, block, up_parts, gate_out, full, total, *links
+    two_ref, d_ups_ref, gate_parts, block, mixed_ref,
+    up_parts, out_parts, gate_out, full_out,
+    full, total, out_total, copied, *links,
 ):
     step = pl.program_id(0)
     line = LineReduce(gate_parts, *links[:5])
     plane = PlaneGather(block, full, *links[5:])
+    rows = two_ref.shape[0]
+    outward = pltpu.make_async_copy(full, full_out, copied)
 
     @pl.when(step == 0)
     def _():
@@ -1313,7 +1398,7 @@
 
     total[...] += contract_first(two_ref[...], d_ups_ref[...])
 
-    @pl.when(step == PLANE - 2)
+    @pl.when(step == PLANE - 3)
     def _():
         plane.relay(0)
 
@@ -1321,78 +1406,99 @@
     def _():
         plane.relay(1)
         to_parts(total, up_parts)
+        plane.rest()
         line.forward()
-        plane.rest()
         plane.end()
+        outward.start()
+        out_total[...] = contract_first(full[0], mixed_ref[0:rows, :])
+
+        def add(b, unused):
+            at = pl.ds(pl.multiple_of(b * rows, rows), rows)
+            out_total[...] += contract_first(full[b], mixed_ref[at, :])
+            return unused
+
+        lax.fori_loop(1, PLANE, add, 0)
+        to_parts(out_total, out_parts)
 
         def write(at, value):
             gate_out[at, :] = value
 
         line.finish(write)
-
-
-def turn(two_group, d_ups, gate_parts, block):
+        outward.wait()
+
+
+def turn(two_group, d_ups, gate_parts, block, mixed):
     length, width = two_group.shape
-    units = d_ups.shape[1]
+    units, chans = d_ups.shape[1], mixed.shape[1]
     rows, share = length // PLANE, width // LINE
     tile = lambda columns: pl.BlockSpec((rows, columns), lambda i: (i, 0))
     return pl.pallas_call(
         turn_body,
         grid=(PLANE,),
-        in_specs=[tile(width), tile(units), once(gate_parts.shape), ANYWHERE],
-        out_specs=[once(gate_parts.shape), once((share, units)), ANYWHERE],
+        in_specs=[
+            tile(width), tile(units), once(gate_parts.shape), ANYWHERE, once(mixed.shape)
+        ],
+        out_specs=[
+            once(gate_parts.shape), once((LINE, share, chans)), once((share, units)), ANYWHERE
+        ],
         out_shape=[
             jax.ShapeDtypeStruct(gate_parts.shape, jnp.bfloat16),
+            jax.ShapeDtypeStruct((LINE, share, chans), jnp.bfloat16),
             jax.ShapeDtypeStruct((share, units), jnp.float32),
             jax.ShapeDtypeStruct((PLANE, rows, width), jnp.bfloat16),
         ],
         scratch_shapes=[
+            pltpu.VMEM((PLANE, rows, width), jnp.bfloat16),
             pltpu.VMEM((width, units), jnp.float32),
+            pltpu.VMEM((width, chans), jnp.float32),
+            pltpu.SemaphoreType.DMA,
             *LineReduce.buffers(share, units),
             *LineReduce.semaphores,
             *PlaneGather.semaphores,
         ],
         compiler_params=pltpu.CompilerParams(
-            collective_id=5, has_side_effects=True, vmem_limit_bytes=48 * 2**20
+            collective_id=5, has_side_effects=True, vmem_limit_bytes=56 * 2**20
         ),
         name="turn",
-    )(two_group, d_ups, gate_parts, block)
+    )(two_group, d_ups, gate_parts, block, mixed)
 
 
 def backward_linked_body(
-    d_res_ref, xw_ref, yw_ref, ow_ref, taps_ref, vec_ref, wr_ref, we_ref, keep_ref,
-    u_ref, u_prev_ref, by_ref, before_ref, states_ref, normed_ref, mixed_ref, up_parts,
+    d_res_ref, xy_ref, ow_ref, taps_ref, vec_ref, wr_ref, we_ref, keep_ref,
+    u_ref, u_prev_ref, by_ref, before_ref, states_ref, normed_ref, up_parts, out_parts,
     x_ref, gain_ref, d_residual_ref,
-    x_parts, y_parts, out_parts, up_out, in_grad, gain_out, taps_out, vec_out, wr_out, we_out,
-    d_bx, d_by, x_total, y_total, out_total, eight, *rest,
+    xy_parts, up_out, out_out, in_grad, gain_out, taps_out, vec_out, wr_out, we_out,
+    d_xy, xy_total, eight, *rest,
 ):
     scratch, links = rest[:11], rest[11:]
     step = pl.program_id(0)
     block = PLANE - 1 - step
     line = LineReduce(up_parts, *links[:5])
-    plane = PlaneReduce(*links[5:])
+    out_line = LineReduce(out_parts, *links[5:10])
+    plane = PlaneReduce(*links[10:])
 
     @pl.when(step == 0)
     def _():
         meet(True, "near")
         line.start()
-        x_total[...] = jnp.zeros_like(x_total)
-        y_total[...] = jnp.zeros_like(y_total)
-        out_total[...] = jnp.zeros_like(out_total)
+        out_line.start()
+        xy_total[...] = jnp.zeros_like(xy_total)
 
     @pl.when(step > 0)
     def _():
         plane.pass_on(block + 1)
 
+    @pl.when(step > 2)
+    def _():
+        plane.relay(block + 3)
+
     value = backward_step(
-        d_res_ref, xw_ref, yw_ref, ow_ref, taps_ref, vec_ref, wr_ref, we_ref, keep_ref,
-        u_ref, u_prev_ref, by_ref, before_ref, states_ref, d_bx, d_by,
+        d_res_ref, xy_ref, ow_ref, taps_ref, vec_ref, wr_ref, we_ref, keep_ref,
+        u_ref, u_prev_ref, by_ref, before_ref, states_ref, d_xy,
         taps_out, vec_out, wr_out, we_out, *scratch,
     )
     plane.put(block, value)
-    x_total[...] += contract_first(normed_ref[...], d_bx[...])
-    y_total[...] += contract_first(normed_ref[...], d_by[...])
-    out_total[...] += contract_first(d_res_ref[...], mixed_ref[...])
+    xy_total[...] += contract_first(normed_ref[...], d_xy[...])
 
     @pl.when(step == 4)
     def _():
@@ -1400,10 +1506,12 @@
 
     @pl.when(step == PLANE - 1)
     def _():
+        plane.relay(block + 2)
         plane.pass_on(block)
-        to_parts(x_total, x_parts)
-        to_parts(y_total, y_parts)
-        to_parts(out_total, out_parts)
+        plane.relay(block + 1)
+        to_parts(xy_total, xy_parts)
+        plane.relay(block)
+        out_line.forward()
         plane.arrive()
         eight[...] = jnp.zeros_like(eight)
 
@@ -1422,41 +1530,43 @@
         def write(at, value):
             up_out[at, :] = value
 
+        def write_out(at, value):
+            out_out[at, :] = value
+
         line.finish(write)
+        out_line.finish(write_out)
         plane.finish()
 
 
 def backward_linked(
-    d_res, xw, yw, ow, taps, vec, wr, we, keep, u, by, before, states, normed, mixed, up_parts,
+    d_res, xy, ow, taps, vec, wr, we, keep, u, by, before, states, normed, up_parts, out_parts,
     layer_in, gain, d_residual,
 ):
     length, width = d_res.shape
-    chans, units = xw.shape[1], up_parts.shape[2]
+    chans, units = ow.shape[1], up_parts.shape[2]
     rows, share = length // PLANE, width // LINE
     tile = lambda columns: pl.BlockSpec((rows, columns), lambda i: (PLANE - 1 - i, 0))
     ahead = pl.BlockSpec(
         (16, chans), lambda i: (jnp.maximum((PLANE - 1 - i) * (rows // 16) - 1, 0), 0)
     )
-    weights = (LINE, share, chans)
     return pl.pallas_call(
         backward_linked_body,
         grid=(PLANE,),
         in_specs=[
-            tile(width), once(xw.shape), once(yw.shape), once(ow.shape), once(taps.shape),
+            tile(width), once(xy.shape), once(ow.shape), once(taps.shape),
             once(vec.shape), once(wr.shape), once(we.shape), tile(keep.shape[1]),
-            tile(chans), ahead, tile(chans), tile(chans), tile(chans), tile(width), tile(chans),
-            once(up_parts.shape), once(layer_in.shape), once(gain.shape), once(d_residual.shape),
+            tile(chans), ahead, tile(chans), tile(chans), tile(chans), tile(width),
+            once(up_parts.shape), once(out_parts.shape), once(layer_in.shape), once(gain.shape), once(d_residual.shape),
         ],
         out_specs=[
-            once(weights), once(weights), once(weights), once((share, units)),
+            once((LINE, share, 2 * chans)), once((share, units)), once((share, chans)),
             once((rows, width)), once((1, width)), once(taps.shape), once(vec.shape),
             once(wr.shape), once(we.shape),
         ],
         out_shape=[
-            jax.ShapeDtypeStruct(weights, jnp.bfloat16),
-            jax.ShapeDtypeStruct(weights, jnp.bfloat16),
-            jax.ShapeDtypeStruct(weights, jnp.bfloat16),
+            jax.ShapeDtypeStruct((LINE, share, 2 * chans), jnp.bfloat16),
             jax.ShapeDtypeStruct((share, units), jnp.float32),
+            jax.ShapeDtypeStruct((share, chans), jnp.float32),
             jax.ShapeDtypeStruct((rows, width), jnp.bfloat16),
             jax.ShapeDtypeStruct((1, width), jnp.float32),
             jax.ShapeDtypeStruct(taps.shape, jnp.float32),
@@ -1465,11 +1575,8 @@
             jax.ShapeDtypeStruct(we.shape, jnp.float32),
         ],
         scratch_shapes=[
-            pltpu.VMEM((rows, chans), jnp.bfloat16),
-            pltpu.VMEM((rows, chans), jnp.bfloat16),
-            pltpu.VMEM((width, chans), jnp.float32),
-            pltpu.VMEM((width, chans), jnp.float32),
-            pltpu.VMEM((width, chans), jnp.float32),
+            pltpu.VMEM((rows, 2 * chans), jnp.bfloat16),
+            pltpu.VMEM((width, 2 * chans), jnp.float32),
             pltpu.VMEM((8, width), jnp.float32),
             pltpu.VMEM((rows + 8, chans), jnp.float32),
             pltpu.VMEM((rows, chans), jnp.float32),
@@ -1484,6 +1591,8 @@
             pltpu.VMEM((64, chans), jnp.float32),
             *LineReduce.buffers(share, units),
             *LineReduce.semaphores,
+            *LineReduce.buffers(share, chans),
+            *LineReduce.semaphores,
             *PlaneReduce.buffers(rows, width),
             *PlaneReduce.semaphores,
         ],
@@ -1492,26 +1601,22 @@
         ),
         name="mixer_backward_linked",
     )(
-        d_res, xw, yw, ow, taps, vec, wr, we, keep, u, u, by, before, states, normed, mixed,
-        up_parts, layer_in, gain, d_residual,
+        d_res, xy, ow, taps, vec, wr, we, keep, u, u, by, before, states, normed,
+        up_parts, out_parts, layer_in, gain, d_residual,
     )
 
 
 def close_body(
-    hidden_ref, down_ref, x_parts, y_parts, out_parts, residual_ref, gains_ref, small,
-    layer_out, x_out, y_out, out_out, gains_out, small_out,
+    hidden_ref, down_ref, xy_parts, residual_ref, gains_ref, small,
+    layer_out, xy_out, gains_out, small_out,
     gathered, line_gains, both_gains, plane_gains,
     gain_sent, gain_arrived, wide_sent, wide_arrived, *links,
 ):
     r, h = lax.axis_index("row"), lax.axis_index("head")
     step = pl.program_id(0)
-    reduces = [
-        LineReduce(parts, *links[5 * k : 5 * k + 5])
-        for k, parts in enumerate((out_parts, x_parts, y_parts))
-    ]
-    outs = (out_out, x_out, y_out)
-    line = LineGather(small, gathered, *links[15:18])
-    plane = PlaneReduce(*links[18:26])
+    xy_line = LineReduce(xy_parts, *links[0:5])
+    line = LineGather(small, gathered, *links[5:8])
+    plane = PlaneReduce(*links[8:18])
 
     def to_row(t, owner):
         return send_to(
@@ -1531,12 +1636,15 @@
         for place in range(1, LINE):
             to_row(lax.rem(r + place, LINE), r).start()
         line.start()
-        for item in reduces:
-            item.start()
+        xy_line.start()
 
     @pl.when(step > 0)
     def _():
         plane.pass_on(step - 1)
+
+    @pl.when(step > 2)
+    def _():
+        plane.relay(step - 3)
 
     plane.put(step, contract_last(hidden_ref[...], down_ref[...]).astype(jnp.bfloat16))
 
@@ -1553,9 +1661,12 @@
 
     @pl.when(step == PLANE - 1)
     def _():
+        plane.relay(step - 2)
         plane.pass_on(step)
-        reduces[0].forward()
+        plane.relay(step - 1)
+        plane.relay(step)
         line.forward()
+        xy_line.forward()
         total = both_gains[...]
         for place in range(1, PLANE):
             owner = lax.rem(h + place, PLANE)
@@ -1563,7 +1674,6 @@
             total = total + plane_gains[owner]
         mine = lax.broadcasted_iota(jnp.int32, total.shape, 0) == h
         gains_out[...] = jnp.sum(jnp.where(mine, total, 0.0), axis=0, keepdims=True)
-        reduces[1].forward()
         plane.arrive()
 
         def make(i, unused):
@@ -1572,18 +1682,16 @@
             return unused
 
         lax.fori_loop(0, residual_ref.shape[0] // CHUNK, make, 0)
-        reduces[2].forward()
         line.finish()
         total = gathered[0].astype(jnp.float32)
         for t in range(1, LINE):
             total = total + gathered[t].astype(jnp.float32)
         small_out[...] = total
-        for item, out in zip(reduces, outs):
-
-            def write(at, value, out=out):
-                out[at, :] = value
-
-            item.finish(write)
+
+        def write(at, value):
+            xy_out[at, :] = value
+
+        xy_line.finish(write)
         plane.finish()
         for place in range(1, LINE):
             to_row(lax.rem(r + place, LINE), r).wait_send()
@@ -1591,27 +1699,23 @@
             over_plane(place, h).wait_send()
 
 
-def close_block(hidden, down, x_parts, y_parts, out_parts, residual, gains, small):
+def close_block(hidden, down, xy_parts, residual, gains, small):
     length, units = hidden.shape
     rows, width = residual.shape
-    share, chans = x_parts.shape[1:]
+    share, columns = xy_parts.shape[1:]
     return pl.pallas_call(
         close_body,
         grid=(PLANE,),
         in_specs=[
             pl.BlockSpec((rows, units), lambda i: (i, 0)), once(down.shape),
-            once(x_parts.shape), once(y_parts.shape), once(out_parts.shape),
-            once(residual.shape), once(gains.shape), once(small.shape),
+            once(xy_parts.shape), once(residual.shape), once(gains.shape), once(small.shape),
         ],
         out_specs=[
-            once((rows, width)), once((share, chans)), once((share, chans)),
-            once((share, chans)), once((1, gains.shape[2])), once(small.shape),
+            once((rows, width)), once((share, columns)), once((1, gains.shape[2])), once(small.shape),
         ],
         out_shape=[
             jax.ShapeDtypeStruct((rows, width), jnp.bfloat16),
-            jax.ShapeDtypeStruct((share, chans), jnp.float32),
-            jax.ShapeDtypeStruct((share, chans), jnp.float32),
-            jax.ShapeDtypeStruct((share, chans), jnp.float32),
+            jax.ShapeDtypeStruct((share, columns), jnp.float32),
             jax.ShapeDtypeStruct((1, gains.shape[2]), jnp.float32),
             jax.ShapeDtypeStruct(small.shape, jnp.float32),
         ],
@@ -1624,9 +1728,7 @@
             pltpu.SemaphoreType.DMA((LINE,)),
             pltpu.SemaphoreType.DMA((PLANE,)),
             pltpu.SemaphoreType.DMA((PLANE,)),
-            *LineReduce.buffers(share, chans), *LineReduce.semaphores,
-            *LineReduce.buffers(share, chans), *LineReduce.semaphores,
-            *LineReduce.buffers(share, chans), *LineReduce.semaphores,
+            *LineReduce.buffers(share, columns), *LineReduce.semaphores,
             *LineGather.semaphores,
             *PlaneReduce.buffers(rows, width), *PlaneReduce.semaphores,
         ],
@@ -1634,7 +1736,7 @@
             collective_id=7, has_side_effects=True, vmem_limit_bytes=56 * 2**20
         ),
         name="close_block",
-    )(hidden, down, x_parts, y_parts, out_parts, residual, gains, small)
+    )(hidden, down, xy_parts, residual, gains, small)
 
 
 def mixer_params(
@@ -1686,8 +1788,8 @@
     widen = lambda values: jnp.pad(values, ((0, 0), (0, chans - used)))
     mix_full = gather(mix_gain, ("row", "head"), 0)
     ffn_full = gather(ffn_gain, ("row", "head"), 0)
-    x_rows = gather(widen(x_weight), "row", 0)
-    y_rows = gather(widen(y_weight), "row", 0)
+    xy_shard = jnp.concatenate([widen(x_weight), widen(y_weight)], axis=1)
+    xy_rows = gather(xy_shard, "row", 0)
     out_rows = gather(widen(out_weight), "row", 0)
     gate_rows = gather(gate_weight, "row", 0)
     up_rows = gather(up_weight, "row", 0)
@@ -1702,7 +1804,7 @@
     normed_f, norm_back_one = jax.vjp(norm_apply, inputs, mix_full.astype(jnp.float32))
     normed_group = gather(normed_f.astype(jnp.bfloat16), "head", 0)
     u, by, before, states, mixed, part = mixer_forward(
-        normed_group, x_rows, y_rows, out_rows, taps, vec, wr, we, keep, ROWS
+        normed_group, xy_rows, out_rows, taps, vec, wr, we, keep, ROWS
     )
     residual = inputs + scatter(part, "head", 0).astype(jnp.float32)
     normed_two_f, norm_back_two = jax.vjp(norm_apply, residual, ffn_full.astype(jnp.float32))
@@ -1727,12 +1829,11 @@
     d_resid_norm, d_ffn_gain = norm_back_two(d_two)
     d_residual = cotangent.astype(jnp.float32) + d_resid_norm
     d_res_group = gather(d_residual.astype(jnp.bfloat16), "head", 0)
-    d_bx, d_by, d_part, d_taps, d_vec, d_wr, d_we = mixer_backward(
-        d_res_group, x_rows, y_rows, out_rows, taps, vec, wr, we, keep, u, by, before, states, ROWS
+    d_xy, d_part, d_taps, d_vec, d_wr, d_we = mixer_backward(
+        d_res_group, xy_rows, out_rows, taps, vec, wr, we, keep, u, by, before, states, ROWS
     )
     out_grad = scatter(contract_first(d_res_group, mixed).astype(jnp.bfloat16), "row", 0)
-    x_grad = scatter(contract_first(normed_group, d_bx).astype(jnp.bfloat16), "row", 0)
-    y_grad = scatter(contract_first(normed_group, d_by).astype(jnp.bfloat16), "row", 0)
+    xy_grad = scatter(contract_first(normed_group, d_xy).astype(jnp.bfloat16), "row", 0)
     d_normed = scatter(d_part, "head", 0).astype(jnp.float32)
     d_inputs, d_mix_gain = norm_back_one(d_normed)
     layer_in_grad = (d_inputs + d_residual).astype(jnp.bfloat16)
@@ -1755,8 +1856,8 @@
         layer_in_grad,
         mix_part,
         ffn_part_grad,
-        wide(x_grad),
-        wide(y_grad),
+        wide(xy_grad),
+        wide(xy_grad[:, chans:]),
         wide(out_grad),
         *small,
         gate_grad.astype(jnp.float32),
@@ -1796,31 +1897,34 @@
     own_gains = jnp.concatenate([mix_gain, ffn_gain]).astype(jnp.float32)
     tile = jnp.broadcast_to(own_gains, (8, own_gains.shape[0]))
 
-    normed_group, x_rows, y_rows, out_rows, gains = open_block(
-        layer_in, tile, (widen(x_weight), widen(y_weight), widen(out_weight))
-    )
-    normed_group, x_rows, y_rows, out_rows = map(flat, (normed_group, x_rows, y_rows, out_rows))
+    normed_group, xy_rows, out_rows, gains = open_block(
+        layer_in,
+        tile,
+        (jnp.concatenate([widen(x_weight), widen(y_weight)], axis=1), widen(out_weight)),
+    )
+    normed_group, xy_rows, out_rows = map(flat, (normed_group, xy_rows, out_rows))
     u, by, before, states, mixed, residual, normed_two, gate_rows = forward_linked(
-        normed_group, x_rows, y_rows, out_rows, taps, vec, wr, we, keep, layer_in, gains[1:2],
-        gate_weight,
-    )
-    two_group, up_rows = spread(normed_two, up_weight, 2)
-    gate_rows, two_group, up_rows = map(flat, (gate_rows, two_group, up_rows))
-    gates, ups, hidden, cot_group, down_rows = ffn_up(
-        two_group, gate_rows, up_rows, cotangent, down_weight
-    )
-    cot_group, down_rows = map(flat, (cot_group, down_rows))
-
-    d_gates, d_ups, gate_parts, down_grad, d_residual, d_low, d_ffn_gain = ffn_back(
-        cot_group, hidden, two_group, gates, ups, gate_rows, up_rows, down_rows, residual,
+        normed_group, xy_rows, out_rows, taps, vec, wr, we, keep, layer_in, gains[1:2], gate_weight
+    )
+    gate_rows = flat(gate_rows)
+    two_group, cot_group, up_rows, down_rows, gates, ups, hidden, down_parts = ffn_up(
+        normed_two, gate_rows, cotangent, up_weight, down_weight
+    )
+    two_group, cot_group, up_rows, down_rows = map(
+        flat, (two_group, cot_group, up_rows, down_rows)
+    )
+    d_ups, gate_parts, down_grad, d_residual, d_low, d_ffn_gain = ffn_back(
+        cot_group, two_group, gates, ups, gate_rows, up_rows, down_rows, down_parts, residual,
         cotangent, gains[1:2],
     )
-    up_parts, gate_grad, d_res_group = turn(two_group, d_ups, gate_parts, d_low)
+    up_parts, out_parts, gate_grad, d_res_group = turn(
+        two_group, d_ups, gate_parts, d_low, mixed
+    )
     (
-        x_parts, y_parts, out_parts, up_grad, layer_in_grad, d_mix_gain, d_taps, d_vec, d_wr, d_we,
+        xy_parts, up_grad, out_grad, layer_in_grad, d_mix_gain, d_taps, d_vec, d_wr, d_we,
     ) = backward_linked(
-        flat(d_res_group), x_rows, y_rows, out_rows, taps, vec, wr, we, keep, u, by, before,
-        states, normed_group, mixed, up_parts, layer_in, gains[0:1], d_residual,
+        flat(d_res_group), xy_rows, out_rows, taps, vec, wr, we, keep, u, by, before, states,
+        normed_group, up_parts, out_parts, layer_in, gains[0:1], d_residual,
     )
 
     share = mix_gain.shape[0]
@@ -1837,8 +1941,8 @@
         axis=0,
     ).astype(jnp.bfloat16)
     packed = jnp.pad(packed, ((0, -packed.shape[0] % 16), (0, chans - used)))
-    layer_out, x_grad, y_grad, out_grad, gain_grads, sums = close_block(
-        hidden, down_rows, x_parts, y_parts, out_parts, residual, gain_terms, packed
+    layer_out, xy_grad, gain_grads, sums = close_block(
+        hidden, down_rows, xy_parts, residual, gain_terms, packed
     )
     gates_end = heads * head_width
     wide = lambda values: values[:, :used]
@@ -1847,8 +1951,8 @@
         layer_in_grad,
         gain_grads[0, :share],
         gain_grads[0, share:],
-        wide(x_grad),
-        wide(y_grad),
+        wide(xy_grad),
+        wide(xy_grad[:, chans:]),
         wide(out_grad),
         sums[gates_end : gates_end + 4, :used],
         sums[gates_end + 4, :used],

time: 820 us -> 692 us (0.84); the launches traced: 819 us -> 682 us
  Pallas kernels: 761 us -> 640 us
  local copies, waits for them, and re-layouts: 49.5 us -> 34.1 us
    pallas_call x4 -> x3, Pallas kernels: 351 us -> 295 us  [the longest x1 114 us: ffn_up(): pl.pallas_call(ffn_up_body, in_specs=[IN_VMEM, IN_VMEM, ANYWHERE, ANYWHER...]
    pallas_call x1, Pallas kernels: 104 us -> 78.2 us  [close_block(): pl.pallas_call(close_body, grid=(PLANE,), in_specs=[pl.BlockSpec((rows, u...]
    pallas_call x1, Pallas kernels: 137 us -> 116 us  [backward_linked(): pl.pallas_call(backward_linked_body, grid=(PLANE,), in_specs=[tile(width)...]
    unnamed x75 -> x57, local copies, waits for them, and re-layouts: 35 us -> 21.3 us
    pallas_call x1, Pallas kernels: 94.9 us -> 84.5 us  [forward_linked(): pl.pallas_call(forward_linked_body, grid=(PLANE,), in_specs=[tile(width),...]
    pallas_call x1, Pallas kernels: 74.5 us -> 65.6 us  [turn(): pl.pallas_call(turn_body, grid=(PLANE,), in_specs=[tile(width), tile(unit...]
where the time goes in v4:
time: 692 us; the launch traced here: 682 us
  Pallas kernels  640 us (92%)
  local copies, waits for them, and re-layouts  34.1 us (5%)
  other arithmetic  7.19 us (1%)
    pallas_call x1, Pallas kernels, backward_linked(): pl.pallas_call(backward_linked_body, grid=(PLANE,), in_specs=[tile(width)...  116 us
    pallas_call x1, Pallas kernels, ffn_up(): pl.pallas_call(ffn_up_body, in_specs=[IN_VMEM, IN_VMEM, ANYWHERE, ANYWHER...  114 us
    pallas_call x1, Pallas kernels, ffn_back(): pl.pallas_call(ffn_back_body, grid=(PLANE,), in_specs=[tile(width), tile(...  96.1 us
    pallas_call x1, Pallas kernels, open_block(): pl.pallas_call(open_body, in_specs=[IN_VMEM, IN_VMEM] + [ANYWHERE] * 2, o...  84.7 us
    pallas_call x1, Pallas kernels, forward_linked(): pl.pallas_call(forward_linked_body, grid=(PLANE,), in_specs=[tile(width),...  84.5 us
    pallas_call x1, Pallas kernels, close_block(): pl.pallas_call(close_body, grid=(PLANE,), in_specs=[pl.BlockSpec((rows, u...  78.2 us
    pallas_call x1, Pallas kernels, turn(): pl.pallas_call(turn_body, grid=(PLANE,), in_specs=[tile(width), tile(unit...  65.6 us
    unnamed x57, local copies, waits for them, and re-layouts  21.3 us

profile of v4, /device:TPU:0, one launch (start us, length us, event | category | flops | bytes accessed | tf_op | source)
XLA Modules:
  0.0 682.1 jit_solution(11942883271979341376)
XLA Ops:
  1.5 1.2 copy.71
  2.7 1.3 copy.70
  4.4 84.7 %open_block.1 = (bf16[8,256,2048]{2,1,0:T(8,128)(2,1)S(1)}, bf16[4,512,768]{2,1,0:T(8,128)(2,1)S(1)}, bf16[4,512,384]{2,1,0:T(8,128)(2,1)S(1)}, f32[2,2048]{1,0:T(2,128)S(1)}) custom-call(bf16[256,2048]{1,0:T(8,128)(2,1)S(1)} %copy-done.2, f32[8,128]{1,0:T(8,128)S(1)} %broadcast_in_dim.6.tile_ref, bf16[512,768]{1,0:T(8,128)(2,1)S(1)} %fusion.2.xy_shard, ...), custom_call_target="tpu_custom_call" | custom-call | tf_op jit(solution)/shard_map/open_block/pallas_call | solution.py:992
  89.1 3.3 copy-done
  92.4 1.8 copy-done.1
  94.2 1.1 copy-done.3
  99.4 1.3 copy.77.keep_ref
  101.3 84.5 %mixer_forward_linked.1 = (bf16[2048,384]{1,0:T(8,128)(2,1)}, f32[2048,384]{1,0:T(8,128)}, f32[2048,384]{1,0:T(8,128)}, bf16[2048,384]{1,0:T(8,128)(2,1)}, bf16[...) custom-call(bf16[2048,2048]{1,0:T(8,128)(2,1)} %bitcast.37, ...), custom_call_target="tpu_custom_call" | custom-call | tf_op jit(solution)/shard_map/mixer_forward_linked/pallas_call | solution.py:1076
  185.8 114.3 %ffn_up.1 = (bf16[8,256,2048]{2,1,0:T(8,128)(2,1)}, bf16[8,256,2048]{2,1,0:T(8,128)(2,1)}, bf16[4,512,768]{2,1,0:T(8,128)(2,1)}, bf16[4,512,768]{2,1,0:T(8,128)(...) custom-call(bf16[256,2048]{1,0:T(8,128)(2,1)} %get-tuple-element.64., ...), custom_call_target="tpu_custom_call" | custom-call | tf_op jit(solution)/shard_map/ffn_up/pallas_call | solution.py:1206
  300.2 96.1 %ffn_back.1 = (bf16[2048,768]{1,0:T(8,128)(2,1)}, bf16[4,512,768]{2,1,0:T(8,128)(2,1)}, f32[512,768]{1,0:T(8,128)}, f32[256,2048]{1,0:T(8,128)}, bf16[256,2048]{1,0:T(8,128)(2,1)}, /*index=5*/f32[1,2048]{1,0:T(1,128)}) custom-call(bf16[2048,2048]{1,0:T(8,128)(2,1)} %bitcast.50, bf16[2048,2048]{1,0:T(8,128)(2,1)} %bitcast.43, ...), custom_call_target="tpu_custom_call" | custom-call | tf_op jit(solution)/shard_map/ffn_back/pallas_call | solution.py:1344
  396.3 65.6 %turn.1 = (bf16[4,512,768]{2,1,0:T(8,128)(2,1)}, bf16[4,512,384]{2,1,0:T(8,128)(2,1)}, f32[512,768]{1,0:T(8,128)}, bf16[8,256,2048]{2,1,0:T(8,128)(2,1)}) custom-call(bf16[2048,2048]{1,0:T(8,128)(2,1)} %bitcast.44, bf16[2048,768]{1,0:T(8,128)(2,1)} %get-tuple-element.75.d_ups_ref, bf16[4,512,768]{2,1,0:T(8,128)(2,1)} %get-tuple-element.76.gate_parts, ...), custom_call_target="tpu_custom_call" | custom-call | tf_op jit(solution)/shard_map/turn/pallas_call | solution.py:1435
  462.0 116.1 %mixer_backward_linked.1 = (bf16[4,512,768]{2,1,0:T(8,128)(2,1)}, f32[512,768]{1,0:T(8,128)}, f32[512,384]{1,0:T(8,128)}, bf16[256,2048]{1,0:T(8,128)(2,1)}, f32...) custom-call(bf16[2048,2048]{1,0:T(8,128)(2,1)} %bitcast.49, ...), custom_call_target="tpu_custom_call" | custom-call | tf_op jit(solution)/shard_map/mixer_backward_linked/pallas_call | solution.py:1552
  579.4 1.4 reduce.15
  581.5 1.1 convert.26
  582.7 1.1 convert.25
  587.2 78.2 %close_block.1 = (bf16[256,2048]{1,0:T(8,128)(2,1)}, f32[512,768]{1,0:T(8,128)}, f32[1,128]{1,0:T(1,128)}, f32[352,384]{1,0:T(8,128)}) custom-call(bf16[2048,768]{1,0:T(8,128)(2,1)} %get-tuple-element.66.hidden_ref, bf16[2048,768]{1,0:T(8,128)(2,1)} %bitcast.46, bf16[4,512,768]{2,1,0:T(8,128)(2,1)} %get-tuple-element.87.xy_parts, ...), custom_call_target="tpu_custom_call" | custom-call | tf_op jit(solution)/shard_map/close_block/pallas_call | solution.py:1706
  665.4 1.3 slice_bitcast_fusion
  666.7 1.5 fusion.19
  668.2 1.1 copy.81
  669.3 1.1 copy.82
  670.4 1.1 copy.83
  677.0 1.1 copy.105
  678.9 1.1 copy.106
  680.9 1.1 copy.107
  (96 shorter events, 18.2 us)
Async XLA Ops:
  0.7 3.4 copy-start.13
  2.7 1.8 copy-start.2
  4.1 91.2 %copy-start.17 = (f32[4,342]{1,0:T(4,128)S(1)}, f32[4,342]{1,0:T(4,128)}, u32[]{:S(2)}) copy-start(f32[4,342]{1,0:T(4,128)} %param.25) | copy-start | bytes 16420
  4.1 91.8 %copy-start.18 = (f32[342]{0:T(512)S(1)}, f32[342]{0:T(512)}, u32[]{:S(2)}) copy-start(f32[342]{0:T(512)} %param.26) | copy-start | bytes 4108
  4.1 91.8 %copy-start.19 = (f32[342]{0:T(512)S(1)}, f32[342]{0:T(512)}, u32[]{:S(2)}) copy-start(f32[342]{0:T(512)} %param.28) | copy-start | bytes 4108
  4.1 91.8 %copy-start.20 = (f32[342]{0:T(512)S(1)}, f32[342]{0:T(512)}, u32[]{:S(2)}) copy-start(f32[342]{0:T(512)} %param.30) | copy-start | bytes 4108
  4.1 91.9 %copy-start.16 = (f32[342]{0:T(512)S(1)}, f32[342]{0:T(512)}, u32[]{:S(2)}) copy-start(f32[342]{0:T(512)} %param.31) | copy-start | bytes 4108
  4.1 92.5 %copy-start.11 = (bf16[2,171,171]{2,0,1:T(2,128)(2,1)S(1)}, bf16[2,171,171]{2,0,1:T(2,128)(2,1)}, u32[]{:S(2)}) copy-start(bf16[2,171,171]{2,0,1:T(2,128)(2,1)} %param.27) | copy-start | bytes 350896
  4.4 93.4 %copy-start.12 = (bf16[2,171,171]{2,0,1:T(2,128)(2,1)S(1)}, bf16[2,171,171]{2,0,1:T(2,128)(2,1)}, u32[]{:S(2)}) copy-start(bf16[2,171,171]{2,0,1:T(2,128)(2,1)} %param.29) | copy-start | bytes 350896
  89.1 3.3 copy-start
  92.4 1.8 copy-start.1
  94.2 1.1 copy-start.3
  96.7 2.3 copy-start.14
  462.0 116.6 %copy-start.15 = (f32[1,2048]{1,0:T(1,128)S(1)}, f32[1,2048]{1,0:T(1,128)}, u32[]{:S(2)}) copy-start(f32[1,2048]{1,0:T(1,128)} %get-tuple-element.89) | copy-start | bytes 24580
  578.1 6.0 copy-start.21
  668.2 2.2 copy-start.10
  668.2 3.3 copy-start.9
  672.7 2.3 copy-start.8
  672.9 3.0 copy-start.7
  675.0 1.9 copy-start.5
  677.0 2.0 copy-start.6
  678.9 2.0 copy-start.4

commit v5 on v4

--- a/solution.py
+++ b/solution.py
@@ -1,3 +1,5 @@
+import functools
+
 import jax
 import jax.numpy as jnp
 from jax import lax
@@ -87,7 +89,7 @@
 
 
 def forward_step(
-    normed_ref, xy_ref, ow_ref, taps_ref, vec_ref, wr_ref, we_ref, keep_ref,
+    normed_ref, xy_ref, taps_ref, vec_ref, wr_ref, we_ref, keep_ref,
     u_ref, by_ref, before_ref, states_ref, mixed_ref,
     window, conv, conv_low, rate, entry, carry,
 ):
@@ -141,17 +143,17 @@
         return states[CHUNK - 1 : CHUNK, :]
 
     carry[0:1, :] = lax.fori_loop(0, rows // CHUNK, scan_step, carry[0:1, :], unroll=UNROLL)
-    return contract_last(mixed_ref[...], ow_ref[...]).astype(jnp.bfloat16)
 
 
 def forward_body(
     normed_ref, xy_ref, ow_ref, taps_ref, vec_ref, wr_ref, we_ref, keep_ref,
     u_ref, by_ref, before_ref, states_ref, mixed_ref, part_ref, *scratch,
 ):
-    part_ref[...] = forward_step(
-        normed_ref, xy_ref, ow_ref, taps_ref, vec_ref, wr_ref, we_ref, keep_ref,
+    forward_step(
+        normed_ref, xy_ref, taps_ref, vec_ref, wr_ref, we_ref, keep_ref,
         u_ref, by_ref, before_ref, states_ref, mixed_ref, *scratch,
     )
+    part_ref[...] = contract_last(mixed_ref[...], ow_ref[...]).astype(jnp.bfloat16)
 
 
 def backward_step(
@@ -482,34 +484,35 @@
         pltpu.SemaphoreType.DMA((2,)),
     )
 
-    def __init__(self, shard, full, sent, arrived, other):
+    def __init__(self, shard, full, sent, arrived, other, source=None, target=None):
         self.r = lax.axis_index("row")
-        self.shard, self.full, self.sent, self.arrived, self.other = (
-            shard, full, sent, arrived, other,
-        )
-
-    def near(self, t):
-        gap = self.r - t
-        return (gap != 0) & (gap < 3) & (gap > -3)
+        self.shard, self.full = shard, full
+        self.sent, self.arrived, self.other = sent, arrived, other
+        self.source = shard if source is None else shard.at[source]
+        self.target = target
+
+    def slot(self, origin):
+        return self.full.at[origin] if self.target is None else self.full.at[origin, self.target]
 
     def own(self, t):
         return send_to(
-            self.shard, self.full.at[self.r], self.sent.at[t], self.arrived.at[self.r], "row", t
+            self.source, self.slot(self.r), self.sent.at[t], self.arrived.at[self.r], "row", t
         )
 
     def handed(self, origin, target):
         return send_to(
-            self.full.at[origin], self.full.at[origin], self.other.at[0], self.arrived.at[origin],
+            self.slot(origin), self.slot(origin), self.other.at[0], self.arrived.at[origin],
             "row", target,
         )
 
     def local(self):
-        return pltpu.make_async_copy(self.shard, self.full.at[self.r], self.other.at[1])
+        return pltpu.make_async_copy(self.source, self.slot(self.r), self.other.at[1])
 
     def start(self):
-        for t in range(LINE):
-
-            @pl.when(self.near(t))
+        for gap in (2, -2, 1, -1):
+            t = self.r + gap
+
+            @pl.when((t >= 0) & (t < LINE))
             def _(t=t):
                 self.own(t).start()
 
@@ -528,12 +531,13 @@
         r = self.r
         for t in range(LINE):
             known = (r == t) | ((r == 2) & (t == 0)) | ((r == 1) & (t == 3))
+            near = (r != t) & (r - t < 3) & (t - r < 3)
 
             @pl.when(jnp.logical_not(known))
             def _(t=t):
                 self.handed(t, t).wait_recv()
 
-            @pl.when(self.near(t))
+            @pl.when(near)
             def _(t=t):
                 self.own(t).wait_send()
 
@@ -675,13 +679,14 @@
     semaphores = (
         pltpu.SemaphoreType.DMA((PIECES, 7)),
         pltpu.SemaphoreType.DMA((PIECES, 7)),
-        pltpu.SemaphoreType.DMA((1,)),
+        pltpu.SemaphoreType.DMA((PIECES,)),
     )
     first = tuple(range(PIECES // 2))
     second = tuple(range(PIECES // 2, PIECES))
 
-    def __init__(self, block, full, sent, arrived, other):
+    def __init__(self, block, full, sent, arrived, other, source=None, target=None):
         h = lax.axis_index("head")
+        self.source, self.target = source, target
         self.h, self.side, self.x, self.y = h, sibling_of(h), across_of(h), along_of(h)
         self.far = across_of(self.y)
         self.block, self.full = block, full
@@ -689,11 +694,18 @@
         self.rows = block.shape[0] // PIECES
 
     def piece(self, owner, c):
-        return self.full.at[owner, pl.ds(c * self.rows, self.rows)]
+        rows = pl.ds(c * self.rows, self.rows)
+        if self.target is None:
+            return self.full.at[owner, rows]
+        return self.full.at[owner, rows, self.target]
+
+    def mine(self, c):
+        rows = pl.ds(c * self.rows, self.rows)
+        return self.block.at[rows] if self.source is None else self.block.at[rows, self.source]
 
     def own(self, c, lane, target):
         return send_to(
-            self.block.at[pl.ds(c * self.rows, self.rows)], self.piece(self.h, c),
+            self.mine(c), self.piece(self.h, c),
             self.sent.at[c, lane], self.arrived.at[c, lane], "head", target,
         )
 
@@ -703,8 +715,8 @@
             self.arrived.at[c, lane], "head", target,
         )
 
-    def local(self):
-        return pltpu.make_async_copy(self.block, self.full.at[self.h], self.other.at[0])
+    def local(self, c):
+        return pltpu.make_async_copy(self.mine(c), self.piece(self.h, c), self.other.at[c])
 
     def start(self):
         for a, b in zip(self.first, self.second):
@@ -715,7 +727,7 @@
             self.own(a, 2, self.y).start()
         for c in range(PIECES):
             self.own(c, 0, self.side).start()
-        self.local().start()
+            self.local(c).start()
 
     def relay(self, place):
         a, b = self.first[place], self.second[place]
@@ -748,7 +760,7 @@
         for c in range(PIECES):
             for lane in range(7):
                 self.own(c, lane, side).wait_send()
-        self.local().wait()
+            self.local(c).wait()
 
 
 class PlaneReduce:
@@ -908,20 +920,27 @@
 def scatter(values, axis_name, axis):
     return lax.psum_scatter(values, axis_name, scatter_dimension=axis, tiled=True)
 
+def once(shape):
+    return pl.BlockSpec(
+        shape, lambda i: (0,) * len(shape), pipeline_mode=pl.Buffered(buffer_count=1)
+    )
+
+
 def norm_rows(rows, gain):
     return rows * lax.rsqrt(jnp.mean(rows * rows, axis=-1, keepdims=True) + EPSILON) * gain
 
 
 def open_body(
-    x_ref, tile_ref, xy_shard, out_shard, full, xy_full, out_full, gains_ref,
+    x_ref, tile_ref, cot, xy_shard, out_shard, full, cot_out, xy_full, out_full, gains_ref,
     normed, column, spread, gain_sent, gain_arrived, wide_sent, wide_arrived, *semaphores,
 ):
     r, h = lax.axis_index("row"), lax.axis_index("head")
-    lines = [
-        LineGather(src, dst, *semaphores[3 * k : 3 * k + 3])
-        for k, (src, dst) in enumerate(((xy_shard, xy_full), (out_shard, out_full)))
-    ]
+    xy_line = LineGather(xy_shard, xy_full, *semaphores[0:3])
+    out_line = LineGather(out_shard, out_full, *semaphores[3:6])
     plane = PlaneGather(normed, full, *semaphores[6:9])
+    cot_plane = PlaneGather(
+        cot, cot_out, *semaphores[9:12], source=pl.ds(0, cot_out.shape[2])
+    )
     meet(True, "all")
 
     def up_line(t):
@@ -943,12 +962,13 @@
     column[r] = tile_ref[...]
     for step in range(1, LINE):
         up_line(lax.rem(r + step, LINE)).start()
-    for line in lines:
-        line.start()
+    xy_line.start()
+    out_line.start()
     for step in range(1, LINE):
         from_line(lax.rem(r + step, LINE)).wait_recv()
     for step in range(1, PLANE):
         over_plane(step, h).start()
+    cot_plane.start()
     spread[h] = column[...]
     for step in range(1, PLANE):
         over_plane(step, lax.rem(h + step, PLANE)).wait_recv()
@@ -972,30 +992,37 @@
 
     lax.fori_loop(0, x_ref.shape[0] // CHUNK, make, 0)
     plane.start()
+    cot_plane.relay(0)
+    cot_plane.relay(1)
+    cot_plane.rest()
     plane.relay(0)
-    lines[0].forward()
+    xy_line.forward()
     plane.relay(1)
+    cot_plane.end()
     plane.rest()
     plane.end()
-    for line in lines[1:]:
-        line.forward()
-    for line in lines:
-        line.finish()
+    out_line.forward()
+    xy_line.finish()
+    out_line.finish()
     for step in range(1, LINE):
         up_line(lax.rem(r + step, LINE)).wait_send()
     for step in range(1, PLANE):
         over_plane(step, h).wait_send()
 
 
-def open_block(layer_in, tile, weights):
+def open_block(layer_in, tile, cot, xy_shard, out_shard):
     rows, width = layer_in.shape
     return pl.pallas_call(
         open_body,
-        in_specs=[IN_VMEM, IN_VMEM] + [ANYWHERE] * 2,
-        out_specs=[ANYWHERE] * 3 + [IN_VMEM],
-        out_shape=[jax.ShapeDtypeStruct((PLANE, rows, width), jnp.bfloat16)]
-        + [jax.ShapeDtypeStruct((LINE,) + item.shape, item.dtype) for item in weights]
-        + [jax.ShapeDtypeStruct((2, width), jnp.float32)],
+        in_specs=[IN_VMEM, IN_VMEM, ANYWHERE, ANYWHERE, ANYWHERE],
+        out_specs=[ANYWHERE] * 4 + [IN_VMEM],
+        out_shape=[
+            jax.ShapeDtypeStruct((PLANE, rows, width), jnp.bfloat16),
+            jax.ShapeDtypeStruct((PLANE, rows, width // 2), jnp.bfloat16),
+            jax.ShapeDtypeStruct((LINE,) + xy_shard.shape, jnp.bfloat16),
+            jax.ShapeDtypeStruct((LINE,) + out_shard.shape, jnp.bfloat16),
+            jax.ShapeDtypeStruct((2, width), jnp.float32),
+        ],
         scratch_shapes=[
             pltpu.VMEM((rows, width), jnp.bfloat16),
             pltpu.VMEM((LINE,) + tile.shape, jnp.float32),
@@ -1005,29 +1032,31 @@
             pltpu.SemaphoreType.DMA((PLANE,)),
             pltpu.SemaphoreType.DMA((PLANE,)),
             *(LineGather.semaphores * 2),
-            *PlaneGather.semaphores,
+            *(PlaneGather.semaphores * 2),
         ],
         compiler_params=pltpu.CompilerParams(
-            collective_id=0, has_side_effects=True, vmem_limit_bytes=24 * 2**20
+            collective_id=0, has_side_effects=True, vmem_limit_bytes=61 * 2**20
         ),
         name="open_block",
-    )(layer_in, tile, *weights)
+    )(layer_in, tile, cot, xy_shard, out_shard)
 
 
 def forward_linked_body(
     normed_ref, xy_ref, ow_ref, taps_ref, vec_ref, wr_ref, we_ref, keep_ref,
-    x_ref, gain_ref, shard,
-    u_ref, by_ref, before_ref, states_ref, mixed_ref, residual_ref, two_ref, gathered,
+    x_ref, gain_ref, gate_shard, up_shard,
+    u_ref, by_ref, before_ref, states_ref, mixed_ref, residual_ref, two_ref, gate_out, up_out,
     window, conv, conv_low, rate, entry, carry, *links,
 ):
     step = pl.program_id(0)
     plane = PlaneReduce(*links[:10])
-    line = LineGather(shard, gathered, *links[10:13])
+    gate_line = LineGather(gate_shard, gate_out, *links[10:13])
+    up_line = LineGather(up_shard, up_out, *links[13:16], source=pl.ds(0, up_out.shape[1]))
 
     @pl.when(step == 0)
     def _():
         meet(True, "near")
-        line.start()
+        gate_line.start()
+        up_line.start()
 
     @pl.when(step > 0)
     def _():
@@ -1037,16 +1066,16 @@
     def _():
         plane.relay(step - 3)
 
-    value = forward_step(
-        normed_ref, xy_ref, ow_ref, taps_ref, vec_ref, wr_ref, we_ref, keep_ref,
+    forward_step(
+        normed_ref, xy_ref, taps_ref, vec_ref, wr_ref, we_ref, keep_ref,
         u_ref, by_ref, before_ref, states_ref, mixed_ref,
         window, conv, conv_low, rate, entry, carry,
     )
-    plane.put(step, value)
+    plane.put(step, contract_last(mixed_ref[...], ow_ref[...]).astype(jnp.bfloat16))
 
     @pl.when(step == 6)
     def _():
-        line.forward()
+        gate_line.forward()
 
     @pl.when(step == PLANE - 1)
     def _():
@@ -1054,6 +1083,7 @@
         plane.pass_on(step)
         plane.relay(step - 1)
         plane.relay(step)
+        up_line.forward()
         plane.arrive()
 
         def make(i, unused):
@@ -1065,23 +1095,25 @@
 
         lax.fori_loop(0, x_ref.shape[0] // CHUNK, make, 0)
         plane.finish()
-        line.finish()
-
-
-def forward_linked(normed, xy, ow, taps, vec, wr, we, keep, layer_in, gain, shard):
+        gate_line.finish()
+        up_line.finish()
+
+
+def forward_linked(normed, xy, ow, taps, vec, wr, we, keep, layer_in, gain, gate_shard, up_shard):
     length, width = normed.shape
     chans = ow.shape[1]
     rows = length // PLANE
+    share, units = up_shard.shape
     tile = lambda columns: pl.BlockSpec((rows, columns), lambda i: (i, 0))
     return pl.pallas_call(
         forward_linked_body,
         grid=(PLANE,),
         in_specs=[
-            tile(width), whole(xy.shape), whole(ow.shape), whole(taps.shape),
-            whole(vec.shape), whole(wr.shape), whole(we.shape), tile(keep.shape[1]),
-            whole(layer_in.shape), whole(gain.shape), ANYWHERE,
-        ],
-        out_specs=[tile(chans)] * 5 + [whole((rows, width))] * 2 + [ANYWHERE],
+            tile(width), once(xy.shape), once(ow.shape), once(taps.shape),
+            once(vec.shape), once(wr.shape), once(we.shape), tile(keep.shape[1]),
+            once(layer_in.shape), once(gain.shape), ANYWHERE, ANYWHERE,
+        ],
+        out_specs=[tile(chans)] * 5 + [once((rows, width))] * 2 + [ANYWHERE] * 2,
         out_shape=[
             jax.ShapeDtypeStruct((length, chans), jnp.bfloat16),
             jax.ShapeDtypeStruct((length, chans), jnp.float32),
@@ -1090,7 +1122,8 @@
             jax.ShapeDtypeStruct((length, chans), jnp.bfloat16),
             jax.ShapeDtypeStruct((rows, width), jnp.float32),
             jax.ShapeDtypeStruct((rows, width), jnp.bfloat16),
-            jax.ShapeDtypeStruct((LINE,) + shard.shape, shard.dtype),
+            jax.ShapeDtypeStruct((LINE,) + gate_shard.shape, jnp.bfloat16),
+            jax.ShapeDtypeStruct((LINE, share // 2, units), jnp.bfloat16),
         ],
         scratch_shapes=[
             pltpu.VMEM((rows + 8, chans), jnp.float32),
@@ -1101,27 +1134,35 @@
             pltpu.VMEM((8, chans), jnp.float32),
             *PlaneReduce.buffers(rows, width),
             *PlaneReduce.semaphores,
-            *LineGather.semaphores,
+            *(LineGather.semaphores * 2),
         ],
         compiler_params=pltpu.CompilerParams(
-            collective_id=1, has_side_effects=True, vmem_limit_bytes=56 * 2**20
+            collective_id=1, has_side_effects=True, vmem_limit_bytes=61 * 2**20
         ),
         name="mixer_forward_linked",
-    )(normed, xy, ow, taps, vec, wr, we, keep, layer_in, gain, shard)
+    )(normed, xy, ow, taps, vec, wr, we, keep, layer_in, gain, gate_shard, up_shard)
 
 
 def ffn_up_body(
-    own_two, gate_ref, own_cot, up_shard, down_shard,
+    own_two, gate_ref, own_cot, cot_half, up_half, up_shard, down_shard,
     two_out, cot_out, up_out, down_out, gates_out, ups_out, hidden_out, down_parts,
-    two, cot, up, gates, ups, hidden, total, copied, *semaphores,
+    two, cot, up, gates, ups, hidden, total, copied, brought, *semaphores,
 ):
     h = lax.axis_index("head")
     rows = own_two.shape[0]
     units = gates.shape[1]
-    up_line = LineGather(up_shard, up, *semaphores[0:3])
+    width, share = own_two.shape[1], up.shape[1]
+    late_rows, late_columns = pl.ds(share // 2, share // 2), pl.ds(width // 2, width // 2)
+    up_line = LineGather(up_shard, up, *semaphores[0:3], source=late_rows, target=late_rows)
     down_line = LineGather(down_shard, down_out, *semaphores[3:6])
     two_plane = PlaneGather(own_two, two, *semaphores[6:9])
-    cot_plane = PlaneGather(own_cot, cot, *semaphores[9:12])
+    cot_plane = PlaneGather(
+        own_cot, cot, *semaphores[9:12], source=late_columns, target=late_columns
+    )
+    inward = [
+        pltpu.make_async_copy(up_half, up.at[:, pl.ds(0, share // 2)], brought.at[0]),
+        pltpu.make_async_copy(cot_half, cot.at[:, :, pl.ds(0, width // 2)], brought.at[1]),
+    ]
     outward = [
         pltpu.make_async_copy(src, dst, copied.at[k])
         for k, (src, dst) in enumerate(
@@ -1135,6 +1176,8 @@
     up_line.start()
     down_line.start()
     two_plane.start()
+    for copy in inward:
+        copy.start()
 
     def at_block(block):
         return pl.ds(pl.multiple_of(block * rows, rows), rows)
@@ -1160,12 +1203,13 @@
     outward[3].start()
     cot_plane.rest()
     up_line.finish()
+    for copy in inward:
+        copy.wait()
     outward[2].start()
 
     def make_hidden(block, unused):
         at = at_block(block)
         value = jnp.zeros((rows, units), jnp.float32)
-        share = up.shape[1]
         for t in range(LINE):
             value = value + dot_plain(two[block, :, t * share : (t + 1) * share], up[t])
         ups[at, :] = value
@@ -1197,7 +1241,7 @@
         copy.wait()
 
 
-def ffn_up(own_two, gate, own_cot, up_shard, down_shard):
+def ffn_up(own_two, gate, own_cot, cot_half, up_half, up_shard, down_shard):
     rows, width = own_two.shape
     share, units = up_shard.shape
     length = rows * PLANE
@@ -1205,7 +1249,7 @@
     weight = jax.ShapeDtypeStruct((LINE, share, units), jnp.bfloat16)
     return pl.pallas_call(
         ffn_up_body,
-        in_specs=[IN_VMEM, IN_VMEM, ANYWHERE, ANYWHERE, ANYWHERE],
+        in_specs=[IN_VMEM, IN_VMEM] + [ANYWHERE] * 5,
         out_specs=[ANYWHERE] * 7 + [IN_VMEM],
         out_shape=[
             group,
@@ -1226,18 +1270,21 @@
             pltpu.VMEM((length, units), jnp.bfloat16),
             pltpu.VMEM((width, units), jnp.float32),
             pltpu.SemaphoreType.DMA((6,)),
+            pltpu.SemaphoreType.DMA((2,)),
             *(LineGather.semaphores * 2),
             *(PlaneGather.semaphores * 2),
         ],
         compiler_params=pltpu.CompilerParams(
-            collective_id=2, has_side_effects=True, vmem_limit_bytes=60 * 2**20
+            collective_id=2, has_side_effects=True, vmem_limit_bytes=61 * 2**20
         ),
         name="ffn_up",
-    )(own_two, gate, own_cot, up_shard, down_shard)
-def once(shape):
-    return pl.BlockSpec(
-        shape, lambda i: (0,) * len(shape), pipeline_mode=pl.Buffered(buffer_count=1)
-    )
+    )(own_two, gate, own_cot, cot_half, up_half, up_shard, down_shard)
+def far_first(step):
+    chip = lax.div(lax.axis_index("head"), 2)
+    place = lax.div(step, 2)
+    x = lax.rem(lax.rem(chip, 2) + 1 - lax.div(place, 2), 2)
+    y = lax.rem(lax.div(chip, 2) + 1 + lax.rem(place, 2), 2)
+    return 2 * (2 * y + x) + lax.rem(step, 2)
 
 
 def norm_back(rows, gain, incoming):
@@ -1280,11 +1327,11 @@
 
     @pl.when(step > 0)
     def _():
-        plane.pass_on(step - 1)
+        plane.pass_on(far_first(step - 1))
 
     @pl.when(step > 2)
     def _():
-        plane.relay(step - 3)
+        plane.relay(far_first(step - 3))
 
     d_hidden[...] = dot_plain(cot_ref[...], down_ref[...])
 
@@ -1298,7 +1345,7 @@
 
     lax.fori_loop(0, rows // CHUNK, make, 0, unroll=UNROLL)
     value = contract_last(d_gates[...], gate_ref[...]) + contract_last(d_ups_ref[...], up_ref[...])
-    plane.put(step, value.astype(jnp.bfloat16))
+    plane.put(far_first(step), value.astype(jnp.bfloat16))
     total[...] += contract_first(two_ref[...], d_gates[...])
 
     @pl.when(step == 4)
@@ -1307,11 +1354,11 @@
 
     @pl.when(step == PLANE - 1)
     def _():
-        plane.relay(step - 2)
-        plane.pass_on(step)
-        plane.relay(step - 1)
+        plane.relay(far_first(step - 2))
+        plane.pass_on(far_first(step))
+        plane.relay(far_first(step - 1))
         to_parts(total, gate_parts)
-        plane.relay(step)
+        plane.relay(far_first(step))
         plane.arrive()
         eight[...] = jnp.zeros_like(eight)
 
@@ -1340,7 +1387,7 @@
     length, width = cot_group.shape
     units = gate.shape[1]
     rows, share = length // PLANE, width // LINE
-    tile = lambda columns: pl.BlockSpec((rows, columns), lambda i: (i, 0))
+    tile = lambda columns: pl.BlockSpec((rows, columns), lambda i: (far_first(i), 0))
     return pl.pallas_call(
         ffn_back_body,
         grid=(PLANE,),
@@ -1372,7 +1419,7 @@
             *PlaneReduce.semaphores,
         ],
         compiler_params=pltpu.CompilerParams(
-            collective_id=4, has_side_effects=True, vmem_limit_bytes=60 * 2**20
+            collective_id=4, has_side_effects=True, vmem_limit_bytes=61 * 2**20
         ),
         name="ffn_back",
     )(cot_group, two_group, gates, ups, gate, up, down, parts, residual, own_cot, gain)
@@ -1401,13 +1448,13 @@
     @pl.when(step == PLANE - 3)
     def _():
         plane.relay(0)
+        line.forward()
 
     @pl.when(step == PLANE - 1)
     def _():
         plane.relay(1)
         to_parts(total, up_parts)
         plane.rest()
-        line.forward()
         plane.end()
         outward.start()
         out_total[...] = contract_first(full[0], mixed_ref[0:rows, :])
@@ -1457,25 +1504,68 @@
             *PlaneGather.semaphores,
         ],
         compiler_params=pltpu.CompilerParams(
-            collective_id=5, has_side_effects=True, vmem_limit_bytes=56 * 2**20
+            collective_id=5, has_side_effects=True, vmem_limit_bytes=61 * 2**20
         ),
         name="turn",
     )(two_group, d_ups, gate_parts, block, mixed)
 
 
+def pack_small(head_width, taps, vec, params, wr, we, small):
+    columns = small.shape[1]
+    step = 16
+    last = (2 * head_width + 7) // 8 * 8
+
+    def move(i, unused):
+        at = pl.ds(pl.multiple_of(i * step, step), step)
+        shape = (step, columns)
+        row = lax.broadcasted_iota(jnp.int32, shape, 0) + i * step
+        left = lax.broadcasted_iota(jnp.int32, shape, 1) < head_width
+        rate, entry = wr[at, :], we[at, :]
+        first = jnp.where(left, rate, pltpu.roll(entry, head_width, 1))
+        second = jnp.where(left, pltpu.roll(rate, columns - head_width, 1), entry)
+        small[at, :] = jnp.where(row < head_width, first, second).astype(jnp.bfloat16)
+        return unused
+
+    lax.fori_loop(0, last // step, move, 0)
+    scaled = vec[0:4, :] * jnp.concatenate(
+        [jnp.ones((3, columns), jnp.float32), params[4:5, :]], axis=0
+    )
+    tail = jnp.concatenate([taps[...], scaled], axis=0).astype(jnp.bfloat16)
+    here = last // step * step
+    rate, entry = wr[here : here + 8, :], we[here : here + 8, :]
+    left = lax.broadcasted_iota(jnp.int32, (8, columns), 1) < head_width
+    rest = jnp.where(left, pltpu.roll(rate, columns - head_width, 1), entry).astype(jnp.bfloat16)
+    small[here : here + 16, :] = jnp.concatenate([rest, tail], axis=0)
+
+
+def split_gains(mix, ffn, out):
+    share = out.shape[2] // 2
+    low = lax.broadcasted_iota(jnp.int32, (1, 2 * share), 1) < share
+    for r in range(LINE):
+        lines = []
+        for pair in range(PLANE // 2):
+            at = (r * (PLANE // 2) + pair) * 2 * share
+            one, two = mix[:, at : at + 2 * share], ffn[:, at : at + 2 * share]
+            lines.append(jnp.where(low, one, pltpu.roll(two, share, 1)))
+            lines.append(jnp.where(low, pltpu.roll(one, share, 1), two))
+        out[r] = jnp.concatenate(lines, axis=0)
+
+
 def backward_linked_body(
+    head_width,
     d_res_ref, xy_ref, ow_ref, taps_ref, vec_ref, wr_ref, we_ref, keep_ref,
     u_ref, u_prev_ref, by_ref, before_ref, states_ref, normed_ref, up_parts, out_parts,
-    x_ref, gain_ref, d_residual_ref,
-    xy_parts, up_out, out_out, in_grad, gain_out, taps_out, vec_out, wr_out, we_out,
-    d_xy, xy_total, eight, *rest,
+    x_ref, gain_ref, d_residual_ref, ffn_gain_ref,
+    xy_parts, up_out, out_out, in_grad, gains_out, small_out,
+    taps_sum, vec_sum, wr_sum, we_sum, small, gathered, d_xy, xy_total, eight, *rest,
 ):
     scratch, links = rest[:11], rest[11:]
     step = pl.program_id(0)
     block = PLANE - 1 - step
     line = LineReduce(up_parts, *links[:5])
     out_line = LineReduce(out_parts, *links[5:10])
-    plane = PlaneReduce(*links[10:])
+    small_line = LineGather(small, gathered, *links[10:13])
+    plane = PlaneReduce(*links[13:])
 
     @pl.when(step == 0)
     def _():
@@ -1495,7 +1585,7 @@
     value = backward_step(
         d_res_ref, xy_ref, ow_ref, taps_ref, vec_ref, wr_ref, we_ref, keep_ref,
         u_ref, u_prev_ref, by_ref, before_ref, states_ref, d_xy,
-        taps_out, vec_out, wr_out, we_out, *scratch,
+        taps_sum, vec_sum, wr_sum, we_sum, *scratch,
     )
     plane.put(block, value)
     xy_total[...] += contract_first(normed_ref[...], d_xy[...])
@@ -1508,10 +1598,13 @@
     def _():
         plane.relay(block + 2)
         plane.pass_on(block)
+        pack_small(head_width, taps_sum, vec_sum, vec_ref, wr_sum, we_sum, small)
+        small_line.start()
         plane.relay(block + 1)
         to_parts(xy_total, xy_parts)
         plane.relay(block)
         out_line.forward()
+        small_line.forward()
         plane.arrive()
         eight[...] = jnp.zeros_like(eight)
 
@@ -1525,7 +1618,7 @@
             return unused
 
         lax.fori_loop(0, x_ref.shape[0] // CHUNK, back, 0)
-        gain_out[...] = jnp.sum(eight[...], axis=0, keepdims=True)
+        split_gains(jnp.sum(eight[...], axis=0, keepdims=True), ffn_gain_ref[...], gains_out)
 
         def write(at, value):
             up_out[at, :] = value
@@ -1535,12 +1628,23 @@
 
         line.finish(write)
         out_line.finish(write_out)
+        small_line.finish()
+
+        def add_small(i, unused):
+            at = pl.ds(pl.multiple_of(i * CHUNK, CHUNK), CHUNK)
+            total = gathered[0, at, :].astype(jnp.float32)
+            for t in range(1, LINE):
+                total = total + gathered[t, at, :].astype(jnp.float32)
+            small_out[at, :] = total
+            return unused
+
+        lax.fori_loop(0, small.shape[0] // CHUNK, add_small, 0)
         plane.finish()
 
 
 def backward_linked(
     d_res, xy, ow, taps, vec, wr, we, keep, u, by, before, states, normed, up_parts, out_parts,
-    layer_in, gain, d_residual,
+    layer_in, gain, d_residual, ffn_gain, head_width,
 ):
     length, width = d_res.shape
     chans, units = ow.shape[1], up_parts.shape[2]
@@ -1549,32 +1653,36 @@
     ahead = pl.BlockSpec(
         (16, chans), lambda i: (jnp.maximum((PLANE - 1 - i) * (rows // 16) - 1, 0), 0)
     )
+    small = ((2 * head_width + 7) // 8 * 8 // 16 * 16 + 16, chans)
+    gain_terms = (LINE, PLANE, width // (LINE * PLANE) * 2)
     return pl.pallas_call(
-        backward_linked_body,
+        functools.partial(backward_linked_body, head_width),
         grid=(PLANE,),
         in_specs=[
             tile(width), once(xy.shape), once(ow.shape), once(taps.shape),
             once(vec.shape), once(wr.shape), once(we.shape), tile(keep.shape[1]),
             tile(chans), ahead, tile(chans), tile(chans), tile(chans), tile(width),
-            once(up_parts.shape), once(out_parts.shape), once(layer_in.shape), once(gain.shape), once(d_residual.shape),
+            once(up_parts.shape), once(out_parts.shape), once(layer_in.shape), once(gain.shape), once(d_residual.shape), once(ffn_gain.shape),
         ],
         out_specs=[
             once((LINE, share, 2 * chans)), once((share, units)), once((share, chans)),
-            once((rows, width)), once((1, width)), once(taps.shape), once(vec.shape),
-            once(wr.shape), once(we.shape),
+            once((rows, width)), once(gain_terms), once(small),
         ],
         out_shape=[
             jax.ShapeDtypeStruct((LINE, share, 2 * chans), jnp.bfloat16),
             jax.ShapeDtypeStruct((share, units), jnp.float32),
             jax.ShapeDtypeStruct((share, chans), jnp.float32),
             jax.ShapeDtypeStruct((rows, width), jnp.bfloat16),
-            jax.ShapeDtypeStruct((1, width), jnp.float32),
-            jax.ShapeDtypeStruct(taps.shape, jnp.float32),
-            jax.ShapeDtypeStruct(vec.shape, jnp.float32),
-            jax.ShapeDtypeStruct(wr.shape, jnp.float32),
-            jax.ShapeDtypeStruct(we.shape, jnp.float32),
+            jax.ShapeDtypeStruct(gain_terms, jnp.float32),
+            jax.ShapeDtypeStruct(small, jnp.float32),
         ],
         scratch_shapes=[
+            pltpu.VMEM(taps.shape, jnp.float32),
+            pltpu.VMEM(vec.shape, jnp.float32),
+            pltpu.VMEM(wr.shape, jnp.float32),
+            pltpu.VMEM(we.shape, jnp.float32),
+            pltpu.VMEM(small, jnp.bfloat16),
+            pltpu.VMEM((LINE,) + small, jnp.bfloat16),
             pltpu.VMEM((rows, 2 * chans), jnp.bfloat16),
             pltpu.VMEM((width, 2 * chans), jnp.float32),
             pltpu.VMEM((8, width), jnp.float32),
@@ -1593,30 +1701,30 @@
             *LineReduce.semaphores,
             *LineReduce.buffers(share, chans),
             *LineReduce.semaphores,
+            *LineGather.semaphores,
             *PlaneReduce.buffers(rows, width),
             *PlaneReduce.semaphores,
         ],
         compiler_params=pltpu.CompilerParams(
-            collective_id=6, has_side_effects=True, vmem_limit_bytes=62 * 2**20
+            collective_id=6, has_side_effects=True, vmem_limit_bytes=61 * 2**20
         ),
         name="mixer_backward_linked",
     )(
         d_res, xy, ow, taps, vec, wr, we, keep, u, u, by, before, states, normed,
-        up_parts, out_parts, layer_in, gain, d_residual,
+        up_parts, out_parts, layer_in, gain, d_residual, ffn_gain,
     )
 
 
 def close_body(
-    hidden_ref, down_ref, xy_parts, residual_ref, gains_ref, small,
-    layer_out, xy_out, gains_out, small_out,
-    gathered, line_gains, both_gains, plane_gains,
+    hidden_ref, down_ref, xy_parts, residual_ref, gains_ref,
+    layer_out, xy_out, gains_out,
+    line_gains, both_gains, plane_gains,
     gain_sent, gain_arrived, wide_sent, wide_arrived, *links,
 ):
     r, h = lax.axis_index("row"), lax.axis_index("head")
     step = pl.program_id(0)
     xy_line = LineReduce(xy_parts, *links[0:5])
-    line = LineGather(small, gathered, *links[5:8])
-    plane = PlaneReduce(*links[8:18])
+    plane = PlaneReduce(*links[5:])
 
     def to_row(t, owner):
         return send_to(
@@ -1635,18 +1743,17 @@
         meet(True, "all")
         for place in range(1, LINE):
             to_row(lax.rem(r + place, LINE), r).start()
-        line.start()
         xy_line.start()
 
     @pl.when(step > 0)
     def _():
-        plane.pass_on(step - 1)
+        plane.pass_on(far_first(step - 1))
 
     @pl.when(step > 2)
     def _():
-        plane.relay(step - 3)
-
-    plane.put(step, contract_last(hidden_ref[...], down_ref[...]).astype(jnp.bfloat16))
+        plane.relay(far_first(step - 3))
+
+    plane.put(far_first(step), contract_last(hidden_ref[...], down_ref[...]).astype(jnp.bfloat16))
 
     @pl.when(step == 2)
     def _():
@@ -1661,11 +1768,10 @@
 
     @pl.when(step == PLANE - 1)
     def _():
-        plane.relay(step - 2)
-        plane.pass_on(step)
-        plane.relay(step - 1)
-        plane.relay(step)
-        line.forward()
+        plane.relay(far_first(step - 2))
+        plane.pass_on(far_first(step))
+        plane.relay(far_first(step - 1))
+        plane.relay(far_first(step))
         xy_line.forward()
         total = both_gains[...]
         for place in range(1, PLANE):
@@ -1682,12 +1788,6 @@
             return unused
 
         lax.fori_loop(0, residual_ref.shape[0] // CHUNK, make, 0)
-        line.finish()
-        total = gathered[0].astype(jnp.float32)
-        for t in range(1, LINE):
-            total = total + gathered[t].astype(jnp.float32)
-        small_out[...] = total
-
         def write(at, value):
             xy_out[at, :] = value
 
@@ -1699,7 +1799,7 @@
             over_plane(place, h).wait_send()
 
 
-def close_block(hidden, down, xy_parts, residual, gains, small):
+def close_block(hidden, down, xy_parts, residual, gains):
     length, units = hidden.shape
     rows, width = residual.shape
     share, columns = xy_parts.shape[1:]
@@ -1707,20 +1807,18 @@
         close_body,
         grid=(PLANE,),
         in_specs=[
-            pl.BlockSpec((rows, units), lambda i: (i, 0)), once(down.shape),
-            once(xy_parts.shape), once(residual.shape), once(gains.shape), once(small.shape),
+            pl.BlockSpec((rows, units), lambda i: (far_first(i), 0)), once(down.shape),
+            once(xy_parts.shape), once(residual.shape), once(gains.shape),
         ],
         out_specs=[
-            once((rows, width)), once((share, columns)), once((1, gains.shape[2])), once(small.shape),
+            once((rows, width)), once((share, columns)), once((1, gains.shape[2])),
         ],
         out_shape=[
             jax.ShapeDtypeStruct((rows, width), jnp.bfloat16),
             jax.ShapeDtypeStruct((share, columns), jnp.float32),
             jax.ShapeDtypeStruct((1, gains.shape[2]), jnp.float32),
-            jax.ShapeDtypeStruct(small.shape, jnp.float32),
         ],
         scratch_shapes=[
-            pltpu.VMEM((LINE,) + small.shape, jnp.bfloat16),
             pltpu.VMEM(gains.shape, jnp.float32),
             pltpu.VMEM(gains.shape[1:], jnp.float32),
             pltpu.VMEM((PLANE,) + gains.shape[1:], jnp.float32),
@@ -1729,14 +1827,13 @@
             pltpu.SemaphoreType.DMA((PLANE,)),
             pltpu.SemaphoreType.DMA((PLANE,)),
             *LineReduce.buffers(share, columns), *LineReduce.semaphores,
-            *LineGather.semaphores,
             *PlaneReduce.buffers(rows, width), *PlaneReduce.semaphores,
         ],
         compiler_params=pltpu.CompilerParams(
-            collective_id=7, has_side_effects=True, vmem_limit_bytes=56 * 2**20
+            collective_id=7, has_side_effects=True, vmem_limit_bytes=61 * 2**20
         ),
         name="close_block",
-    )(hidden, down, xy_parts, residual, gains, small)
+    )(hidden, down, xy_parts, residual, gains)
 
 
 def mixer_params(
@@ -1752,7 +1849,7 @@
             jnp.pad(rate_bias, spare),
             jnp.pad(entry_bias, spare),
             -8.0 * jax.nn.softplus(-decay_wide),
-            blank,
+            8.0 * jax.nn.sigmoid(-decay_wide),
             blank,
             blank,
             blank,
@@ -1897,18 +1994,21 @@
     own_gains = jnp.concatenate([mix_gain, ffn_gain]).astype(jnp.float32)
     tile = jnp.broadcast_to(own_gains, (8, own_gains.shape[0]))
 
-    normed_group, xy_rows, out_rows, gains = open_block(
+    normed_group, cot_half, xy_rows, out_rows, gains = open_block(
         layer_in,
         tile,
-        (jnp.concatenate([widen(x_weight), widen(y_weight)], axis=1), widen(out_weight)),
+        cotangent,
+        jnp.concatenate([widen(x_weight), widen(y_weight)], axis=1),
+        widen(out_weight),
     )
     normed_group, xy_rows, out_rows = map(flat, (normed_group, xy_rows, out_rows))
-    u, by, before, states, mixed, residual, normed_two, gate_rows = forward_linked(
-        normed_group, xy_rows, out_rows, taps, vec, wr, we, keep, layer_in, gains[1:2], gate_weight
+    u, by, before, states, mixed, residual, normed_two, gate_rows, up_half = forward_linked(
+        normed_group, xy_rows, out_rows, taps, vec, wr, we, keep, layer_in, gains[1:2],
+        gate_weight, up_weight,
     )
     gate_rows = flat(gate_rows)
     two_group, cot_group, up_rows, down_rows, gates, ups, hidden, down_parts = ffn_up(
-        normed_two, gate_rows, cotangent, up_weight, down_weight
+        normed_two, gate_rows, cotangent, cot_half, up_half, up_weight, down_weight
     )
     two_group, cot_group, up_rows, down_rows = map(
         flat, (two_group, cot_group, up_rows, down_rows)
@@ -1920,30 +2020,16 @@
     up_parts, out_parts, gate_grad, d_res_group = turn(
         two_group, d_ups, gate_parts, d_low, mixed
     )
-    (
-        xy_parts, up_grad, out_grad, layer_in_grad, d_mix_gain, d_taps, d_vec, d_wr, d_we,
-    ) = backward_linked(
+    xy_parts, up_grad, out_grad, layer_in_grad, gain_terms, sums = backward_linked(
         flat(d_res_group), xy_rows, out_rows, taps, vec, wr, we, keep, u, by, before, states,
-        normed_group, up_parts, out_parts, layer_in, gains[0:1], d_residual,
-    )
-
+        normed_group, up_parts, out_parts, layer_in, gains[0:1], d_residual, d_ffn_gain,
+        head_width,
+    )
+    layer_out, xy_grad, gain_grads = close_block(
+        hidden, down_rows, xy_parts, residual, gain_terms
+    )
     share = mix_gain.shape[0]
-    split = lambda values: values.reshape(LINE, PLANE, share)
-    gain_terms = jnp.concatenate([split(d_mix_gain), split(d_ffn_gain)], axis=2)
-    blocks = [slice(h * head_width, (h + 1) * head_width) for h in range(heads)]
-    packed = jnp.concatenate(
-        [jnp.concatenate([d_wr[at, at], d_we[at, at]], axis=1) for at in blocks]
-        + [
-            d_taps[:, :used],
-            d_vec[0:3, :used],
-            d_vec[3:4, :used] * (8.0 * jax.nn.sigmoid(-decay_param)),
-        ],
-        axis=0,
-    ).astype(jnp.bfloat16)
-    packed = jnp.pad(packed, ((0, -packed.shape[0] % 16), (0, chans - used)))
-    layer_out, xy_grad, gain_grads, sums = close_block(
-        hidden, down_rows, xy_parts, residual, gain_terms, packed
-    )
+    ends = -(-used // 8) * 8
     gates_end = heads * head_width
     wide = lambda values: values[:, :used]
     return (
@@ -1954,13 +2040,13 @@
         wide(xy_grad),
         wide(xy_grad[:, chans:]),
         wide(out_grad),
-        sums[gates_end : gates_end + 4, :used],
-        sums[gates_end + 4, :used],
+        sums[ends : ends + 4, :used],
+        sums[ends + 4, :used],
         sums[:gates_end, :head_width].reshape(heads, head_width, head_width),
-        sums[gates_end + 5, :used],
+        sums[ends + 5, :used],
         sums[:gates_end, head_width : 2 * head_width].reshape(heads, head_width, head_width),
-        sums[gates_end + 6, :used],
-        sums[gates_end + 7, :used],
+        sums[ends + 6, :used],
+        sums[ends + 7, :used],
         gate_grad,
         up_grad,
         down_grad,

time: 692 us -> 640 us (0.925)
  Pallas kernels: 640 us -> 598 us
    pallas_call x1, Pallas kernels: 96.1 us -> 74.3 us  [ffn_back(): pl.pallas_call(ffn_back_body, grid=(PLANE,), in_specs=[tile(width), tile(...]
    pallas_call x1, Pallas kernels: 78.2 us -> 67.3 us  [close_block(): pl.pallas_call(close_body, grid=(PLANE,), in_specs=[pl.BlockSpec((rows, u...]
    pallas_call x3, Pallas kernels: 315 us -> 305 us  [the longest x1 111 us: backward_linked(): pl.pallas_call(functools.partial(backward_linked_body, head_width), grid=...]
    unnamed x57 -> x37, local copies, waits for them, and re-layouts: 21.3 us -> 13 us
where the time goes in v5:
time: 640 us; the launch traced here: 631 us
  Pallas kernels  598 us (93%)
  local copies, waits for them, and re-layouts  27.4 us (4%)
    pallas_call x1, Pallas kernels, backward_linked(): pl.pallas_call(functools.partial(backward_linked_body, head_width), grid=...  111 us
    pallas_call x1, Pallas kernels, ffn_up(): pl.pallas_call(ffn_up_body, in_specs=[IN_VMEM, IN_VMEM] + [ANYWHERE] * 5,...  106 us
    pallas_call x1, Pallas kernels, open_block(): pl.pallas_call(open_body, in_specs=[IN_VMEM, IN_VMEM, ANYWHERE, ANYWHERE,...  87.4 us
    pallas_call x1, Pallas kernels, forward_linked(): pl.pallas_call(forward_linked_body, grid=(PLANE,), in_specs=[tile(width),...  84.4 us
    pallas_call x1, Pallas kernels, ffn_back(): pl.pallas_call(ffn_back_body, grid=(PLANE,), in_specs=[tile(width), tile(...  74.3 us
    pallas_call x1, Pallas kernels, turn(): pl.pallas_call(turn_body, grid=(PLANE,), in_specs=[tile(width), tile(unit...  67.6 us
    pallas_call x1, Pallas kernels, close_block(): pl.pallas_call(close_body, grid=(PLANE,), in_specs=[pl.BlockSpec((rows, u...  67.3 us
    unnamed x37, local copies, waits for them, and re-layouts  13 us

profile of v5, /device:TPU:0, one launch (start us, length us, event | category | flops | bytes accessed | tf_op | source)
XLA Modules:
  0.0 631.0 jit_solution(12239079542480403721)
XLA Ops:
  5.5 1.3 pad.72.taps_ref
  8.6 1.4 fusion.22
  12.5 1.0 fusion.2.xy_shard
  14.5 1.3 copy.77.keep_ref
  15.8 87.4 %open_block.1 = (bf16[8,256,2048]{2,1,0:T(8,128)(2,1)}, bf16[8,256,1024]{2,1,0:T(8,128)(2,1)}, bf16[4,512,768]{2,1,0:T(8,128)(2,1)}, bf16[4,512,384]{2,1,0:T(8,128)(2,1)}, f32[2,2048]{1,0:T(2,128)}) custom-call(bf16[256,2048]{1,0:T(8,128)(2,1)} %x_ref.5, f32[8,128]{1,0:T(8,128)} %broadcast_in_dim.3.tile_ref, bf16[256,2048]{1,0:T(8,128)(2,1)} %own_cot_ref.1, ...), custom_call_target="tpu_custom_call" | custom-call | tf_op jit(solution)/shard_map/open_block/pallas_call | solution.py:1015
  103.2 1.4 fusion.23
  104.6 84.4 %mixer_forward_linked.1 = (bf16[2048,384]{1,0:T(8,128)(2,1)}, f32[2048,384]{1,0:T(8,128)}, f32[2048,384]{1,0:T(8,128)}, bf16[2048,384]{1,0:T(8,128)(2,1)}, bf16[...) custom-call(bf16[2048,2048]{1,0:T(8,128)(2,1)} %bitcast.37, ...), custom_call_target="tpu_custom_call" | custom-call | tf_op jit(solution)/shard_map/mixer_forward_linked/pallas_call | solution.py:1108
  189.0 106.4 %ffn_up.1 = (bf16[8,256,2048]{2,1,0:T(8,128)(2,1)}, bf16[8,256,2048]{2,1,0:T(8,128)(2,1)}, bf16[4,512,768]{2,1,0:T(8,128)(2,1)}, bf16[4,512,768]{2,1,0:T(8,128)(...) custom-call(bf16[256,2048]{1,0:T(8,128)(2,1)} %get-tuple-element.62., ...), custom_call_target="tpu_custom_call" | custom-call | tf_op jit(solution)/shard_map/ffn_up/pallas_call | solution.py:1250
  295.5 74.3 %ffn_back.1 = (bf16[2048,768]{1,0:T(8,128)(2,1)}, bf16[4,512,768]{2,1,0:T(8,128)(2,1)}, f32[512,768]{1,0:T(8,128)}, f32[256,2048]{1,0:T(8,128)}, bf16[256,2048]{1,0:T(8,128)(2,1)}, /*index=5*/f32[1,2048]{1,0:T(1,128)}) custom-call(bf16[2048,2048]{1,0:T(8,128)(2,1)} %bitcast.48, bf16[2048,2048]{1,0:T(8,128)(2,1)} %bitcast.39, ...), custom_call_target="tpu_custom_call" | custom-call | tf_op jit(solution)/shard_map/ffn_back/pallas_call | solution.py:1391
  369.8 67.6 %turn.1 = (bf16[4,512,768]{2,1,0:T(8,128)(2,1)}, bf16[4,512,384]{2,1,0:T(8,128)(2,1)}, f32[512,768]{1,0:T(8,128)}, bf16[8,256,2048]{2,1,0:T(8,128)(2,1)}) custom-call(bf16[2048,2048]{1,0:T(8,128)(2,1)} %bitcast.40, bf16[2048,768]{1,0:T(8,128)(2,1)} %get-tuple-element.75.d_ups_ref, bf16[4,512,768]{2,1,0:T(8,128)(2,1)} %get-tuple-element.76.gate_parts, ...), custom_call_target="tpu_custom_call" | custom-call | tf_op jit(solution)/shard_map/turn/pallas_call | solution.py:1482
  437.3 111.1 %mixer_backward_linked.1 = (bf16[4,512,768]{2,1,0:T(8,128)(2,1)}, f32[512,768]{1,0:T(8,128)}, f32[512,384]{1,0:T(8,128)}, bf16[256,2048]{1,0:T(8,128)(2,1)}, f32[4,8,128]{2,1,0:T(8,128)}, /*index=5*/f32[352,384]{1,0:T(8,128)}) custom-call(bf16[2048,2048]{1,0:T(8,128)(2,1)} %bitcast.47, bf16[2048,768]{1,0:T(8,128)(2,1)} %bitcast.42, ...), custom_call_target="tpu_custom_call" | custom-call | tf_op jit(solution)/shard_map/mixer_backward_linked/pallas_call | solution.py:1658
  548.5 67.3 %close_block.1 = (bf16[256,2048]{1,0:T(8,128)(2,1)}, f32[512,768]{1,0:T(8,128)}, f32[1,128]{1,0:T(1,128)}) custom-call(bf16[2048,768]{1,0:T(8,128)(2,1)} %get-tuple-element.66.hidden_ref, bf16[2048,768]{1,0:T(8,128)(2,1)} %bitcast.44, bf16[4,512,768]{2,1,0:T(8,128)(2,1)} %get-tuple-element.88.xy_parts, f32[256,2048]{1,0:T(8,128)} %get-tuple-element.74.residual_ref, ...), custom_call_target="tpu_custom_call" | custom-call | tf_op jit(solution)/shard_map/close_block/pallas_call | solution.py:1806
  615.7 1.3 slice_bitcast_fusion
  618.5 1.0 copy.85
  619.5 1.0 copy.84
  620.5 1.1 copy.83
  621.7 1.1 copy.82
  622.9 1.1 copy.81
  624.0 1.0 copy.103
  624.9 1.0 copy.104
  625.9 1.1 copy.105
  627.1 0.8 copy-done.2
  627.9 1.1 copy.106
  629.9 1.1 copy.107
  (60 shorter events, 12.4 us)
Async XLA Ops:
  0.7 10.3 %copy-start.8 = (bf16[2,171,171]{2,0,1:T(2,128)(2,1)S(1)}, bf16[2,171,171]{2,0,1:T(2,128)(2,1)}, u32[]{:S(2)}) copy-start(bf16[2,171,171]{2,0,1:T(2,128)(2,1)} %param.29) | copy-start | bytes 350896
  8.6 3.4 copy-start.9
  10.0 2.2 copy-start.10
  11.2 2.3 copy-start.11
  548.4 68.6 %copy-start.6 = (f32[352,384]{1,0:T(8,128)S(1)}, f32[352,384]{1,0:T(8,128)}, u32[]{:S(2)}) copy-start(f32[352,384]{1,0:T(8,128)} %get-tuple-element.95) | copy-start | bytes 1622020
  618.3 2.3 copy-start.7
  618.4 3.2 copy-start.3
  621.7 2.2 copy-start.5
  622.9 2.1 copy-start.4
  624.0 1.9 copy-start.1
  625.9 2.0 copy-start.2
  627.9 2.0 copy-start

commit v6 on v5

--- a/solution.py
+++ b/solution.py
@@ -101,7 +101,7 @@
         carry[...] = jnp.zeros_like(carry)
 
     chans = u_ref.shape[1]
-    branches = dot_plain(normed_ref[...], xy_ref[...])
+    branches = contract_last(normed_ref[...], xy_ref[...])
     branch_x = branches[:, :chans].astype(jnp.bfloat16)
     u_ref[...] = branch_x
     window[pl.ds(8, rows), :] = branch_x.astype(jnp.float32)
@@ -153,19 +153,18 @@
         normed_ref, xy_ref, taps_ref, vec_ref, wr_ref, we_ref, keep_ref,
         u_ref, by_ref, before_ref, states_ref, mixed_ref, *scratch,
     )
-    part_ref[...] = contract_last(mixed_ref[...], ow_ref[...]).astype(jnp.bfloat16)
+    part_ref[...] = dot_plain(mixed_ref[...], ow_ref[...]).astype(jnp.bfloat16)
 
 
 def backward_step(
-    d_res_ref, xy_ref, ow_ref, taps_ref, vec_ref, wr_ref, we_ref, keep_ref,
+    first_step, last_step, d_mixed, taps_ref, vec_ref, wr_ref, we_ref, keep_ref,
     u_ref, u_prev_ref, by_ref, before_ref, states_ref,
     d_xy_ref, taps_out, vec_out, wr_out, we_out,
-    window, conv, conv_low, rate, entry, d_mixed, d_conv, g_rate, g_entry, carry, sums,
+    window, conv, conv_low, rate, entry, d_conv, g_rate, g_entry, carry, sums,
 ):
-    rows, chans = d_res_ref.shape[0], u_ref.shape[1]
-    step_id = pl.program_id(0)
-
-    @pl.when(step_id == 0)
+    rows, chans = u_ref.shape
+
+    @pl.when(first_step)
     def _():
         d_conv[pl.ds(rows, 8), :] = jnp.zeros_like(d_conv[pl.ds(rows, 8), :])
         carry[...] = jnp.zeros_like(carry)
@@ -173,11 +172,10 @@
         wr_out[...] = jnp.zeros_like(wr_out)
         we_out[...] = jnp.zeros_like(we_out)
 
-    @pl.when(step_id > 0)
+    @pl.when(jnp.logical_not(first_step))
     def _():
         d_conv[pl.ds(rows, 8), :] = d_conv[0:8, :]
 
-    d_mixed[...] = dot_plain(d_res_ref[...], ow_ref[...])
     window[0:8, :] = u_prev_ref[8:16, :].astype(jnp.float32)
     window[pl.ds(8, rows), :] = u_ref[...].astype(jnp.float32)
 
@@ -267,7 +265,7 @@
 
     lax.fori_loop(0, rows // CHUNK, back_step, 0, unroll=UNROLL)
 
-    @pl.when(step_id == pl.num_programs(0) - 1)
+    @pl.when(last_step)
     def _():
         vec_out[...] = jnp.zeros_like(vec_out)
         for place in range(4):
@@ -278,18 +276,20 @@
                 sums[32 + 8 * place : 40 + 8 * place, :], axis=0, keepdims=True
             )
 
-    return contract_last(d_xy_ref[...], xy_ref[...]).astype(jnp.bfloat16)
-
 
 def backward_body(
     d_res_ref, xy_ref, ow_ref, taps_ref, vec_ref, wr_ref, we_ref, keep_ref,
     u_ref, u_prev_ref, by_ref, before_ref, states_ref,
-    d_xy_ref, part_ref, *rest,
+    d_xy_ref, part_ref, taps_out, vec_out, wr_out, we_out, d_mixed, *scratch,
 ):
-    part_ref[...] = backward_step(
-        d_res_ref, xy_ref, ow_ref, taps_ref, vec_ref, wr_ref, we_ref, keep_ref,
-        u_ref, u_prev_ref, by_ref, before_ref, states_ref, d_xy_ref, *rest,
-    )
+    step = pl.program_id(0)
+    d_mixed[...] = contract_last(d_res_ref[...], ow_ref[...])
+    backward_step(
+        step == 0, step == pl.num_programs(0) - 1, d_mixed, taps_ref, vec_ref, wr_ref,
+        we_ref, keep_ref, u_ref, u_prev_ref, by_ref, before_ref, states_ref, d_xy_ref,
+        taps_out, vec_out, wr_out, we_out, *scratch,
+    )
+    part_ref[...] = dot_plain(d_xy_ref[...], xy_ref[...]).astype(jnp.bfloat16)
 
 
 def whole(shape):
@@ -298,7 +298,7 @@
 
 def mixer_forward(normed, xy, ow, taps, vec, wr, we, keep, rows):
     length, width = normed.shape
-    chans = ow.shape[1]
+    chans = ow.shape[0]
     tile = lambda columns: pl.BlockSpec((rows, columns), lambda i: (i, 0))
     return pl.pallas_call(
         forward_body,
@@ -336,7 +336,7 @@
 
 def mixer_backward(d_res, xy, ow, taps, vec, wr, we, keep, u, by, before, states, rows):
     length, width = d_res.shape
-    chans = ow.shape[1]
+    chans = ow.shape[0]
     blocks = length // rows
     tile = lambda columns: pl.BlockSpec((rows, columns), lambda i: (blocks - 1 - i, 0))
     ahead = pl.BlockSpec(
@@ -363,10 +363,10 @@
             jax.ShapeDtypeStruct(we.shape, jnp.float32),
         ],
         scratch_shapes=[
+            pltpu.VMEM((rows, chans), jnp.float32),
             pltpu.VMEM((rows + 8, chans), jnp.float32),
             pltpu.VMEM((rows, chans), jnp.float32),
             pltpu.VMEM((rows, chans), jnp.bfloat16),
-            pltpu.VMEM((rows, chans), jnp.float32),
             pltpu.VMEM((rows, chans), jnp.float32),
             pltpu.VMEM((rows, chans), jnp.float32),
             pltpu.VMEM((rows + 8, chans), jnp.float32),
@@ -477,6 +477,28 @@
     pl.semaphore_wait(barrier, count)
 
 
+class Bring:
+    def __init__(self, sources, places, semaphores):
+        self.copies = [
+            pltpu.make_async_copy(src, dst, semaphores.at[k])
+            for k, (src, dst) in enumerate(zip(sources, places))
+        ]
+
+    def start(self):
+        for copy in self.copies:
+            copy.start()
+
+    def wait(self, *which):
+        for k in which:
+            self.copies[k].wait()
+
+
+def held(*arrays):
+    return [pltpu.VMEM(item.shape, item.dtype) for item in arrays] + [
+        pltpu.SemaphoreType.DMA((len(arrays),))
+    ]
+
+
 class LineGather:
     semaphores = (
         pltpu.SemaphoreType.DMA((LINE,)),
@@ -484,15 +506,10 @@
         pltpu.SemaphoreType.DMA((2,)),
     )
 
-    def __init__(self, shard, full, sent, arrived, other, source=None, target=None):
+    def __init__(self, source, slot, sent, arrived, other):
         self.r = lax.axis_index("row")
-        self.shard, self.full = shard, full
+        self.source, self.slot = source, slot
         self.sent, self.arrived, self.other = sent, arrived, other
-        self.source = shard if source is None else shard.at[source]
-        self.target = target
-
-    def slot(self, origin):
-        return self.full.at[origin] if self.target is None else self.full.at[origin, self.target]
 
     def own(self, t):
         return send_to(
@@ -564,19 +581,19 @@
             pltpu.VMEM((rows, width), jnp.bfloat16),
         ]
 
-    def __init__(self, parts, landed, passed, sent, arrived, other):
+    def __init__(self, source, parts, landed, passed, sent, arrived, other):
         self.r = lax.axis_index("row")
-        self.parts, self.landed, self.passed = parts, landed, passed
+        self.source, self.parts, self.landed, self.passed = source, parts, landed, passed
         self.sent, self.arrived, self.other = sent, arrived, other
 
     def to_pass(self, me, origin, via):
         return send_to(
-            self.parts.at[origin], self.passed, self.sent.at[origin], self.other.at[0], "row", via
+            self.source.at[origin], self.passed, self.sent.at[origin], self.other.at[0], "row", via
         )
 
     def direct(self, t):
         return send_to(
-            self.parts.at[t], self.landed.at[self.r], self.sent.at[t], self.arrived.at[self.r],
+            self.source.at[t], self.landed.at[self.r], self.sent.at[t], self.arrived.at[self.r],
             "row", t,
         )
 
@@ -611,7 +628,7 @@
             def _(me=me, end=end):
                 self.to_pass(me, end, end).wait_recv()
                 rows = self.passed.shape[0]
-                step = 64
+                step = 32
 
                 def add(i, unused):
                     at = pl.ds(pl.multiple_of(i * step, step), step)
@@ -631,7 +648,7 @@
             @pl.when(jnp.logical_not(unsent_to(r, t)))
             def _(t=t):
                 send_to(
-                    self.parts.at[t], self.landed.at[t], self.sent.at[t], self.arrived.at[t],
+                    self.source.at[t], self.landed.at[t], self.sent.at[t], self.arrived.at[t],
                     "row", t,
                 ).wait_recv()
 
@@ -745,16 +762,23 @@
             self.hand(self.y, a, 2, self.y).wait_recv()
             self.hand(self.y, a, 5, self.side).start()
 
-    def end(self):
+    def beside(self):
+        for c in range(PIECES):
+            self.hand(self.side, c, 0, self.side).wait_recv()
+
+    def far_side(self):
         for pair in zip(self.first, self.second):
             for c in pair:
                 self.hand(self.far, c, 3, self.side).wait_recv()
                 self.hand(self.far, c, 6, self.side).start()
+
+    def end(self, beside=True):
         side = self.side
+        if beside:
+            self.beside()
         for c in range(PIECES):
             for owner, lane in (
-                (side, 0), (across_of(side), 4), (along_of(side), 5),
-                (across_of(along_of(side)), 6),
+                (across_of(side), 4), (along_of(side), 5), (across_of(along_of(side)), 6)
             ):
                 self.hand(owner, c, lane, side).wait_recv()
         for c in range(PIECES):
@@ -930,17 +954,86 @@
     return rows * lax.rsqrt(jnp.mean(rows * rows, axis=-1, keepdims=True) + EPSILON) * gain
 
 
+def lay_out_params(
+    taps_ref, biases, decay_ref, rate_ref, entry_ref, resets_ref,
+    taps_out, vec_out, wr_out, we_out, keep_out, square, moved,
+):
+    used, width = decay_ref.shape[1], rate_ref.shape[1]
+    columns = vec_out.shape[1]
+    taps_out[...] = jnp.zeros_like(taps_out)
+    taps_out[:, 0:used] = taps_ref[...]
+    vec_out[...] = jnp.zeros_like(vec_out)
+    for k, bias in enumerate(biases):
+        vec_out[k : k + 1, 0:used] = bias[...]
+    vec_out[3:4, :] = jnp.full((1, columns), 2.0, jnp.float32)
+    vec_out[3:4, 0:used] = decay_ref[...]
+    decay = vec_out[3:4, :]
+    vec_out[3:4, :] = -8.0 * jnp.log1p(jnp.exp(-decay))
+    vec_out[4:5, :] = 8.0 * jax.nn.sigmoid(-decay)
+    for source, out in ((rate_ref, wr_out), (entry_ref, we_out)):
+        square[...] = jnp.zeros_like(square)
+        square[0:width, 0:width] = source[1].astype(jnp.float32)
+        moved[...] = pltpu.roll(pltpu.roll(square[...], width, 0), width, 1)
+        square[...] = jnp.zeros_like(square)
+        square[0:width, 0:width] = source[0].astype(jnp.float32)
+        out[...] = (square[...] + moved[...]).astype(jnp.bfloat16)
+    resets = resets_ref[...]
+    first = lax.broadcasted_iota(jnp.int32, resets.shape, 1) == 0
+    one = jnp.where(first | (resets > 0), 0.0, 1.0)
+    length = resets.shape[1]
+    two = one * pltpu.roll(one, 1, 1)
+    three = two * pltpu.roll(one, 2, 1)
+    ahead = [pltpu.roll(item, length - k, 1) for k, item in ((1, one), (2, two), (3, three))]
+    rows = jnp.concatenate(
+        [one, one, two, three, *ahead, one, jnp.zeros((120, length), jnp.float32)], axis=0
+    )
+    for k in range(length // 128):
+        turned = rows[:, k * 128 : (k + 1) * 128].T
+        keep_out[k * 128 : (k + 1) * 128, :] = turned[:, 0:8]
+
+
 def open_body(
-    x_ref, tile_ref, cot, xy_shard, out_shard, full, cot_out, xy_full, out_full, gains_ref,
-    normed, column, spread, gain_sent, gain_arrived, wide_sent, wide_arrived, *semaphores,
+    x_ref, mix_ref, ffn_ref, cot, xt_ref, yt_ref, ot_ref,
+    taps_ref, conv_bias, rate_bias, entry_bias, decay_ref, rate_ref, entry_ref, resets_ref,
+    full, cot_out, xy_full, out_full, gains_ref, taps_out, vec_out, wr_out, we_out, keep_out,
+    shards, blank, square, moved,
+    normed, column, spread, gain_sent, gain_arrived, wide_sent, wide_arrived, wiped, *semaphores,
 ):
     r, h = lax.axis_index("row"), lax.axis_index("head")
-    xy_line = LineGather(xy_shard, xy_full, *semaphores[0:3])
-    out_line = LineGather(out_shard, out_full, *semaphores[3:6])
-    plane = PlaneGather(normed, full, *semaphores[6:9])
+    held_rows, share = shards.shape[1:]
+    used, chans = xt_ref.shape[0], out_full.shape[0]
+
+    def slot(full, first):
+        def at(origin):
+            lanes = pl.ds(pl.multiple_of(origin * share, share), share)
+            return full.at[pl.ds(first, held_rows), lanes]
+
+        return at
+
+    lines = [
+        LineGather(shards.at[k], slot(dst, first), *semaphores[3 * k : 3 * k + 3])
+        for k, (dst, first) in enumerate(((xy_full, 0), (xy_full, chans), (out_full, 0)))
+    ]
+    wipes = [
+        pltpu.make_async_copy(
+            blank, dst.at[pl.ds(first + held_rows, chans - held_rows)], wiped.at[k]
+        )
+        for k, (dst, first) in enumerate(((xy_full, 0), (xy_full, chans), (out_full, 0)))
+    ]
+    plane = PlaneGather(normed, full, *semaphores[9:12])
     cot_plane = PlaneGather(
-        cot, cot_out, *semaphores[9:12], source=pl.ds(0, cot_out.shape[2])
-    )
+        cot, cot_out, *semaphores[12:15], source=pl.ds(0, cot_out.shape[2])
+    )
+    for k, source in enumerate((xt_ref, yt_ref, ot_ref)):
+        shards[k, held_rows - 16 :, :] = jnp.zeros((16, share), jnp.bfloat16)
+        shards[k, 0:used, :] = source[...]
+    gain_share = mix_ref.shape[1]
+    low = lax.broadcasted_iota(jnp.int32, (8, 2 * gain_share), 1) < gain_share
+    column[r] = jnp.zeros_like(column[r])
+    column[r, 0:1, 0:gain_share] = mix_ref[...].astype(jnp.float32)
+    column[r, 1:2, 0:gain_share] = ffn_ref[...].astype(jnp.float32)
+    rows = column[r]
+    column[r] = jnp.where(low, rows, pltpu.roll(pltpu.roll(rows, gain_share, 1), 7, 0))
     meet(True, "all")
 
     def up_line(t):
@@ -959,11 +1052,13 @@
             lax.rem(h + step, PLANE),
         )
 
-    column[r] = tile_ref[...]
     for step in range(1, LINE):
         up_line(lax.rem(r + step, LINE)).start()
-    xy_line.start()
-    out_line.start()
+    for line in lines:
+        line.start()
+    blank[...] = jnp.zeros_like(blank)
+    for wipe in wipes:
+        wipe.start()
     for step in range(1, LINE):
         from_line(lax.rem(r + step, LINE)).wait_recv()
     for step in range(1, PLANE):
@@ -973,15 +1068,15 @@
     for step in range(1, PLANE):
         over_plane(step, lax.rem(h + step, PLANE)).wait_recv()
 
-    share = tile_ref.shape[1] // 2
-    low = lax.broadcasted_iota(jnp.int32, (1, 2 * share), 1) < share
+    low = lax.broadcasted_iota(jnp.int32, (1, 2 * gain_share), 1) < gain_share
     for line_place in range(LINE):
         for pair in range(PLANE // 2):
             even = spread[2 * pair, line_place][0:1, :]
             odd = spread[2 * pair + 1, line_place][0:1, :]
-            at = (line_place * (PLANE // 2) + pair) * 2 * share
-            gains_ref[0:1, at : at + 2 * share] = jnp.where(low, even, pltpu.roll(odd, share, 1))
-            gains_ref[1:2, at : at + 2 * share] = jnp.where(low, pltpu.roll(even, share, 1), odd)
+            at = (line_place * (PLANE // 2) + pair) * 2 * gain_share
+            end = at + 2 * gain_share
+            gains_ref[0:1, at:end] = jnp.where(low, even, pltpu.roll(odd, gain_share, 1))
+            gains_ref[1:2, at:end] = jnp.where(low, pltpu.roll(even, gain_share, 1), odd)
 
     def make(i, unused):
         at = pl.ds(pl.multiple_of(i * CHUNK, CHUNK), CHUNK)
@@ -992,71 +1087,100 @@
 
     lax.fori_loop(0, x_ref.shape[0] // CHUNK, make, 0)
     plane.start()
+    lay_out_params(
+        taps_ref, (conv_bias, rate_bias, entry_bias), decay_ref, rate_ref, entry_ref, resets_ref,
+        taps_out, vec_out, wr_out, we_out, keep_out, square, moved,
+    )
     cot_plane.relay(0)
     cot_plane.relay(1)
+    lines[0].forward()
     cot_plane.rest()
     plane.relay(0)
-    xy_line.forward()
     plane.relay(1)
+    lines[1].forward()
+    cot_plane.far_side()
     cot_plane.end()
     plane.rest()
+    plane.far_side()
     plane.end()
-    out_line.forward()
-    xy_line.finish()
-    out_line.finish()
+    lines[2].forward()
+    for line in lines:
+        line.finish()
+    for wipe in wipes:
+        wipe.wait()
     for step in range(1, LINE):
         up_line(lax.rem(r + step, LINE)).wait_send()
     for step in range(1, PLANE):
         over_plane(step, h).wait_send()
 
 
-def open_block(layer_in, tile, cot, xy_shard, out_shard):
+def open_block(layer_in, gains, cot, weights, params):
     rows, width = layer_in.shape
+    used, share = weights[0].shape
+    chans, held_rows = -(-used // 128) * 128, -(-used // 16) * 16
+    length = params[-1].shape[1]
+    tile = (8, 2 * gains[0].shape[1])
     return pl.pallas_call(
         open_body,
-        in_specs=[IN_VMEM, IN_VMEM, ANYWHERE, ANYWHERE, ANYWHERE],
-        out_specs=[ANYWHERE] * 4 + [IN_VMEM],
+        in_specs=[IN_VMEM, IN_VMEM, IN_VMEM, ANYWHERE] + [IN_VMEM] * 11,
+        out_specs=[ANYWHERE] * 4 + [IN_VMEM] * 6,
         out_shape=[
             jax.ShapeDtypeStruct((PLANE, rows, width), jnp.bfloat16),
             jax.ShapeDtypeStruct((PLANE, rows, width // 2), jnp.bfloat16),
-            jax.ShapeDtypeStruct((LINE,) + xy_shard.shape, jnp.bfloat16),
-            jax.ShapeDtypeStruct((LINE,) + out_shard.shape, jnp.bfloat16),
+            jax.ShapeDtypeStruct((2 * chans, width), jnp.bfloat16),
+            jax.ShapeDtypeStruct((chans, width), jnp.bfloat16),
             jax.ShapeDtypeStruct((2, width), jnp.float32),
+            jax.ShapeDtypeStruct((4, chans), jnp.float32),
+            jax.ShapeDtypeStruct((8, chans), jnp.float32),
+            jax.ShapeDtypeStruct((chans, chans), jnp.bfloat16),
+            jax.ShapeDtypeStruct((chans, chans), jnp.bfloat16),
+            jax.ShapeDtypeStruct((length, 8), jnp.float32),
         ],
         scratch_shapes=[
+            pltpu.VMEM((3, held_rows, share), jnp.bfloat16),
+            pltpu.VMEM((chans - held_rows, width), jnp.bfloat16),
+            pltpu.VMEM((chans, chans), jnp.float32),
+            pltpu.VMEM((chans, chans), jnp.float32),
             pltpu.VMEM((rows, width), jnp.bfloat16),
-            pltpu.VMEM((LINE,) + tile.shape, jnp.float32),
-            pltpu.VMEM((PLANE, LINE) + tile.shape, jnp.float32),
+            pltpu.VMEM((LINE,) + tile, jnp.float32),
+            pltpu.VMEM((PLANE, LINE) + tile, jnp.float32),
             pltpu.SemaphoreType.DMA((LINE,)),
             pltpu.SemaphoreType.DMA((LINE,)),
             pltpu.SemaphoreType.DMA((PLANE,)),
             pltpu.SemaphoreType.DMA((PLANE,)),
-            *(LineGather.semaphores * 2),
+            pltpu.SemaphoreType.DMA((3,)),
+            *(LineGather.semaphores * 3),
             *(PlaneGather.semaphores * 2),
         ],
         compiler_params=pltpu.CompilerParams(
             collective_id=0, has_side_effects=True, vmem_limit_bytes=61 * 2**20
         ),
         name="open_block",
-    )(layer_in, tile, cot, xy_shard, out_shard)
+    )(layer_in, *gains, cot, *weights, *params)
 
 
 def forward_linked_body(
-    normed_ref, xy_ref, ow_ref, taps_ref, vec_ref, wr_ref, we_ref, keep_ref,
-    x_ref, gain_ref, gate_shard, up_shard,
+    normed_ref, xy_hbm, ow_hbm, taps_ref, vec_ref, wr_ref, we_ref, keep_ref,
+    x_hbm, gain_ref, gate_shard, up_shard,
     u_ref, by_ref, before_ref, states_ref, mixed_ref, residual_ref, two_ref, gate_out, up_out,
+    xy_ref, ow_ref, x_ref, brought,
     window, conv, conv_low, rate, entry, carry, *links,
 ):
     step = pl.program_id(0)
     plane = PlaneReduce(*links[:10])
-    gate_line = LineGather(gate_shard, gate_out, *links[10:13])
-    up_line = LineGather(up_shard, up_out, *links[13:16], source=pl.ds(0, up_out.shape[1]))
+    gate_line = LineGather(gate_shard, lambda t: gate_out.at[t], *links[10:13])
+    first_rows = up_shard.at[pl.ds(0, up_out.shape[1])]
+    up_line = LineGather(first_rows, lambda t: up_out.at[t], *links[13:16])
+
+    bring = Bring((xy_hbm, ow_hbm, x_hbm), (xy_ref, ow_ref, x_ref), brought)
 
     @pl.when(step == 0)
     def _():
+        bring.start()
         meet(True, "near")
         gate_line.start()
         up_line.start()
+        bring.wait(0, 1, 2)
 
     @pl.when(step > 0)
     def _():
@@ -1071,7 +1195,7 @@
         u_ref, by_ref, before_ref, states_ref, mixed_ref,
         window, conv, conv_low, rate, entry, carry,
     )
-    plane.put(step, contract_last(mixed_ref[...], ow_ref[...]).astype(jnp.bfloat16))
+    plane.put(step, dot_plain(mixed_ref[...], ow_ref[...]).astype(jnp.bfloat16))
 
     @pl.when(step == 6)
     def _():
@@ -1101,7 +1225,7 @@
 
 def forward_linked(normed, xy, ow, taps, vec, wr, we, keep, layer_in, gain, gate_shard, up_shard):
     length, width = normed.shape
-    chans = ow.shape[1]
+    chans = ow.shape[0]
     rows = length // PLANE
     share, units = up_shard.shape
     tile = lambda columns: pl.BlockSpec((rows, columns), lambda i: (i, 0))
@@ -1109,9 +1233,9 @@
         forward_linked_body,
         grid=(PLANE,),
         in_specs=[
-            tile(width), once(xy.shape), once(ow.shape), once(taps.shape),
+            tile(width), ANYWHERE, ANYWHERE, once(taps.shape),
             once(vec.shape), once(wr.shape), once(we.shape), tile(keep.shape[1]),
-            once(layer_in.shape), once(gain.shape), ANYWHERE, ANYWHERE,
+            ANYWHERE, once(gain.shape), ANYWHERE, ANYWHERE,
         ],
         out_specs=[tile(chans)] * 5 + [once((rows, width))] * 2 + [ANYWHERE] * 2,
         out_shape=[
@@ -1126,6 +1250,7 @@
             jax.ShapeDtypeStruct((LINE, share // 2, units), jnp.bfloat16),
         ],
         scratch_shapes=[
+            *held(xy, ow, layer_in),
             pltpu.VMEM((rows + 8, chans), jnp.float32),
             pltpu.VMEM((rows, chans), jnp.float32),
             pltpu.VMEM((rows, chans), jnp.bfloat16),
@@ -1151,18 +1276,26 @@
     h = lax.axis_index("head")
     rows = own_two.shape[0]
     units = gates.shape[1]
-    width, share = own_two.shape[1], up.shape[1]
-    late_rows, late_columns = pl.ds(share // 2, share // 2), pl.ds(width // 2, width // 2)
-    up_line = LineGather(up_shard, up, *semaphores[0:3], source=late_rows, target=late_rows)
-    down_line = LineGather(down_shard, down_out, *semaphores[3:6])
+    width, share = own_two.shape[1], up_shard.shape[0]
+    half = share // 2
+    late_columns = pl.ds(width // 2, width // 2)
+    up_line = LineGather(
+        up_shard.at[pl.ds(half, half)],
+        lambda t: up.at[pl.ds(pl.multiple_of(t * share + half, half), half)],
+        *semaphores[0:3],
+    )
+    down_line = LineGather(down_shard, lambda t: down_out.at[t], *semaphores[3:6])
     two_plane = PlaneGather(own_two, two, *semaphores[6:9])
     cot_plane = PlaneGather(
         own_cot, cot, *semaphores[9:12], source=late_columns, target=late_columns
     )
     inward = [
-        pltpu.make_async_copy(up_half, up.at[:, pl.ds(0, share // 2)], brought.at[0]),
-        pltpu.make_async_copy(cot_half, cot.at[:, :, pl.ds(0, width // 2)], brought.at[1]),
+        pltpu.make_async_copy(up_half.at[t], up.at[pl.ds(t * share, half)], brought.at[t])
+        for t in range(LINE)
     ]
+    inward.append(
+        pltpu.make_async_copy(cot_half, cot.at[:, :, pl.ds(0, width // 2)], brought.at[LINE])
+    )
     outward = [
         pltpu.make_async_copy(src, dst, copied.at[k])
         for k, (src, dst) in enumerate(
@@ -1182,26 +1315,29 @@
     def at_block(block):
         return pl.ds(pl.multiple_of(block * rows, rows), rows)
 
-    def make_gates(k, unused):
-        block = lax.rem(h + k, PLANE)
+    def make_gates(block):
         gates[at_block(block), :] = dot_plain(two[block], gate_ref[...])
-        return unused
 
     gates[at_block(h), :] = dot_plain(own_two[...], gate_ref[...])
     two_plane.relay(0)
+    two_plane.beside()
+    make_gates(two_plane.side)
     two_plane.relay(1)
+    cot_plane.start()
     two_plane.rest()
-    cot_plane.start()
-    two_plane.end()
+    make_gates(two_plane.x)
+    make_gates(two_plane.y)
+    up_line.forward()
+    two_plane.far_side()
+    make_gates(two_plane.far)
+    two_plane.end(beside=False)
     outward[0].start()
-    up_line.forward()
-    lax.fori_loop(1, 3, make_gates, 0)
     cot_plane.relay(0)
-    lax.fori_loop(3, 6, make_gates, 0)
+    make_gates(across_of(two_plane.side))
+    make_gates(along_of(two_plane.side))
     cot_plane.relay(1)
-    lax.fori_loop(6, PLANE, make_gates, 0)
+    make_gates(across_of(along_of(two_plane.side)))
     outward[3].start()
-    cot_plane.rest()
     up_line.finish()
     for copy in inward:
         copy.wait()
@@ -1209,10 +1345,7 @@
 
     def make_hidden(block, unused):
         at = at_block(block)
-        value = jnp.zeros((rows, units), jnp.float32)
-        for t in range(LINE):
-            value = value + dot_plain(two[block, :, t * share : (t + 1) * share], up[t])
-        ups[at, :] = value
+        ups[at, :] = dot_plain(two[block], up[...])
 
         def make(i, unused):
             here = pl.ds(pl.multiple_of(block * rows + i * CHUNK, CHUNK), CHUNK)
@@ -1222,12 +1355,16 @@
         lax.fori_loop(0, rows // CHUNK, make, 0, unroll=UNROLL)
         return unused
 
-    lax.fori_loop(0, PLANE, make_hidden, 0)
+    lax.fori_loop(0, 2, make_hidden, 0)
+    cot_plane.rest()
+    lax.fori_loop(2, 5, make_hidden, 0)
+    cot_plane.far_side()
+    down_line.forward()
+    lax.fori_loop(5, PLANE, make_hidden, 0)
     outward[4].start()
     outward[5].start()
     cot_plane.end()
     outward[1].start()
-    down_line.forward()
     total[...] = contract_first(cot[0], hidden[0:rows, :])
 
     def add_down(block, unused):
@@ -1254,7 +1391,7 @@
         out_shape=[
             group,
             group,
-            weight,
+            jax.ShapeDtypeStruct((width, units), jnp.bfloat16),
             weight,
             jax.ShapeDtypeStruct((length, units), jnp.float32),
             jax.ShapeDtypeStruct((length, units), jnp.float32),
@@ -1264,13 +1401,13 @@
         scratch_shapes=[
             pltpu.VMEM((PLANE, rows, width), jnp.bfloat16),
             pltpu.VMEM((PLANE, rows, width), jnp.bfloat16),
-            pltpu.VMEM((LINE, share, units), jnp.bfloat16),
+            pltpu.VMEM((width, units), jnp.bfloat16),
             pltpu.VMEM((length, units), jnp.float32),
             pltpu.VMEM((length, units), jnp.float32),
             pltpu.VMEM((length, units), jnp.bfloat16),
             pltpu.VMEM((width, units), jnp.float32),
             pltpu.SemaphoreType.DMA((6,)),
-            pltpu.SemaphoreType.DMA((2,)),
+            pltpu.SemaphoreType.DMA((LINE + 1,)),
             *(LineGather.semaphores * 2),
             *(PlaneGather.semaphores * 2),
         ],
@@ -1308,64 +1445,100 @@
     lax.fori_loop(0, rows // step, move, 0)
 
 
+def to_turned_parts(total, parts, places):
+    share = parts.shape[2]
+    step = 32
+    for first, target, count in places:
+
+        def move(i, unused, first=first, target=target):
+            here = pl.ds(pl.multiple_of(first + i * step, step), step)
+            at = pl.ds(pl.multiple_of(target + i * step, step), step)
+            for t in range(LINE):
+                parts[t, at, :] = total[here, t * share : (t + 1) * share].astype(jnp.bfloat16)
+            return unused
+
+        lax.fori_loop(0, count // step, move, 0)
+
+
 def ffn_back_body(
-    cot_ref, two_ref, gates_ref, ups_ref, gate_ref, up_ref, down_ref, parts,
-    residual_ref, own_cot_ref, gain_ref,
+    cot_ref, two_ref, gates_ref, ups_ref, gate_hbm, up_hbm, down_hbm, parts_hbm,
+    residual_hbm, own_cot_hbm, gain_ref,
     d_ups_ref, gate_parts, down_out, d_res_ref, d_low_ref, gain_out,
+    gate_ref, up_ref, down_ref, parts, brought, late,
     total, d_gates, d_hidden, eight, *links,
 ):
     step = pl.program_id(0)
-    line = LineReduce(parts, *links[:5])
+    line = LineReduce(parts_hbm, parts, *links[:5])
     plane = PlaneReduce(*links[5:])
     rows = cot_ref.shape[0]
 
+    bring = Bring(
+        (down_hbm, gate_hbm, up_hbm, parts_hbm), (down_ref, gate_ref, up_ref, parts), brought
+    )
+    into_outputs = Bring((residual_hbm, own_cot_hbm), (d_res_ref, d_low_ref), late)
+
     @pl.when(step == 0)
     def _():
+        bring.start()
         meet(True, "near")
         line.start()
-        total[...] = jnp.zeros_like(total)
-
-    @pl.when(step > 0)
+        into_outputs.start()
+        bring.wait(0, 1, 2, 3)
+
+    @pl.when((step > 2) & (step <= PLANE + 2))
+    def _():
+        plane.relay(far_first(step - 3))
+
+    @pl.when(step < PLANE)
+    def _():
+        d_hidden[...] = dot_plain(cot_ref[...], down_ref[...])
+
+        def make(i, unused):
+            at = pl.ds(pl.multiple_of(i * CHUNK, CHUNK), CHUNK)
+            gelu_gate, slope = gelu_both(gates_ref[at, :])
+            through = d_hidden[at, :]
+            d_gates[step, at, :] = (through * ups_ref[at, :] * slope).astype(jnp.bfloat16)
+            d_ups_ref[at, :] = (through * gelu_gate).astype(jnp.bfloat16)
+            return unused
+
+        lax.fori_loop(0, rows // CHUNK, make, 0, unroll=UNROLL)
+
+        @pl.when(step > 0)
+        def _():
+            plane.pass_on(far_first(step - 1))
+
+        value = contract_last(d_gates[step], gate_ref[...]) + contract_last(
+            d_ups_ref[...], up_ref[...]
+        )
+        plane.put(far_first(step), value.astype(jnp.bfloat16))
+
+    @pl.when(step == PLANE)
+    def _():
+        total[...] = contract_first(two_ref[...], d_gates[0])
+
+    @pl.when(step > PLANE)
+    def _():
+        total[...] += contract_first(two_ref[...], d_gates[step - PLANE])
+
+    @pl.when(step == PLANE)
     def _():
         plane.pass_on(far_first(step - 1))
 
-    @pl.when(step > 2)
-    def _():
-        plane.relay(far_first(step - 3))
-
-    d_hidden[...] = dot_plain(cot_ref[...], down_ref[...])
-
-    def make(i, unused):
-        at = pl.ds(pl.multiple_of(i * CHUNK, CHUNK), CHUNK)
-        gelu_gate, slope = gelu_both(gates_ref[at, :])
-        through = d_hidden[at, :]
-        d_gates[at, :] = (through * ups_ref[at, :] * slope).astype(jnp.bfloat16)
-        d_ups_ref[at, :] = (through * gelu_gate).astype(jnp.bfloat16)
-        return unused
-
-    lax.fori_loop(0, rows // CHUNK, make, 0, unroll=UNROLL)
-    value = contract_last(d_gates[...], gate_ref[...]) + contract_last(d_ups_ref[...], up_ref[...])
-    plane.put(far_first(step), value.astype(jnp.bfloat16))
-    total[...] += contract_first(two_ref[...], d_gates[...])
-
-    @pl.when(step == 4)
+    @pl.when(step == 5)
     def _():
         line.forward()
 
-    @pl.when(step == PLANE - 1)
-    def _():
-        plane.relay(far_first(step - 2))
-        plane.pass_on(far_first(step))
-        plane.relay(far_first(step - 1))
+    @pl.when(step == 2 * PLANE - 1)
+    def _():
         to_parts(total, gate_parts)
-        plane.relay(far_first(step))
         plane.arrive()
+        into_outputs.wait(0, 1)
         eight[...] = jnp.zeros_like(eight)
 
         def back(i, unused):
             at = pl.ds(pl.multiple_of(i * CHUNK, CHUNK), CHUNK)
-            d_rows, d_gain = norm_back(residual_ref[at, :], gain_ref[...], plane.total(at))
-            d_residual = own_cot_ref[at, :].astype(jnp.float32) + d_rows
+            d_rows, d_gain = norm_back(d_res_ref[at, :], gain_ref[...], plane.total(at))
+            d_residual = d_low_ref[at, :].astype(jnp.float32) + d_rows
             d_res_ref[at, :] = d_residual
             d_low_ref[at, :] = d_residual.astype(jnp.bfloat16)
             eight[...] += sum_eight(d_gain)
@@ -1387,14 +1560,18 @@
     length, width = cot_group.shape
     units = gate.shape[1]
     rows, share = length // PLANE, width // LINE
-    tile = lambda columns: pl.BlockSpec((rows, columns), lambda i: (far_first(i), 0))
+    tile = lambda columns: pl.BlockSpec(
+        (rows, columns), lambda i: (far_first(jnp.minimum(i, PLANE - 1)), 0)
+    )
+    later = lambda columns: pl.BlockSpec(
+        (rows, columns), lambda i: (far_first(jnp.maximum(i - PLANE, 0)), 0)
+    )
     return pl.pallas_call(
         ffn_back_body,
-        grid=(PLANE,),
+        grid=(2 * PLANE,),
         in_specs=[
-            tile(width), tile(width), tile(units), tile(units), once(gate.shape),
-            once(up.shape), once(down.shape), once(parts.shape), once(residual.shape),
-            once(own_cot.shape), once(gain.shape),
+            tile(width), later(width), tile(units), tile(units),
+            *([ANYWHERE] * 6), once(gain.shape),
         ],
         out_specs=[
             tile(units), once((LINE, share, units)), once((share, units)),
@@ -1409,8 +1586,10 @@
             jax.ShapeDtypeStruct((1, width), jnp.float32),
         ],
         scratch_shapes=[
+            *held(gate, up, down, parts),
+            pltpu.SemaphoreType.DMA((2,)),
             pltpu.VMEM((width, units), jnp.float32),
-            pltpu.VMEM((rows, units), jnp.bfloat16),
+            pltpu.VMEM((PLANE, rows, units), jnp.bfloat16),
             pltpu.VMEM((rows, units), jnp.float32),
             pltpu.VMEM((8, width), jnp.float32),
             *LineReduce.buffers(share, units),
@@ -1419,62 +1598,81 @@
             *PlaneReduce.semaphores,
         ],
         compiler_params=pltpu.CompilerParams(
-            collective_id=4, has_side_effects=True, vmem_limit_bytes=61 * 2**20
+            collective_id=4, has_side_effects=True, vmem_limit_bytes=63 * 2**20
         ),
         name="ffn_back",
     )(cot_group, two_group, gates, ups, gate, up, down, parts, residual, own_cot, gain)
 
 
 def turn_body(
-    two_ref, d_ups_ref, gate_parts, block, mixed_ref,
-    up_parts, out_parts, gate_out, full_out,
-    full, total, out_total, copied, *links,
+    two_ref, d_ups_ref, parts_hbm, block, mixed_hbm, ow_hbm,
+    up_parts, out_parts, gate_out, d_mixed_out,
+    gate_parts, mixed_ref, ow_ref, brought,
+    full, total, out_total, *links,
 ):
     step = pl.program_id(0)
-    line = LineReduce(gate_parts, *links[:5])
+    line = LineReduce(parts_hbm, gate_parts, *links[:5])
     plane = PlaneGather(block, full, *links[5:])
     rows = two_ref.shape[0]
-    outward = pltpu.make_async_copy(full, full_out, copied)
+
+    bring = Bring(
+        (parts_hbm, mixed_hbm, ow_hbm), (gate_parts, mixed_ref, ow_ref), brought
+    )
 
     @pl.when(step == 0)
     def _():
+        bring.start()
         meet(True, "near")
         line.start()
         plane.start()
-        total[...] = jnp.zeros_like(total)
-
-    total[...] += contract_first(two_ref[...], d_ups_ref[...])
-
-    @pl.when(step == PLANE - 3)
+        total[...] = contract_first(two_ref[...], d_ups_ref[...])
+
+    @pl.when(step > 0)
+    def _():
+        total[...] += contract_first(two_ref[...], d_ups_ref[...])
+
+    @pl.when(step == 3)
     def _():
         plane.relay(0)
+
+    @pl.when(step == PLANE - 2)
+    def _():
+        plane.relay(1)
+
+    @pl.when(step == PLANE - 1)
+    def _():
+        bring.wait(0, 1, 2)
         line.forward()
 
-    @pl.when(step == PLANE - 1)
-    def _():
-        plane.relay(1)
+        def add(owner, start=False):
+            at = pl.ds(pl.multiple_of(owner * rows, rows), rows)
+            d_mixed_out[at, :] = contract_last(full[owner], ow_ref[...])
+            value = contract_first(mixed_ref[at, :], full[owner])
+            out_total[...] = value if start else out_total[...] + value
+
+        plane.beside()
+        add(plane.side, start=True)
         to_parts(total, up_parts)
         plane.rest()
-        plane.end()
-        outward.start()
-        out_total[...] = contract_first(full[0], mixed_ref[0:rows, :])
-
-        def add(b, unused):
-            at = pl.ds(pl.multiple_of(b * rows, rows), rows)
-            out_total[...] += contract_first(full[b], mixed_ref[at, :])
-            return unused
-
-        lax.fori_loop(1, PLANE, add, 0)
-        to_parts(out_total, out_parts)
+        add(plane.x)
+        add(plane.y)
+        plane.far_side()
+        add(plane.far)
+        plane.end(beside=False)
+        add(plane.h)
+        add(across_of(plane.side))
+        add(along_of(plane.side))
+        add(across_of(along_of(plane.side)))
+        kept = out_parts.shape[1]
+        to_turned_parts(out_total, out_parts, ((0, 0, kept),))
 
         def write(at, value):
             gate_out[at, :] = value
 
         line.finish(write)
-        outward.wait()
-
-
-def turn(two_group, d_ups, gate_parts, block, mixed):
+
+
+def turn(two_group, d_ups, gate_parts, block, mixed, ow, kept):
     length, width = two_group.shape
     units, chans = d_ups.shape[1], mixed.shape[1]
     rows, share = length // PLANE, width // LINE
@@ -1483,22 +1681,23 @@
         turn_body,
         grid=(PLANE,),
         in_specs=[
-            tile(width), tile(units), once(gate_parts.shape), ANYWHERE, once(mixed.shape)
+            tile(width), tile(units), ANYWHERE, ANYWHERE, ANYWHERE, ANYWHERE,
         ],
         out_specs=[
-            once(gate_parts.shape), once((LINE, share, chans)), once((share, units)), ANYWHERE
+            once(gate_parts.shape), once((LINE, kept, share)), once((share, units)),
+            once((length, chans)),
         ],
         out_shape=[
             jax.ShapeDtypeStruct(gate_parts.shape, jnp.bfloat16),
-            jax.ShapeDtypeStruct((LINE, share, chans), jnp.bfloat16),
+            jax.ShapeDtypeStruct((LINE, kept, share), jnp.bfloat16),
             jax.ShapeDtypeStruct((share, units), jnp.float32),
-            jax.ShapeDtypeStruct((PLANE, rows, width), jnp.bfloat16),
+            jax.ShapeDtypeStruct((length, chans), jnp.float32),
         ],
         scratch_shapes=[
+            *held(gate_parts, mixed, ow),
             pltpu.VMEM((PLANE, rows, width), jnp.bfloat16),
             pltpu.VMEM((width, units), jnp.float32),
-            pltpu.VMEM((width, chans), jnp.float32),
-            pltpu.SemaphoreType.DMA,
+            pltpu.VMEM((chans, width), jnp.float32),
             *LineReduce.buffers(share, units),
             *LineReduce.semaphores,
             *PlaneGather.semaphores,
@@ -1507,7 +1706,7 @@
             collective_id=5, has_side_effects=True, vmem_limit_bytes=61 * 2**20
         ),
         name="turn",
-    )(two_group, d_ups, gate_parts, block, mixed)
+    )(two_group, d_ups, gate_parts, block, mixed, ow)
 
 
 def pack_small(head_width, taps, vec, params, wr, we, small):
@@ -1536,6 +1735,8 @@
     left = lax.broadcasted_iota(jnp.int32, (8, columns), 1) < head_width
     rest = jnp.where(left, pltpu.roll(rate, columns - head_width, 1), entry).astype(jnp.bfloat16)
     small[here : here + 16, :] = jnp.concatenate([rest, tail], axis=0)
+    if small.shape[0] > here + 16:
+        small[here + 16 :, :] = jnp.zeros_like(small[here + 16 :, :])
 
 
 def split_gains(mix, ffn, out):
@@ -1553,143 +1754,179 @@
 
 def backward_linked_body(
     head_width,
-    d_res_ref, xy_ref, ow_ref, taps_ref, vec_ref, wr_ref, we_ref, keep_ref,
-    u_ref, u_prev_ref, by_ref, before_ref, states_ref, normed_ref, up_parts, out_parts,
-    x_ref, gain_ref, d_residual_ref, ffn_gain_ref,
+    d_mixed_ref, xy_hbm, taps_ref, vec_ref, wr_ref, we_ref, keep_ref,
+    u_ref, u_prev_ref, by_ref, before_ref, states_ref, normed_ref, up_hbm, out_hbm,
+    x_hbm, gain_ref, d_residual_hbm, ffn_gain_ref,
     xy_parts, up_out, out_out, in_grad, gains_out, small_out,
-    taps_sum, vec_sum, wr_sum, we_sum, small, gathered, d_xy, xy_total, eight, *rest,
+    xy_ref, up_parts, out_parts, brought, late,
+    out_sum, taps_sum, vec_sum, wr_sum, we_sum, small, small_parts, d_xy, d_all, xy_total, eight, *rest,
 ):
-    scratch, links = rest[:11], rest[11:]
+    scratch, links = rest[:10], rest[10:]
     step = pl.program_id(0)
     block = PLANE - 1 - step
-    line = LineReduce(up_parts, *links[:5])
-    out_line = LineReduce(out_parts, *links[5:10])
-    small_line = LineGather(small, gathered, *links[10:13])
-    plane = PlaneReduce(*links[13:])
+    line = LineReduce(up_hbm, up_parts, *links[:5])
+    out_line = LineReduce(out_hbm, out_parts, *links[5:10])
+    small_line = LineReduce(small_parts, small_parts, *links[10:15])
+    plane = PlaneReduce(*links[15:])
+
+    bring = Bring(
+        (xy_hbm, up_hbm, out_hbm), (xy_ref, up_parts, out_parts), brought
+    )
+    d_residual_ref = xy_total.at[0 : x_hbm.shape[0]]
+    bring_late = Bring((x_hbm, d_residual_hbm), (in_grad, d_residual_ref), late)
 
     @pl.when(step == 0)
     def _():
+        bring.start()
         meet(True, "near")
         line.start()
         out_line.start()
-        xy_total[...] = jnp.zeros_like(xy_total)
-
-    @pl.when(step > 0)
-    def _():
-        plane.pass_on(block + 1)
-
-    @pl.when(step > 2)
+        bring.wait(0, 1, 2)
+
+    @pl.when((step > 2) & (step <= PLANE))
     def _():
         plane.relay(block + 3)
 
-    value = backward_step(
-        d_res_ref, xy_ref, ow_ref, taps_ref, vec_ref, wr_ref, we_ref, keep_ref,
-        u_ref, u_prev_ref, by_ref, before_ref, states_ref, d_xy,
-        taps_sum, vec_sum, wr_sum, we_sum, *scratch,
-    )
-    plane.put(block, value)
-    xy_total[...] += contract_first(normed_ref[...], d_xy[...])
-
     @pl.when(step == 4)
     def _():
         line.forward()
 
-    @pl.when(step == PLANE - 1)
-    def _():
-        plane.relay(block + 2)
-        plane.pass_on(block)
+    @pl.when(step < PLANE)
+    def _():
+        backward_step(
+            step == 0, step == PLANE - 1, d_mixed_ref, taps_ref, vec_ref, wr_ref, we_ref,
+            keep_ref, u_ref, u_prev_ref, by_ref, before_ref, states_ref, d_xy,
+            taps_sum, vec_sum, wr_sum, we_sum, *scratch,
+        )
+        d_all[step] = d_xy[...]
+
+        @pl.when(step > 0)
+        def _():
+            plane.pass_on(block + 1)
+
+        plane.put(block, dot_plain(d_xy[...], xy_ref[...]).astype(jnp.bfloat16))
+
+    @pl.when(step == PLANE)
+    def _():
         pack_small(head_width, taps_sum, vec_sum, vec_ref, wr_sum, we_sum, small)
+        share = small_parts.shape[1]
+        for t in range(LINE):
+            small_parts[t] = small[t * share : (t + 1) * share, :]
         small_line.start()
-        plane.relay(block + 1)
-        to_parts(xy_total, xy_parts)
-        plane.relay(block)
+        xy_total[...] = contract_first(d_all[0], normed_ref[...])
+
+    @pl.when(step == PLANE)
+    def _():
+        plane.pass_on(0)
+
+    @pl.when(step > PLANE)
+    def _():
+        xy_total[...] += contract_first(d_all[step - PLANE], normed_ref[...])
+
+    @pl.when(step == PLANE + 2)
+    def _():
+        plane.relay(1)
+
+    @pl.when(step == PLANE + 4)
+    def _():
         out_line.forward()
+
+    @pl.when(step == PLANE + 5)
+    def _():
+        plane.relay(0)
+
+    @pl.when(step == 2 * PLANE - 1)
+    def _():
         small_line.forward()
+        kept, chans = out_parts.shape[1], d_xy.shape[1] // 2
+        to_turned_parts(xy_total, xy_parts, ((0, 0, kept), (chans, kept, kept)))
+        bring_late.start()
         plane.arrive()
+        bring_late.wait(0, 1)
         eight[...] = jnp.zeros_like(eight)
 
         def back(i, unused):
             at = pl.ds(pl.multiple_of(i * CHUNK, CHUNK), CHUNK)
             d_rows, d_gain = norm_back(
-                x_ref[at, :].astype(jnp.float32), gain_ref[...], plane.total(at)
+                in_grad[at, :].astype(jnp.float32), gain_ref[...], plane.total(at)
             )
-            in_grad[at, :] = (d_residual_ref[at, :] + d_rows).astype(jnp.bfloat16)
+            in_grad[at, :] = (xy_total[at, :] + d_rows).astype(jnp.bfloat16)
             eight[...] += sum_eight(d_gain)
             return unused
 
-        lax.fori_loop(0, x_ref.shape[0] // CHUNK, back, 0)
+        lax.fori_loop(0, in_grad.shape[0] // CHUNK, back, 0)
         split_gains(jnp.sum(eight[...], axis=0, keepdims=True), ffn_gain_ref[...], gains_out)
 
         def write(at, value):
             up_out[at, :] = value
 
         def write_out(at, value):
-            out_out[at, :] = value
+            out_sum[at, :] = value
+
+        def write_small(at, value):
+            small_out[at, :] = value.astype(jnp.bfloat16)
 
         line.finish(write)
         out_line.finish(write_out)
-        small_line.finish()
-
-        def add_small(i, unused):
-            at = pl.ds(pl.multiple_of(i * CHUNK, CHUNK), CHUNK)
-            total = gathered[0, at, :].astype(jnp.float32)
-            for t in range(1, LINE):
-                total = total + gathered[t, at, :].astype(jnp.float32)
-            small_out[at, :] = total
-            return unused
-
-        lax.fori_loop(0, small.shape[0] // CHUNK, add_small, 0)
+        out_out[...] = out_sum[0 : out_out.shape[0], :]
+        small_line.finish(write_small)
         plane.finish()
 
 
 def backward_linked(
-    d_res, xy, ow, taps, vec, wr, we, keep, u, by, before, states, normed, up_parts, out_parts,
-    layer_in, gain, d_residual, ffn_gain, head_width,
+    d_mixed, xy, taps, vec, wr, we, keep, u, by, before, states, normed, up_parts, out_parts,
+    layer_in, gain, d_residual, ffn_gain, head_width, used,
 ):
-    length, width = d_res.shape
-    chans, units = ow.shape[1], up_parts.shape[2]
+    length, width = normed.shape
+    chans, units = d_mixed.shape[1], up_parts.shape[2]
     rows, share = length // PLANE, width // LINE
-    tile = lambda columns: pl.BlockSpec((rows, columns), lambda i: (PLANE - 1 - i, 0))
-    ahead = pl.BlockSpec(
-        (16, chans), lambda i: (jnp.maximum((PLANE - 1 - i) * (rows // 16) - 1, 0), 0)
-    )
-    small = ((2 * head_width + 7) // 8 * 8 // 16 * 16 + 16, chans)
+    kept = out_parts.shape[1]
+    place = lambda i: PLANE - 1 - jnp.minimum(i, PLANE - 1)
+    tile = lambda columns: pl.BlockSpec((rows, columns), lambda i: (place(i), 0))
+    later = lambda columns: pl.BlockSpec(
+        (rows, columns), lambda i: (PLANE - 1 - jnp.maximum(i - PLANE, 0), 0)
+    )
+    ahead = pl.BlockSpec((16, chans), lambda i: (jnp.maximum(place(i) * (rows // 16) - 1, 0), 0))
+    small_share = -(-((2 * head_width + 7) // 8 * 8 + 8) // (LINE * 32)) * 32
     gain_terms = (LINE, PLANE, width // (LINE * PLANE) * 2)
     return pl.pallas_call(
         functools.partial(backward_linked_body, head_width),
-        grid=(PLANE,),
+        grid=(2 * PLANE,),
         in_specs=[
-            tile(width), once(xy.shape), once(ow.shape), once(taps.shape),
-            once(vec.shape), once(wr.shape), once(we.shape), tile(keep.shape[1]),
-            tile(chans), ahead, tile(chans), tile(chans), tile(chans), tile(width),
-            once(up_parts.shape), once(out_parts.shape), once(layer_in.shape), once(gain.shape), once(d_residual.shape), once(ffn_gain.shape),
+            tile(chans), ANYWHERE, once(taps.shape), once(vec.shape), once(wr.shape),
+            once(we.shape), tile(keep.shape[1]), tile(chans), ahead, tile(chans), tile(chans),
+            tile(chans), later(width), ANYWHERE, ANYWHERE,
+            ANYWHERE, once(gain.shape), ANYWHERE, once(ffn_gain.shape),
         ],
         out_specs=[
-            once((LINE, share, 2 * chans)), once((share, units)), once((share, chans)),
-            once((rows, width)), once(gain_terms), once(small),
+            once((LINE, 2 * kept, share)), once((share, units)), once((used, share)),
+            once((rows, width)), once(gain_terms), once((small_share, chans)),
         ],
         out_shape=[
-            jax.ShapeDtypeStruct((LINE, share, 2 * chans), jnp.bfloat16),
+            jax.ShapeDtypeStruct((LINE, 2 * kept, share), jnp.bfloat16),
             jax.ShapeDtypeStruct((share, units), jnp.float32),
-            jax.ShapeDtypeStruct((share, chans), jnp.float32),
+            jax.ShapeDtypeStruct((used, share), jnp.float32),
             jax.ShapeDtypeStruct((rows, width), jnp.bfloat16),
             jax.ShapeDtypeStruct(gain_terms, jnp.float32),
-            jax.ShapeDtypeStruct(small, jnp.float32),
+            jax.ShapeDtypeStruct((small_share, chans), jnp.bfloat16),
         ],
         scratch_shapes=[
+            *held(xy, up_parts, out_parts),
+            pltpu.SemaphoreType.DMA((2,)),
+            pltpu.VMEM((kept, share), jnp.float32),
             pltpu.VMEM(taps.shape, jnp.float32),
             pltpu.VMEM(vec.shape, jnp.float32),
             pltpu.VMEM(wr.shape, jnp.float32),
             pltpu.VMEM(we.shape, jnp.float32),
-            pltpu.VMEM(small, jnp.bfloat16),
-            pltpu.VMEM((LINE,) + small, jnp.bfloat16),
+            pltpu.VMEM((LINE * small_share, chans), jnp.bfloat16),
+            pltpu.VMEM((LINE, small_share, chans), jnp.bfloat16),
             pltpu.VMEM((rows, 2 * chans), jnp.bfloat16),
-            pltpu.VMEM((width, 2 * chans), jnp.float32),
+            pltpu.VMEM((PLANE, rows, 2 * chans), jnp.bfloat16),
+            pltpu.VMEM((2 * chans, width), jnp.float32),
             pltpu.VMEM((8, width), jnp.float32),
             pltpu.VMEM((rows + 8, chans), jnp.float32),
             pltpu.VMEM((rows, chans), jnp.float32),
             pltpu.VMEM((rows, chans), jnp.bfloat16),
-            pltpu.VMEM((rows, chans), jnp.float32),
             pltpu.VMEM((rows, chans), jnp.float32),
             pltpu.VMEM((rows, chans), jnp.float32),
             pltpu.VMEM((rows + 8, chans), jnp.float32),
@@ -1699,9 +1936,10 @@
             pltpu.VMEM((64, chans), jnp.float32),
             *LineReduce.buffers(share, units),
             *LineReduce.semaphores,
-            *LineReduce.buffers(share, chans),
+            *LineReduce.buffers(kept, share),
             *LineReduce.semaphores,
-            *LineGather.semaphores,
+            *LineReduce.buffers(small_share, chans),
+            *LineReduce.semaphores,
             *PlaneReduce.buffers(rows, width),
             *PlaneReduce.semaphores,
         ],
@@ -1710,21 +1948,23 @@
         ),
         name="mixer_backward_linked",
     )(
-        d_res, xy, ow, taps, vec, wr, we, keep, u, u, by, before, states, normed,
+        d_mixed, xy, taps, vec, wr, we, keep, u, u, by, before, states, normed,
         up_parts, out_parts, layer_in, gain, d_residual, ffn_gain,
     )
 
 
 def close_body(
-    hidden_ref, down_ref, xy_parts, residual_ref, gains_ref,
-    layer_out, xy_out, gains_out,
-    line_gains, both_gains, plane_gains,
+    hidden_ref, down_hbm, xy_hbm, residual_hbm, gains_ref, small,
+    layer_out, x_out, y_out, gains_out, small_out,
+    down_ref, xy_parts, residual_ref, brought, xy_sum,
+    gathered, line_gains, both_gains, plane_gains,
     gain_sent, gain_arrived, wide_sent, wide_arrived, *links,
 ):
     r, h = lax.axis_index("row"), lax.axis_index("head")
     step = pl.program_id(0)
-    xy_line = LineReduce(xy_parts, *links[0:5])
-    plane = PlaneReduce(*links[5:])
+    xy_line = LineReduce(xy_hbm, xy_parts, *links[0:5])
+    small_line = LineGather(small, lambda t: gathered.at[t], *links[5:8])
+    plane = PlaneReduce(*links[8:])
 
     def to_row(t, owner):
         return send_to(
@@ -1738,12 +1978,19 @@
             "head", lax.rem(h + place, PLANE),
         )
 
+    bring = Bring(
+        (down_hbm, xy_hbm, residual_hbm), (down_ref, xy_parts, residual_ref), brought
+    )
+
     @pl.when(step == 0)
     def _():
+        bring.start()
         meet(True, "all")
         for place in range(1, LINE):
             to_row(lax.rem(r + place, LINE), r).start()
+        small_line.start()
         xy_line.start()
+        bring.wait(0, 1, 2)
 
     @pl.when(step > 0)
     def _():
@@ -1768,11 +2015,12 @@
 
     @pl.when(step == PLANE - 1)
     def _():
+        small_line.forward()
+        xy_line.forward()
         plane.relay(far_first(step - 2))
         plane.pass_on(far_first(step))
         plane.relay(far_first(step - 1))
         plane.relay(far_first(step))
-        xy_line.forward()
         total = both_gains[...]
         for place in range(1, PLANE):
             owner = lax.rem(h + place, PLANE)
@@ -1789,9 +2037,14 @@
 
         lax.fori_loop(0, residual_ref.shape[0] // CHUNK, make, 0)
         def write(at, value):
-            xy_out[at, :] = value
+            xy_sum[at, :] = value
 
         xy_line.finish(write)
+        used, kept = x_out.shape[0], xy_sum.shape[0] // 2
+        x_out[...] = xy_sum[0:used, :]
+        y_out[...] = xy_sum[kept : kept + used, :]
+        small_line.finish()
+        small_out[...] = gathered[...].astype(jnp.float32)
         plane.finish()
         for place in range(1, LINE):
             to_row(lax.rem(r + place, LINE), r).wait_send()
@@ -1799,26 +2052,32 @@
             over_plane(place, h).wait_send()
 
 
-def close_block(hidden, down, xy_parts, residual, gains):
+def close_block(hidden, down, xy_parts, residual, gains, small, used):
     length, units = hidden.shape
     rows, width = residual.shape
-    share, columns = xy_parts.shape[1:]
+    both, share = xy_parts.shape[1:]
     return pl.pallas_call(
         close_body,
         grid=(PLANE,),
         in_specs=[
-            pl.BlockSpec((rows, units), lambda i: (far_first(i), 0)), once(down.shape),
-            once(xy_parts.shape), once(residual.shape), once(gains.shape),
+            pl.BlockSpec((rows, units), lambda i: (far_first(i), 0)), ANYWHERE,
+            ANYWHERE, ANYWHERE, once(gains.shape), once(small.shape),
         ],
         out_specs=[
-            once((rows, width)), once((share, columns)), once((1, gains.shape[2])),
+            once((rows, width)), once((used, share)), once((used, share)), once((1, gains.shape[2])),
+            once((LINE,) + small.shape),
         ],
         out_shape=[
             jax.ShapeDtypeStruct((rows, width), jnp.bfloat16),
-            jax.ShapeDtypeStruct((share, columns), jnp.float32),
+            jax.ShapeDtypeStruct((used, share), jnp.float32),
+            jax.ShapeDtypeStruct((used, share), jnp.float32),
             jax.ShapeDtypeStruct((1, gains.shape[2]), jnp.float32),
+            jax.ShapeDtypeStruct((LINE,) + small.shape, jnp.float32),
         ],
         scratch_shapes=[
+            *held(down, xy_parts, residual),
+            pltpu.VMEM((both, share), jnp.float32),
+            pltpu.VMEM((LINE,) + small.shape, jnp.bfloat16),
             pltpu.VMEM(gains.shape, jnp.float32),
             pltpu.VMEM(gains.shape[1:], jnp.float32),
             pltpu.VMEM((PLANE,) + gains.shape[1:], jnp.float32),
@@ -1826,14 +2085,15 @@
             pltpu.SemaphoreType.DMA((LINE,)),
             pltpu.SemaphoreType.DMA((PLANE,)),
             pltpu.SemaphoreType.DMA((PLANE,)),
-            *LineReduce.buffers(share, columns), *LineReduce.semaphores,
+            *LineReduce.buffers(both, share), *LineReduce.semaphores,
+            *LineGather.semaphores,
             *PlaneReduce.buffers(rows, width), *PlaneReduce.semaphores,
         ],
         compiler_params=pltpu.CompilerParams(
             collective_id=7, has_side_effects=True, vmem_limit_bytes=61 * 2**20
         ),
         name="close_block",
-    )(hidden, down, xy_parts, residual, gains)
+    )(hidden, down, xy_parts, residual, gains, small)
 
 
 def mixer_params(
@@ -1886,8 +2146,8 @@
     mix_full = gather(mix_gain, ("row", "head"), 0)
     ffn_full = gather(ffn_gain, ("row", "head"), 0)
     xy_shard = jnp.concatenate([widen(x_weight), widen(y_weight)], axis=1)
-    xy_rows = gather(xy_shard, "row", 0)
-    out_rows = gather(widen(out_weight), "row", 0)
+    xy_rows = gather(xy_shard, "row", 0).T
+    out_rows = gather(widen(out_weight), "row", 0).T
     gate_rows = gather(gate_weight, "row", 0)
     up_rows = gather(up_weight, "row", 0)
     down_rows = gather(down_weight, "row", 0)
@@ -1984,24 +2244,26 @@
 ):
     heads, head_width = rate_weight.shape[:2]
     used = conv_bias.shape[0]
-    chans = -(-used // 128) * 128
-    widen = lambda values: jnp.pad(values, ((0, 0), (0, chans - used)))
+    kept = -(-used // 16) * 16
     flat = lambda values: values.reshape((-1, values.shape[-1]))
-    taps, vec, wr, we = mixer_params(
-        conv_weight, conv_bias, rate_weight, rate_bias, entry_weight, entry_bias, decay_param, chans
-    )
-    keep = keep_columns(resets)
-    own_gains = jnp.concatenate([mix_gain, ffn_gain]).astype(jnp.float32)
-    tile = jnp.broadcast_to(own_gains, (8, own_gains.shape[0]))
-
-    normed_group, cot_half, xy_rows, out_rows, gains = open_block(
+    line = lambda values: values.reshape(1, -1)
+    normed_group, cot_half, xy_rows, out_rows, gains, taps, vec, wr, we, keep = open_block(
         layer_in,
-        tile,
+        (line(mix_gain), line(ffn_gain)),
         cotangent,
-        jnp.concatenate([widen(x_weight), widen(y_weight)], axis=1),
-        widen(out_weight),
-    )
-    normed_group, xy_rows, out_rows = map(flat, (normed_group, xy_rows, out_rows))
+        (x_weight.T, y_weight.T, out_weight.T),
+        (
+            conv_weight,
+            line(conv_bias),
+            line(rate_bias),
+            line(entry_bias),
+            line(decay_param),
+            rate_weight,
+            entry_weight,
+            resets,
+        ),
+    )
+    normed_group = flat(normed_group)
     u, by, before, states, mixed, residual, normed_two, gate_rows, up_half = forward_linked(
         normed_group, xy_rows, out_rows, taps, vec, wr, we, keep, layer_in, gains[1:2],
         gate_weight, up_weight,
@@ -2010,36 +2272,34 @@
     two_group, cot_group, up_rows, down_rows, gates, ups, hidden, down_parts = ffn_up(
         normed_two, gate_rows, cotangent, cot_half, up_half, up_weight, down_weight
     )
-    two_group, cot_group, up_rows, down_rows = map(
-        flat, (two_group, cot_group, up_rows, down_rows)
-    )
+    two_group, cot_group, down_rows = map(flat, (two_group, cot_group, down_rows))
     d_ups, gate_parts, down_grad, d_residual, d_low, d_ffn_gain = ffn_back(
         cot_group, two_group, gates, ups, gate_rows, up_rows, down_rows, down_parts, residual,
         cotangent, gains[1:2],
     )
-    up_parts, out_parts, gate_grad, d_res_group = turn(
-        two_group, d_ups, gate_parts, d_low, mixed
-    )
-    xy_parts, up_grad, out_grad, layer_in_grad, gain_terms, sums = backward_linked(
-        flat(d_res_group), xy_rows, out_rows, taps, vec, wr, we, keep, u, by, before, states,
+    up_parts, out_parts, gate_grad, d_mixed = turn(
+        two_group, d_ups, gate_parts, d_low, mixed, out_rows, kept
+    )
+    xy_parts, up_grad, out_grad, layer_in_grad, gain_terms, small = backward_linked(
+        d_mixed, xy_rows, taps, vec, wr, we, keep, u, by, before, states,
         normed_group, up_parts, out_parts, layer_in, gains[0:1], d_residual, d_ffn_gain,
-        head_width,
-    )
-    layer_out, xy_grad, gain_grads = close_block(
-        hidden, down_rows, xy_parts, residual, gain_terms
-    )
+        head_width, used,
+    )
+    layer_out, x_grad, y_grad, gain_grads, sums = close_block(
+        hidden, down_rows, xy_parts, residual, gain_terms, small, used
+    )
+    sums = flat(sums)
     share = mix_gain.shape[0]
     ends = -(-used // 8) * 8
     gates_end = heads * head_width
-    wide = lambda values: values[:, :used]
     return (
         layer_out,
         layer_in_grad,
         gain_grads[0, :share],
         gain_grads[0, share:],
-        wide(xy_grad),
-        wide(xy_grad[:, chans:]),
-        wide(out_grad),
+        x_grad.T,
+        y_grad.T,
+        out_grad.T,
         sums[ends : ends + 4, :used],
         sums[ends + 4, :used],
         sums[:gates_end, :head_width].reshape(heads, head_width, head_width),

time: 640 us -> 584 us (0.912)
  Pallas kernels: 598 us -> 546 us
    pallas_call x1, Pallas kernels: 106 us -> 86.3 us  [ffn_up(): pl.pallas_call(ffn_up_body, in_specs=[IN_VMEM, IN_VMEM] + [ANYWHERE] * 5,...]
    pallas_call x2, Pallas kernels: 162 us -> 146 us  [the longest x1 82.2 us: open_block(): pl.pallas_call(open_body, in_specs=[IN_VMEM, IN_VMEM, IN_VMEM, ANYWHERE]...]
    pallas_call x1, Pallas kernels: 67.3 us -> 57 us  [close_block(): pl.pallas_call(close_body, grid=(PLANE,), in_specs=[pl.BlockSpec((rows, u...]
    pallas_call x1, Pallas kernels: 111 us -> 102 us  [backward_linked(): pl.pallas_call(functools.partial(backward_linked_body, head_width), grid=...]
    unnamed x37 -> x28, local copies, waits for them, and re-layouts: 13 us -> 13.2 us
where the time goes in v6:
time: 584 us; the launch traced here: 572 us
  Pallas kernels  546 us (93%)
  local copies, waits for them, and re-layouts  25 us (4%)
    pallas_call x1, Pallas kernels, backward_linked(): pl.pallas_call(functools.partial(backward_linked_body, head_width), grid=...  102 us
    pallas_call x1, Pallas kernels, ffn_up(): pl.pallas_call(ffn_up_body, in_specs=[IN_VMEM, IN_VMEM] + [ANYWHERE] * 5,...  86.3 us
    pallas_call x1, Pallas kernels, forward_linked(): pl.pallas_call(forward_linked_body, grid=(PLANE,), in_specs=[tile(width),...  82.4 us
    pallas_call x1, Pallas kernels, open_block(): pl.pallas_call(open_body, in_specs=[IN_VMEM, IN_VMEM, IN_VMEM, ANYWHERE]...  82.2 us
    pallas_call x1, Pallas kernels, turn(): pl.pallas_call(turn_body, grid=(PLANE,), in_specs=[tile(width), tile(unit...  71.7 us
    pallas_call x1, Pallas kernels, ffn_back(): pl.pallas_call(ffn_back_body, grid=(2 * PLANE,), in_specs=[tile(width), l...  63.8 us
    pallas_call x1, Pallas kernels, close_block(): pl.pallas_call(close_body, grid=(PLANE,), in_specs=[pl.BlockSpec((rows, u...  57 us
    unnamed x28, local copies, waits for them, and re-layouts  13.2 us

profile of v6, /device:TPU:0, one launch (start us, length us, event | category | flops | bytes accessed | tf_op | source)
XLA Modules:
  0.0 571.9 jit_solution(1326981365067345990)
XLA Ops:
  0.7 1.2 reshape.78.conv_bias
  1.9 1.2 reshape.79.rate_bias
  3.1 1.2 reshape.80.entry_bias
  4.4 1.2 reshape.81.decay_ref
  5.6 1.6 copy.37.rate_ref
  7.2 1.6 copy.38.entry_ref
  8.9 82.2 %open_block.1 = (bf16[8,256,2048]{2,1,0:T(8,128)(2,1)}, bf16[8,256,1024]{2,1,0:T(8,128)(2,1)}, bf16[768,2048]{1,0:T(8,128)(2,1)}, bf16[384,2048]{1,0:T(8,128)(2,...) custom-call(bf16[256,2048]{1,0:T(8,128)(2,1)} %x_hbm.3, ...), custom_call_target="tpu_custom_call" | custom-call | tf_op jit(solution)/shard_map/open_block/pallas_call | solution.py:1123
  91.0 1.4 fusion.1
  92.4 82.4 %mixer_forward_linked.1 = (bf16[2048,384]{1,0:T(8,128)(2,1)}, f32[2048,384]{1,0:T(8,128)}, f32[2048,384]{1,0:T(8,128)}, bf16[2048,384]{1,0:T(8,128)(2,1)}, bf16[...) custom-call(bf16[2048,2048]{1,0:T(8,128)(2,1)} %bitcast.18, ...), custom_call_target="tpu_custom_call" | custom-call | tf_op jit(solution)/shard_map/mixer_forward_linked/pallas_call | solution.py:1232
  174.9 86.3 %ffn_up.1 = (bf16[8,256,2048]{2,1,0:T(8,128)(2,1)}, bf16[8,256,2048]{2,1,0:T(8,128)(2,1)}, bf16[2048,768]{1,0:T(8,128)(2,1)}, bf16[4,512,768]{2,1,0:T(8,128)(2,1...) custom-call(bf16[256,2048]{1,0:T(8,128)(2,1)} %get-tuple-element.74.own, ...), custom_call_target="tpu_custom_call" | custom-call | tf_op jit(solution)/shard_map/ffn_up/pallas_call | solution.py:1387
  261.2 63.8 %ffn_back.1 = (bf16[2048,768]{1,0:T(8,128)(2,1)}, bf16[4,512,768]{2,1,0:T(8,128)(2,1)}, f32[512,768]{1,0:T(8,128)}, f32[256,2048]{1,0:T(8,128)}, bf16[256,2048]{1,0:T(8,128)(2,1)}, /*index=5*/f32[1,2048]{1,0:T(1,128)}) custom-call(bf16[2048,2048]{1,0:T(8,128)(2,1)} %bitcast.26, bf16[2048,2048]{1,0:T(8,128)(2,1)} %bitcast.20, ...), custom_call_target="tpu_custom_call" | custom-call | tf_op jit(solution)/shard_map/ffn_back/pallas_call | solution.py:1569
  324.9 71.7 %turn.1 = (bf16[4,512,768]{2,1,0:T(8,128)(2,1)}, bf16[4,352,512]{2,1,0:T(8,128)(2,1)}, f32[512,768]{1,0:T(8,128)}, f32[2048,384]{1,0:T(8,128)}) custom-call(bf16[2048,2048]{1,0:T(8,128)(2,1)} %bitcast.21, bf16[2048,768]{1,0:T(8,128)(2,1)} %get-tuple-element.87.d_ups_ref, bf16[4,512,768]{2,1,0:T(8,128)(2,1)} %get-tuple-element.88.parts_hbm, ...), custom_call_target="tpu_custom_call" | custom-call | tf_op jit(solution)/shard_map/turn/pallas_call | solution.py:1680
  396.6 102.4 %mixer_backward_linked.1 = (bf16[4,704,512]{2,1,0:T(8,128)(2,1)}, f32[512,768]{1,0:T(8,128)}, f32[342,512]{1,0:T(8,128)}, bf16[256,2048]{1,0:T(8,128)(2,1)}, f32...) custom-call(f32[2048,384]{1,0:T(8,128)} %get-tuple-element.91.d_mixed_ref, bf16[768,2048]{1,0:T(8,128)(2,1)} %get-tuple-element.66.xy_hbm, ...), custom_call_target="tpu_custom_call" | custom-call | tf_op jit(solution)/shard_map/mixer_backward_linked/pallas_call | solution.py:1892
  499.0 57.0 %close_block.1 = (bf16[256,2048]{1,0:T(8,128)(2,1)}, f32[342,512]{1,0:T(8,128)}, f32[342,512]{1,0:T(8,128)}, f32[1,128]{1,0:T(1,128)}, f32[4,96,384]{2,1,0:T(8,128)}) custom-call(bf16[2048,768]{1,0:T(8,128)(2,1)} %get-tuple-element.78.hidden_ref, bf16[2048,768]{1,0:T(8,128)(2,1)} %bitcast.23, bf16[4,704,512]{2,1,0:T(8,128)(2,1)} %get-tuple-element.100.xy_hbm, ...), custom_call_target="tpu_custom_call" | custom-call | tf_op jit(solution)/shard_map/close_block/pallas_call | solution.py:2059
  556.1 1.3 slice_bitcast_fusion
  557.3 1.3 slice.45
  558.6 1.5 slice_reduce_fusion
  560.1 1.3 fusion
  561.5 1.0 copy.42
  562.5 1.0 copy.41
  563.6 1.0 copy.55
  568.1 1.1 copy.60
  569.2 1.1 copy.61
  570.4 1.1 copy.62
  (22 shorter events, 3.6 us)
Async XLA Ops:
  556.1 7.5 %copy-start.4 = (bf16[256,2048]{1,0:T(8,128)(2,1)S(1)}, bf16[256,2048]{1,0:T(8,128)(2,1)}, u32[]{:S(2)}) copy-start(bf16[256,2048]{1,0:T(8,128)(2,1)} %get-tuple-element.157) | copy-start | bytes 3145732
  560.1 4.4 copy-start.3
  562.5 3.0 copy-start.7
  562.5 3.8 copy-start.6
  563.5 3.7 copy-start.5
  564.5 3.5 copy-start.1
  566.4 2.9 copy-start.2
  568.1 2.3 copy-start

commit v7 on v6

--- a/solution.py
+++ b/solution.py
@@ -955,27 +955,25 @@
 
 
 def lay_out_params(
-    taps_ref, biases, decay_ref, rate_ref, entry_ref, resets_ref,
+    taps_ref, rows_ref, gates_ref, resets_ref,
     taps_out, vec_out, wr_out, we_out, keep_out, square, moved,
 ):
-    used, width = decay_ref.shape[1], rate_ref.shape[1]
+    used, width = rows_ref.shape[1], gates_ref.shape[2]
     columns = vec_out.shape[1]
     taps_out[...] = jnp.zeros_like(taps_out)
     taps_out[:, 0:used] = taps_ref[...]
     vec_out[...] = jnp.zeros_like(vec_out)
-    for k, bias in enumerate(biases):
-        vec_out[k : k + 1, 0:used] = bias[...]
     vec_out[3:4, :] = jnp.full((1, columns), 2.0, jnp.float32)
-    vec_out[3:4, 0:used] = decay_ref[...]
+    vec_out[0:4, 0:used] = rows_ref[...]
     decay = vec_out[3:4, :]
     vec_out[3:4, :] = -8.0 * jnp.log1p(jnp.exp(-decay))
     vec_out[4:5, :] = 8.0 * jax.nn.sigmoid(-decay)
-    for source, out in ((rate_ref, wr_out), (entry_ref, we_out)):
+    for k, out in enumerate((wr_out, we_out)):
         square[...] = jnp.zeros_like(square)
-        square[0:width, 0:width] = source[1].astype(jnp.float32)
+        square[0:width, 0:width] = gates_ref[k, 1].astype(jnp.float32)
         moved[...] = pltpu.roll(pltpu.roll(square[...], width, 0), width, 1)
         square[...] = jnp.zeros_like(square)
-        square[0:width, 0:width] = source[0].astype(jnp.float32)
+        square[0:width, 0:width] = gates_ref[k, 0].astype(jnp.float32)
         out[...] = (square[...] + moved[...]).astype(jnp.bfloat16)
     resets = resets_ref[...]
     first = lax.broadcasted_iota(jnp.int32, resets.shape, 1) == 0
@@ -994,7 +992,7 @@
 
 def open_body(
     x_ref, mix_ref, ffn_ref, cot, xt_ref, yt_ref, ot_ref,
-    taps_ref, conv_bias, rate_bias, entry_bias, decay_ref, rate_ref, entry_ref, resets_ref,
+    taps_ref, rows_ref, gates_ref, resets_ref,
     full, cot_out, xy_full, out_full, gains_ref, taps_out, vec_out, wr_out, we_out, keep_out,
     shards, blank, square, moved,
     normed, column, spread, gain_sent, gain_arrived, wide_sent, wide_arrived, wiped, *semaphores,
@@ -1088,7 +1086,7 @@
     lax.fori_loop(0, x_ref.shape[0] // CHUNK, make, 0)
     plane.start()
     lay_out_params(
-        taps_ref, (conv_bias, rate_bias, entry_bias), decay_ref, rate_ref, entry_ref, resets_ref,
+        taps_ref, rows_ref, gates_ref, resets_ref,
         taps_out, vec_out, wr_out, we_out, keep_out, square, moved,
     )
     cot_plane.relay(0)
@@ -1122,7 +1120,7 @@
     tile = (8, 2 * gains[0].shape[1])
     return pl.pallas_call(
         open_body,
-        in_specs=[IN_VMEM, IN_VMEM, IN_VMEM, ANYWHERE] + [IN_VMEM] * 11,
+        in_specs=[IN_VMEM, IN_VMEM, IN_VMEM, ANYWHERE] + [IN_VMEM] * 7,
         out_specs=[ANYWHERE] * 4 + [IN_VMEM] * 6,
         out_shape=[
             jax.ShapeDtypeStruct((PLANE, rows, width), jnp.bfloat16),
@@ -1783,6 +1781,10 @@
         out_line.start()
         bring.wait(0, 1, 2)
 
+    @pl.when((step > 0) & (step <= PLANE))
+    def _():
+        plane.pass_on(block + 1)
+
     @pl.when((step > 2) & (step <= PLANE))
     def _():
         plane.relay(block + 3)
@@ -1799,11 +1801,6 @@
             taps_sum, vec_sum, wr_sum, we_sum, *scratch,
         )
         d_all[step] = d_xy[...]
-
-        @pl.when(step > 0)
-        def _():
-            plane.pass_on(block + 1)
-
         plane.put(block, dot_plain(d_xy[...], xy_ref[...]).astype(jnp.bfloat16))
 
     @pl.when(step == PLANE)
@@ -1814,10 +1811,6 @@
             small_parts[t] = small[t * share : (t + 1) * share, :]
         small_line.start()
         xy_total[...] = contract_first(d_all[0], normed_ref[...])
-
-    @pl.when(step == PLANE)
-    def _():
-        plane.pass_on(0)
 
     @pl.when(step > PLANE)
     def _():
@@ -2096,6 +2089,38 @@
     )(hidden, down, xy_parts, residual, gains, small)
 
 
+def hand_over_body(*refs):
+    count = (len(refs) - 2) // 3
+    sources, targets, held = refs[:count], refs[count : 2 * count], refs[2 * count : 3 * count]
+    inward, outward = (
+        [
+            pltpu.make_async_copy(src, dst, done.at[k])
+            for k, (src, dst) in enumerate(zip(starts, ends))
+        ]
+        for starts, ends, done in ((sources, held, refs[-2]), (held, targets, refs[-1]))
+    )
+    for copy in inward:
+        copy.start()
+    for first, second in zip(inward, outward):
+        first.wait()
+        second.start()
+    for copy in outward:
+        copy.wait()
+
+
+def hand_over(*arrays):
+    return pl.pallas_call(
+        hand_over_body,
+        in_specs=[ANYWHERE] * len(arrays),
+        out_specs=[ANYWHERE] * len(arrays),
+        out_shape=[jax.ShapeDtypeStruct(item.shape, item.dtype) for item in arrays],
+        scratch_shapes=[pltpu.VMEM(item.shape, item.dtype) for item in arrays]
+        + [pltpu.SemaphoreType.DMA((len(arrays),))] * 2,
+        compiler_params=pltpu.CompilerParams(vmem_limit_bytes=61 * 2**20),
+        name="hand_over",
+    )(*arrays)
+
+
 def mixer_params(
     conv_weight, conv_bias, rate_weight, rate_bias, entry_weight, entry_bias, decay_param, chans
 ):
@@ -2254,12 +2279,8 @@
         (x_weight.T, y_weight.T, out_weight.T),
         (
             conv_weight,
-            line(conv_bias),
-            line(rate_bias),
-            line(entry_bias),
-            line(decay_param),
-            rate_weight,
-            entry_weight,
+            jnp.stack([conv_bias, rate_bias, entry_bias, decay_param]),
+            jnp.stack([rate_weight, entry_weight]),
             resets,
         ),
     )
@@ -2291,6 +2312,11 @@
     sums = flat(sums)
     share = mix_gain.shape[0]
     ends = -(-used // 8) * 8
+    (
+        layer_out, layer_in_grad, x_grad, y_grad, out_grad, gate_grad, up_grad, down_grad,
+    ) = hand_over(
+        layer_out, layer_in_grad, x_grad, y_grad, out_grad, gate_grad, up_grad, down_grad
+    )
     gates_end = heads * head_width
     return (
         layer_out,

time: 584 us -> 572 us (0.979)
  local copies, waits for them, and re-layouts: 25 us -> 9.21 us
    unnamed x28 -> x6, local copies, waits for them, and re-layouts: 13.2 us -> 2.01 us
    pallas_call x0 -> x1, Pallas kernels: none -> 7.06 us  [hand_over(): pl.pallas_call(hand_over_body, in_specs=[ANYWHERE] * len(arrays), out_spe...]
    pallas_call x1, Pallas kernels: 102 us -> 96.2 us  [backward_linked(): pl.pallas_call(functools.partial(backward_linked_body, head_width), grid=...]
where the time goes in v7:
time: 572 us; the launch traced here: 561 us
  Pallas kernels  549 us (96%)
  local copies, waits for them, and re-layouts  9.21 us (2%)
    pallas_call x1, Pallas kernels, backward_linked(): pl.pallas_call(functools.partial(backward_linked_body, head_width), grid=...  96.2 us
    pallas_call x1, Pallas kernels, ffn_up(): pl.pallas_call(ffn_up_body, in_specs=[IN_VMEM, IN_VMEM] + [ANYWHERE] * 5,...  86.3 us
    pallas_call x1, Pallas kernels, forward_linked(): pl.pallas_call(forward_linked_body, grid=(PLANE,), in_specs=[tile(width),...  82.5 us
    pallas_call x1, Pallas kernels, open_block(): pl.pallas_call(open_body, in_specs=[IN_VMEM, IN_VMEM, IN_VMEM, ANYWHERE]...  82.2 us
    pallas_call x1, Pallas kernels, turn(): pl.pallas_call(turn_body, grid=(PLANE,), in_specs=[tile(width), tile(unit...  71.6 us
    pallas_call x1, Pallas kernels, ffn_back(): pl.pallas_call(ffn_back_body, grid=(2 * PLANE,), in_specs=[tile(width), l...  63.8 us
    pallas_call x1, Pallas kernels, close_block(): pl.pallas_call(close_body, grid=(PLANE,), in_specs=[pl.BlockSpec((rows, u...  59 us

profile of v7, /device:TPU:0, one launch (start us, length us, event | category | flops | bytes accessed | tf_op | source)
XLA Modules:
  0.0 560.5 jit_solution(3624268484169983825)
XLA Ops:
  0.7 0.7 stack.24
  1.3 0.7 stack.25
  2.0 0.7 stack.26
  2.7 0.7 stack.27
  3.4 0.6 pad_maximum_fusion.1.rows_ref
  4.0 1.0 copy_bitcast_fusion
  5.0 0.8 pad_maximum_fusion.gates_ref
  5.8 82.2 %open_block.1 = (bf16[8,256,2048]{2,1,0:T(8,128)(2,1)}, bf16[8,256,1024]{2,1,0:T(8,128)(2,1)}, bf16[768,2048]{1,0:T(8,128)(2,1)}, bf16[384,2048]{1,0:T(8,128)(2,...) custom-call(bf16[256,2048]{1,0:T(8,128)(2,1)} %x_hbm.3, ...), custom_call_target="tpu_custom_call" | custom-call | tf_op jit(solution)/shard_map/open_block/pallas_call | solution.py:1121
  88.0 1.4 fusion.1
  89.4 82.5 %mixer_forward_linked.1 = (bf16[2048,384]{1,0:T(8,128)(2,1)}, f32[2048,384]{1,0:T(8,128)}, f32[2048,384]{1,0:T(8,128)}, bf16[2048,384]{1,0:T(8,128)(2,1)}, bf16[...) custom-call(bf16[2048,2048]{1,0:T(8,128)(2,1)} %bitcast.22, ...), custom_call_target="tpu_custom_call" | custom-call | tf_op jit(solution)/shard_map/mixer_forward_linked/pallas_call | solution.py:1230
  172.0 86.3 %ffn_up.1 = (bf16[8,256,2048]{2,1,0:T(8,128)(2,1)}, bf16[8,256,2048]{2,1,0:T(8,128)(2,1)}, bf16[2048,768]{1,0:T(8,128)(2,1)}, bf16[4,512,768]{2,1,0:T(8,128)(2,1...) custom-call(bf16[256,2048]{1,0:T(8,128)(2,1)} %get-tuple-element.82.own, ...), custom_call_target="tpu_custom_call" | custom-call | tf_op jit(solution)/shard_map/ffn_up/pallas_call | solution.py:1385
  258.3 63.8 %ffn_back.1 = (bf16[2048,768]{1,0:T(8,128)(2,1)}, bf16[4,512,768]{2,1,0:T(8,128)(2,1)}, f32[512,768]{1,0:T(8,128)}, f32[256,2048]{1,0:T(8,128)}, bf16[256,2048]{1,0:T(8,128)(2,1)}, /*index=5*/f32[1,2048]{1,0:T(1,128)}) custom-call(bf16[2048,2048]{1,0:T(8,128)(2,1)} %bitcast.30, bf16[2048,2048]{1,0:T(8,128)(2,1)} %bitcast.24, ...), custom_call_target="tpu_custom_call" | custom-call | tf_op jit(solution)/shard_map/ffn_back/pallas_call | solution.py:1567
  322.0 71.6 %turn.1 = (bf16[4,512,768]{2,1,0:T(8,128)(2,1)}, bf16[4,352,512]{2,1,0:T(8,128)(2,1)}, f32[512,768]{1,0:T(8,128)}, f32[2048,384]{1,0:T(8,128)}) custom-call(bf16[2048,2048]{1,0:T(8,128)(2,1)} %bitcast.25, bf16[2048,768]{1,0:T(8,128)(2,1)} %get-tuple-element.95.d_ups_ref, bf16[4,512,768]{2,1,0:T(8,128)(2,1)} %get-tuple-element.96.parts_hbm, ...), custom_call_target="tpu_custom_call" | custom-call | tf_op jit(solution)/shard_map/turn/pallas_call | solution.py:1678
  393.7 96.2 %mixer_backward_linked.1 = (bf16[4,704,512]{2,1,0:T(8,128)(2,1)}, f32[512,768]{1,0:T(8,128)}, f32[342,512]{1,0:T(8,128)}, bf16[256,2048]{1,0:T(8,128)(2,1)}, f32...) custom-call(f32[2048,384]{1,0:T(8,128)} %get-tuple-element.99.d_mixed_ref, bf16[768,2048]{1,0:T(8,128)(2,1)} %get-tuple-element.74.xy_hbm, ...), custom_call_target="tpu_custom_call" | custom-call | tf_op jit(solution)/shard_map/mixer_backward_linked/pallas_call | solution.py:1885
  489.9 59.0 %close_block.1 = (bf16[256,2048]{1,0:T(8,128)(2,1)}, f32[342,512]{1,0:T(8,128)}, f32[342,512]{1,0:T(8,128)}, f32[1,128]{1,0:T(1,128)}, f32[4,96,384]{2,1,0:T(8,128)}) custom-call(bf16[2048,768]{1,0:T(8,128)(2,1)} %get-tuple-element.86.hidden_ref, bf16[2048,768]{1,0:T(8,128)(2,1)} %bitcast.27, bf16[4,704,512]{2,1,0:T(8,128)(2,1)} %get-tuple-element.108.xy_hbm, ...), custom_call_target="tpu_custom_call" | custom-call | tf_op jit(solution)/shard_map/close_block/pallas_call | solution.py:2052
  549.0 0.0 copy-start.1
  549.0 0.0 copy-start
  549.0 7.1 %hand_over.1 = (bf16[256,2048]{1,0:T(8,128)(2,1)}, bf16[256,2048]{1,0:T(8,128)(2,1)}, f32[342,512]{1,0:T(8,128)}, f32[342,512]{1,0:T(8,128)}, f32[342,512]{1,0:T...) custom-call(bf16[256,2048]{1,0:T(8,128)(2,1)} %get-tuple-element.111.refs_0_, ...), custom_call_target="tpu_custom_call" | custom-call | tf_op jit(solution)/shard_map/hand_over/pallas_call | solution.py:2112
  556.1 0.6 slice_bitcast_fusion
  556.6 0.6 slice.45
  557.2 0.6 slice_reduce_fusion
  557.9 0.2 fusion
  558.1 1.0 copy.42
  559.1 1.0 copy.41
  (4 shorter events, 0.1 us)
Async XLA Ops:
  549.0 7.1 %copy-start.1 = (f32[1,128]{1,0:T(1,128)S(1)}, f32[1,128]{1,0:T(1,128)}, u32[]{:S(2)}) copy-start(f32[1,128]{1,0:T(1,128)} %get-tuple-element.121) | copy-start | bytes 1540
  549.0 7.7 %copy-start = (f32[4,96,384]{2,1,0:T(8,128)S(1)}, f32[4,96,384]{2,1,0:T(8,128)}, u32[]{:S(2)}) copy-start(f32[4,96,384]{2,1,0:T(8,128)} %get-tuple-element.125) | copy-start | bytes 1769476

commit v8 on v7

--- a/solution.py
+++ b/solution.py
@@ -117,7 +117,7 @@
         conv_low[pl.ds(at, CHUNK), :] = made.astype(jnp.bfloat16)
         return unused
 
-    lax.fori_loop(0, rows // CHUNK, conv_step, 0, unroll=UNROLL)
+    lax.fori_loop(0, rows // CHUNK, conv_step, 0, unroll=2 * UNROLL)
     window[0:8, :] = window[pl.ds(rows, 8), :]
     rate[...] = dot_plain(conv_low[...], wr_ref[...]) + vec_ref[1:2, :]
     entry[...] = dot_plain(conv_low[...], we_ref[...]) + vec_ref[2:3, :]
@@ -142,7 +142,7 @@
         ).astype(jnp.bfloat16)
         return states[CHUNK - 1 : CHUNK, :]
 
-    carry[0:1, :] = lax.fori_loop(0, rows // CHUNK, scan_step, carry[0:1, :], unroll=UNROLL)
+    carry[0:1, :] = lax.fori_loop(0, rows // CHUNK, scan_step, carry[0:1, :], unroll=2 * UNROLL)
 
 
 def forward_body(
@@ -189,7 +189,7 @@
         conv_low[pl.ds(at, CHUNK), :] = made.astype(jnp.bfloat16)
         return unused
 
-    lax.fori_loop(0, rows // CHUNK, conv_step, 0, unroll=UNROLL)
+    lax.fori_loop(0, rows // CHUNK, conv_step, 0, unroll=2 * UNROLL)
     rate[...] = dot_plain(conv_low[...], wr_ref[...]) + vec_ref[1:2, :]
     entry[...] = dot_plain(conv_low[...], we_ref[...]) + vec_ref[2:3, :]
 
@@ -235,7 +235,7 @@
         sums[24:32, :] += fold(g_log * rate_gate)
         return passed[0:1, :]
 
-    carry[0:1, :] = lax.fori_loop(0, rows // CHUNK, scan_step, carry[0:1, :], unroll=UNROLL)
+    carry[0:1, :] = lax.fori_loop(0, rows // CHUNK, scan_step, carry[0:1, :], unroll=2 * UNROLL)
     wr_out[...] += contract_first(conv_low[...], g_rate[...])
     we_out[...] += contract_first(conv_low[...], g_entry[...])
     d_conv[0:rows, :] += contract_last(g_rate[...], wr_ref[...]) + contract_last(
@@ -263,7 +263,7 @@
         d_xy_ref[here, :chans] = total.astype(jnp.bfloat16)
         return unused
 
-    lax.fori_loop(0, rows // CHUNK, back_step, 0, unroll=UNROLL)
+    lax.fori_loop(0, rows // CHUNK, back_step, 0, unroll=2 * UNROLL)
 
     @pl.when(last_step)
     def _():
@@ -615,9 +615,10 @@
             def _(me=me, end=end, via=via):
                 self.to_pass(me, end, via).start()
 
-        for t in range(LINE):
-
-            @pl.when(self.plain(t))
+        for gap in (2, -2, 1, -1):
+            t = self.r + gap
+
+            @pl.when((t >= 0) & (t < LINE) & self.plain(t))
             def _(t=t):
                 self.direct(t).start()
 
@@ -993,7 +994,7 @@
 def open_body(
     x_ref, mix_ref, ffn_ref, cot, xt_ref, yt_ref, ot_ref,
     taps_ref, rows_ref, gates_ref, resets_ref,
-    full, cot_out, xy_full, out_full, gains_ref, taps_out, vec_out, wr_out, we_out, keep_out,
+    full, cot_out, xy_full, out_full, mix_out, ffn_out, taps_out, vec_out, wr_out, we_out, keep_out,
     shards, blank, square, moved,
     normed, column, spread, gain_sent, gain_arrived, wide_sent, wide_arrived, wiped, *semaphores,
 ):
@@ -1073,17 +1074,17 @@
             odd = spread[2 * pair + 1, line_place][0:1, :]
             at = (line_place * (PLANE // 2) + pair) * 2 * gain_share
             end = at + 2 * gain_share
-            gains_ref[0:1, at:end] = jnp.where(low, even, pltpu.roll(odd, gain_share, 1))
-            gains_ref[1:2, at:end] = jnp.where(low, pltpu.roll(even, gain_share, 1), odd)
+            mix_out[0:1, at:end] = jnp.where(low, even, pltpu.roll(odd, gain_share, 1))
+            ffn_out[0:1, at:end] = jnp.where(low, pltpu.roll(even, gain_share, 1), odd)
 
     def make(i, unused):
         at = pl.ds(pl.multiple_of(i * CHUNK, CHUNK), CHUNK)
-        normed[at, :] = norm_rows(x_ref[at, :].astype(jnp.float32), gains_ref[0:1, :]).astype(
+        normed[at, :] = norm_rows(x_ref[at, :].astype(jnp.float32), mix_out[...]).astype(
             jnp.bfloat16
         )
         return unused
 
-    lax.fori_loop(0, x_ref.shape[0] // CHUNK, make, 0)
+    lax.fori_loop(0, x_ref.shape[0] // CHUNK, make, 0, unroll=UNROLL)
     plane.start()
     lay_out_params(
         taps_ref, rows_ref, gates_ref, resets_ref,
@@ -1121,13 +1122,14 @@
     return pl.pallas_call(
         open_body,
         in_specs=[IN_VMEM, IN_VMEM, IN_VMEM, ANYWHERE] + [IN_VMEM] * 7,
-        out_specs=[ANYWHERE] * 4 + [IN_VMEM] * 6,
+        out_specs=[ANYWHERE] * 4 + [IN_VMEM] * 7,
         out_shape=[
             jax.ShapeDtypeStruct((PLANE, rows, width), jnp.bfloat16),
             jax.ShapeDtypeStruct((PLANE, rows, width // 2), jnp.bfloat16),
             jax.ShapeDtypeStruct((2 * chans, width), jnp.bfloat16),
             jax.ShapeDtypeStruct((chans, width), jnp.bfloat16),
-            jax.ShapeDtypeStruct((2, width), jnp.float32),
+            jax.ShapeDtypeStruct((1, width), jnp.float32),
+            jax.ShapeDtypeStruct((1, width), jnp.float32),
             jax.ShapeDtypeStruct((4, chans), jnp.float32),
             jax.ShapeDtypeStruct((8, chans), jnp.float32),
             jax.ShapeDtypeStruct((chans, chans), jnp.bfloat16),
@@ -1215,7 +1217,7 @@
             two_ref[at, :] = norm_rows(residual, gain_ref[...]).astype(jnp.bfloat16)
             return unused
 
-        lax.fori_loop(0, x_ref.shape[0] // CHUNK, make, 0)
+        lax.fori_loop(0, x_ref.shape[0] // CHUNK, make, 0, unroll=UNROLL)
         plane.finish()
         gate_line.finish()
         up_line.finish()
@@ -1522,7 +1524,7 @@
     def _():
         plane.pass_on(far_first(step - 1))
 
-    @pl.when(step == 5)
+    @pl.when(step == 3)
     def _():
         line.forward()
 
@@ -1542,7 +1544,7 @@
             eight[...] += sum_eight(d_gain)
             return unused
 
-        lax.fori_loop(0, rows // CHUNK, back, 0)
+        lax.fori_loop(0, rows // CHUNK, back, 0, unroll=UNROLL)
         gain_out[...] = jnp.sum(eight[...], axis=0, keepdims=True)
 
         def write(at, value):
@@ -1635,12 +1637,13 @@
 
     @pl.when(step == PLANE - 2)
     def _():
+        bring.wait(0)
+        line.forward()
         plane.relay(1)
 
     @pl.when(step == PLANE - 1)
     def _():
-        bring.wait(0, 1, 2)
-        line.forward()
+        bring.wait(1, 2)
 
         def add(owner, start=False):
             at = pl.ds(pl.multiple_of(owner * rows, rows), rows)
@@ -1789,7 +1792,7 @@
     def _():
         plane.relay(block + 3)
 
-    @pl.when(step == 4)
+    @pl.when(step == 3)
     def _():
         line.forward()
 
@@ -1847,7 +1850,7 @@
             eight[...] += sum_eight(d_gain)
             return unused
 
-        lax.fori_loop(0, in_grad.shape[0] // CHUNK, back, 0)
+        lax.fori_loop(0, in_grad.shape[0] // CHUNK, back, 0, unroll=UNROLL)
         split_gains(jnp.sum(eight[...], axis=0, keepdims=True), ffn_gain_ref[...], gains_out)
 
         def write(at, value):
@@ -2272,21 +2275,28 @@
     kept = -(-used // 16) * 16
     flat = lambda values: values.reshape((-1, values.shape[-1]))
     line = lambda values: values.reshape(1, -1)
-    normed_group, cot_half, xy_rows, out_rows, gains, taps, vec, wr, we, keep = open_block(
+    vectors = (conv_bias, rate_bias, entry_bias, decay_param)
+    place = lax.broadcasted_iota(jnp.int32, (len(vectors), used), 0)
+    rows = jnp.zeros((len(vectors), used), jnp.float32)
+    for k, vector in enumerate(vectors):
+        rows = jnp.where(place == k, vector[None, :], rows)
+    (
+        normed_group, cot_half, xy_rows, out_rows, mix_full, ffn_full, taps, vec, wr, we, keep,
+    ) = open_block(
         layer_in,
         (line(mix_gain), line(ffn_gain)),
         cotangent,
         (x_weight.T, y_weight.T, out_weight.T),
         (
             conv_weight,
-            jnp.stack([conv_bias, rate_bias, entry_bias, decay_param]),
+            rows,
             jnp.stack([rate_weight, entry_weight]),
             resets,
         ),
     )
     normed_group = flat(normed_group)
     u, by, before, states, mixed, residual, normed_two, gate_rows, up_half = forward_linked(
-        normed_group, xy_rows, out_rows, taps, vec, wr, we, keep, layer_in, gains[1:2],
+        normed_group, xy_rows, out_rows, taps, vec, wr, we, keep, layer_in, ffn_full,
         gate_weight, up_weight,
     )
     gate_rows = flat(gate_rows)
@@ -2296,14 +2306,14 @@
     two_group, cot_group, down_rows = map(flat, (two_group, cot_group, down_rows))
     d_ups, gate_parts, down_grad, d_residual, d_low, d_ffn_gain = ffn_back(
         cot_group, two_group, gates, ups, gate_rows, up_rows, down_rows, down_parts, residual,
-        cotangent, gains[1:2],
+        cotangent, ffn_full,
     )
     up_parts, out_parts, gate_grad, d_mixed = turn(
         two_group, d_ups, gate_parts, d_low, mixed, out_rows, kept
     )
     xy_parts, up_grad, out_grad, layer_in_grad, gain_terms, small = backward_linked(
         d_mixed, xy_rows, taps, vec, wr, we, keep, u, by, before, states,
-        normed_group, up_parts, out_parts, layer_in, gains[0:1], d_residual, d_ffn_gain,
+        normed_group, up_parts, out_parts, layer_in, mix_full, d_residual, d_ffn_gain,
         head_width, used,
     )
     layer_out, x_grad, y_grad, gain_grads, sums = close_block(

time: 572 us -> 553 us (0.967)
  Pallas kernels: 549 us -> 535 us
    pallas_call x1, Pallas kernels: 71.6 us -> 60.7 us  [turn(): pl.pallas_call(turn_body, grid=(PLANE,), in_specs=[tile(width), tile(unit...]
where the time goes in v8:
time: 553 us; the launch traced here: 544 us
  Pallas kernels  535 us (97%)
    pallas_call x1, Pallas kernels, backward_linked(): pl.pallas_call(functools.partial(backward_linked_body, head_width), grid=...  94.3 us
    pallas_call x1, Pallas kernels, ffn_up(): pl.pallas_call(ffn_up_body, in_specs=[IN_VMEM, IN_VMEM] + [ANYWHERE] * 5,...  87.1 us
    pallas_call x1, Pallas kernels, open_block(): pl.pallas_call(open_body, in_specs=[IN_VMEM, IN_VMEM, IN_VMEM, ANYWHERE]...  82.2 us
    pallas_call x1, Pallas kernels, forward_linked(): pl.pallas_call(forward_linked_body, grid=(PLANE,), in_specs=[tile(width),...  81.3 us
    pallas_call x1, Pallas kernels, ffn_back(): pl.pallas_call(ffn_back_body, grid=(2 * PLANE,), in_specs=[tile(width), l...  63.8 us
    pallas_call x1, Pallas kernels, turn(): pl.pallas_call(turn_body, grid=(PLANE,), in_specs=[tile(width), tile(unit...  60.7 us
    pallas_call x1, Pallas kernels, close_block(): pl.pallas_call(close_body, grid=(PLANE,), in_specs=[pl.BlockSpec((rows, u...  58.9 us

profile of v8, /device:TPU:0, one launch (start us, length us, event | category | flops | bytes accessed | tf_op | source)
XLA Modules:
  0.0 543.9 jit_solution(16225508903168546825)
XLA Ops:
  0.7 1.4 select_select_fusion.rows_ref
  2.1 1.0 copy_bitcast_fusion
  3.1 0.8 pad_maximum_fusion.gates_ref
  3.9 82.2 %open_block.1 = (bf16[8,256,2048]{2,1,0:T(8,128)(2,1)}, bf16[8,256,1024]{2,1,0:T(8,128)(2,1)}, bf16[768,2048]{1,0:T(8,128)(2,1)}, bf16[384,2048]{1,0:T(8,128)(2,...) custom-call(bf16[256,2048]{1,0:T(8,128)(2,1)} %x_hbm.3, ...), custom_call_target="tpu_custom_call" | custom-call | tf_op jit(solution)/shard_map/open_block/pallas_call | solution.py:1122
  86.1 81.3 %mixer_forward_linked.1 = (bf16[2048,384]{1,0:T(8,128)(2,1)}, f32[2048,384]{1,0:T(8,128)}, f32[2048,384]{1,0:T(8,128)}, bf16[2048,384]{1,0:T(8,128)(2,1)}, bf16[...) custom-call(bf16[2048,2048]{1,0:T(8,128)(2,1)} %bitcast.22, ...), custom_call_target="tpu_custom_call" | custom-call | tf_op jit(solution)/shard_map/mixer_forward_linked/pallas_call | solution.py:1232
  167.4 87.1 %ffn_up.1 = (bf16[8,256,2048]{2,1,0:T(8,128)(2,1)}, bf16[8,256,2048]{2,1,0:T(8,128)(2,1)}, bf16[2048,768]{1,0:T(8,128)(2,1)}, bf16[4,512,768]{2,1,0:T(8,128)(2,1...) custom-call(bf16[256,2048]{1,0:T(8,128)(2,1)} %get-tuple-element.83.own, ...), custom_call_target="tpu_custom_call" | custom-call | tf_op jit(solution)/shard_map/ffn_up/pallas_call | solution.py:1387
  254.5 63.8 %ffn_back.1 = (bf16[2048,768]{1,0:T(8,128)(2,1)}, bf16[4,512,768]{2,1,0:T(8,128)(2,1)}, f32[512,768]{1,0:T(8,128)}, f32[256,2048]{1,0:T(8,128)}, bf16[256,2048]{1,0:T(8,128)(2,1)}, /*index=5*/f32[1,2048]{1,0:T(1,128)}) custom-call(bf16[2048,2048]{1,0:T(8,128)(2,1)} %bitcast.30, bf16[2048,2048]{1,0:T(8,128)(2,1)} %bitcast.24, ...), custom_call_target="tpu_custom_call" | custom-call | tf_op jit(solution)/shard_map/ffn_back/pallas_call | solution.py:1569
  318.3 60.7 %turn.1 = (bf16[4,512,768]{2,1,0:T(8,128)(2,1)}, bf16[4,352,512]{2,1,0:T(8,128)(2,1)}, f32[512,768]{1,0:T(8,128)}, f32[2048,384]{1,0:T(8,128)}) custom-call(bf16[2048,2048]{1,0:T(8,128)(2,1)} %bitcast.25, bf16[2048,768]{1,0:T(8,128)(2,1)} %get-tuple-element.96.d_ups_ref, bf16[4,512,768]{2,1,0:T(8,128)(2,1)} %get-tuple-element.97.parts_hbm, ...), custom_call_target="tpu_custom_call" | custom-call | tf_op jit(solution)/shard_map/turn/pallas_call | solution.py:1681
  379.0 94.3 %mixer_backward_linked.1 = (bf16[4,704,512]{2,1,0:T(8,128)(2,1)}, f32[512,768]{1,0:T(8,128)}, f32[342,512]{1,0:T(8,128)}, bf16[256,2048]{1,0:T(8,128)(2,1)}, f32...) custom-call(f32[2048,384]{1,0:T(8,128)} %get-tuple-element.100.d_mixed_ref, bf16[768,2048]{1,0:T(8,128)(2,1)} %get-tuple-element.75.xy_hbm, ...), custom_call_target="tpu_custom_call" | custom-call | tf_op jit(solution)/shard_map/mixer_backward_linked/pallas_call | solution.py:1888
  473.4 58.9 %close_block.1 = (bf16[256,2048]{1,0:T(8,128)(2,1)}, f32[342,512]{1,0:T(8,128)}, f32[342,512]{1,0:T(8,128)}, f32[1,128]{1,0:T(1,128)}, f32[4,96,384]{2,1,0:T(8,128)}) custom-call(bf16[2048,768]{1,0:T(8,128)(2,1)} %get-tuple-element.87.hidden_ref, bf16[2048,768]{1,0:T(8,128)(2,1)} %bitcast.27, bf16[4,704,512]{2,1,0:T(8,128)(2,1)} %get-tuple-element.110.xy_hbm, ...), custom_call_target="tpu_custom_call" | custom-call | tf_op jit(solution)/shard_map/close_block/pallas_call | solution.py:2055
  532.3 0.0 copy-start.1
  532.4 0.0 copy-start
  532.4 7.1 %hand_over.1 = (bf16[256,2048]{1,0:T(8,128)(2,1)}, bf16[256,2048]{1,0:T(8,128)(2,1)}, f32[342,512]{1,0:T(8,128)}, f32[342,512]{1,0:T(8,128)}, f32[342,512]{1,0:T...) custom-call(bf16[256,2048]{1,0:T(8,128)(2,1)} %get-tuple-element.113.refs_0_, ...), custom_call_target="tpu_custom_call" | custom-call | tf_op jit(solution)/shard_map/hand_over/pallas_call | solution.py:2115
  539.4 0.0 copy-done.1
  539.4 0.6 slice_bitcast_fusion
  540.0 0.0 copy-done
  540.0 0.6 slice.36
  540.6 0.6 slice_reduce_fusion
  541.2 0.2 fusion
  541.4 1.0 copy.42
  542.5 1.0 copy.41
  (4 shorter events, 0.1 us)
Async XLA Ops:
  532.3 7.1 %copy-start.1 = (f32[1,128]{1,0:T(1,128)S(1)}, f32[1,128]{1,0:T(1,128)}, u32[]{:S(2)}) copy-start(f32[1,128]{1,0:T(1,128)} %get-tuple-element.123) | copy-start | bytes 1540
  532.4 7.7 %copy-start = (f32[4,96,384]{2,1,0:T(8,128)S(1)}, f32[4,96,384]{2,1,0:T(8,128)}, u32[]{:S(2)}) copy-start(f32[4,96,384]{2,1,0:T(8,128)} %get-tuple-element.127) | copy-start | bytes 1769476

commit v9 on v8

--- a/solution.py
+++ b/solution.py
@@ -1162,8 +1162,8 @@
 def forward_linked_body(
     normed_ref, xy_hbm, ow_hbm, taps_ref, vec_ref, wr_ref, we_ref, keep_ref,
     x_hbm, gain_ref, gate_shard, up_shard,
-    u_ref, by_ref, before_ref, states_ref, mixed_ref, residual_ref, two_ref, gate_out, up_out,
-    xy_ref, ow_ref, x_ref, brought,
+    u_ref, by_ref, before_ref, states_ref, mixed_ref, residual_out, two_out, gate_out, up_out,
+    xy_ref, ow_ref, x_ref, brought, residual_ref, two_ref, taken,
     window, conv, conv_low, rate, entry, carry, *links,
 ):
     step = pl.program_id(0)
@@ -1172,6 +1172,7 @@
     first_rows = up_shard.at[pl.ds(0, up_out.shape[1])]
     up_line = LineGather(first_rows, lambda t: up_out.at[t], *links[13:16])
 
+    take = Bring((residual_ref, two_ref), (residual_out, two_out), taken)
     bring = Bring((xy_hbm, ow_hbm, x_hbm), (xy_ref, ow_ref, x_ref), brought)
 
     @pl.when(step == 0)
@@ -1218,9 +1219,11 @@
             return unused
 
         lax.fori_loop(0, x_ref.shape[0] // CHUNK, make, 0, unroll=UNROLL)
+        take.start()
         plane.finish()
         gate_line.finish()
         up_line.finish()
+        take.wait(0, 1)
 
 
 def forward_linked(normed, xy, ow, taps, vec, wr, we, keep, layer_in, gain, gate_shard, up_shard):
@@ -1237,7 +1240,7 @@
             once(vec.shape), once(wr.shape), once(we.shape), tile(keep.shape[1]),
             ANYWHERE, once(gain.shape), ANYWHERE, ANYWHERE,
         ],
-        out_specs=[tile(chans)] * 5 + [once((rows, width))] * 2 + [ANYWHERE] * 2,
+        out_specs=[tile(chans)] * 5 + [ANYWHERE] * 4,
         out_shape=[
             jax.ShapeDtypeStruct((length, chans), jnp.bfloat16),
             jax.ShapeDtypeStruct((length, chans), jnp.float32),
@@ -1251,6 +1254,9 @@
         ],
         scratch_shapes=[
             *held(xy, ow, layer_in),
+            pltpu.VMEM((rows, width), jnp.float32),
+            pltpu.VMEM((rows, width), jnp.bfloat16),
+            pltpu.SemaphoreType.DMA((2,)),
             pltpu.VMEM((rows + 8, chans), jnp.float32),
             pltpu.VMEM((rows, chans), jnp.float32),
             pltpu.VMEM((rows, chans), jnp.bfloat16),
@@ -1270,8 +1276,8 @@
 
 def ffn_up_body(
     own_two, gate_ref, own_cot, cot_half, up_half, up_shard, down_shard,
-    two_out, cot_out, up_out, down_out, gates_out, ups_out, hidden_out, down_parts,
-    two, cot, up, gates, ups, hidden, total, copied, brought, *semaphores,
+    two_out, cot_out, up_out, down_out, gates_out, ups_out, hidden_out, parts_out,
+    two, cot, up, gates, ups, hidden, total, down_parts, copied, brought, *semaphores,
 ):
     h = lax.axis_index("head")
     rows = own_two.shape[0]
@@ -1301,7 +1307,7 @@
         for k, (src, dst) in enumerate(
             (
                 (two, two_out), (cot, cot_out), (up, up_out), (gates, gates_out),
-                (ups, ups_out), (hidden, hidden_out),
+                (ups, ups_out), (hidden, hidden_out), (down_parts, parts_out),
             )
         )
     ]
@@ -1373,6 +1379,7 @@
 
     lax.fori_loop(1, PLANE, add_down, 0)
     to_parts(total, down_parts)
+    outward[6].start()
     down_line.finish()
     for copy in outward:
         copy.wait()
@@ -1387,7 +1394,7 @@
     return pl.pallas_call(
         ffn_up_body,
         in_specs=[IN_VMEM, IN_VMEM] + [ANYWHERE] * 5,
-        out_specs=[ANYWHERE] * 7 + [IN_VMEM],
+        out_specs=[ANYWHERE] * 8,
         out_shape=[
             group,
             group,
@@ -1406,7 +1413,8 @@
             pltpu.VMEM((length, units), jnp.float32),
             pltpu.VMEM((length, units), jnp.bfloat16),
             pltpu.VMEM((width, units), jnp.float32),
-            pltpu.SemaphoreType.DMA((6,)),
+            pltpu.VMEM((LINE, share, units), jnp.bfloat16),
+            pltpu.SemaphoreType.DMA((7,)),
             pltpu.SemaphoreType.DMA((LINE + 1,)),
             *(LineGather.semaphores * 2),
             *(PlaneGather.semaphores * 2),
@@ -1463,8 +1471,8 @@
 def ffn_back_body(
     cot_ref, two_ref, gates_ref, ups_ref, gate_hbm, up_hbm, down_hbm, parts_hbm,
     residual_hbm, own_cot_hbm, gain_ref,
-    d_ups_ref, gate_parts, down_out, d_res_ref, d_low_ref, gain_out,
-    gate_ref, up_ref, down_ref, parts, brought, late,
+    d_ups_ref, parts_out, down_out, d_res_ref, d_low_ref, gain_out,
+    gate_ref, up_ref, down_ref, parts, brought, late, gate_parts, taken,
     total, d_gates, d_hidden, eight, *links,
 ):
     step = pl.program_id(0)
@@ -1475,6 +1483,7 @@
     bring = Bring(
         (down_hbm, gate_hbm, up_hbm, parts_hbm), (down_ref, gate_ref, up_ref, parts), brought
     )
+    take = Bring((gate_parts,), (parts_out,), taken)
     into_outputs = Bring((residual_hbm, own_cot_hbm), (d_res_ref, d_low_ref), late)
 
     @pl.when(step == 0)
@@ -1531,6 +1540,7 @@
     @pl.when(step == 2 * PLANE - 1)
     def _():
         to_parts(total, gate_parts)
+        take.start()
         plane.arrive()
         into_outputs.wait(0, 1)
         eight[...] = jnp.zeros_like(eight)
@@ -1552,6 +1562,7 @@
 
         line.finish(write)
         plane.finish()
+        take.wait(0)
 
 
 def ffn_back(
@@ -1574,7 +1585,7 @@
             *([ANYWHERE] * 6), once(gain.shape),
         ],
         out_specs=[
-            tile(units), once((LINE, share, units)), once((share, units)),
+            tile(units), ANYWHERE, once((share, units)),
             once((rows, width)), once((rows, width)), once((1, width)),
         ],
         out_shape=[
@@ -1588,6 +1599,7 @@
         scratch_shapes=[
             *held(gate, up, down, parts),
             pltpu.SemaphoreType.DMA((2,)),
+            *held(parts),
             pltpu.VMEM((width, units), jnp.float32),
             pltpu.VMEM((PLANE, rows, units), jnp.bfloat16),
             pltpu.VMEM((rows, units), jnp.float32),
@@ -1606,8 +1618,8 @@
 
 def turn_body(
     two_ref, d_ups_ref, parts_hbm, block, mixed_hbm, ow_hbm,
-    up_parts, out_parts, gate_out, d_mixed_out,
-    gate_parts, mixed_ref, ow_ref, brought,
+    up_hbm, out_hbm, gate_out, d_mixed_hbm,
+    gate_parts, mixed_ref, ow_ref, brought, up_parts, out_parts, d_mixed_out, taken,
     full, total, out_total, *links,
 ):
     step = pl.program_id(0)
@@ -1615,6 +1627,9 @@
     plane = PlaneGather(block, full, *links[5:])
     rows = two_ref.shape[0]
 
+    take = Bring(
+        (up_parts, out_parts, d_mixed_out), (up_hbm, out_hbm, d_mixed_hbm), taken
+    )
     bring = Bring(
         (parts_hbm, mixed_hbm, ow_hbm), (gate_parts, mixed_ref, ow_ref), brought
     )
@@ -1654,6 +1669,7 @@
         plane.beside()
         add(plane.side, start=True)
         to_parts(total, up_parts)
+        take.copies[0].start()
         plane.rest()
         add(plane.x)
         add(plane.y)
@@ -1664,13 +1680,16 @@
         add(across_of(plane.side))
         add(along_of(plane.side))
         add(across_of(along_of(plane.side)))
+        take.copies[2].start()
         kept = out_parts.shape[1]
         to_turned_parts(out_total, out_parts, ((0, 0, kept),))
+        take.copies[1].start()
 
         def write(at, value):
             gate_out[at, :] = value
 
         line.finish(write)
+        take.wait(0, 1, 2)
 
 
 def turn(two_group, d_ups, gate_parts, block, mixed, ow, kept):
@@ -1685,8 +1704,7 @@
             tile(width), tile(units), ANYWHERE, ANYWHERE, ANYWHERE, ANYWHERE,
         ],
         out_specs=[
-            once(gate_parts.shape), once((LINE, kept, share)), once((share, units)),
-            once((length, chans)),
+            ANYWHERE, ANYWHERE, once((share, units)), ANYWHERE,
         ],
         out_shape=[
             jax.ShapeDtypeStruct(gate_parts.shape, jnp.bfloat16),
@@ -1696,6 +1714,10 @@
         ],
         scratch_shapes=[
             *held(gate_parts, mixed, ow),
+            pltpu.VMEM(gate_parts.shape, jnp.bfloat16),
+            pltpu.VMEM((LINE, kept, share), jnp.bfloat16),
+            pltpu.VMEM((length, chans), jnp.float32),
+            pltpu.SemaphoreType.DMA((3,)),
             pltpu.VMEM((PLANE, rows, width), jnp.bfloat16),
             pltpu.VMEM((width, units), jnp.float32),
             pltpu.VMEM((chans, width), jnp.float32),
@@ -1758,8 +1780,8 @@
     d_mixed_ref, xy_hbm, taps_ref, vec_ref, wr_ref, we_ref, keep_ref,
     u_ref, u_prev_ref, by_ref, before_ref, states_ref, normed_ref, up_hbm, out_hbm,
     x_hbm, gain_ref, d_residual_hbm, ffn_gain_ref,
-    xy_parts, up_out, out_out, in_grad, gains_out, small_out,
-    xy_ref, up_parts, out_parts, brought, late,
+    parts_out, up_out, out_out, in_grad, gains_out, small_out,
+    xy_ref, up_parts, out_parts, brought, late, xy_parts, taken,
     out_sum, taps_sum, vec_sum, wr_sum, we_sum, small, small_parts, d_xy, d_all, xy_total, eight, *rest,
 ):
     scratch, links = rest[:10], rest[10:]
@@ -1773,6 +1795,7 @@
     bring = Bring(
         (xy_hbm, up_hbm, out_hbm), (xy_ref, up_parts, out_parts), brought
     )
+    take = Bring((xy_parts,), (parts_out,), taken)
     d_residual_ref = xy_total.at[0 : x_hbm.shape[0]]
     bring_late = Bring((x_hbm, d_residual_hbm), (in_grad, d_residual_ref), late)
 
@@ -1837,6 +1860,12 @@
         kept, chans = out_parts.shape[1], d_xy.shape[1] // 2
         to_turned_parts(xy_total, xy_parts, ((0, 0, kept), (chans, kept, kept)))
         bring_late.start()
+        take.start()
+
+        def write(at, value):
+            up_out[at, :] = value
+
+        line.finish(write)
         plane.arrive()
         bring_late.wait(0, 1)
         eight[...] = jnp.zeros_like(eight)
@@ -1853,20 +1882,17 @@
         lax.fori_loop(0, in_grad.shape[0] // CHUNK, back, 0, unroll=UNROLL)
         split_gains(jnp.sum(eight[...], axis=0, keepdims=True), ffn_gain_ref[...], gains_out)
 
-        def write(at, value):
-            up_out[at, :] = value
-
         def write_out(at, value):
             out_sum[at, :] = value
 
         def write_small(at, value):
             small_out[at, :] = value.astype(jnp.bfloat16)
 
-        line.finish(write)
         out_line.finish(write_out)
         out_out[...] = out_sum[0 : out_out.shape[0], :]
         small_line.finish(write_small)
         plane.finish()
+        take.wait(0)
 
 
 def backward_linked(
@@ -1895,7 +1921,7 @@
             ANYWHERE, once(gain.shape), ANYWHERE, once(ffn_gain.shape),
         ],
         out_specs=[
-            once((LINE, 2 * kept, share)), once((share, units)), once((used, share)),
+            ANYWHERE, once((share, units)), once((used, share)),
             once((rows, width)), once(gain_terms), once((small_share, chans)),
         ],
         out_shape=[
@@ -1909,6 +1935,8 @@
         scratch_shapes=[
             *held(xy, up_parts, out_parts),
             pltpu.SemaphoreType.DMA((2,)),
+            pltpu.VMEM((LINE, 2 * kept, share), jnp.bfloat16),
+            pltpu.SemaphoreType.DMA((1,)),
             pltpu.VMEM((kept, share), jnp.float32),
             pltpu.VMEM(taps.shape, jnp.float32),
             pltpu.VMEM(vec.shape, jnp.float32),

time: 553 us -> 548 us (level)
  no operation moved by 1% of the time
where the time goes in v9:
time: 548 us; the launch traced here: 539 us
  Pallas kernels  530 us (97%)
    pallas_call x1, Pallas kernels, backward_linked(): pl.pallas_call(functools.partial(backward_linked_body, head_width), grid=...  94.2 us
    pallas_call x1, Pallas kernels, ffn_up(): pl.pallas_call(ffn_up_body, in_specs=[IN_VMEM, IN_VMEM] + [ANYWHERE] * 5,...  85.4 us
    pallas_call x1, Pallas kernels, open_block(): pl.pallas_call(open_body, in_specs=[IN_VMEM, IN_VMEM, IN_VMEM, ANYWHERE]...  82.2 us
    pallas_call x1, Pallas kernels, forward_linked(): pl.pallas_call(forward_linked_body, grid=(PLANE,), in_specs=[tile(width),...  80.2 us
    pallas_call x1, Pallas kernels, ffn_back(): pl.pallas_call(ffn_back_body, grid=(2 * PLANE,), in_specs=[tile(width), l...  62.9 us
    pallas_call x1, Pallas kernels, close_block(): pl.pallas_call(close_body, grid=(PLANE,), in_specs=[pl.BlockSpec((rows, u...  59.8 us
    pallas_call x1, Pallas kernels, turn(): pl.pallas_call(turn_body, grid=(PLANE,), in_specs=[tile(width), tile(unit...  58.6 us

profile of v9, /device:TPU:0, one launch (start us, length us, event | category | flops | bytes accessed | tf_op | source)
XLA Modules:
  0.0 538.8 jit_solution(11706047847887320976)
XLA Ops:
  0.7 1.4 select_select_fusion.rows_ref
  2.1 1.0 copy_bitcast_fusion
  3.1 0.8 pad_maximum_fusion.gates_ref
  3.9 82.2 %open_block.1 = (bf16[8,256,2048]{2,1,0:T(8,128)(2,1)}, bf16[8,256,1024]{2,1,0:T(8,128)(2,1)}, bf16[768,2048]{1,0:T(8,128)(2,1)}, bf16[384,2048]{1,0:T(8,128)(2,...) custom-call(bf16[256,2048]{1,0:T(8,128)(2,1)} %x_hbm.3, ...), custom_call_target="tpu_custom_call" | custom-call | tf_op jit(solution)/shard_map/open_block/pallas_call | solution.py:1122
  86.1 80.2 %mixer_forward_linked.1 = (bf16[2048,384]{1,0:T(8,128)(2,1)}, f32[2048,384]{1,0:T(8,128)}, f32[2048,384]{1,0:T(8,128)}, bf16[2048,384]{1,0:T(8,128)(2,1)}, bf16[...) custom-call(bf16[2048,2048]{1,0:T(8,128)(2,1)} %bitcast.22, ...), custom_call_target="tpu_custom_call" | custom-call | tf_op jit(solution)/shard_map/mixer_forward_linked/pallas_call | solution.py:1235
  166.3 85.4 %ffn_up.1 = (bf16[8,256,2048]{2,1,0:T(8,128)(2,1)}, bf16[8,256,2048]{2,1,0:T(8,128)(2,1)}, bf16[2048,768]{1,0:T(8,128)(2,1)}, bf16[4,512,768]{2,1,0:T(8,128)(2,1...) custom-call(bf16[256,2048]{1,0:T(8,128)(2,1)} %get-tuple-element.83.own, ...), custom_call_target="tpu_custom_call" | custom-call | tf_op jit(solution)/shard_map/ffn_up/pallas_call | solution.py:1394
  251.7 62.9 %ffn_back.1 = (bf16[2048,768]{1,0:T(8,128)(2,1)}, bf16[4,512,768]{2,1,0:T(8,128)(2,1)}, f32[512,768]{1,0:T(8,128)}, f32[256,2048]{1,0:T(8,128)}, bf16[256,2048]{1,0:T(8,128)(2,1)}, /*index=5*/f32[1,2048]{1,0:T(1,128)}) custom-call(bf16[2048,2048]{1,0:T(8,128)(2,1)} %bitcast.30, bf16[2048,2048]{1,0:T(8,128)(2,1)} %bitcast.24, ...), custom_call_target="tpu_custom_call" | custom-call | tf_op jit(solution)/shard_map/ffn_back/pallas_call | solution.py:1580
  314.6 58.6 %turn.1 = (bf16[4,512,768]{2,1,0:T(8,128)(2,1)}, bf16[4,352,512]{2,1,0:T(8,128)(2,1)}, f32[512,768]{1,0:T(8,128)}, f32[2048,384]{1,0:T(8,128)}) custom-call(bf16[2048,2048]{1,0:T(8,128)(2,1)} %bitcast.25, bf16[2048,768]{1,0:T(8,128)(2,1)} %get-tuple-element.96.d_ups_ref, bf16[4,512,768]{2,1,0:T(8,128)(2,1)} %get-tuple-element.97.parts_hbm, ...), custom_call_target="tpu_custom_call" | custom-call | tf_op jit(solution)/shard_map/turn/pallas_call | solution.py:1700
  373.2 94.2 %mixer_backward_linked.1 = (bf16[4,704,512]{2,1,0:T(8,128)(2,1)}, f32[512,768]{1,0:T(8,128)}, f32[342,512]{1,0:T(8,128)}, bf16[256,2048]{1,0:T(8,128)(2,1)}, f32...) custom-call(f32[2048,384]{1,0:T(8,128)} %get-tuple-element.100.d_mixed_ref, bf16[768,2048]{1,0:T(8,128)(2,1)} %get-tuple-element.75.xy_hbm, ...), custom_call_target="tpu_custom_call" | custom-call | tf_op jit(solution)/shard_map/mixer_backward_linked/pallas_call | solution.py:1914
  467.4 59.8 %close_block.1 = (bf16[256,2048]{1,0:T(8,128)(2,1)}, f32[342,512]{1,0:T(8,128)}, f32[342,512]{1,0:T(8,128)}, f32[1,128]{1,0:T(1,128)}, f32[4,96,384]{2,1,0:T(8,128)}) custom-call(bf16[2048,768]{1,0:T(8,128)(2,1)} %get-tuple-element.87.hidden_ref, bf16[2048,768]{1,0:T(8,128)(2,1)} %bitcast.27, bf16[4,704,512]{2,1,0:T(8,128)(2,1)} %get-tuple-element.110.xy_hbm, ...), custom_call_target="tpu_custom_call" | custom-call | tf_op jit(solution)/shard_map/close_block/pallas_call | solution.py:2083
  527.3 0.0 copy-start.1
  527.3 0.0 copy-start
  527.3 7.1 %hand_over.1 = (bf16[256,2048]{1,0:T(8,128)(2,1)}, bf16[256,2048]{1,0:T(8,128)(2,1)}, f32[342,512]{1,0:T(8,128)}, f32[342,512]{1,0:T(8,128)}, f32[342,512]{1,0:T...) custom-call(bf16[256,2048]{1,0:T(8,128)(2,1)} %get-tuple-element.113.refs_0_, ...), custom_call_target="tpu_custom_call" | custom-call | tf_op jit(solution)/shard_map/hand_over/pallas_call | solution.py:2143
  534.4 0.0 copy-done.1
  534.4 0.6 slice_bitcast_fusion
  535.0 0.0 copy-done
  535.0 0.6 slice.36
  535.6 0.6 slice_reduce_fusion
  536.2 0.2 fusion
  536.4 1.0 copy.42
  537.4 1.0 copy.41
  (4 shorter events, 0.1 us)
Async XLA Ops:
  527.3 7.1 %copy-start.1 = (f32[1,128]{1,0:T(1,128)S(1)}, f32[1,128]{1,0:T(1,128)}, u32[]{:S(2)}) copy-start(f32[1,128]{1,0:T(1,128)} %get-tuple-element.123) | copy-start | bytes 1540
  527.3 7.7 %copy-start = (f32[4,96,384]{2,1,0:T(8,128)S(1)}, f32[4,96,384]{2,1,0:T(8,128)}, u32[]{:S(2)}) copy-start(f32[4,96,384]{2,1,0:T(8,128)} %get-tuple-element.127) | copy-start | bytes 1769476

commit v10 on v9

--- a/solution.py
+++ b/solution.py
@@ -992,10 +992,10 @@
 
 
 def open_body(
-    x_ref, mix_ref, ffn_ref, cot, xt_ref, yt_ref, ot_ref,
+    x_hbm, mix_ref, ffn_ref, cot, x_weight, y_weight, out_weight,
     taps_ref, rows_ref, gates_ref, resets_ref,
     full, cot_out, xy_full, out_full, mix_out, ffn_out, taps_out, vec_out, wr_out, we_out, keep_out,
-    shards, blank, square, moved,
+    x_ref, xt_ref, yt_ref, ot_ref, brought, shards, blank, square, moved,
     normed, column, spread, gain_sent, gain_arrived, wide_sent, wide_arrived, wiped, *semaphores,
 ):
     r, h = lax.axis_index("row"), lax.axis_index("head")
@@ -1023,9 +1023,10 @@
     cot_plane = PlaneGather(
         cot, cot_out, *semaphores[12:15], source=pl.ds(0, cot_out.shape[2])
     )
-    for k, source in enumerate((xt_ref, yt_ref, ot_ref)):
-        shards[k, held_rows - 16 :, :] = jnp.zeros((16, share), jnp.bfloat16)
-        shards[k, 0:used, :] = source[...]
+    bring = Bring(
+        (x_weight, y_weight, out_weight, x_hbm), (xt_ref, yt_ref, ot_ref, x_ref), brought
+    )
+    bring.start()
     gain_share = mix_ref.shape[1]
     low = lax.broadcasted_iota(jnp.int32, (8, 2 * gain_share), 1) < gain_share
     column[r] = jnp.zeros_like(column[r])
@@ -1053,7 +1054,10 @@
 
     for step in range(1, LINE):
         up_line(lax.rem(r + step, LINE)).start()
-    for line in lines:
+    for k, (line, source) in enumerate(zip(lines, (xt_ref, yt_ref, ot_ref))):
+        bring.wait(k)
+        shards[k, held_rows - 16 :, :] = jnp.zeros((16, share), jnp.bfloat16)
+        shards[k, 0:used, :] = source[...]
         line.start()
     blank[...] = jnp.zeros_like(blank)
     for wipe in wipes:
@@ -1076,6 +1080,8 @@
             end = at + 2 * gain_share
             mix_out[0:1, at:end] = jnp.where(low, even, pltpu.roll(odd, gain_share, 1))
             ffn_out[0:1, at:end] = jnp.where(low, pltpu.roll(even, gain_share, 1), odd)
+
+    bring.wait(3)
 
     def make(i, unused):
         at = pl.ds(pl.multiple_of(i * CHUNK, CHUNK), CHUNK)
@@ -1121,7 +1127,7 @@
     tile = (8, 2 * gains[0].shape[1])
     return pl.pallas_call(
         open_body,
-        in_specs=[IN_VMEM, IN_VMEM, IN_VMEM, ANYWHERE] + [IN_VMEM] * 7,
+        in_specs=[ANYWHERE, IN_VMEM, IN_VMEM] + [ANYWHERE] * 4 + [IN_VMEM] * 4,
         out_specs=[ANYWHERE] * 4 + [IN_VMEM] * 7,
         out_shape=[
             jax.ShapeDtypeStruct((PLANE, rows, width), jnp.bfloat16),
@@ -1137,6 +1143,7 @@
             jax.ShapeDtypeStruct((length, 8), jnp.float32),
         ],
         scratch_shapes=[
+            *held(layer_in, *weights),
             pltpu.VMEM((3, held_rows, share), jnp.bfloat16),
             pltpu.VMEM((chans - held_rows, width), jnp.bfloat16),
             pltpu.VMEM((chans, chans), jnp.float32),

time: 548 us -> 547 us (level)
  no operation moved by 1% of the time
where the time goes in v10:
time: 547 us; the launch traced here: 538 us
  Pallas kernels  530 us (97%)
    pallas_call x1, Pallas kernels, backward_linked(): pl.pallas_call(functools.partial(backward_linked_body, head_width), grid=...  94.2 us
    pallas_call x1, Pallas kernels, ffn_up(): pl.pallas_call(ffn_up_body, in_specs=[IN_VMEM, IN_VMEM] + [ANYWHERE] * 5,...  85.4 us
    pallas_call x1, Pallas kernels, open_block(): pl.pallas_call(open_body, in_specs=[ANYWHERE, IN_VMEM, IN_VMEM] + [ANYWHE...  81.5 us
    pallas_call x1, Pallas kernels, forward_linked(): pl.pallas_call(forward_linked_body, grid=(PLANE,), in_specs=[tile(width),...  80.2 us
    pallas_call x1, Pallas kernels, ffn_back(): pl.pallas_call(ffn_back_body, grid=(2 * PLANE,), in_specs=[tile(width), l...  62.9 us
    pallas_call x1, Pallas kernels, close_block(): pl.pallas_call(close_body, grid=(PLANE,), in_specs=[pl.BlockSpec((rows, u...  59.8 us
    pallas_call x1, Pallas kernels, turn(): pl.pallas_call(turn_body, grid=(PLANE,), in_specs=[tile(width), tile(unit...  58.6 us

profile of v10, /device:TPU:0, one launch (start us, length us, event | category | flops | bytes accessed | tf_op | source)
XLA Modules:
  0.0 538.2 jit_solution(13193744697975272168)
XLA Ops:
  0.7 1.4 select_select_fusion.rows_ref
  2.1 1.0 copy_bitcast_fusion
  3.1 0.8 pad_maximum_fusion.gates_ref
  3.9 81.5 %open_block.1 = (bf16[8,256,2048]{2,1,0:T(8,128)(2,1)}, bf16[8,256,1024]{2,1,0:T(8,128)(2,1)}, bf16[768,2048]{1,0:T(8,128)(2,1)}, bf16[384,2048]{1,0:T(8,128)(2,...) custom-call(bf16[256,2048]{1,0:T(8,128)(2,1)} %x_hbm.5, ...), custom_call_target="tpu_custom_call" | custom-call | tf_op jit(solution)/shard_map/open_block/pallas_call | solution.py:1128
  85.4 80.2 %mixer_forward_linked.1 = (bf16[2048,384]{1,0:T(8,128)(2,1)}, f32[2048,384]{1,0:T(8,128)}, f32[2048,384]{1,0:T(8,128)}, bf16[2048,384]{1,0:T(8,128)(2,1)}, bf16[...) custom-call(bf16[2048,2048]{1,0:T(8,128)(2,1)} %bitcast.22, ...), custom_call_target="tpu_custom_call" | custom-call | tf_op jit(solution)/shard_map/mixer_forward_linked/pallas_call | solution.py:1242
  165.6 85.4 %ffn_up.1 = (bf16[8,256,2048]{2,1,0:T(8,128)(2,1)}, bf16[8,256,2048]{2,1,0:T(8,128)(2,1)}, bf16[2048,768]{1,0:T(8,128)(2,1)}, bf16[4,512,768]{2,1,0:T(8,128)(2,1...) custom-call(bf16[256,2048]{1,0:T(8,128)(2,1)} %get-tuple-element.83.own, ...), custom_call_target="tpu_custom_call" | custom-call | tf_op jit(solution)/shard_map/ffn_up/pallas_call | solution.py:1401
  251.0 62.9 %ffn_back.1 = (bf16[2048,768]{1,0:T(8,128)(2,1)}, bf16[4,512,768]{2,1,0:T(8,128)(2,1)}, f32[512,768]{1,0:T(8,128)}, f32[256,2048]{1,0:T(8,128)}, bf16[256,2048]{1,0:T(8,128)(2,1)}, /*index=5*/f32[1,2048]{1,0:T(1,128)}) custom-call(bf16[2048,2048]{1,0:T(8,128)(2,1)} %bitcast.30, bf16[2048,2048]{1,0:T(8,128)(2,1)} %bitcast.24, ...), custom_call_target="tpu_custom_call" | custom-call | tf_op jit(solution)/shard_map/ffn_back/pallas_call | solution.py:1587
  313.9 58.6 %turn.1 = (bf16[4,512,768]{2,1,0:T(8,128)(2,1)}, bf16[4,352,512]{2,1,0:T(8,128)(2,1)}, f32[512,768]{1,0:T(8,128)}, f32[2048,384]{1,0:T(8,128)}) custom-call(bf16[2048,2048]{1,0:T(8,128)(2,1)} %bitcast.25, bf16[2048,768]{1,0:T(8,128)(2,1)} %get-tuple-element.96.d_ups_ref, bf16[4,512,768]{2,1,0:T(8,128)(2,1)} %get-tuple-element.97.parts_hbm, ...), custom_call_target="tpu_custom_call" | custom-call | tf_op jit(solution)/shard_map/turn/pallas_call | solution.py:1707
  372.5 94.2 %mixer_backward_linked.1 = (bf16[4,704,512]{2,1,0:T(8,128)(2,1)}, f32[512,768]{1,0:T(8,128)}, f32[342,512]{1,0:T(8,128)}, bf16[256,2048]{1,0:T(8,128)(2,1)}, f32...) custom-call(f32[2048,384]{1,0:T(8,128)} %get-tuple-element.100.d_mixed_ref, bf16[768,2048]{1,0:T(8,128)(2,1)} %get-tuple-element.75.xy_hbm, ...), custom_call_target="tpu_custom_call" | custom-call | tf_op jit(solution)/shard_map/mixer_backward_linked/pallas_call | solution.py:1921
  466.8 59.8 %close_block.1 = (bf16[256,2048]{1,0:T(8,128)(2,1)}, f32[342,512]{1,0:T(8,128)}, f32[342,512]{1,0:T(8,128)}, f32[1,128]{1,0:T(1,128)}, f32[4,96,384]{2,1,0:T(8,128)}) custom-call(bf16[2048,768]{1,0:T(8,128)(2,1)} %get-tuple-element.87.hidden_ref, bf16[2048,768]{1,0:T(8,128)(2,1)} %bitcast.27, bf16[4,704,512]{2,1,0:T(8,128)(2,1)} %get-tuple-element.110.xy_hbm, ...), custom_call_target="tpu_custom_call" | custom-call | tf_op jit(solution)/shard_map/close_block/pallas_call | solution.py:2090
  526.6 0.0 copy-start.1
  526.6 0.0 copy-start
  526.6 7.1 %hand_over.1 = (bf16[256,2048]{1,0:T(8,128)(2,1)}, bf16[256,2048]{1,0:T(8,128)(2,1)}, f32[342,512]{1,0:T(8,128)}, f32[342,512]{1,0:T(8,128)}, f32[342,512]{1,0:T...) custom-call(bf16[256,2048]{1,0:T(8,128)(2,1)} %get-tuple-element.113.refs_0_, ...), custom_call_target="tpu_custom_call" | custom-call | tf_op jit(solution)/shard_map/hand_over/pallas_call | solution.py:2150
  533.7 0.0 copy-done.1
  533.7 0.6 slice_bitcast_fusion
  534.3 0.0 copy-done
  534.3 0.6 slice.36
  534.9 0.6 slice_reduce_fusion
  535.5 0.2 fusion
  535.7 1.0 copy.42
  536.7 1.0 copy.41
  (4 shorter events, 0.1 us)
Async XLA Ops:
  526.6 7.1 %copy-start.1 = (f32[1,128]{1,0:T(1,128)S(1)}, f32[1,128]{1,0:T(1,128)}, u32[]{:S(2)}) copy-start(f32[1,128]{1,0:T(1,128)} %get-tuple-element.123) | copy-start | bytes 1540
  526.6 7.7 %copy-start = (f32[4,96,384]{2,1,0:T(8,128)S(1)}, f32[4,96,384]{2,1,0:T(8,128)}, u32[]{:S(2)}) copy-start(f32[4,96,384]{2,1,0:T(8,128)} %get-tuple-element.127) | copy-start | bytes 1769476
